TPU v7x, 32 devices: a whole 2x2x4 slice. The times are simulated.
32 devices in a mesh: dp: 8 (over z, y), mp: 4 (over x, core).
Axes of the slice: x: 2, y: 2, z: 4, core: 2. Of those that a mesh axis runs over, the one named last changes fastest.
Arguments:
- weights: bfloat16 [14336, 8, 128], P('mp'), may hold values from -0.1875 to 0.1875
- hidden: bfloat16 [2048, 14336], P('dp', 'mp'), may hold values from -6 to 6
- cotangent: bfloat16 [2048, 8192], P('dp', 'mp'), may hold values from -6 to 6
- sketch: float32 [128, 8192], P(None, ('dp', 'mp')), may hold values from -0.046875 to 0.046875
- projection: float32 [128, 4, 3584], P(None, 'mp', 'dp'), may hold values from -0.046875 to 0.046875
- pattern: int32 [112, 8], P('mp'), may hold values from 0 to 63, as said below
Outputs:
- input_grad: bfloat16 [2048, 14336], P('dp', 'mp')
- direction: float32 [4, 3584, 8, 128], P('mp', 'dp')
Inputs may be any that keep to these rules, and one draw needn't show every extreme that they name: `pattern`: each block row names 8 different column blocks.
All inputs are finite; a program needn't handle non-finite values.
Results may differ from a plain program's by a relative error of at most 0.001.
Values may be sent and summed in bfloat16 or wider, within the bound.
No kernel may reach another device: no remote copies, remote signals or barrier semaphores. Data moves between devices by JAX's collectives and lax.ppermute only.
A program may use at most 192 MiB of HBM per device.

v0:
```python
import math

import jax
import jax.numpy as jnp
from jax import lax
from jax.sharding import PartitionSpec as P

NS_STEPS = 5


shift_eps = 0.0001


def matmul(operand_a, operand_b):
    return jnp.dot(
        operand_a, operand_b, precision=lax.Precision.HIGHEST, preferred_element_type=jnp.float32
    )


def root_factor(gram):
    identity = jnp.eye(gram.shape[0], dtype=jnp.float32)
    shifted = gram + shift_eps * identity
    frobenius = jnp.sqrt(jnp.sum(shifted * shifted))
    root_iter = shifted / frobenius
    inverse_iter = identity
    for iteration in range(NS_STEPS):
        middle = 0.5 * (3.0 * identity - matmul(inverse_iter, root_iter))
        root_iter = matmul(root_iter, middle)
        inverse_iter = matmul(middle, inverse_iter)
    shifted_root = (
        0.5 * jnp.sqrt(frobenius) * (root_iter + root_iter.T) + math.sqrt(shift_eps) * identity
    )
    factor = jnp.linalg.cholesky(shifted_root)
    solved = jax.scipy.linalg.cho_solve((factor, True), inverse_iter.T)
    return -solved.T / (math.sqrt(shift_eps) * jnp.sqrt(frobenius))


def per_device(weights, hidden, cotangent, sketch, projection, pattern):
    highest = lax.Precision.HIGHEST
    tok_rows = hidden.shape[0]
    mp_rows = weights.shape[0]
    slots = weights.shape[1]
    block_size = weights.shape[2]
    block_rows = mp_rows // block_size
    dp_size = lax.axis_size("dp")
    dev_rows = mp_rows // dp_size
    all_tokens = tok_rows * dp_size
    rank = sketch.shape[0]
    full_cot = lax.all_gather(cotangent, "mp", axis=1, tiled=True)
    width = full_cot.shape[1]
    col_blocks = width // block_size
    cot_blocks = full_cot.reshape(tok_rows, col_blocks, block_size)
    chosen = jnp.take(cot_blocks, pattern.reshape(-1), axis=1).reshape(
        tok_rows, block_rows, slots, block_size
    )
    weight_blocks = weights.reshape(block_rows, block_size, slots, block_size)
    input_grad = jnp.einsum(
        "trkn,rikn->tri", chosen, weight_blocks, preferred_element_type=jnp.float32
    )
    input_grad = input_grad.reshape(tok_rows, mp_rows).astype(jnp.bfloat16)
    hidden_blocks = hidden.reshape(tok_rows, block_rows, block_size)
    local_grad = (
        jnp.einsum("tri,trkn->rikn", hidden_blocks, chosen, preferred_element_type=jnp.float32)
        / all_tokens
    )
    local_grad = local_grad.reshape(mp_rows, slots, block_size)
    grad_rows = lax.psum_scatter(local_grad, "dp", scatter_dimension=0, tiled=True)
    group_count = (dev_rows - 1) // block_size + 2
    row_start = lax.axis_index("dp") * dev_rows
    row_block = (row_start + jnp.arange(dev_rows, dtype=jnp.int32)) // block_size
    first_block = row_start // block_size
    group_blocks = first_block + jnp.arange(group_count, dtype=jnp.int32)
    member = (row_block[:, None] == group_blocks[None, :]).astype(jnp.float32)
    group_cols = jnp.take(pattern, jnp.minimum(group_blocks, block_rows - 1), axis=0)
    proj_rows = projection.reshape(rank, dev_rows)
    masked_proj = proj_rows[:, :, None] * member[None, :, :]
    per_group = jnp.einsum("mib,ikn->mbkn", masked_proj, grad_rows, precision=highest)
    start = jnp.zeros((rank, col_blocks, block_size), jnp.float32)
    compress_part = start.at[:, group_cols, :].add(per_group)
    compress_part = compress_part.reshape(rank, width)
    compressed = lax.psum(compress_part, ("dp", "mp"))
    sketch_full = lax.all_gather(sketch, ("dp", "mp"), axis=1, tiled=True)
    stacked = jnp.concatenate([sketch_full, compressed], axis=0)
    gram = matmul(stacked, stacked.T)
    mixing = root_factor(gram)
    stacked_blocks = stacked.reshape(2 * rank, col_blocks, block_size)
    selected = jnp.take(stacked_blocks, group_cols, axis=1)
    projected_all = jnp.einsum("ikn,mbkn->ibm", grad_rows, selected, precision=highest)
    projected = jnp.einsum("ibm,ib->im", projected_all, member, precision=highest)
    mixed = matmul(projected, mixing)
    corr_all = jnp.einsum("im,mbkn->ibkn", mixed, selected, precision=highest)
    correction = jnp.einsum("ibkn,ib->ikn", corr_all, member, precision=highest)
    direction = grad_rows / math.sqrt(shift_eps) + correction
    return (input_grad, direction.reshape(1, dev_rows, slots, block_size))


def solution(mesh):
    return jax.shard_map(
        per_device,
        mesh=mesh,
        in_specs=(
            P("mp", None, None),
            P("dp", "mp"),
            P("dp", "mp"),
            P(None, ("dp", "mp")),
            P(None, "mp", "dp"),
            P("mp", None),
        ),
        out_specs=(P("dp", "mp"), P("mp", "dp", None, None)),
        check_vma=False,
    )
```

profile of v0, /device:TPU:0, one launch (start us, length us, event | category | flops | bytes accessed | tf_op | source)
XLA Modules:
  0.0 673.6 jit_solution(13117200124326443357)
XLA Ops:
  15.0 33.2 %all-gather.3.cloned.1.call-done = bf16[256,8192]{0,1:T(8,128)(2,1)} async-done(((bf16[256,2048]{0,1:T(8,128)(2,1)}), bf16[256,8192]{0,1:T(8,128)(2,1)}) %all-gather.3.cloned.1.call-update) | async-done | bytes 4194320 | tf_op jit(solution)/shard_map/all_gather | solution.py:49
  48.2 6.4 copy.30
  54.6 11.4 %gather_fusion = bf16[224,256,128]{2,1,0:T(8,128)(2,1)} fusion(bf16[256,64,128]{2,0,1:T(8,128)(2,1)} %copy.30, s32[1024]{0:T(1024)S(1)} %pad_clamp_fusion.2), kind=kCustom, calls=%fused_computation | custom fusion | bytes 29361024 | tf_op jit(solution)/shard_map/jit(_take)/gather | solution.py:53
  66.0 10.4 %multiply_bitcast_fusion = f32[28,128,8,128]{3,1,2,0:T(8,128)} fusion(bf16[256,28,128,1]{0,2,3,1:T(8,128)(2,1)S(1)} %bitcast.153, bf16[256,28,8,128]{3,0,2,1:T(8,128)(2,1)} %bitcast.146, pred[28,8]{1,0:T(8,128)(4,1)S(1)} %copy.27), kind=kOutput, calls=%fused_computation.8 | convolution fusion | flops 1890058240 | bytes 31195360 | tf_op jit(solution)/shard_map/tri,trkn->rikn/dot_general | solution.py:63
  76.4 23.7 %copy.33 = f32[28,128,8,128]{3,2,1,0:T(8,128)} copy(f32[28,128,8,128]{3,1,2,0:T(8,128)} %multiply_bitcast_fusion) | data formatting | bytes 29360128 | tf_op jit(solution)/shard_map/div | solution.py:63
  103.6 243.6 %reduce-scatter.2.cloned.1.call-done = f32[448,8,128]{2,1,0:T(8,128)} async-done(((f32[3584,8,128]{2,1,0:T(8,128)}), f32[448,8,128]{2,1,0:T(8,128)}) %reduce-scatter.2.cloned.1.call-update) | async-done | bytes 1835024 | tf_op jit(solution)/shard_map/reduce_scatter | solution.py:67
  347.2 6.1 fusion.22
  355.8 9.7 %scatter_fusion = f32[128,64,128]{2,0,1:T(8,128)} fusion(f32[128,64,128]{2,0,1:T(8,128)} %broadcast_in_dim.48, s32[40]{0:T(128)S(1)} %reshape.270, f32[40,128,128]{2,1,0:T(8,128)S(1)} %bitcast.154), kind=kCustom, calls=%fused_computation.3 | custom fusion | flops 655360 | bytes 7864480 | tf_op jit(solution)/shard_map/scatter-add | solution.py:79
  365.5 5.6 copy.37
  371.2 10.5 %bitcast_convert_fusion = bf16[28,256,128]{1,2,0:T(8,128)(2,1)S(1)} fusion(bf16[28,128,8,128]{3,2,1,0:T(8,128)(2,1)} %bitcast.159, bf16[256,28,8,128]{3,0,2,1:T(8,128)(2,1)} %bitcast.147, pred[28,8]{1,0:T(8,128)(4,1)S(1)} %copy.27), kind=kOutput, calls=%fused_computation.21 | convolution fusion | flops 1887305728 | bytes 23855328 | tf_op jit(solution)/shard_map/trkn,rikn->tri/dot_general | solution.py:57
  384.3 4.5 constant_dynamic-update-slice_fusion.1
  388.8 123.4 %all-reduce.3.cloned.1.call-done = f32[128,8192]{0,1:T(8,128)} async-done(((f32[128,8192]{0,1:T(8,128)}), f32[128,8192]{0,1:T(8,128)}) %all-reduce.3.cloned.1.call-update) | async-done | bytes 4194320 | tf_op jit(solution)/shard_map/psum | solution.py:81
  512.2 4.5 constant_dynamic-update-slice_fusion
  516.6 20.1 %multiply_reduce_fusion = (f32[]{:T(128)}, f32[256,256]{1,0:T(8,128)S(1)}) fusion(f32[256,8192]{0,1:T(8,128)} %constant_dynamic-update-slice_fusion), kind=kOutput, calls=%fused_computation.65 | convolution fusion | flops 6442778624 | bytes 8650756 | tf_op jit(solution)/shard_map/dot_general | solution.py:15
  543.6 11.7 %cholesky.49 = f32[128,128]{1,0:T(8,128)S(1)} custom-call(f32[128,128]{1,0:T(8,128)S(1)} %cholesky.115), custom_call_target="Cholesky" | custom-call | tf_op jit(solution)/shard_map/jit(cholesky)/cholesky | solution.py:33
  555.4 9.2 %copy.38 = f32[256,64,128]{2,0,1:T(8,128)} copy(f32[256,64,128]{0,2,1:T(8,128)} %bitcast.145) | data formatting | bytes 16777216 | tf_op jit(solution)/shard_map/reshape | solution.py:86
  564.6 9.8 %custom-call.18 = f32[1,128,128]{1,2,0:T(8,128)S(1)} custom-call(f32[1,128,128]{2,1,0:T(8,128)S(1)} %get-tuple-element.29), custom_call_target="InvertDiagBlocksLowerTriangular" | custom-call | tf_op jit(solution)/shard_map/jit(cholesky)/cholesky | solution.py:33
  574.9 11.7 %cholesky.103 = f32[128,128]{1,0:T(8,128)S(1)} custom-call(f32[128,128]{1,0:T(8,128)S(1)} %convolution_subtract_fusion.7), custom_call_target="Cholesky" | custom-call | tf_op jit(solution)/shard_map/jit(cholesky)/cholesky | solution.py:33
  588.7 3.9 while.1
  592.6 20.1 %custom-call.19 = f32[2,128,128]{1,2,0:T(8,128)S(1)} custom-call(f32[2,128,128]{2,1,0:T(8,128)S(1)} %get-tuple-element.9), custom_call_target="InvertDiagBlocksLowerTriangular" | custom-call | tf_op jit(solution)/shard_map/jit(_cho_solve)/triangular_solve | solution.py:34
  614.5 6.8 %gather_fusion.2 = f32[40,256,128]{2,1,0:T(8,128)} fusion(f32[256,64,128]{2,0,1:T(8,128)} %copy.38, s32[1024]{0:T(1024)S(1)} %pad_clamp_fusion), kind=kCustom, calls=%fused_computation.2 | custom fusion | bytes 10485920 | tf_op jit(solution)/shard_map/jit(_take)/gather | solution.py:87
  621.3 10.5 %fusion.26 = f32[448,5,256]{2,0,1:T(8,128)S(1)} fusion(f32[448,8,128]{2,1,0:T(8,128)S(1)} %copy-done.1, f32[5,8,256,128]{3,2,1,0:T(8,128)} %bitcast.149, pred[5,8]{1,0:T(8,128)(4,1)S(1)} %compare_and_fusion), kind=kOutput, calls=%fused_computation.34 | convolution fusion | flops 7047741440 | bytes 9371688 | tf_op jit(solution)/shard_map/ikn,mbkn->ibm/dot_general | solution.py:88
  636.0 8.7 %fusion.7 = f32[448,5,8,128]{3,0,2,1:T(8,128)S(1)} fusion(f32[448,256,1,1]{1,0,3,2:T(8,128)S(1)} %convolution_bitcast_fusion, f32[5,8,256,128]{3,2,1,0:T(8,128)S(1)} %bitcast.150, pred[5,8]{1,0:T(8,128)(4,1)S(1)} %compare_and_fusion), kind=kOutput, calls=%fused_computation.15 | convolution fusion | flops 7047741440 | bytes 14876712 | tf_op jit(solution)/shard_map/im,mbkn->ibkn/dot_general | solution.py:91
  644.7 19.8 %fusion = f32[448,1,8,128]{3,1,2,0:T(1,128)S(1)} fusion(pred[448,5,1,1]{1,2,3,0:T(4,128)(4,1)S(1)} %copy.51, f32[448,5,8,128]{3,0,2,1:T(8,128)S(1)} %fusion.7), kind=kOutput, calls=%fused_computation.6 | convolution fusion | flops 27525120 | bytes 11012288 | tf_op jit(solution)/shard_map/ibkn,ib->ikn/dot_general | solution.py:92
  (84 shorter events, 34.0 us)
Async XLA Ops:
  8.0 40.2 %all-gather.3.cloned.1.call-start = ((), (), s32[]{:S(2)}) async-start(), calls=%async_computation.1 | async-start | bytes 5242880 | tf_op jit(solution)/shard_map/all_gather | solution.py:49
  10.3 336.9 %reduce-scatter.2.cloned.1.call-start = ((), (), s32[]{:S(2)}) async-start(), calls=%async_computation.2 | async-start | bytes 16515072 | tf_op jit(solution)/shard_map/reduce_scatter | solution.py:67
  100.1 0.9 copy-start.3
  100.1 247.1 %copy-start.2 = (f32[128,1,448]{0,2,1:T(8,128)S(1)}, f32[128,1,448]{0,2,1:T(8,128)}, u32[]{:S(2)}) copy-start(f32[128,1,448]{0,2,1:T(8,128)} %param.10) | copy-start | bytes 688132
  100.1 284.2 %all-gather.5.cloned.1.call-start = ((), (), s32[]{:S(2)}) async-start(), calls=%async_computation.3 | async-start | bytes 4325376 | tf_op jit(solution)/shard_map/all_gather | solution.py:82
  101.7 410.4 %all-reduce.3.cloned.1.call-start = ((), (), s32[]{:S(2)}) async-start(), calls=%async_computation.4 | async-start | bytes 8388608 | tf_op jit(solution)/shard_map/psum | solution.py:81
  614.5 6.8 %copy-start.1 = (f32[448,8,128]{2,1,0:T(8,128)S(1)}, f32[448,8,128]{2,1,0:T(8,128)}, u32[]{:S(2)}) copy-start(f32[448,8,128]{2,1,0:T(8,128)} %reduce-scatter.2.cloned.1.call-done) | copy-start | bytes 5505028
  631.8 4.2 copy-start
Sparse Core Ops, SparseCore 0:
  11.0 37.1 all-gather.2
  100.2 246.9 reduce-scatter.1
Sparse Core Ops, SparseCore 1:
  104.0 157.3 all-gather.4
  371.2 140.9 all-reduce.2
where the time goes:
time: 678 us; the launch traced here: 674 us
  waiting for transfers between devices  400 us (59%)
  matrix products  98.2 us (14%)
  local copies, waits for them, and re-layouts  90.4 us (13%)
  other arithmetic  66.4 us (10%)
  between operations  18.2 us (3%)
    reduce_scatter x1, waiting for transfers between devices, per_device(): lax.psum_scatter(local_grad, 'dp', scatter_dimension=0, tiled=True)  244 us
    psum x1, waiting for transfers between devices, per_device(): compressed = lax.psum(compress_part, ('dp', 'mp'))  123 us
    another operation x6, other arithmetic, root_factor(): factor = jnp.linalg.cholesky(shifted_root)  34 us
    all_gather x1, waiting for transfers between devices, per_device(): full_cot = lax.all_gather(cotangent, 'mp', axis=1, tiled=True)  33.2 us
    dot_general x17, matrix products, matmul(): jnp.dot(operand_a, operand_b, precision=lax.Precision.HIGHEST, preferred_...  26.5 us
    div x1, local copies, waits for them, and re-layouts, per_device(): jnp.einsum('tri,trkn->rikn', hidden_blocks, chosen, preferred_element_typ...  23.7 us
    another operation x3, other arithmetic, root_factor(): solved = jax.scipy.linalg.cho_solve((factor, True), inverse_iter.T)  20.1 us
    dot_general x1, matrix products, per_device(): correction = jnp.einsum('ibkn,ib->ikn', corr_all, member, precision=highest)  19.8 us
  transfers between devices with their start and end apart: 4, of which 3 were waited for; matrix products, arithmetic and copies ran while one was open for 7% of the time, Pallas kernels for 0%

commit v1 on v0

v1 whole, which is shorter than its diff:
```python
import functools
import math

import jax
import jax.numpy as jnp
from jax import lax
from jax.experimental import pallas as pl
from jax.experimental.pallas import tpu as pltpu
from jax.sharding import PartitionSpec as P

NS_STEPS = 5
SHIFT_EPS = 0.0001
PROJ_SCALE = 1024.0

BF = jnp.bfloat16
F16 = jnp.float16
F32 = jnp.float32
HIGHEST = lax.Precision.HIGHEST
VMEM = pl.BlockSpec(memory_space=pltpu.VMEM)
ANY = pl.BlockSpec(memory_space=pl.ANY)


def params(mib=48):
    return pltpu.CompilerParams(vmem_limit_bytes=mib * 1024 * 1024)


def dot(a, b):
    return jnp.dot(a, b, preferred_element_type=F32)


def dot_nt(a, b):
    return lax.dot_general(a, b, (((1,), (1,)), ((), ())), preferred_element_type=F32)


def split2(value):
    high = value.astype(BF)
    return high, (value - high.astype(F32)).astype(BF)


def split2_xla(value):
    high = lax.reduce_precision(value, exponent_bits=8, mantissa_bits=7)
    return high.astype(BF), (value - high).astype(BF)


def load_shards(shard_refs, held, sems):
    copies = [
        pltpu.make_async_copy(ref, held.at[i], sems.at[i]) for i, ref in enumerate(shard_refs)
    ]
    for copy in copies:
        copy.start()
    for copy in copies:
        copy.wait()


def column_block(held, base, block, per_shard, block_size):
    shard = block // per_shard
    offset = pl.multiple_of((block - shard * per_shard) * block_size, block_size)
    return held[base + shard, :, pl.ds(offset, block_size)]


def compress_kernel(n_shards, per_shard, scale, pat, *refs):
    shards = refs[:n_shards]
    hid_ref, ph_ref, pl_ref, out_ref, held, sems = refs[n_shards:]
    row = pl.program_id(0)
    blk = out_ref.shape[1]

    @pl.when(row == 0)
    def _():
        load_shards(shards, held, sems)
        out_ref[...] = jnp.zeros_like(out_ref)

    hid = hid_ref[...]
    q = dot(ph_ref[...], hid) + dot(pl_ref[...], hid)
    left = jnp.concatenate(split2(q * scale), axis=0)
    slots = 8
    for j in range(0, slots, 2):
        c0, c1 = pat[row * slots + j], pat[row * slots + j + 1]
        chosen = jnp.concatenate(
            [column_block(held, 0, c, per_shard, blk) for c in (c0, c1)], axis=1
        )
        part = dot(left, chosen)
        part = part[:blk] + part[blk:]
        out_ref[c0] += part[:, :blk]
        out_ref[c1] += part[:, blk:]


def grad_kernel(n_shards, per_shard, blk, pat, *refs):
    shards = refs[: 2 * n_shards]
    own_ref, got_ref, out_ref, top_ref, held, sems = refs[2 * n_shards :]
    row = pl.program_id(0)

    @pl.when(row == 0)
    def _():
        load_shards(shards, held, sems)
        top_ref[...] = jnp.zeros_like(top_ref)

    own, got = own_ref[...].astype(BF), got_ref[...].astype(BF)
    slots = 8
    top = top_ref[...]
    for j in range(0, slots, 2):
        cs = (pat[row * slots + j], pat[row * slots + j + 1])
        part = None
        for base, hid in ((0, own), (n_shards, got)):
            chosen = jnp.concatenate(
                [column_block(held, base, c, per_shard, blk) for c in cs], axis=1
            )
            term = dot(hid, chosen)
            part = term if part is None else part + term
        out_ref[:, j * blk : (j + 2) * blk] = part
        size = jnp.abs(part)
        for i in range(0, part.shape[0], 8):
            top = jnp.maximum(top, size[i : i + 8])
    top_ref[...] = top


def input_grad_kernel(n_shards, per_shard, blk, pat, *refs):
    shards = refs[:n_shards]
    w_ref, out_ref, held, sems = refs[n_shards:]
    row = pl.program_id(0)

    @pl.when(row == 0)
    def _():
        load_shards(shards, held, sems)

    slots = 8
    chosen = jnp.concatenate(
        [column_block(held, 0, pat[row * slots + j], per_shard, blk) for j in range(slots)], axis=1
    )
    out_ref[...] = dot_nt(chosen, w_ref[...]).astype(BF)


def sketch_gram_kernel(sh_ref, sl_ref, out_ref):
    out_ref[...] = jnp.zeros_like(out_ref)
    for s in range(sh_ref.shape[0]):
        high, low = sh_ref[s], sl_ref[s]
        out_ref[...] += dot_nt(high, high) + (dot_nt(high, low) + dot_nt(low, high))


def cross_gram_kernel(ch_ref, cl_ref, sh_ref, sl_ref, out_ref):
    rank = ch_ref.shape[1]
    per = ch_ref.shape[0] // sh_ref.shape[0]
    with_sketch = jnp.zeros((rank, rank), F32)
    with_self = jnp.zeros((rank, rank), F32)
    for s in range(sh_ref.shape[0]):
        high = jnp.concatenate([ch_ref[per * s + b] for b in range(per)], axis=1)
        low = jnp.concatenate([cl_ref[per * s + b] for b in range(per)], axis=1)
        sh, sl = sh_ref[s], sl_ref[s]
        with_sketch += dot_nt(high, sh) + (dot_nt(high, sl) + dot_nt(low, sh))
        with_self += dot_nt(high, high) + (dot_nt(high, low) + dot_nt(low, high))
    out_ref[:, :rank] = with_sketch
    out_ref[:, rank:] = with_self


def mixing_kernel(ss_ref, cross_ref, out_ref):
    rank = ss_ref.shape[0]
    size = 2 * rank
    sqrt_eps = math.sqrt(SHIFT_EPS)

    def mm(a, b):
        return jnp.dot(a, b, precision=HIGHEST, preferred_element_type=F32)

    cross = cross_ref[...]
    gram = jnp.concatenate(
        [jnp.concatenate([ss_ref[...], cross[:, :rank].T], axis=1), cross], axis=0
    )
    rows = lax.broadcasted_iota(jnp.int32, (size, size), 0)
    cols = lax.broadcasted_iota(jnp.int32, (size, size), 1)
    identity = jnp.where(rows == cols, 1.0, 0.0).astype(F32)
    shifted = gram + SHIFT_EPS * identity
    frobenius = jnp.sqrt(jnp.sum(shifted * shifted, keepdims=True))
    root = shifted / frobenius
    inverse = identity
    for step in range(NS_STEPS):
        product = root if step == 0 else mm(inverse, root)
        middle = 0.5 * (3.0 * identity - product)
        root = mm(root, middle)
        inverse = middle if step == 0 else mm(middle, inverse)
    sqrt_fro = jnp.sqrt(frobenius)
    half = 0.5 * sqrt_fro * (root + root.T) + sqrt_eps * identity
    guess = inverse / (sqrt_fro + sqrt_eps * 1.5**NS_STEPS)

    def residual(x):
        r = identity - mm(half, x)
        return r, jnp.max(jnp.abs(r))

    def keep_going(state):
        return jnp.logical_and(state[3] < 48, state[2] > 2e-6)

    def improve(state):
        x, r, _, count = state
        x = x + mm(x, r)
        r, size = residual(x)
        return x, r, size, count + 1

    r, top = residual(guess)
    x, r, _, _ = lax.while_loop(keep_going, improve, (guess, r, top, jnp.int32(0)))
    x = x + mm(x, r)
    out_ref[...] = -mm(inverse, x) / (sqrt_eps * sqrt_fro)


def gathered(held_sk, held_cp, c_sk, c_cp, blk, per):
    shard = c_sk // per
    offset = pl.multiple_of((c_sk - shard * per) * blk, blk)
    return held_sk[shard, :, pl.ds(offset, blk)], held_cp[c_cp]


def project_kernel(per, pat_sk, pat_cp, g_ref, skh, skl, cph, cpl, out_ref):
    row = pl.program_id(0)
    blk = cph.shape[1]
    slots = 8
    rows = g_ref.shape[0]
    total = jnp.zeros(out_ref.shape, F32)
    for k in range(slots):
        c_sk, c_cp = pat_sk[row * slots + k], pat_cp[row * slots + k]
        high = jnp.concatenate(gathered(skh, cph, c_sk, c_cp, blk, per), axis=0)
        low = jnp.concatenate(gathered(skl, cpl, c_sk, c_cp, blk, per), axis=0)
        g = g_ref[:, k * blk : (k + 1) * blk]
        gh = g.astype(BF).astype(F32)
        both = dot_nt(jnp.concatenate([gh, g - gh], axis=0).astype(BF), high)
        total += both[:rows] + both[rows:] + dot_nt(g.astype(BF), low)
    out_ref[...] = total


def direction_kernel(per, pat_sk, pat_cp, g_ref, p_ref, m_ref, skh, skl, cph, cpl, out_ref):
    row = pl.program_id(0)
    blk = cph.shape[1]
    slots = 8
    rows = g_ref.shape[0]
    mixed = jnp.dot(p_ref[...], m_ref[...], precision=HIGHEST, preferred_element_type=F32)
    mixed_high = mixed.astype(BF).astype(F32)
    stacked = jnp.concatenate([mixed_high, mixed - mixed_high], axis=0).astype(BF)
    mixed_bf = mixed.astype(BF)
    for k in range(slots):
        c_sk, c_cp = pat_sk[row * slots + k], pat_cp[row * slots + k]
        high = jnp.concatenate(gathered(skh, cph, c_sk, c_cp, blk, per), axis=0)
        low = jnp.concatenate(gathered(skl, cpl, c_sk, c_cp, blk, per), axis=0)
        both = dot(stacked, high)
        corr = both[:rows] + both[rows:] + dot(mixed_bf, low)
        out_ref[:, k, :] = g_ref[:, k * blk : (k + 1) * blk] * (1.0 / math.sqrt(SHIFT_EPS)) + corr


def cost(flops, moved):
    return pl.CostEstimate(flops=int(flops), bytes_accessed=int(moved), transcendentals=0)


def per_device(weights, hidden, cotangent, sketch, projection, pattern):
    tok_rows = hidden.shape[0]
    mp_rows, slots, blk = weights.shape
    block_rows = mp_rows // blk
    n_dp, n_mp = lax.axis_size("dp"), lax.axis_size("mp")
    dev_rows = mp_rows // n_dp
    all_tokens = tok_rows * n_dp
    rank = sketch.shape[0]
    shard_cols = cotangent.shape[1]
    per_shard = shard_cols // blk
    col_blocks = per_shard * n_mp
    outer = n_dp // 2
    dp, mp = lax.axis_index("dp"), lax.axis_index("mp")
    side = dp % 2

    def swap(x, axis, bit):
        size = lax.axis_size(axis)
        return lax.ppermute(x, axis, [(i, i ^ bit) for i in range(size)])

    x_half = swap(cotangent, "mp", 2)
    y_own = swap(cotangent, "dp", 1)
    own = [cotangent, swap(cotangent, "mp", 1), x_half, swap(x_half, "mp", 1)]
    pattern_rel = jnp.bitwise_xor(pattern, mp * per_shard)

    proj16 = (projection.reshape(rank, dev_rows) * PROJ_SCALE).astype(F16)
    proj_all = lax.all_to_all(
        jnp.broadcast_to(proj16[None], (n_dp, rank, dev_rows)), "dp", 0, 0
    )
    proj_all = proj_all.transpose(1, 0, 2).reshape(rank, mp_rows).astype(F32)
    proj_high, proj_low = split2_xla(proj_all)
    sketch_all = lax.all_gather(sketch.astype(F16), ("dp", "mp"), axis=0, tiled=False)
    width = sketch_all.shape[2]
    if width < blk:
        sketch_all = sketch_all.reshape(col_blocks, blk // width, rank, width)
        sketch_all = sketch_all.transpose(0, 2, 1, 3).reshape(col_blocks, rank, blk)
    sk_high, sk_low = split2_xla(sketch_all.astype(F32))

    hid_t = hidden.T
    hid_parts = hid_t.reshape(outer, 2, dev_rows, tok_rows)
    hid_own = lax.dynamic_index_in_dim(hid_parts, side, 1, keepdims=False)
    hid_send = lax.dynamic_index_in_dim(hid_parts, 1 - side, 1, keepdims=False)

    scratch = lambda n: [
        pltpu.VMEM((n, tok_rows, shard_cols), BF),
        pltpu.SemaphoreType.DMA((n,)),
    ]
    pat_all = pattern_rel.reshape(-1)
    partial_c = pl.pallas_call(
        functools.partial(
            compress_kernel, n_mp, per_shard, 1.0 / (PROJ_SCALE * all_tokens)
        ),
        grid_spec=pltpu.PrefetchScalarGridSpec(
            num_scalar_prefetch=1,
            grid=(block_rows,),
            in_specs=[ANY] * n_mp
            + [
                pl.BlockSpec((blk, tok_rows), lambda i, pat: (i, 0)),
                pl.BlockSpec((rank, blk), lambda i, pat: (0, i)),
                pl.BlockSpec((rank, blk), lambda i, pat: (0, i)),
            ],
            out_specs=pl.BlockSpec((col_blocks, rank, blk), lambda i, pat: (0, 0, 0)),
            scratch_shapes=scratch(n_mp),
        ),
        out_shape=jax.ShapeDtypeStruct((col_blocks, rank, blk), F32),
        compiler_params=params(),
        cost_estimate=cost(4 * mp_rows * slots * blk * tok_rows, 12 << 20),
        name="compress",
    )(pat_all, *own, hid_t, proj_high, proj_low)

    quarters = partial_c.reshape(n_mp, per_shard, rank, blk)
    keep = jnp.stack([quarters[0], quarters[2]])
    sent = swap(jnp.stack([quarters[1], quarters[3]]).astype(F16), "mp", 1)
    keep = keep + sent.astype(F32)
    quarter = keep[0] + swap(keep[1].astype(F16), "mp", 2).astype(F32)
    pieces = quarter.astype(F16).reshape(n_dp, per_shard * rank // n_dp, blk)
    pieces = lax.all_to_all(pieces, "dp", 0, 0)
    piece = jnp.sum(pieces.astype(F32), axis=0).astype(F16)
    quarter16 = lax.all_to_all(jnp.broadcast_to(piece[None], pieces.shape), "dp", 0, 0)
    quarter16 = quarter16.reshape(per_shard, rank, blk)

    sk_per = sk_high.shape[2] // blk
    sk_quarter = col_blocks // sk_per // n_mp
    qh, ql = split2_xla(quarter16.astype(F32))
    cross = pl.pallas_call(
        cross_gram_kernel,
        in_specs=[VMEM] * 4,
        out_specs=VMEM,
        out_shape=jax.ShapeDtypeStruct((rank, 2 * rank), F32),
        compiler_params=params(),
        name="cross_gram",
    )(
        qh,
        ql,
        lax.dynamic_slice_in_dim(sk_high, mp * sk_quarter, sk_quarter, 0),
        lax.dynamic_slice_in_dim(sk_low, mp * sk_quarter, sk_quarter, 0),
    )
    sketch_gram = pl.pallas_call(
        sketch_gram_kernel,
        in_specs=[VMEM] * 2,
        out_specs=VMEM,
        out_shape=jax.ShapeDtypeStruct((rank, rank), F32),
        compiler_params=params(),
        cost_estimate=cost(6 * rank * rank * col_blocks * blk, 4 << 20),
        name="sketch_gram",
    )(sk_high, sk_low)
    cross = cross + swap(cross, "mp", 2)
    cross = cross + swap(cross, "mp", 1)
    mixing = pl.pallas_call(
        mixing_kernel,
        in_specs=[VMEM] * 2,
        out_specs=VMEM,
        out_shape=jax.ShapeDtypeStruct((2 * rank, 2 * rank), F32),
        compiler_params=params(),
        cost_estimate=cost(30 * 12 * (2 * rank) ** 3, 1 << 20),
        name="mixing",
    )(sketch_gram, cross)

    far = swap(quarter16, "mp", 2)
    near = swap(jnp.stack([quarter16, far]), "mp", 1)
    comp16 = jnp.stack([quarter16, near[0], far, near[1]]).reshape(col_blocks, rank, blk)
    cp_high, cp_low = split2_xla(comp16.astype(F32))

    y_x = swap(y_own, "mp", 2)
    y_group = [y_own, swap(y_own, "mp", 1), y_x, swap(y_x, "mp", 1)]
    hid_send, _ = lax.optimization_barrier((hid_send, y_own))
    hid_got = swap(hid_send, "dp", 1)
    group = math.gcd(dev_rows, blk)
    per_dev = dev_rows // group
    half_rows = outer * dev_rows
    hid_type = BF if group % 16 == 0 else F32
    group_start = (
        (2 * jnp.arange(outer, dtype=jnp.int32) + side)[:, None] * dev_rows
        + group * jnp.arange(per_dev, dtype=jnp.int32)[None, :]
    )
    pat_half = jnp.take(pattern_rel, (group_start // blk).reshape(-1), axis=0).reshape(-1)
    grad_half, top = pl.pallas_call(
        functools.partial(grad_kernel, n_mp, per_shard, blk),
        grid_spec=pltpu.PrefetchScalarGridSpec(
            num_scalar_prefetch=1,
            grid=(outer * per_dev,),
            in_specs=[ANY] * (2 * n_mp)
            + [pl.BlockSpec((group, tok_rows), lambda i, pat: (i, 0))] * 2,
            out_specs=[
                pl.BlockSpec((group, slots * blk), lambda i, pat: (i, 0)),
                pl.BlockSpec((8, 2 * blk), lambda i, pat: (0, 0)),
            ],
            scratch_shapes=scratch(2 * n_mp),
        ),
        out_shape=[
            jax.ShapeDtypeStruct((half_rows, slots * blk), F32),
            jax.ShapeDtypeStruct((8, 2 * blk), F32),
        ],
        compiler_params=params(),
        cost_estimate=cost(4 * half_rows * slots * blk * tok_rows, 18 << 20),
        name="pair_grad",
    )(
        pat_half,
        *own,
        *y_group,
        hid_own.reshape(half_rows, tok_rows).astype(hid_type),
        hid_got.reshape(half_rows, tok_rows).astype(hid_type),
    )
    biggest = jnp.maximum(jnp.max(top), 1e-30)
    scale = 16384.0 / biggest
    packed = (grad_half * scale).astype(F16).reshape(outer, dev_rows, slots * blk)
    lanes = [[2 * i + s for i in range(outer)] for s in range(2)]
    packed = lax.all_to_all(packed, "dp", 0, 0, axis_index_groups=lanes)
    unscale = lax.all_to_all(
        jnp.broadcast_to(biggest / (16384.0 * all_tokens), (outer, 8, 128)),
        "dp", 0, 0, axis_index_groups=lanes,
    )
    grad = jnp.sum(packed.astype(F32) * unscale[:, :1, :1], axis=0)

    input_grad = pl.pallas_call(
        functools.partial(input_grad_kernel, n_mp, per_shard, blk),
        grid_spec=pltpu.PrefetchScalarGridSpec(
            num_scalar_prefetch=1,
            grid=(block_rows,),
            in_specs=[ANY] * n_mp + [pl.BlockSpec((blk, slots * blk), lambda i, pat: (i, 0))],
            out_specs=pl.BlockSpec((tok_rows, blk), lambda i, pat: (0, i)),
            scratch_shapes=scratch(n_mp),
        ),
        out_shape=jax.ShapeDtypeStruct((tok_rows, mp_rows), BF),
        compiler_params=params(),
        cost_estimate=cost(2 * mp_rows * slots * blk * tok_rows, 14 << 20),
        name="input_grad",
    )(pat_all, *own, weights.reshape(mp_rows, slots * blk))

    my_start = dp * dev_rows + group * jnp.arange(per_dev, dtype=jnp.int32)
    pat_abs = jnp.take(pattern, my_start // blk, axis=0).reshape(-1)
    pat_rel = jnp.bitwise_xor(pat_abs, mp * per_shard)
    projected = pl.pallas_call(
        functools.partial(project_kernel, sk_per),
        grid_spec=pltpu.PrefetchScalarGridSpec(
            num_scalar_prefetch=2,
            grid=(per_dev,),
            in_specs=[pl.BlockSpec((group, slots * blk), lambda i, a, b: (i, 0))] + [VMEM] * 4,
            out_specs=pl.BlockSpec((group, 2 * rank), lambda i, a, b: (i, 0)),
        ),
        out_shape=jax.ShapeDtypeStruct((dev_rows, 2 * rank), F32),
        compiler_params=params(),
        cost_estimate=cost(6 * dev_rows * slots * blk * 2 * rank, 12 << 20),
        name="project",
    )(pat_abs, pat_rel, grad, sk_high, sk_low, cp_high, cp_low)
    direction = pl.pallas_call(
        functools.partial(direction_kernel, sk_per),
        grid_spec=pltpu.PrefetchScalarGridSpec(
            num_scalar_prefetch=2,
            grid=(per_dev,),
            in_specs=[
                pl.BlockSpec((group, slots * blk), lambda i, a, b: (i, 0)),
                pl.BlockSpec((group, 2 * rank), lambda i, a, b: (i, 0)),
            ]
            + [VMEM] * 5,
            out_specs=pl.BlockSpec((group, slots, blk), lambda i, a, b: (i, 0, 0)),
        ),
        out_shape=jax.ShapeDtypeStruct((dev_rows, slots, blk), F32),
        compiler_params=params(),
        cost_estimate=cost(6 * dev_rows * slots * blk * 2 * rank, 14 << 20),
        name="direction",
    )(pat_abs, pat_rel, grad, projected, mixing, sk_high, sk_low, cp_high, cp_low)
    return (input_grad, direction.reshape(1, dev_rows, slots, blk))


def solution(mesh):
    return jax.shard_map(
        per_device,
        mesh=mesh,
        in_specs=(
            P("mp", None, None),
            P("dp", "mp"),
            P("dp", "mp"),
            P(None, ("dp", "mp")),
            P(None, "mp", "dp"),
            P("mp", None),
        ),
        out_specs=(P("dp", "mp"), P("mp", "dp", None, None)),
        check_vma=False,
    )
```

time: 678 us -> 388 us (0.57)
  waiting for transfers between devices: 400 us -> 67.1 us
  blocking collectives: 0 us -> 107 us
  Pallas kernels: 0 us -> 103 us
  matrix products: 98.2 us -> 0 us
  local copies, waits for them, and re-layouts: 90.4 us -> 26.6 us
  starting transfers between devices: 0.17 us -> 41.5 us
  other arithmetic: 66.4 us -> 33.5 us
  between operations: 18.2 us -> 1.75 us
    reduce_scatter x1 -> x0, waiting for transfers between devices: 244 us -> none  [per_device(): lax.psum_scatter(local_grad, 'dp', scatter_dimension=0, tiled=True)]
    psum x1 -> x0, waiting for transfers between devices: 123 us -> none  [per_device(): compressed = lax.psum(compress_part, ('dp', 'mp'))]
    all_gather x0 -> x1, blocking collectives: none -> 107 us  [per_device(): lax.all_gather(sketch.astype(F16), ('dp', 'mp'), axis=0, tiled=False)]
    pallas_call x0 -> x8, Pallas kernels: none -> 103 us  [the longest x1 22.9 us: per_device(): pl.pallas_call(functools.partial(compress_kernel, n_mp, per_shard, 1.0 /...]
    dot_general x24 -> x0, matrix products: 96 us -> none  [the longest x17 26.5 us: matmul(): jnp.dot(operand_a, operand_b, precision=lax.Precision.HIGHEST, preferred_...]
    ppermute x0 -> x14, waiting for transfers between devices: none -> 56.4 us  [swap(): return lax.ppermute(x, axis, [(i, i ^ bit) for i in range(size)])]
    another operation x9 -> x4, other arithmetic: 54.1 us -> 6.46 us  [the longest x6 34 us: root_factor(): factor = jnp.linalg.cholesky(shifted_root)]
    all_gather x2 -> x0, waiting for transfers between devices: 33.2 us -> none  [the longest x1 33.2 us: per_device(): full_cot = lax.all_gather(cotangent, 'mp', axis=1, tiled=True)]
  transfers between devices with their start and end apart: 4 -> 19, of which waited for: 3 -> 7; matrix products, arithmetic and copies ran while one was open for 7% -> 13% of each run, Pallas kernels for 0% -> 23%
where the time goes in v1:
time: 388 us; the launch traced here: 381 us
  blocking collectives  107 us (28%)
  Pallas kernels  103 us (27%)
  waiting for transfers between devices  67.1 us (17%)
  starting transfers between devices  41.5 us (11%)
  other arithmetic  33.5 us (9%)
  local copies, waits for them, and re-layouts  26.6 us (7%)
    all_gather x1, blocking collectives, per_device(): lax.all_gather(sketch.astype(F16), ('dp', 'mp'), axis=0, tiled=False)  107 us
    ppermute x14, waiting for transfers between devices, swap(): return lax.ppermute(x, axis, [(i, i ^ bit) for i in range(size)])  56.4 us
    pallas_call x1, Pallas kernels, per_device(): pl.pallas_call(functools.partial(compress_kernel, n_mp, per_shard, 1.0 /...  22.9 us
    pallas_call x1, Pallas kernels, per_device(): pl.pallas_call(functools.partial(grad_kernel, n_mp, per_shard, blk), grid...  22.7 us
    pallas_call x1, Pallas kernels, per_device(): pl.pallas_call(functools.partial(input_grad_kernel, n_mp, per_shard, blk)...  21.8 us
    pallas_call x1, Pallas kernels, per_device(): pl.pallas_call(mixing_kernel, in_specs=[VMEM] * 2, out_specs=VMEM, out_sh...  16 us
    unnamed x31, local copies, waits for them, and re-layouts  14.8 us
    ppermute x14, starting transfers between devices, swap(): return lax.ppermute(x, axis, [(i, i ^ bit) for i in range(size)])  14.4 us
  transfers between devices with their start and end apart: 19, of which 7 were waited for; matrix products, arithmetic and copies ran while one was open for 13% of the time, Pallas kernels for 23%

profile of v1, /device:TPU:0, one launch (start us, length us, event | category | flops | bytes accessed | tf_op | source)
XLA Modules:
  0.0 380.9 jit_solution(16142627231891088193)
XLA Ops:
  2.7 7.3 %all-to-all-start.2 = ((f16[8,128,448]{1,2,0:T(8,128)(2,1)}), f16[8,128,448]{1,2,0:T(8,128)(2,1)}, u32[]{:S(2)}, u32[]{:S(2)}) async-start(f16[8,128,448]{1,2,0:T(8,128)(2,1)} %broadcast_in_dim.42), calls=%async_computation.2 | async-start | bytes 1835008 | tf_op jit(solution)/shard_map/all_to_all | solution.py:271
  13.6 21.1 %collective-permute-done.1.refs_2_ = bf16[256,2048]{1,0:T(8,128)(2,1)S(1)} collective-permute-done((bf16[256,2048]{1,0:T(8,128)(2,1)S(1)}, bf16[256,2048]{1,0:T(8,128)(2,1)S(1)}, u32[]{:S(2)}, u32[]{:S(2)}) %collective-permute-start.1) | collective-permute-done | bytes 1048608 | tf_op jit(solution)/shard_map/ppermute | solution.py:263
  34.8 4.1 %copy.24 = bf16[256,3584]{0,1:T(8,128)(2,1)} copy(bf16[256,3584]{1,0:T(8,128)(2,1)} %param.7) | data formatting | bytes 3670016 | tf_op args[1]
  45.9 22.9 %compress.1 = f32[64,128,128]{2,1,0:T(8,128)} custom-call(s32[224]{0:T(256)S(1)} %reshape.234.pat, bf16[256,2048]{1,0:T(8,128)(2,1)S(1)} %copy-done.3, bf16[256,2048]{1,0:T(8,128)(2,1)S(1)} %collective-permute-done.refs_1_, bf16[256,2048]{1,0:T(8,128)(2,1)S(1)} %collective-permute-done.1.refs_2_, bf16[256,2048]{1,0:T(8,128)(2,1)} %collective-permute-done.2.refs_3_, ...), custom_call_target="tpu_custom_call" | custom-call | flops 3758096384 | bytes 12582912 | tf_op jit(solution)/shard_map/compress/pallas_call | solution.py:293
  83.9 15.0 %collective-permute-done.5.refs_6_ = bf16[256,2048]{1,0:T(8,128)(2,1)} collective-permute-done((bf16[256,2048]{1,0:T(8,128)(2,1)}, bf16[256,2048]{1,0:T(8,128)(2,1)}, u32[]{:S(2)}, u32[]{:S(2)}) %collective-permute-start.5) | collective-permute-done | bytes 1048608 | tf_op jit(solution)/shard_map/ppermute | solution.py:263
  98.9 10.6 %collective-permute-done.9 = f16[16,128,128]{2,1,0:T(8,128)(2,1)} collective-permute-done((f16[16,128,128]{2,1,0:T(8,128)(2,1)}, f16[16,128,128]{2,1,0:T(8,128)(2,1)}, u32[]{:S(2)}, u32[]{:S(2)}) %collective-permute-start.9) | collective-permute-done | bytes 524320 | tf_op jit(solution)/shard_map/ppermute | solution.py:263
  111.5 5.7 %all-to-all-start.3 = ((f16[8,256,128]{2,1,0:T(8,128)(2,1)}), f16[8,256,128]{2,1,0:T(8,128)(2,1)}, u32[]{:S(2)}, u32[]{:S(2)}) async-start(f16[8,256,128]{2,1,0:T(8,128)(2,1)} %bitcast.56), calls=%async_computation.3 | async-start | bytes 1048576 | tf_op jit(solution)/shard_map/all_to_all | solution.py:321
  119.2 22.7 %pair_grad.1 = (f32[1792,1024]{1,0:T(8,128)}, f32[8,256]{1,0:T(8,128)S(1)}) custom-call(s32[224]{0:T(256)S(1)} %select_n.110.pat, bf16[256,2048]{1,0:T(8,128)(2,1)S(1)} %copy-done.3, bf16[256,2048]{1,0:T(8,128)(2,1)S(1)} %collective-permute-done.refs_1_, bf16[256,2048]{1,0:T(8,128)(2,1)S(1)} %collective-permute-done.1.refs_2_, ...), custom_call_target="tpu_custom_call" | custom-call | flops 1879048192 | bytes 18874368 | tf_op jit(solution)/shard_map/pair_grad/pallas_call | solution.py:381
  143.8 5.1 %all-to-all-start.1 = ((f32[4,8,128]{2,1,0:T(8,128)}), f32[4,8,128]{2,1,0:T(8,128)S(1)}, u32[]{:S(2)}, u32[]{:S(2)}) async-start(f32[4,8,128]{2,1,0:T(8,128)} %broadcast_in_dim.41), calls=%async_computation.1 | async-start | bytes 32768 | tf_op jit(solution)/shard_map/all_to_all | solution.py:413
  150.0 4.5 %all-to-all-done.1 = f32[4,8,128]{2,1,0:T(8,128)S(1)} async-done(((f32[4,8,128]{2,1,0:T(8,128)}), f32[4,8,128]{2,1,0:T(8,128)S(1)}, u32[]{:S(2)}, u32[]{:S(2)}) %all-to-all-start.1) | async-done | bytes 16416 | tf_op jit(solution)/shard_map/all_to_all | solution.py:413
  155.4 4.2 %all-to-all-start.4 = ((f16[8,256,128]{2,1,0:T(8,128)(2,1)}), f16[8,256,128]{2,1,0:T(8,128)(2,1)}, u32[]{:S(2)}, u32[]{:S(2)}) async-start(f16[8,256,128]{2,1,0:T(8,128)(2,1)} %broadcast_in_dim.43), calls=%async_computation.4 | async-start | bytes 1048576 | tf_op jit(solution)/shard_map/all_to_all | solution.py:323
  159.6 6.1 %multiply_convert_fusion = f16[1792,1024]{1,0:T(8,128)(2,1)} fusion(f32[1792,1024]{1,0:T(8,128)} %get-tuple-element.6, f32[]{:T(128)S(6)} %div.62), kind=kLoop, calls=%fused_computation.4 | loop fusion | flops 3670016 | bytes 11010052 | tf_op jit(solution)/shard_map/convert_element_type | solution.py:410
  165.7 6.3 %all-to-all-done.4 = f16[8,256,128]{2,1,0:T(8,128)(2,1)} async-done(((f16[8,256,128]{2,1,0:T(8,128)(2,1)}), f16[8,256,128]{2,1,0:T(8,128)(2,1)}, u32[]{:S(2)}, u32[]{:S(2)}) %all-to-all-start.4) | async-done | bytes 524320 | tf_op jit(solution)/shard_map/all_to_all | solution.py:323
  172.0 4.9 %all-to-all-start = ((f16[4,448,1024]{2,1,0:T(8,128)(2,1)}), f16[4,448,1024]{2,1,0:T(8,128)(2,1)}, u32[]{:S(2)}, u32[]{:S(2)}) async-start(f16[4,448,1024]{2,1,0:T(8,128)(2,1)} %bitcast.50), calls=%async_computation | async-start | bytes 7340032 | tf_op jit(solution)/shard_map/all_to_all | solution.py:412
  177.5 107.5 %all-gather.2 = f16[4096,256]{1,0:T(8,128)(2,1)S(1)} all-gather(f16[128,256]{1,0:T(8,128)(2,1)S(1)} %convert_element_type.90), channel_id=2, replica_groups=mesh['dp'=8,'mp'=4] {'dp','mp'}, dimensions={0}, use_global_device_ids=true | all-gather | bytes 2162688 | tf_op jit(solution)/shard_map/all_gather | solution.py:276
  286.9 4.9 %collective-permute-start.10 = (f16[16,128,128]{2,1,0:T(8,128)(2,1)}, f16[16,128,128]{2,1,0:T(8,128)(2,1)}, u32[]{:S(2)}, u32[]{:S(2)}) collective-permute-start(f16[16,128,128]{2,1,0:T(8,128)(2,1)} %bitcast.22), channel_id=1, source_target_pairs={{0,2},{1,3},{2,0},{3,1},{4,6},{5,7},{6,4},{7,5},{8,10},{9,11},{10,... | collective-permute-start | bytes 1572872 | tf_op jit(solution)/shard_map/ppermute | solution.py:263
  295.8 9.0 %collective-permute-done.10 = f16[16,128,128]{2,1,0:T(8,128)(2,1)} collective-permute-done((f16[16,128,128]{2,1,0:T(8,128)(2,1)}, f16[16,128,128]{2,1,0:T(8,128)(2,1)}, u32[]{:S(2)}, u32[]{:S(2)}) %collective-permute-start.10) | collective-permute-done | bytes 524320 | tf_op jit(solution)/shard_map/ppermute | solution.py:263
  306.4 8.0 %copy.29 = bf16[448,8,8,128]{3,1,2,0:T(8,128)(2,1)} copy(bf16[448,8,8,128]{3,2,1,0:T(8,128)(2,1)} %bitcast.52) | data formatting | bytes 14680064
  316.9 21.8 %input_grad.1 = bf16[256,3584]{1,0:T(8,128)(2,1)} custom-call(s32[224]{0:T(256)S(1)} %reshape.234.pat, bf16[256,2048]{1,0:T(8,128)(2,1)S(1)} %copy-done.3, bf16[256,2048]{1,0:T(8,128)(2,1)S(1)} %copy-done.7, bf16[256,2048]{1,0:T(8,128)(2,1)S(1)} %copy-done.5, bf16[256,2048]{1,0:T(8,128)(2,1)} %collective-permute-done.2.refs_3_, bf16[3584,1024]{1,0:T(8,128)(2,1)} %bitcast.49), custom_call_target="tpu_custom_call" | custom-call | flops 1879048192 | bytes 14680064 | tf_op jit(solution)/shard_map/input_grad/pallas_call | solution.py:419
  338.8 16.0 %mixing.1.m_ref = f32[256,256]{1,0:T(8,128)S(1)} custom-call(f32[128,128]{1,0:T(8,128)S(1)} %sketch_gram.1.ss_ref, f32[128,256]{1,0:T(8,128)S(1)} %add.159.cross_ref), custom_call_target="tpu_custom_call" | custom-call | flops 6039797760 | bytes 1048576 | tf_op jit(solution)/shard_map/mixing/pallas_call | solution.py:353
  357.0 3.6 fusion.1
  360.6 3.5 multiply_reduce_fusion.g_ref
  364.0 6.9 %project.1.p_ref = f32[448,256]{1,0:T(8,128)S(1)} custom-call(s32[56]{0:T(128)S(1)} %select_n.103.pat_sk, s32[56]{0:T(128)S(1)} %broadcast_xor_fusion.1.pat_cp, f32[448,1024]{1,0:T(8,128)S(1)} %multiply_reduce_fusion.g_ref, bf16[32,128,256]{2,1,0:T(8,128)(2,1)S(1)} %copy-done.2, bf16[32,128,256]{2,1,0:T(8,128)(2,1)} %copy-done, ...), custom_call_target="tpu_custom_call" | custom-call | flops 704643072 | bytes 12582912 | tf_op jit(solution)/shard_map/project/pallas_call | solution.py:437
  371.0 9.9 %direction.1 = f32[448,8,128]{2,1,0:T(8,128)} custom-call(s32[56]{0:T(128)S(1)} %select_n.103.pat_sk, s32[56]{0:T(128)S(1)} %broadcast_xor_fusion.1.pat_cp, f32[448,1024]{1,0:T(8,128)S(1)} %multiply_reduce_fusion.g_ref, f32[448,256]{1,0:T(8,128)S(1)} %project.1.p_ref, f32[256,256]{1,0:T(8,128)S(1)} %mixing.1.m_ref, bf16[32,128,256]{2,1,0:T(8,128)(2,1)S(1)} %copy-done.2, ...), custom_call_target="tpu_custom_call" | custom-call | flops 704643072 | bytes 14680064 | tf_op jit(solution)/shard_map/direction/pallas_call | solution.py:450
  (105 shorter events, 47.8 us)
Async XLA Ops:
  0.6 12.9 %copy-start.13 = (s32[28,8]{0,1:T(8,128)S(1)}, s32[28,8]{0,1:T(8,128)}, u32[]{:S(2)}) copy-start(s32[28,8]{0,1:T(8,128)} %param.11) | copy-start | bytes 2692
  2.7 36.2 %all-to-all-start.2 = ((f16[8,128,448]{1,2,0:T(8,128)(2,1)}), f16[8,128,448]{1,2,0:T(8,128)(2,1)}, u32[]{:S(2)}, u32[]{:S(2)}) async-start(f16[8,128,448]{1,2,0:T(8,128)(2,1)} %broadcast_in_dim.42), calls=%async_computation.2 | async-start | bytes 1835008 | tf_op jit(solution)/shard_map/all_to_all | solution.py:271
  10.0 24.7 %collective-permute-start.1 = (bf16[256,2048]{1,0:T(8,128)(2,1)S(1)}, bf16[256,2048]{1,0:T(8,128)(2,1)S(1)}, u32[]{:S(2)}, u32[]{:S(2)}) collective-permute-start(bf16[256,2048]{1,0:T(8,128)(2,1)S(1)} %copy-done.3), channel_id=1, source_target_pairs={{0,2},{1,3},{2,0},{3,1},{4,6},{5,7},{6,4},{7,5},{8,10},{9,11},{10,... | collective-permute-start | bytes 3145736 | tf_op jit(solution)/shard_map/ppermute | solution.py:263
  11.6 34.3 %collective-permute-start = (bf16[256,2048]{1,0:T(8,128)(2,1)S(1)}, bf16[256,2048]{1,0:T(8,128)(2,1)S(1)}, u32[]{:S(2)}, u32[]{:S(2)}) collective-permute-start(bf16[256,2048]{1,0:T(8,128)(2,1)S(1)} %copy-done.3), channel_id=1, source_target_pairs={{0,1},{1,0},{2,3},{3,2},{4,5},{5,4},{6,7},{7,6},{8,9},{9,8},{10,11... | collective-permute-start | bytes 3145736 | tf_op jit(solution)/shard_map/ppermute | solution.py:263
  11.6 61.0 %collective-permute-start.3 = (bf16[256,2048]{1,0:T(8,128)(2,1)S(1)}, bf16[256,2048]{1,0:T(8,128)(2,1)}, u32[]{:S(2)}, u32[]{:S(2)}) collective-permute-start(bf16[256,2048]{1,0:T(8,128)(2,1)S(1)} %copy-done.3), channel_id=1, source_target_pairs={{0,4},{4,0},{8,12},{12,8},{16,20},{20,16},{24,28},{28,24},{1,5},{5... | collective-permute-start | bytes 3145736 | tf_op jit(solution)/shard_map/ppermute | solution.py:263
  34.7 83.2 %copy-start.4 = (bf16[256,2048]{1,0:T(8,128)(2,1)}, bf16[256,2048]{1,0:T(8,128)(2,1)S(1)}, u32[]{:S(2)}) copy-start(bf16[256,2048]{1,0:T(8,128)(2,1)S(1)} %collective-permute-done.1.refs_2_) | copy-start | bytes 3145732
  34.7 11.2 %collective-permute-start.2 = (bf16[256,2048]{1,0:T(8,128)(2,1)S(1)}, bf16[256,2048]{1,0:T(8,128)(2,1)}, u32[]{:S(2)}, u32[]{:S(2)}) collective-permute-start(bf16[256,2048]{1,0:T(8,128)(2,1)S(1)} %collective-permute-done.1.refs_2_), channel_id=1, source_target_pairs={{0,1},{1,0},{2,3},{3,2},{4,5},{5,4},{6,7},{7,6},{8,9},{9,8},{10,11... | collective-permute-start | bytes 3145736 | tf_op jit(solution)/shard_map/ppermute | solution.py:263
  45.9 72.1 %copy-start.6 = (bf16[256,2048]{1,0:T(8,128)(2,1)}, bf16[256,2048]{1,0:T(8,128)(2,1)S(1)}, u32[]{:S(2)}) copy-start(bf16[256,2048]{1,0:T(8,128)(2,1)S(1)} %collective-permute-done.refs_1_) | copy-start | bytes 3145732
  72.3 2.7 collective-permute-start.8
  72.6 26.3 %collective-permute-start.5 = (bf16[256,2048]{1,0:T(8,128)(2,1)}, bf16[256,2048]{1,0:T(8,128)(2,1)}, u32[]{:S(2)}, u32[]{:S(2)}) collective-permute-start(bf16[256,2048]{1,0:T(8,128)(2,1)} %collective-permute-done.3.refs_4_), channel_id=1, source_target_pairs={{0,2},{1,3},{2,0},{3,1},{4,6},{5,7},{6,4},{7,5},{8,10},{9,11},{10,... | collective-permute-start | bytes 3145736 | tf_op jit(solution)/shard_map/ppermute | solution.py:263
  77.5 31.9 %collective-permute-start.9 = (f16[16,128,128]{2,1,0:T(8,128)(2,1)}, f16[16,128,128]{2,1,0:T(8,128)(2,1)}, u32[]{:S(2)}, u32[]{:S(2)}) collective-permute-start(f16[16,128,128]{2,1,0:T(8,128)(2,1)} %fusion.6), channel_id=1, source_target_pairs={{0,2},{1,3},{2,0},{3,1},{4,6},{5,7},{6,4},{7,5},{8,10},{9,11},{10,... | collective-permute-start | bytes 1572872 | tf_op jit(solution)/shard_map/ppermute | solution.py:263
  79.3 30.2 %copy-start.11 = (f32[2,16,128,128]{3,2,1,0:T(8,128)S(1)}, f32[2,16,128,128]{3,2,1,0:T(8,128)}, u32[]{:S(2)}) copy-start(f32[2,16,128,128]{3,2,1,0:T(8,128)} %copy-done.10) | copy-start | bytes 6291460
  82.2 35.7 %collective-permute-start.7 = (bf16[4,448,256]{2,1,0:T(8,128)(2,1)}, bf16[4,448,256]{2,1,0:T(8,128)(2,1)}, u32[]{:S(2)}, u32[]{:S(2)}) collective-permute-start(bf16[4,448,256]{2,1,0:T(8,128)(2,1)} %get-tuple-element.5), channel_id=1, source_target_pairs={{0,4},{4,0},{8,12},{12,8},{16,20},{20,16},{24,28},{28,24},{1,5},{5... | collective-permute-start | bytes 2752520 | tf_op jit(solution)/shard_map/ppermute | solution.py:263
  83.9 34.0 %collective-permute-start.4 = (bf16[256,2048]{1,0:T(8,128)(2,1)}, bf16[256,2048]{1,0:T(8,128)(2,1)}, u32[]{:S(2)}, u32[]{:S(2)}) collective-permute-start(bf16[256,2048]{1,0:T(8,128)(2,1)} %collective-permute-done.3.refs_4_), channel_id=1, source_target_pairs={{0,1},{1,0},{2,3},{3,2},{4,5},{5,4},{6,7},{7,6},{8,9},{9,8},{10,11... | collective-permute-start | bytes 3145736 | tf_op jit(solution)/shard_map/ppermute | solution.py:263
  98.9 19.1 %collective-permute-start.6 = (bf16[256,2048]{1,0:T(8,128)(2,1)}, bf16[256,2048]{1,0:T(8,128)(2,1)}, u32[]{:S(2)}, u32[]{:S(2)}) collective-permute-start(bf16[256,2048]{1,0:T(8,128)(2,1)} %collective-permute-done.5.refs_6_), channel_id=1, source_target_pairs={{0,1},{1,0},{2,3},{3,2},{4,5},{5,4},{6,7},{7,6},{8,9},{9,8},{10,11... | collective-permute-start | bytes 3145736 | tf_op jit(solution)/shard_map/ppermute | solution.py:263
  111.5 31.7 %all-to-all-start.3 = ((f16[8,256,128]{2,1,0:T(8,128)(2,1)}), f16[8,256,128]{2,1,0:T(8,128)(2,1)}, u32[]{:S(2)}, u32[]{:S(2)}) async-start(f16[8,256,128]{2,1,0:T(8,128)(2,1)} %bitcast.56), calls=%async_computation.3 | async-start | bytes 1048576 | tf_op jit(solution)/shard_map/all_to_all | solution.py:321
  143.8 10.7 %all-to-all-start.1 = ((f32[4,8,128]{2,1,0:T(8,128)}), f32[4,8,128]{2,1,0:T(8,128)S(1)}, u32[]{:S(2)}, u32[]{:S(2)}) async-start(f32[4,8,128]{2,1,0:T(8,128)} %broadcast_in_dim.41), calls=%async_computation.1 | async-start | bytes 32768 | tf_op jit(solution)/shard_map/all_to_all | solution.py:413
  155.4 16.6 %all-to-all-start.4 = ((f16[8,256,128]{2,1,0:T(8,128)(2,1)}), f16[8,256,128]{2,1,0:T(8,128)(2,1)}, u32[]{:S(2)}, u32[]{:S(2)}) async-start(f16[8,256,128]{2,1,0:T(8,128)(2,1)} %broadcast_in_dim.43), calls=%async_computation.4 | async-start | bytes 1048576 | tf_op jit(solution)/shard_map/all_to_all | solution.py:323
  172.0 188.6 %all-to-all-start = ((f16[4,448,1024]{2,1,0:T(8,128)(2,1)}), f16[4,448,1024]{2,1,0:T(8,128)(2,1)}, u32[]{:S(2)}, u32[]{:S(2)}) async-start(f16[4,448,1024]{2,1,0:T(8,128)(2,1)} %bitcast.50), calls=%async_computation | async-start | bytes 7340032 | tf_op jit(solution)/shard_map/all_to_all | solution.py:412
  286.9 27.6 %copy-start = (bf16[32,128,256]{2,1,0:T(8,128)(2,1)}, bf16[32,128,256]{2,1,0:T(8,128)(2,1)S(1)}, u32[]{:S(2)}) copy-start(bf16[32,128,256]{2,1,0:T(8,128)(2,1)S(1)} %get-tuple-element.14.skl.sl_ref) | copy-start | bytes 6291460
  286.9 17.9 %collective-permute-start.10 = (f16[16,128,128]{2,1,0:T(8,128)(2,1)}, f16[16,128,128]{2,1,0:T(8,128)(2,1)}, u32[]{:S(2)}, u32[]{:S(2)}) collective-permute-start(f16[16,128,128]{2,1,0:T(8,128)(2,1)} %bitcast.22), channel_id=1, source_target_pairs={{0,2},{1,3},{2,0},{3,1},{4,6},{5,7},{6,4},{7,5},{8,10},{9,11},{10,... | collective-permute-start | bytes 1572872 | tf_op jit(solution)/shard_map/ppermute | solution.py:263
  295.3 20.9 %collective-permute-start.12 = (f32[128,256]{1,0:T(8,128)S(1)}, f32[128,256]{1,0:T(8,128)S(1)}, u32[]{:S(2)}, u32[]{:S(2)}) collective-permute-start(f32[128,256]{1,0:T(8,128)S(1)} %cross_gram.1), channel_id=1, source_target_pairs={{0,2},{1,3},{2,0},{3,1},{4,6},{5,7},{6,4},{7,5},{8,10},{9,11},{10,... | collective-permute-start | bytes 393224 | tf_op jit(solution)/shard_map/ppermute | solution.py:263
  306.3 48.4 %collective-permute-start.11 = (f16[2,16,128,128]{3,2,1,0:T(8,128)(2,1)S(1)}, f16[2,16,128,128]{3,2,1,0:T(8,128)(2,1)S(1)}, u32[]{:S(2)}, u32[]{:S(2)}) collective-permute-start(f16[2,16,128,128]{3,2,1,0:T(8,128)(2,1)S(1)} %pad_maximum_fusion.2), channel_id=1, source_target_pairs={{0,1},{1,0},{2,3},{3,2},{4,5},{5,4},{6,7},{7,6},{8,9},{9,8},{10,11... | collective-permute-start | bytes 3145736 | tf_op jit(solution)/shard_map/ppermute | solution.py:263
  316.3 22.4 %collective-permute-start.13 = (f32[128,256]{1,0:T(8,128)S(1)}, f32[128,256]{1,0:T(8,128)S(1)}, u32[]{:S(2)}, u32[]{:S(2)}) collective-permute-start(f32[128,256]{1,0:T(8,128)S(1)} %add.158), channel_id=1, source_target_pairs={{0,1},{1,0},{2,3},{3,2},{4,5},{5,4},{6,7},{7,6},{8,9},{9,8},{10,11... | collective-permute-start | bytes 393224 | tf_op jit(solution)/shard_map/ppermute | solution.py:263
  (9 other events, 36.2 us)

commit v2 on v1

v2 whole, which is shorter than its diff:
```python
import functools
import math

import jax
import jax.numpy as jnp
from jax import lax
from jax.experimental import pallas as pl
from jax.experimental.pallas import tpu as pltpu
from jax.sharding import PartitionSpec as P

NS_STEPS = 5
SHIFT_EPS = 0.0001
PROJ_SCALE = 1024.0
SLOTS = 8

BF = jnp.bfloat16
F16 = jnp.float16
F32 = jnp.float32
HIGHEST = lax.Precision.HIGHEST
VMEM = pl.BlockSpec(memory_space=pltpu.VMEM)
ANY = pl.BlockSpec(memory_space=pl.ANY)


SMALL = pl.CostEstimate(flops=1, bytes_accessed=1, transcendentals=0)


def params(mib=48):
    return pltpu.CompilerParams(vmem_limit_bytes=mib * 1024 * 1024)


def dot(a, b):
    return jnp.dot(a, b, preferred_element_type=F32)


def dot_nt(a, b):
    return lax.dot_general(a, b, (((1,), (1,)), ((), ())), preferred_element_type=F32)


def split2(value):
    high = value.astype(BF)
    return high, (value - high.astype(F32)).astype(BF)


def split2_xla(value):
    high = lax.reduce_precision(value, exponent_bits=8, mantissa_bits=7)
    return high.astype(BF), (value - high).astype(BF)


def load_all(pairs, sems):
    copies = [pltpu.make_async_copy(src, dst, sems.at[i]) for i, (src, dst) in enumerate(pairs)]
    for copy in copies:
        copy.start()
    for copy in copies:
        copy.wait()


def column_block(held, block, per_shard, size):
    shard = block // per_shard
    offset = pl.multiple_of((block - shard * per_shard) * size, size)
    return held[shard, :, pl.ds(offset, size)]


def compress_kernel(n_shards, per_shard, scale, per_step, pat, *refs):
    shards = refs[:n_shards]
    hid_ref, proj_ref, out_ref, held, sems = refs[n_shards:]
    blk = out_ref.shape[1]

    @pl.when(pl.program_id(0) == 0)
    def _():
        load_all([(ref, held.at[i]) for i, ref in enumerate(shards)], sems)
        out_ref[...] = jnp.zeros_like(out_ref)

    for u in range(per_step):
        row = pl.program_id(0) * per_step + u
        span = slice(u * blk, (u + 1) * blk)
        hid = hid_ref[span, :]
        ph, pl_ = split2(proj_ref[:, span])
        left = jnp.concatenate(split2((dot(ph, hid) + dot(pl_, hid)) * scale), axis=0)
        cols = [pat[row * SLOTS + j] for j in range(SLOTS)]
        parts = []
        for j in range(0, SLOTS, 2):
            chosen = jnp.concatenate(
                [column_block(held, c, per_shard, blk) for c in cols[j : j + 2]], axis=1
            )
            part = dot(left, chosen)
            parts.append(part[:blk] + part[blk:])
        sums = [
            out_ref[c] + parts[j // 2][:, (j % 2) * blk : (j % 2 + 1) * blk]
            for j, c in enumerate(cols)
        ]
        for c, total in zip(cols, sums):
            out_ref[c] = total


def grad_kernel(n_shards, per_shard, blk, window, n_windows, starts, pat, *refs):
    shards = refs[: 2 * n_shards]
    own_ref, got_ref, out_ref, top_ref, held, sems = refs[2 * n_shards :]
    toks = own_ref.shape[1]

    @pl.when(pl.program_id(0) == 0)
    def _():
        load_all(
            [
                (ref, held.at[i % n_shards, pl.ds(i // n_shards * toks, toks)])
                for i, ref in enumerate(shards)
            ],
            sems,
        )
        top_ref[...] = jnp.zeros_like(top_ref)

    top = top_ref[...]
    for w in range(n_windows):
        index = pl.program_id(0) * n_windows + w
        rows = pl.ds(pl.multiple_of(starts[index], window // 2 if window >= 32 else 8), window)
        hid = jnp.concatenate([own_ref[rows, :], got_ref[rows, :]], axis=1).astype(BF)
        for j in range(0, SLOTS, 2):
            chosen = jnp.concatenate(
                [column_block(held, pat[index * SLOTS + j + i], per_shard, blk) for i in (0, 1)],
                axis=1,
            )
            part = dot(hid, chosen)
            out_ref[rows, j * blk : (j + 2) * blk] = part
            size = jnp.abs(part)
            for i in range(0, window, 8):
                top = jnp.maximum(top, size[i : i + 8])
    top_ref[...] = top


def input_grad_kernel(n_shards, per_shard, blk, per_step, pat, *refs):
    shards = refs[:n_shards]
    w_ref, out_ref, held, sems = refs[n_shards:]

    @pl.when(pl.program_id(0) == 0)
    def _():
        load_all([(ref, held.at[i]) for i, ref in enumerate(shards)], sems)

    for u in range(per_step):
        row = pl.program_id(0) * per_step + u
        chosen = jnp.concatenate(
            [column_block(held, pat[row * SLOTS + j], per_shard, blk) for j in range(SLOTS)], axis=1
        )
        span = slice(u * blk, (u + 1) * blk)
        out_ref[:, span] = dot_nt(chosen, w_ref[span, :]).astype(BF)


def sketch_gram_kernel(sh_ref, sl_ref, out_ref):
    out_ref[...] = jnp.zeros_like(out_ref)
    for s in range(sh_ref.shape[0]):
        high, low = sh_ref[s], sl_ref[s]
        out_ref[...] += dot_nt(high, high) + (dot_nt(high, low) + dot_nt(low, high))


def cross_gram_kernel(ch_ref, cl_ref, sh_ref, sl_ref, out_ref):
    rank = ch_ref.shape[1]
    per = ch_ref.shape[0] // sh_ref.shape[0]
    with_sketch = jnp.zeros((rank, rank), F32)
    with_self = jnp.zeros((rank, rank), F32)
    for s in range(sh_ref.shape[0]):
        high = jnp.concatenate([ch_ref[per * s + b] for b in range(per)], axis=1)
        low = jnp.concatenate([cl_ref[per * s + b] for b in range(per)], axis=1)
        sh, sl = sh_ref[s], sl_ref[s]
        with_sketch += dot_nt(high, sh) + (dot_nt(high, sl) + dot_nt(low, sh))
        with_self += dot_nt(high, high) + (dot_nt(high, low) + dot_nt(low, high))
    out_ref[:, :rank] = with_sketch
    out_ref[:, rank:] = with_self


def mixing_kernel(ss_ref, cross_ref, out_ref):
    rank = ss_ref.shape[0]
    size = 2 * rank
    sqrt_eps = math.sqrt(SHIFT_EPS)

    def mm(a, b):
        return jnp.dot(a, b, precision=HIGHEST, preferred_element_type=F32)

    cross = cross_ref[...]
    gram = jnp.concatenate(
        [jnp.concatenate([ss_ref[...], cross[:, :rank].T], axis=1), cross], axis=0
    )
    rows = lax.broadcasted_iota(jnp.int32, (size, size), 0)
    cols = lax.broadcasted_iota(jnp.int32, (size, size), 1)
    identity = jnp.where(rows == cols, 1.0, 0.0).astype(F32)
    shifted = gram + SHIFT_EPS * identity
    frobenius = jnp.sqrt(jnp.sum(shifted * shifted, keepdims=True))
    root = shifted / frobenius
    inverse = identity
    for step in range(NS_STEPS):
        product = root if step == 0 else mm(inverse, root)
        middle = 0.5 * (3.0 * identity - product)
        root = mm(root, middle)
        inverse = middle if step == 0 else mm(middle, inverse)
    sqrt_fro = jnp.sqrt(frobenius)
    half = 0.5 * sqrt_fro * (root + root.T) + sqrt_eps * identity
    guess = inverse / (sqrt_fro + sqrt_eps * 1.5**NS_STEPS)

    def residual(x):
        r = identity - mm(half, x)
        return r, jnp.max(jnp.abs(r))

    def keep_going(state):
        return jnp.logical_and(state[3] < 48, state[2] > 2e-6)

    def improve(state):
        x, r, _, count = state
        x = x + mm(x, r)
        r, size = residual(x)
        return x, r, size, count + 1

    r, top = residual(guess)
    x, r, _, _ = lax.while_loop(keep_going, improve, (guess, r, top, jnp.int32(0)))
    x = x + mm(x, r)
    out_ref[...] = -mm(inverse, x) / (sqrt_eps * sqrt_fro)


def direction_kernel(per, window, n_windows, starts, pat_sk, pat_cp, *refs):
    g_ref, m_ref, skh, skl = refs[:4]
    parts, (out_ref, cph, cpl, sems) = refs[4:-4], refs[-4:]
    blk = cph.shape[2]
    half = len(parts) // 2
    pairs, at = [], 0
    for i in range(half):
        size = parts[i].shape[0]
        pairs += [(parts[i], cph.at[pl.ds(at, size)]), (parts[half + i], cpl.at[pl.ds(at, size)])]
        at += size
    load_all(pairs, sems)

    def gathered(sk, cp, c_sk, c_cp):
        shard = c_sk // per
        offset = pl.multiple_of((c_sk - shard * per) * blk, blk)
        return jnp.concatenate([sk[shard, :, pl.ds(offset, blk)], cp[c_cp]], axis=0)

    for w in range(n_windows):
        rows = pl.ds(pl.multiple_of(starts[w], window // 2 if window >= 32 else 8), window)
        cols = [(pat_sk[w * SLOTS + k], pat_cp[w * SLOTS + k]) for k in range(SLOTS)]
        g = g_ref[rows, :]
        g_high = g.astype(BF).astype(F32)
        g_both = jnp.concatenate([g_high, g - g_high], axis=0).astype(BF)
        high = [gathered(skh, cph, *c) for c in cols]
        low = [gathered(skl, cpl, *c) for c in cols]
        both = dot_nt(g_both, jnp.concatenate(high, axis=1))
        projected = both[:window] + both[window:]
        projected += dot_nt(g_high.astype(BF), jnp.concatenate(low, axis=1))
        mixed = jnp.dot(projected, m_ref[...], precision=HIGHEST, preferred_element_type=F32)
        mixed_high = mixed.astype(BF).astype(F32)
        mixed_both = jnp.concatenate([mixed_high, mixed - mixed_high], axis=0).astype(BF)
        for k in range(0, SLOTS, 2):
            both = dot(mixed_both, jnp.concatenate(high[k : k + 2], axis=1))
            corr = both[:window] + both[window:]
            corr += dot(mixed_high.astype(BF), jnp.concatenate(low[k : k + 2], axis=1))
            corr += g[:, k * blk : (k + 2) * blk] * (1.0 / math.sqrt(SHIFT_EPS))
            out_ref[rows, k, :] = corr[:, :blk]
            out_ref[rows, k + 1, :] = corr[:, blk:]


def windows_of(start, dev_rows, blk):
    group = math.gcd(dev_rows, blk)
    if dev_rows % blk == blk // 2 and dev_rows > blk:
        whole = dev_rows // blk
        odd = (start // group) % 2
        later = odd * group + blk * jnp.arange(whole, dtype=jnp.int32)
        first = jnp.where(odd == 1, 0, dev_rows - blk)
        first_row = jnp.where(odd == 1, start, start + dev_rows - group)
        starts = jnp.concatenate([first[None], later])
        inside = jnp.concatenate([first_row[None], start + later])
        return blk, starts.astype(jnp.int32), (inside // blk).astype(jnp.int32)
    starts = group * jnp.arange(dev_rows // group, dtype=jnp.int32)
    return group, starts, (start + starts) // blk


def per_device(weights, hidden, cotangent, sketch, projection, pattern):
    tok_rows = hidden.shape[0]
    mp_rows, slots, blk = weights.shape
    block_rows = mp_rows // blk
    n_dp, n_mp = lax.axis_size("dp"), lax.axis_size("mp")
    dev_rows = mp_rows // n_dp
    all_tokens = tok_rows * n_dp
    rank = sketch.shape[0]
    shard_cols = cotangent.shape[1]
    per_shard = shard_cols // blk
    col_blocks = per_shard * n_mp
    outer = n_dp // 2
    per_step = 4 if block_rows % 4 == 0 else 1
    dp, mp = lax.axis_index("dp"), lax.axis_index("mp")
    side = dp % 2

    def swap(x, axis, bit):
        size = lax.axis_size(axis)
        return lax.ppermute(x, axis, [(i, i ^ bit) for i in range(size)])

    def after(x, *others):
        return lax.optimization_barrier((x, *others))[0]

    def over_dp(x):
        return lax.all_to_all(jnp.broadcast_to(x[None], (n_dp, *x.shape)), "dp", 0, 0)

    x_half = swap(cotangent, "mp", 2)
    y_own = swap(cotangent, "dp", 1)
    core_half = swap(cotangent, "mp", 1)
    y_x = swap(y_own, "mp", 2)
    own = [cotangent, core_half, x_half, swap(x_half, "mp", 1)]
    pattern_rel = jnp.bitwise_xor(pattern, mp * per_shard)

    proj16 = (projection.reshape(rank, dev_rows) * PROJ_SCALE).astype(F16)
    proj_all = over_dp(after(proj16, core_half))
    proj_all = proj_all.transpose(1, 0, 2).reshape(rank, mp_rows).astype(F32)

    hid_t = hidden.T
    hid_parts = hid_t.reshape(outer, 2, dev_rows, tok_rows)
    hid_own = lax.dynamic_index_in_dim(hid_parts, side, 1, keepdims=False)
    hid_send = lax.dynamic_index_in_dim(hid_parts, 1 - side, 1, keepdims=False)
    hid_got = swap(after(hid_send, y_own), "dp", 1)

    pat_all = pattern_rel.reshape(-1)
    partial_c = pl.pallas_call(
        functools.partial(
            compress_kernel, n_mp, per_shard, 1.0 / (PROJ_SCALE * all_tokens), per_step
        ),
        grid_spec=pltpu.PrefetchScalarGridSpec(
            num_scalar_prefetch=1,
            grid=(block_rows // per_step,),
            in_specs=[ANY] * n_mp
            + [
                pl.BlockSpec((per_step * blk, tok_rows), lambda i, pat: (i, 0)),
                pl.BlockSpec((rank, per_step * blk), lambda i, pat: (0, i)),
            ],
            out_specs=pl.BlockSpec((col_blocks, rank, blk), lambda i, pat: (0, 0, 0)),
            scratch_shapes=[
                pltpu.VMEM((n_mp, tok_rows, shard_cols), BF),
                pltpu.SemaphoreType.DMA((n_mp,)),
            ],
        ),
        out_shape=jax.ShapeDtypeStruct((col_blocks, rank, blk), F32),
        compiler_params=params(),
        cost_estimate=SMALL,
        name="compress",
    )(pat_all, *own, hid_t, proj_all)

    quarters = partial_c.reshape(n_mp, per_shard, rank, blk)
    sent = swap(jnp.stack([quarters[1], quarters[3]]).astype(F16), "mp", 1)
    far_half = (quarters[2] + sent[1].astype(F32)).astype(F16)
    quarter = (quarters[0] + sent[0].astype(F32)) + swap(far_half, "mp", 2).astype(F32)
    pieces = quarter.astype(F16).reshape(n_dp, per_shard * rank // n_dp, blk)
    pieces = lax.all_to_all(pieces, "dp", 0, 0)
    piece = jnp.sum(pieces.astype(F32), axis=0).astype(F16)
    quarter16 = over_dp(piece).reshape(per_shard, rank, blk)

    sk_own = over_dp(after(sketch.astype(F16), sent))
    sk_far = swap(sk_own, "mp", 2)
    sk_near = swap(jnp.stack([sk_own, sk_far]), "mp", 1)
    sk_rel = jnp.stack([sk_own, sk_near[0], sk_far, sk_near[1]])
    sk_abs = jnp.take(sk_rel, jnp.bitwise_xor(jnp.arange(n_mp, dtype=jnp.int32), mp), axis=0)
    width = sketch.shape[1]
    if width < blk:
        sketch_all = sk_abs.reshape(n_mp, col_blocks, blk // width // n_mp, rank, width)
        sketch_all = sketch_all.transpose(1, 3, 2, 0, 4).reshape(col_blocks, rank, blk)
    else:
        sketch_all = sk_abs.swapaxes(0, 1).reshape(n_dp * n_mp, rank, width)
    sk_high, sk_low = split2_xla(sketch_all.astype(F32))

    sk_per = sk_high.shape[2] // blk
    sk_quarter = col_blocks // sk_per // n_mp
    qh, ql = split2_xla(quarter16.astype(F32))
    cross = pl.pallas_call(
        cross_gram_kernel,
        in_specs=[VMEM] * 4,
        out_specs=VMEM,
        out_shape=jax.ShapeDtypeStruct((rank, 2 * rank), F32),
        compiler_params=params(),
        cost_estimate=SMALL,
        name="cross_gram",
    )(
        qh,
        ql,
        lax.dynamic_slice_in_dim(sk_high, mp * sk_quarter, sk_quarter, 0),
        lax.dynamic_slice_in_dim(sk_low, mp * sk_quarter, sk_quarter, 0),
    )
    sketch_gram = pl.pallas_call(
        sketch_gram_kernel,
        in_specs=[VMEM] * 2,
        out_specs=VMEM,
        out_shape=jax.ShapeDtypeStruct((rank, rank), F32),
        compiler_params=params(),
        cost_estimate=SMALL,
        name="sketch_gram",
    )(sk_high, sk_low)
    cross = cross + swap(cross, "mp", 2)
    cross = cross + swap(cross, "mp", 1)
    mixing = pl.pallas_call(
        mixing_kernel,
        in_specs=[VMEM] * 2,
        out_specs=VMEM,
        out_shape=jax.ShapeDtypeStruct((2 * rank, 2 * rank), F32),
        compiler_params=params(),
        cost_estimate=SMALL,
        name="mixing",
    )(sketch_gram, cross)

    far = swap(after(quarter16, cross), "mp", 2)
    near = swap(jnp.stack([quarter16, far]), "mp", 1)
    fh, fl = split2_xla(far.astype(F32))
    nh, nl = split2_xla(near.astype(F32))
    comp_parts = [qh, nh[0], fh, nh[1], ql, nl[0], fl, nl[1]]

    y_group = [y_own, swap(y_own, "mp", 1), y_x, swap(y_x, "mp", 1)]
    half_rows = outer * dev_rows
    devices = 2 * jnp.arange(outer, dtype=jnp.int32) + side
    window, _, _ = windows_of(dp * dev_rows, dev_rows, blk)
    window_starts, window_blocks = jax.vmap(lambda d: windows_of(d * dev_rows, dev_rows, blk)[1:])(
        devices
    )
    n_windows = window_starts.shape[1]
    pat_half = jnp.take(pattern_rel, window_blocks.reshape(-1), axis=0).reshape(-1)
    hid_type = BF if window % 32 == 0 else F32
    grad_half, top = pl.pallas_call(
        functools.partial(grad_kernel, n_mp, per_shard, blk, window, n_windows),
        grid_spec=pltpu.PrefetchScalarGridSpec(
            num_scalar_prefetch=2,
            grid=(outer,),
            in_specs=[ANY] * (2 * n_mp)
            + [pl.BlockSpec((dev_rows, tok_rows), lambda i, a, b: (i, 0))] * 2,
            out_specs=[
                pl.BlockSpec((dev_rows, slots * blk), lambda i, a, b: (i, 0)),
                pl.BlockSpec((8, 2 * blk), lambda i, a, b: (0, 0)),
            ],
            scratch_shapes=[
                pltpu.VMEM((n_mp, 2 * tok_rows, shard_cols), BF),
                pltpu.SemaphoreType.DMA((2 * n_mp,)),
            ],
        ),
        out_shape=[
            jax.ShapeDtypeStruct((half_rows, slots * blk), F32),
            jax.ShapeDtypeStruct((8, 2 * blk), F32),
        ],
        compiler_params=params(),
        cost_estimate=SMALL,
        name="pair_grad",
    )(
        window_starts.reshape(-1),
        pat_half,
        *own,
        *y_group,
        hid_own.reshape(half_rows, tok_rows).astype(hid_type),
        hid_got.reshape(half_rows, tok_rows).astype(hid_type),
    )
    biggest = jnp.maximum(jnp.max(top), 1e-30)
    scale = 16384.0 / biggest
    packed = (grad_half * scale).astype(F16).reshape(outer, dev_rows, slots * blk)
    lanes = [[2 * i + s for i in range(outer)] for s in range(2)]
    unscale = lax.all_to_all(
        jnp.broadcast_to(biggest / (16384.0 * all_tokens), (outer, 8, 128)),
        "dp", 0, 0, axis_index_groups=lanes,
    )
    packed = lax.all_to_all(packed, "dp", 0, 0, axis_index_groups=lanes)
    grad = jnp.sum(packed.astype(F32) * unscale[:, :1, :1], axis=0)

    input_grad = pl.pallas_call(
        functools.partial(input_grad_kernel, n_mp, per_shard, blk, per_step),
        grid_spec=pltpu.PrefetchScalarGridSpec(
            num_scalar_prefetch=1,
            grid=(block_rows // per_step,),
            in_specs=[ANY] * n_mp
            + [pl.BlockSpec((per_step * blk, slots * blk), lambda i, pat: (i, 0))],
            out_specs=pl.BlockSpec((tok_rows, per_step * blk), lambda i, pat: (0, i)),
            scratch_shapes=[
                pltpu.VMEM((n_mp, tok_rows, shard_cols), BF),
                pltpu.SemaphoreType.DMA((n_mp,)),
            ],
        ),
        out_shape=jax.ShapeDtypeStruct((tok_rows, mp_rows), BF),
        compiler_params=params(),
        cost_estimate=SMALL,
        name="input_grad",
    )(pat_all, *own, weights.reshape(mp_rows, slots * blk))

    _, my_starts, my_blocks = windows_of(dp * dev_rows, dev_rows, blk)
    pat_abs = jnp.take(pattern, my_blocks, axis=0).reshape(-1)
    pat_rel = jnp.bitwise_xor(pat_abs, mp * per_shard)
    smem = pl.BlockSpec(memory_space=pltpu.SMEM)
    direction = pl.pallas_call(
        functools.partial(direction_kernel, sk_per, window, n_windows),
        in_specs=[smem] * 3 + [VMEM] * 4 + [ANY] * len(comp_parts),
        out_specs=VMEM,
        out_shape=jax.ShapeDtypeStruct((dev_rows, slots, blk), F32),
        scratch_shapes=[
            pltpu.VMEM((col_blocks, rank, blk), BF),
            pltpu.VMEM((col_blocks, rank, blk), BF),
            pltpu.SemaphoreType.DMA((len(comp_parts),)),
        ],
        compiler_params=params(),
        cost_estimate=SMALL,
        name="direction",
    )(my_starts, pat_abs, pat_rel, grad, mixing, sk_high, sk_low, *comp_parts)
    return (input_grad, direction.reshape(1, dev_rows, slots, blk))


def solution(mesh):
    return jax.shard_map(
        per_device,
        mesh=mesh,
        in_specs=(
            P("mp", None, None),
            P("dp", "mp"),
            P("dp", "mp"),
            P(None, ("dp", "mp")),
            P(None, "mp", "dp"),
            P("mp", None),
        ),
        out_specs=(P("dp", "mp"), P("mp", "dp", None, None)),
        check_vma=False,
    )
```

time: 388 us -> 278 us (0.72); the launches traced: 381 us -> 277 us
  blocking collectives: 107 us -> 0 us
  waiting for transfers between devices: 67.1 us -> 104 us
  Pallas kernels: 103 us -> 66.7 us
  starting transfers between devices: 41.5 us -> 37 us
    all_gather x1 -> x0, blocking collectives: 107 us -> none  [per_device(): lax.all_gather(sketch.astype(F16), ('dp', 'mp'), axis=0, tiled=False)]
    pallas_call x4 -> x3, Pallas kernels: 61.3 us -> 32.3 us  [the longest x1 11.3 us: per_device(): pl.pallas_call(functools.partial(input_grad_kernel, n_mp, per_shard, blk,...]
    all_to_all x2 -> x3, waiting for transfers between devices: 6.25 us -> 20.4 us  [over_dp(): lax.all_to_all(jnp.broadcast_to(x[None], (n_dp, *x.shape)), 'dp', 0, 0)]
    all_to_all x1, waiting for transfers between devices: 0.01 us -> 13 us  [per_device(): pieces = lax.all_to_all(pieces, 'dp', 0, 0)]
    ppermute x14 -> x16, waiting for transfers between devices: 56.4 us -> 63.7 us  [swap(): return lax.ppermute(x, axis, [(i, i ^ bit) for i in range(size)])]
    pallas_call x1, Pallas kernels: 22.9 us -> 16 us  [per_device(): pl.pallas_call(functools.partial(compress_kernel, n_mp, per_shard, 1.0 /...]
    ppermute x14 -> x16, starting transfers between devices: 14.4 us -> 10 us  [swap(): return lax.ppermute(x, axis, [(i, i ^ bit) for i in range(size)])]
    all_to_all x1, waiting for transfers between devices: 0.01 us -> 4.13 us  [per_device(): packed = lax.all_to_all(packed, 'dp', 0, 0, axis_index_groups=lanes)]
  transfers between devices with their start and end apart: 19 -> 22, of which waited for: 7 -> 12; matrix products, arithmetic and copies ran while one was open for 13% -> 19% of each run, Pallas kernels for 23% -> 21%
where the time goes in v2:
time: 278 us; the launch traced here: 277 us
  waiting for transfers between devices  104 us (37%)
  Pallas kernels  66.7 us (24%)
  starting transfers between devices  37 us (13%)
  other arithmetic  36.6 us (13%)
  local copies, waits for them, and re-layouts  30.2 us (11%)
    ppermute x16, waiting for transfers between devices, swap(): return lax.ppermute(x, axis, [(i, i ^ bit) for i in range(size)])  63.7 us
    all_to_all x3, waiting for transfers between devices, over_dp(): lax.all_to_all(jnp.broadcast_to(x[None], (n_dp, *x.shape)), 'dp', 0, 0)  20.4 us
    pallas_call x1, Pallas kernels, per_device(): pl.pallas_call(functools.partial(compress_kernel, n_mp, per_shard, 1.0 /...  16 us
    pallas_call x1, Pallas kernels, per_device(): pl.pallas_call(mixing_kernel, in_specs=[VMEM] * 2, out_specs=VMEM, out_sh...  15.8 us
    unnamed x41, local copies, waits for them, and re-layouts  14.5 us
    all_to_all x3, starting transfers between devices, over_dp(): lax.all_to_all(jnp.broadcast_to(x[None], (n_dp, *x.shape)), 'dp', 0, 0)  14 us
    all_to_all x1, waiting for transfers between devices, per_device(): pieces = lax.all_to_all(pieces, 'dp', 0, 0)  13 us
    pallas_call x1, Pallas kernels, per_device(): pl.pallas_call(functools.partial(input_grad_kernel, n_mp, per_shard, blk,...  11.3 us
  transfers between devices with their start and end apart: 22, of which 12 were waited for; matrix products, arithmetic and copies ran while one was open for 19% of the time, Pallas kernels for 21%

profile of v2, /device:TPU:0, one launch (start us, length us, event | category | flops | bytes accessed | tf_op | source)
XLA Modules:
  0.0 276.9 jit_solution(8856118946372335895)
XLA Ops:
  6.7 6.2 %all-to-all-start.2 = ((f16[8,128,448]{1,2,0:T(8,128)(2,1)}), f16[8,128,448]{1,2,0:T(8,128)(2,1)}, u32[]{:S(2)}, u32[]{:S(2)}) async-start(f16[8,128,448]{1,2,0:T(8,128)(2,1)} %broadcast_in_dim.74), calls=%async_computation.2 | async-start | bytes 1835008 | tf_op jit(solution)/shard_map/all_to_all | solution.py:294
  14.9 12.9 %collective-permute-done.1.refs_2_ = bf16[256,2048]{1,0:T(8,128)(2,1)} collective-permute-done((bf16[256,2048]{1,0:T(8,128)(2,1)}, bf16[256,2048]{1,0:T(8,128)(2,1)}, u32[]{:S(2)}, u32[]{:S(2)}) %collective-permute-start.1) | collective-permute-done | bytes 1048608 | tf_op jit(solution)/shard_map/ppermute | solution.py:288
  30.9 17.1 %collective-permute-done.3.refs_4_ = bf16[256,2048]{1,0:T(8,128)(2,1)} collective-permute-done((bf16[256,2048]{1,0:T(8,128)(2,1)S(1)}, bf16[256,2048]{1,0:T(8,128)(2,1)}, u32[]{:S(2)}, u32[]{:S(2)}) %collective-permute-start.3) | collective-permute-done | bytes 1048608 | tf_op jit(solution)/shard_map/ppermute | solution.py:288
  55.9 16.0 %compress.1 = f32[64,128,128]{2,1,0:T(8,128)} custom-call(s32[224]{0:T(256)S(1)} %reshape.437.pat, bf16[256,2048]{1,0:T(8,128)(2,1)S(1)} %copy-done.3, bf16[256,2048]{1,0:T(8,128)(2,1)S(1)} %copy-done.5, bf16[256,2048]{1,0:T(8,128)(2,1)} %collective-permute-done.1.refs_2_, bf16[256,2048]{1,0:T(8,128)(2,1)} %collective-permute-done.2.refs_3_, ...), custom_call_target="tpu_custom_call" | custom-call | flops 1 | bytes 1 | tf_op jit(solution)/shard_map/compress/pallas_call | solution.py:314
  83.0 18.8 %collective-permute-done.7 = bf16[4,448,256]{2,1,0:T(8,128)(2,1)} collective-permute-done((bf16[4,448,256]{2,1,0:T(8,128)(2,1)}, bf16[4,448,256]{2,1,0:T(8,128)(2,1)}, u32[]{:S(2)}, u32[]{:S(2)}) %collective-permute-start.7) | collective-permute-done | bytes 917536 | tf_op jit(solution)/shard_map/ppermute | solution.py:288
  101.9 11.1 %pair_grad.1 = (f32[1792,1024]{1,0:T(8,128)}, f32[8,256]{1,0:T(8,128)S(1)}) custom-call(s32[16]{0:T(128)S(1)} %reshape.439.starts, s32[128]{0:T(128)S(1)} %select_n.221.pat, bf16[256,2048]{1,0:T(8,128)(2,1)S(1)} %copy-done.3, bf16[256,2048]{1,0:T(8,128)(2,1)S(1)} %copy-done.6, bf16[256,2048]{1,0:T(8,128)(2,1)} %collective-permute-done.1.refs_2_, ...), custom_call_target="tpu_custom_call" | custom-call | flops 1 | bytes 1 | tf_op jit(solution)/shard_map/pair_grad/pallas_call | solution.py:414
  114.9 4.5 %all-to-all-start.1 = ((f32[4,8,128]{2,1,0:T(8,128)}), f32[4,8,128]{2,1,0:T(8,128)S(1)}, u32[]{:S(2)}, u32[]{:S(2)}) async-start(f32[4,8,128]{2,1,0:T(8,128)} %broadcast_in_dim.72), calls=%async_computation.1 | async-start | bytes 32768 | tf_op jit(solution)/shard_map/all_to_all | solution.py:449
  122.0 3.1 %all-to-all-done.1 = f32[4,8,128]{2,1,0:T(8,128)S(1)} async-done(((f32[4,8,128]{2,1,0:T(8,128)}), f32[4,8,128]{2,1,0:T(8,128)S(1)}, u32[]{:S(2)}, u32[]{:S(2)}) %all-to-all-start.1) | async-done | bytes 16416 | tf_op jit(solution)/shard_map/all_to_all | solution.py:449
  125.0 3.5 %all-to-all-start.4 = ((f16[8,256,128]{2,1,0:T(8,128)(2,1)}), f16[8,256,128]{2,1,0:T(8,128)(2,1)S(1)}, u32[]{:S(2)}, u32[]{:S(2)}) async-start(f16[8,256,128]{2,1,0:T(8,128)(2,1)} %bitcast.25), calls=%async_computation.4 | async-start | bytes 1048576 | tf_op jit(solution)/shard_map/all_to_all | solution.py:343
  128.6 13.0 %all-to-all-done.4 = f16[8,256,128]{2,1,0:T(8,128)(2,1)S(1)} async-done(((f16[8,256,128]{2,1,0:T(8,128)(2,1)}), f16[8,256,128]{2,1,0:T(8,128)(2,1)S(1)}, u32[]{:S(2)}, u32[]{:S(2)}) %all-to-all-start.4) | async-done | bytes 524320 | tf_op jit(solution)/shard_map/all_to_all | solution.py:343
  142.4 3.7 %all-to-all-start.3 = ((f16[8,128,256]{2,1,0:T(8,128)(2,1)}), f16[8,128,256]{2,1,0:T(8,128)(2,1)S(1)}, u32[]{:S(2)}, u32[]{:S(2)}) async-start(f16[8,128,256]{2,1,0:T(8,128)(2,1)} %broadcast_in_dim.75), calls=%async_computation.3 | async-start | bytes 1048576 | tf_op jit(solution)/shard_map/all_to_all | solution.py:294
  146.2 13.7 %all-to-all-done.3 = f16[8,128,256]{2,1,0:T(8,128)(2,1)S(1)} async-done(((f16[8,128,256]{2,1,0:T(8,128)(2,1)}), f16[8,128,256]{2,1,0:T(8,128)(2,1)S(1)}, u32[]{:S(2)}, u32[]{:S(2)}) %all-to-all-start.3) | async-done | bytes 524320 | tf_op jit(solution)/shard_map/all_to_all | solution.py:294
  160.8 4.1 %all-to-all-start.5 = ((f16[8,256,128]{2,1,0:T(8,128)(2,1)}), f16[8,256,128]{2,1,0:T(8,128)(2,1)}, u32[]{:S(2)}, u32[]{:S(2)}) async-start(f16[8,256,128]{2,1,0:T(8,128)(2,1)} %broadcast_in_dim.77), calls=%async_computation.5 | async-start | bytes 1048576 | tf_op jit(solution)/shard_map/all_to_all | solution.py:294
  165.6 6.1 %multiply_convert_fusion = f16[1792,1024]{1,0:T(8,128)(2,1)} fusion(f32[1792,1024]{1,0:T(8,128)} %get-tuple-element.9, f32[]{:T(128)S(6)} %div.101), kind=kLoop, calls=%fused_computation.5 | loop fusion | flops 3670016 | bytes 11010052 | tf_op jit(solution)/shard_map/convert_element_type | solution.py:447
  171.7 6.6 %all-to-all-done.5 = f16[8,256,128]{2,1,0:T(8,128)(2,1)} async-done(((f16[8,256,128]{2,1,0:T(8,128)(2,1)}), f16[8,256,128]{2,1,0:T(8,128)(2,1)}, u32[]{:S(2)}, u32[]{:S(2)}) %all-to-all-start.5) | async-done | bytes 524320 | tf_op jit(solution)/shard_map/all_to_all | solution.py:294
  178.3 5.0 %all-to-all-start = ((f16[4,448,1024]{2,1,0:T(8,128)(2,1)}), f16[4,448,1024]{2,1,0:T(8,128)(2,1)}, u32[]{:S(2)}, u32[]{:S(2)}) async-start(f16[4,448,1024]{2,1,0:T(8,128)(2,1)} %bitcast.66), calls=%async_computation | async-start | bytes 7340032 | tf_op jit(solution)/shard_map/all_to_all | solution.py:453
  199.8 5.0 %collective-permute-done.12 = f32[128,256]{1,0:T(8,128)S(1)} collective-permute-done((f32[128,256]{1,0:T(8,128)S(1)}, f32[128,256]{1,0:T(8,128)S(1)}, u32[]{:S(2)}, u32[]{:S(2)}) %collective-permute-start.12) | collective-permute-done | bytes 131104 | tf_op jit(solution)/shard_map/ppermute | solution.py:288
  206.9 4.8 %copy.37 = bf16[448,8,8,128]{3,1,2,0:T(8,128)(2,1)} copy(bf16[448,8,8,128]{3,2,1,0:T(8,128)(2,1)S(1)} %bitcast.69) | data formatting | bytes 14680064
  212.3 8.3 %collective-permute-done.14 = f16[16,128,128]{2,1,0:T(8,128)(2,1)} collective-permute-done((f16[16,128,128]{2,1,0:T(8,128)(2,1)}, f16[16,128,128]{2,1,0:T(8,128)(2,1)}, u32[]{:S(2)}, u32[]{:S(2)}) %collective-permute-start.14) | collective-permute-done | bytes 524320 | tf_op jit(solution)/shard_map/ppermute | solution.py:288
  224.6 11.3 %input_grad.1 = bf16[256,3584]{1,0:T(8,128)(2,1)} custom-call(s32[224]{0:T(256)S(1)} %reshape.437.pat, bf16[256,2048]{1,0:T(8,128)(2,1)S(1)} %copy-done.3, bf16[256,2048]{1,0:T(8,128)(2,1)S(1)} %copy-done.7, bf16[256,2048]{1,0:T(8,128)(2,1)} %collective-permute-done.1.refs_2_, bf16[256,2048]{1,0:T(8,128)(2,1)} %collective-permute-done.2.refs_3_, ...), custom_call_target="tpu_custom_call" | custom-call | flops 1 | bytes 1 | tf_op jit(solution)/shard_map/input_grad/pallas_call | solution.py:456
  237.9 15.8 %mixing.1.refs_1_ = f32[256,256]{1,0:T(8,128)S(1)} custom-call(f32[128,128]{1,0:T(8,128)S(1)} %sketch_gram.1.ss_ref, f32[128,256]{1,0:T(8,128)S(1)} %add.274.cross_ref), custom_call_target="tpu_custom_call" | custom-call | flops 1 | bytes 1 | tf_op jit(solution)/shard_map/mixing/pallas_call | solution.py:388
  258.0 4.1 %all-to-all-done = f16[4,448,1024]{2,1,0:T(8,128)(2,1)} async-done(((f16[4,448,1024]{2,1,0:T(8,128)(2,1)}), f16[4,448,1024]{2,1,0:T(8,128)(2,1)}, u32[]{:S(2)}, u32[]{:S(2)}) %all-to-all-start) | async-done | bytes 3670048 | tf_op jit(solution)/shard_map/all_to_all | solution.py:453
  262.1 4.8 %multiply_reduce_fusion.refs_0_ = f32[448,1024]{1,0:T(8,128)} fusion(f16[4,448,1024]{2,1,0:T(8,128)(2,1)} %all-to-all-done, f32[4]{0:T(128)S(1)} %slice_reduce_fusion), kind=kLoop, calls=%fused_computation.4 | loop fusion | flops 5046272 | bytes 5505040 | tf_op jit(solution)/shard_map/reduce_sum | solution.py:454
  266.9 9.8 %direction.1 = f32[448,8,128]{2,1,0:T(8,128)} custom-call(s32[4]{0:T(128)S(1)} %pad_add_fusion.2.starts, s32[32]{0:T(128)S(1)} %select_n.208.pat_sk, s32[32]{0:T(128)S(1)} %broadcast_xor_fusion.1.pat_cp, f32[448,1024]{1,0:T(8,128)} %multiply_reduce_fusion.refs_0_, f32[256,256]{1,0:T(8,128)S(1)} %mixing.1.refs_1_, bf16[32,128,256]{2,1,0:T(8,128)(2,1)} %copy-done.1, ...), custom_call_target="tpu_custom_call" | custom-call | flops 1 | bytes 1 | tf_op jit(solution)/shard_map/direction/pallas_call | solution.py:479
  (138 shorter events, 65.6 us)
Async XLA Ops:
  0.6 27.2 %copy-start.16 = (s32[28,8]{0,1:T(8,128)S(1)}, s32[28,8]{0,1:T(8,128)}, u32[]{:S(2)}) copy-start(s32[28,8]{0,1:T(8,128)} %param.11) | copy-start | bytes 2692
  0.7 4.1 %collective-permute-start = (bf16[256,2048]{1,0:T(8,128)(2,1)}, bf16[256,2048]{1,0:T(8,128)(2,1)S(1)}, u32[]{:S(2)}, u32[]{:S(2)}) collective-permute-start(bf16[256,2048]{1,0:T(8,128)(2,1)} %refs_0_.5), channel_id=1, source_target_pairs={{0,1},{1,0},{2,3},{3,2},{4,5},{5,4},{6,7},{7,6},{8,9},{9,8},{10,11... | collective-permute-start | bytes 3145736 | tf_op jit(solution)/shard_map/ppermute | solution.py:288
  1.2 26.6 %collective-permute-start.1 = (bf16[256,2048]{1,0:T(8,128)(2,1)}, bf16[256,2048]{1,0:T(8,128)(2,1)}, u32[]{:S(2)}, u32[]{:S(2)}) collective-permute-start(bf16[256,2048]{1,0:T(8,128)(2,1)} %refs_0_.5), channel_id=1, source_target_pairs={{0,2},{1,3},{2,0},{3,1},{4,6},{5,7},{6,4},{7,5},{8,10},{9,11},{10,... | collective-permute-start | bytes 3145736 | tf_op jit(solution)/shard_map/ppermute | solution.py:288
  6.7 42.7 %all-to-all-start.2 = ((f16[8,128,448]{1,2,0:T(8,128)(2,1)}), f16[8,128,448]{1,2,0:T(8,128)(2,1)}, u32[]{:S(2)}, u32[]{:S(2)}) async-start(f16[8,128,448]{1,2,0:T(8,128)(2,1)} %broadcast_in_dim.74), calls=%async_computation.2 | async-start | bytes 1835008 | tf_op jit(solution)/shard_map/all_to_all | solution.py:294
  12.9 35.1 %collective-permute-start.3 = (bf16[256,2048]{1,0:T(8,128)(2,1)S(1)}, bf16[256,2048]{1,0:T(8,128)(2,1)}, u32[]{:S(2)}, u32[]{:S(2)}) collective-permute-start(bf16[256,2048]{1,0:T(8,128)(2,1)S(1)} %copy-done.3), channel_id=1, source_target_pairs={{0,4},{4,0},{8,12},{12,8},{16,20},{20,16},{24,28},{28,24},{1,5},{5... | collective-permute-start | bytes 3145736 | tf_op jit(solution)/shard_map/ppermute | solution.py:288
  27.8 26.9 %collective-permute-start.2 = (bf16[256,2048]{1,0:T(8,128)(2,1)}, bf16[256,2048]{1,0:T(8,128)(2,1)}, u32[]{:S(2)}, u32[]{:S(2)}) collective-permute-start(bf16[256,2048]{1,0:T(8,128)(2,1)} %collective-permute-done.1.refs_2_), channel_id=1, source_target_pairs={{0,1},{1,0},{2,3},{3,2},{4,5},{5,4},{6,7},{7,6},{8,9},{9,8},{10,11... | collective-permute-start | bytes 3145736 | tf_op jit(solution)/shard_map/ppermute | solution.py:288
  48.0 29.4 %collective-permute-start.5 = (bf16[256,2048]{1,0:T(8,128)(2,1)}, bf16[256,2048]{1,0:T(8,128)(2,1)}, u32[]{:S(2)}, u32[]{:S(2)}) collective-permute-start(bf16[256,2048]{1,0:T(8,128)(2,1)} %collective-permute-done.3.refs_4_), channel_id=1, source_target_pairs={{0,2},{1,3},{2,0},{3,1},{4,6},{5,7},{6,4},{7,5},{8,10},{9,11},{10,... | collective-permute-start | bytes 3145736 | tf_op jit(solution)/shard_map/ppermute | solution.py:288
  76.2 3.0 %collective-permute-start.8 = (f16[2,16,128,128]{3,2,1,0:T(8,128)(2,1)}, f16[2,16,128,128]{3,2,1,0:T(8,128)(2,1)}, u32[]{:S(2)}, u32[]{:S(2)}) collective-permute-start(f16[2,16,128,128]{3,2,1,0:T(8,128)(2,1)} %pad_maximum_fusion.1), channel_id=1, source_target_pairs={{0,1},{1,0},{2,3},{3,2},{4,5},{5,4},{6,7},{7,6},{8,9},{9,8},{10,11... | collective-permute-start | bytes 3145736 | tf_op jit(solution)/shard_map/ppermute | solution.py:288
  76.8 25.0 %collective-permute-start.4 = (bf16[256,2048]{1,0:T(8,128)(2,1)}, bf16[256,2048]{1,0:T(8,128)(2,1)}, u32[]{:S(2)}, u32[]{:S(2)}) collective-permute-start(bf16[256,2048]{1,0:T(8,128)(2,1)} %collective-permute-done.3.refs_4_), channel_id=1, source_target_pairs={{0,1},{1,0},{2,3},{3,2},{4,5},{5,4},{6,7},{7,6},{8,9},{9,8},{10,11... | collective-permute-start | bytes 3145736 | tf_op jit(solution)/shard_map/ppermute | solution.py:288
  77.4 24.5 %collective-permute-start.6 = (bf16[256,2048]{1,0:T(8,128)(2,1)}, bf16[256,2048]{1,0:T(8,128)(2,1)}, u32[]{:S(2)}, u32[]{:S(2)}) collective-permute-start(bf16[256,2048]{1,0:T(8,128)(2,1)} %collective-permute-done.5.refs_6_), channel_id=1, source_target_pairs={{0,1},{1,0},{2,3},{3,2},{4,5},{5,4},{6,7},{7,6},{8,9},{9,8},{10,11... | collective-permute-start | bytes 3145736 | tf_op jit(solution)/shard_map/ppermute | solution.py:288
  78.8 23.0 %collective-permute-start.7 = (bf16[4,448,256]{2,1,0:T(8,128)(2,1)}, bf16[4,448,256]{2,1,0:T(8,128)(2,1)}, u32[]{:S(2)}, u32[]{:S(2)}) collective-permute-start(bf16[4,448,256]{2,1,0:T(8,128)(2,1)} %get-tuple-element.8), channel_id=1, source_target_pairs={{0,4},{4,0},{8,12},{12,8},{16,20},{20,16},{24,28},{28,24},{1,5},{5... | collective-permute-start | bytes 2752520 | tf_op jit(solution)/shard_map/ppermute | solution.py:288
  81.7 37.7 %collective-permute-start.11 = (f16[16,128,128]{2,1,0:T(8,128)(2,1)}, f16[16,128,128]{2,1,0:T(8,128)(2,1)}, u32[]{:S(2)}, u32[]{:S(2)}) collective-permute-start(f16[16,128,128]{2,1,0:T(8,128)(2,1)} %fusion.4), channel_id=1, source_target_pairs={{0,2},{1,3},{2,0},{3,1},{4,6},{5,7},{6,4},{7,5},{8,10},{9,11},{10,... | collective-permute-start | bytes 1572872 | tf_op jit(solution)/shard_map/ppermute | solution.py:288
  114.9 10.2 %all-to-all-start.1 = ((f32[4,8,128]{2,1,0:T(8,128)}), f32[4,8,128]{2,1,0:T(8,128)S(1)}, u32[]{:S(2)}, u32[]{:S(2)}) async-start(f32[4,8,128]{2,1,0:T(8,128)} %broadcast_in_dim.72), calls=%async_computation.1 | async-start | bytes 32768 | tf_op jit(solution)/shard_map/all_to_all | solution.py:449
  125.0 16.6 %all-to-all-start.4 = ((f16[8,256,128]{2,1,0:T(8,128)(2,1)}), f16[8,256,128]{2,1,0:T(8,128)(2,1)S(1)}, u32[]{:S(2)}, u32[]{:S(2)}) async-start(f16[8,256,128]{2,1,0:T(8,128)(2,1)} %bitcast.25), calls=%async_computation.4 | async-start | bytes 1048576 | tf_op jit(solution)/shard_map/all_to_all | solution.py:343
  142.4 17.5 %all-to-all-start.3 = ((f16[8,128,256]{2,1,0:T(8,128)(2,1)}), f16[8,128,256]{2,1,0:T(8,128)(2,1)S(1)}, u32[]{:S(2)}, u32[]{:S(2)}) async-start(f16[8,128,256]{2,1,0:T(8,128)(2,1)} %broadcast_in_dim.75), calls=%async_computation.3 | async-start | bytes 1048576 | tf_op jit(solution)/shard_map/all_to_all | solution.py:294
  160.8 17.5 %all-to-all-start.5 = ((f16[8,256,128]{2,1,0:T(8,128)(2,1)}), f16[8,256,128]{2,1,0:T(8,128)(2,1)}, u32[]{:S(2)}, u32[]{:S(2)}) async-start(f16[8,256,128]{2,1,0:T(8,128)(2,1)} %broadcast_in_dim.77), calls=%async_computation.5 | async-start | bytes 1048576 | tf_op jit(solution)/shard_map/all_to_all | solution.py:294
  165.0 18.3 %collective-permute-start.9 = (f16[8,128,256]{2,1,0:T(8,128)(2,1)S(1)}, f16[8,128,256]{2,1,0:T(8,128)(2,1)S(1)}, u32[]{:S(2)}, u32[]{:S(2)}) collective-permute-start(f16[8,128,256]{2,1,0:T(8,128)(2,1)S(1)} %all-to-all-done.3), channel_id=1, source_target_pairs={{0,2},{1,3},{2,0},{3,1},{4,6},{5,7},{6,4},{7,5},{8,10},{9,11},{10,... | collective-permute-start | bytes 1572872 | tf_op jit(solution)/shard_map/ppermute | solution.py:288
  178.3 83.8 %all-to-all-start = ((f16[4,448,1024]{2,1,0:T(8,128)(2,1)}), f16[4,448,1024]{2,1,0:T(8,128)(2,1)}, u32[]{:S(2)}, u32[]{:S(2)}) async-start(f16[4,448,1024]{2,1,0:T(8,128)(2,1)} %bitcast.66), calls=%async_computation | async-start | bytes 7340032 | tf_op jit(solution)/shard_map/all_to_all | solution.py:453
  183.6 2.9 %collective-permute-start.10 = (f16[2,8,128,256]{3,2,1,0:T(8,128)(2,1)S(1)}, f16[2,8,128,256]{3,2,1,0:T(8,128)(2,1)}, u32[]{:S(2)}, u32[]{:S(2)}) collective-permute-start(f16[2,8,128,256]{3,2,1,0:T(8,128)(2,1)S(1)} %pad_maximum_fusion.2), channel_id=1, source_target_pairs={{0,1},{1,0},{2,3},{3,2},{4,5},{5,4},{6,7},{7,6},{8,9},{9,8},{10,11... | collective-permute-start | bytes 3145736 | tf_op jit(solution)/shard_map/ppermute | solution.py:288
  194.9 41.1 %copy-start = (bf16[32,128,256]{2,1,0:T(8,128)(2,1)}, bf16[32,128,256]{2,1,0:T(8,128)(2,1)S(1)}, u32[]{:S(2)}) copy-start(bf16[32,128,256]{2,1,0:T(8,128)(2,1)S(1)} %get-tuple-element.14.sl_ref.refs_3_) | copy-start | bytes 6291460
  199.2 5.6 %collective-permute-start.12 = (f32[128,256]{1,0:T(8,128)S(1)}, f32[128,256]{1,0:T(8,128)S(1)}, u32[]{:S(2)}, u32[]{:S(2)}) collective-permute-start(f32[128,256]{1,0:T(8,128)S(1)} %cross_gram.1), channel_id=1, source_target_pairs={{0,2},{1,3},{2,0},{3,1},{4,6},{5,7},{6,4},{7,5},{8,10},{9,11},{10,... | collective-permute-start | bytes 393224 | tf_op jit(solution)/shard_map/ppermute | solution.py:288
  204.9 1.4 collective-permute-start.13
  206.3 14.4 %collective-permute-start.14 = (f16[16,128,128]{2,1,0:T(8,128)(2,1)}, f16[16,128,128]{2,1,0:T(8,128)(2,1)}, u32[]{:S(2)}, u32[]{:S(2)}) collective-permute-start(f16[16,128,128]{2,1,0:T(8,128)(2,1)} %bitcast.26), channel_id=1, source_target_pairs={{0,2},{1,3},{2,0},{3,1},{4,6},{5,7},{6,4},{7,5},{8,10},{9,11},{10,... | collective-permute-start | bytes 1572872 | tf_op jit(solution)/shard_map/ppermute | solution.py:288
  223.2 31.9 %collective-permute-start.15 = (f16[2,16,128,128]{3,2,1,0:T(8,128)(2,1)}, f16[2,16,128,128]{3,2,1,0:T(8,128)(2,1)}, u32[]{:S(2)}, u32[]{:S(2)}) collective-permute-start(f16[2,16,128,128]{3,2,1,0:T(8,128)(2,1)} %pad_maximum_fusion.3), channel_id=1, source_target_pairs={{0,1},{1,0},{2,3},{3,2},{4,5},{5,4},{6,7},{7,6},{8,9},{9,8},{10,11... | collective-permute-start | bytes 3145736 | tf_op jit(solution)/shard_map/ppermute | solution.py:288
  (17 other events, 150.1 us)

commit v3 on v2

--- a/solution.py
+++ b/solution.py
@@ -60,7 +60,7 @@
     return held[shard, :, pl.ds(offset, size)]
 
 
-def compress_kernel(n_shards, per_shard, scale, per_step, pat, *refs):
+def compress_kernel(n_shards, per_shard, scale, per_step, pat, pat_out, *refs):
     shards = refs[:n_shards]
     hid_ref, proj_ref, out_ref, held, sems = refs[n_shards:]
     blk = out_ref.shape[1]
@@ -84,17 +84,18 @@
             )
             part = dot(left, chosen)
             parts.append(part[:blk] + part[blk:])
+        outs = [pat_out[row * SLOTS + j] for j in range(SLOTS)]
         sums = [
             out_ref[c] + parts[j // 2][:, (j % 2) * blk : (j % 2 + 1) * blk]
-            for j, c in enumerate(cols)
+            for j, c in enumerate(outs)
         ]
-        for c, total in zip(cols, sums):
+        for c, total in zip(outs, sums):
             out_ref[c] = total
 
 
-def grad_kernel(n_shards, per_shard, blk, window, n_windows, starts, pat, *refs):
+def grad_kernel(n_shards, per_shard, blk, window, n_windows, starts, pat, scale, *refs):
     shards = refs[: 2 * n_shards]
-    own_ref, got_ref, out_ref, top_ref, held, sems = refs[2 * n_shards :]
+    own_ref, got_ref, out_ref, held, sems = refs[2 * n_shards :]
     toks = own_ref.shape[1]
 
     @pl.when(pl.program_id(0) == 0)
@@ -106,9 +107,7 @@
             ],
             sems,
         )
-        top_ref[...] = jnp.zeros_like(top_ref)
-
-    top = top_ref[...]
+
     for w in range(n_windows):
         index = pl.program_id(0) * n_windows + w
         rows = pl.ds(pl.multiple_of(starts[index], window // 2 if window >= 32 else 8), window)
@@ -118,12 +117,7 @@
                 [column_block(held, pat[index * SLOTS + j + i], per_shard, blk) for i in (0, 1)],
                 axis=1,
             )
-            part = dot(hid, chosen)
-            out_ref[rows, j * blk : (j + 2) * blk] = part
-            size = jnp.abs(part)
-            for i in range(0, window, 8):
-                top = jnp.maximum(top, size[i : i + 8])
-    top_ref[...] = top
+            out_ref[rows, j * blk : (j + 2) * blk] = dot(hid, chosen) * scale[0]
 
 
 def input_grad_kernel(n_shards, per_shard, blk, per_step, pat, *refs):
@@ -212,7 +206,7 @@
     out_ref[...] = -mm(inverse, x) / (sqrt_eps * sqrt_fro)
 
 
-def direction_kernel(per, window, n_windows, starts, pat_sk, pat_cp, *refs):
+def direction_kernel(per, window, n_windows, starts, pat, *refs):
     g_ref, m_ref, skh, skl = refs[:4]
     parts, (out_ref, cph, cpl, sems) = refs[4:-4], refs[-4:]
     blk = cph.shape[2]
@@ -224,19 +218,19 @@
         at += size
     load_all(pairs, sems)
 
-    def gathered(sk, cp, c_sk, c_cp):
-        shard = c_sk // per
-        offset = pl.multiple_of((c_sk - shard * per) * blk, blk)
-        return jnp.concatenate([sk[shard, :, pl.ds(offset, blk)], cp[c_cp]], axis=0)
+    def gathered(sk, cp, c):
+        shard = c // per
+        offset = pl.multiple_of((c - shard * per) * blk, blk)
+        return jnp.concatenate([sk[shard, :, pl.ds(offset, blk)], cp[c]], axis=0)
 
     for w in range(n_windows):
         rows = pl.ds(pl.multiple_of(starts[w], window // 2 if window >= 32 else 8), window)
-        cols = [(pat_sk[w * SLOTS + k], pat_cp[w * SLOTS + k]) for k in range(SLOTS)]
+        cols = [pat[w * SLOTS + k] for k in range(SLOTS)]
         g = g_ref[rows, :]
         g_high = g.astype(BF).astype(F32)
         g_both = jnp.concatenate([g_high, g - g_high], axis=0).astype(BF)
-        high = [gathered(skh, cph, *c) for c in cols]
-        low = [gathered(skl, cpl, *c) for c in cols]
+        high = [gathered(skh, cph, c) for c in cols]
+        low = [gathered(skl, cpl, c) for c in cols]
         both = dot_nt(g_both, jnp.concatenate(high, axis=1))
         projected = both[:window] + both[window:]
         projected += dot_nt(g_high.astype(BF), jnp.concatenate(low, axis=1))
@@ -293,22 +287,47 @@
     def over_dp(x):
         return lax.all_to_all(jnp.broadcast_to(x[None], (n_dp, *x.shape)), "dp", 0, 0)
 
-    x_half = swap(cotangent, "mp", 2)
-    y_own = swap(cotangent, "dp", 1)
-    core_half = swap(cotangent, "mp", 1)
-    y_x = swap(y_own, "mp", 2)
-    own = [cotangent, core_half, x_half, swap(x_half, "mp", 1)]
-    pattern_rel = jnp.bitwise_xor(pattern, mp * per_shard)
-
+    largest = jnp.stack([jnp.max(jnp.abs(hidden)), jnp.max(jnp.abs(cotangent))]).astype(F32)
+    largest = lax.pmax(jnp.broadcast_to(largest[:, None], (2, 128)), ("dp", "mp"))
+    bound = jnp.maximum(largest[0, 0] * largest[1, 0] * all_tokens, 1e-30)
+    grad_scale = 32768.0 / bound
+
+    width = sketch.shape[1]
     proj16 = (projection.reshape(rank, dev_rows) * PROJ_SCALE).astype(F16)
-    proj_all = over_dp(after(proj16, core_half))
-    proj_all = proj_all.transpose(1, 0, 2).reshape(rank, mp_rows).astype(F32)
-
+    early = over_dp(jnp.concatenate([sketch.astype(F16), proj16], axis=1))
+    proj_all = early[:, :, width:].transpose(1, 0, 2).reshape(rank, mp_rows).astype(F32)
+    sk_own = early[:, :, :width]
     hid_t = hidden.T
     hid_parts = hid_t.reshape(outer, 2, dev_rows, tok_rows)
     hid_own = lax.dynamic_index_in_dim(hid_parts, side, 1, keepdims=False)
     hid_send = lax.dynamic_index_in_dim(hid_parts, 1 - side, 1, keepdims=False)
-    hid_got = swap(after(hid_send, y_own), "dp", 1)
+    x_half, y_own, core_half, proj_all, sk_own, hid_t, hid_own, hid_send, weights_2d = (
+        lax.optimization_barrier(
+            (
+                swap(cotangent, "mp", 2),
+                swap(cotangent, "dp", 1),
+                swap(cotangent, "mp", 1),
+                proj_all,
+                sk_own,
+                hid_t,
+                hid_own,
+                hid_send,
+                weights.reshape(mp_rows, slots * blk),
+            )
+        )
+    )
+    own = [cotangent, core_half, x_half, swap(x_half, "mp", 1)]
+    y_x = swap(y_own, "mp", 2)
+    hid_got = swap(hid_send, "dp", 1)
+    pattern_rel = jnp.bitwise_xor(pattern, mp * per_shard)
+
+    def place(block):
+        if width < blk:
+            return jnp.bitwise_xor(block, mp * per_shard)
+        per = width // blk
+        shard, rest = block // per, block % per
+        near_mp = jnp.bitwise_xor(shard % n_mp, mp)
+        return (near_mp * n_dp + shard // n_mp) * per + rest
 
     pat_all = pattern_rel.reshape(-1)
     partial_c = pl.pallas_call(
@@ -316,14 +335,14 @@
             compress_kernel, n_mp, per_shard, 1.0 / (PROJ_SCALE * all_tokens), per_step
         ),
         grid_spec=pltpu.PrefetchScalarGridSpec(
-            num_scalar_prefetch=1,
+            num_scalar_prefetch=2,
             grid=(block_rows // per_step,),
             in_specs=[ANY] * n_mp
             + [
-                pl.BlockSpec((per_step * blk, tok_rows), lambda i, pat: (i, 0)),
-                pl.BlockSpec((rank, per_step * blk), lambda i, pat: (0, i)),
+                pl.BlockSpec((per_step * blk, tok_rows), lambda i, a, b: (i, 0)),
+                pl.BlockSpec((rank, per_step * blk), lambda i, a, b: (0, i)),
             ],
-            out_specs=pl.BlockSpec((col_blocks, rank, blk), lambda i, pat: (0, 0, 0)),
+            out_specs=pl.BlockSpec((col_blocks, rank, blk), lambda i, a, b: (0, 0, 0)),
             scratch_shapes=[
                 pltpu.VMEM((n_mp, tok_rows, shard_cols), BF),
                 pltpu.SemaphoreType.DMA((n_mp,)),
@@ -333,32 +352,35 @@
         compiler_params=params(),
         cost_estimate=SMALL,
         name="compress",
-    )(pat_all, *own, hid_t, proj_all)
+    )(pat_all, place(pattern).reshape(-1), *own, hid_t, proj_all)
 
     quarters = partial_c.reshape(n_mp, per_shard, rank, blk)
-    sent = swap(jnp.stack([quarters[1], quarters[3]]).astype(F16), "mp", 1)
-    far_half = (quarters[2] + sent[1].astype(F32)).astype(F16)
-    quarter = (quarters[0] + sent[0].astype(F32)) + swap(far_half, "mp", 2).astype(F32)
+    got_far = swap(quarters[3].astype(F16), "mp", 1)
+    got_near = swap(quarters[1].astype(F16), "mp", 1)
+    far_half = (quarters[2] + got_far.astype(F32)).astype(F16)
+    quarter = (quarters[0] + got_near.astype(F32)) + swap(far_half, "mp", 2).astype(F32)
     pieces = quarter.astype(F16).reshape(n_dp, per_shard * rank // n_dp, blk)
     pieces = lax.all_to_all(pieces, "dp", 0, 0)
     piece = jnp.sum(pieces.astype(F32), axis=0).astype(F16)
     quarter16 = over_dp(piece).reshape(per_shard, rank, blk)
 
-    sk_own = over_dp(after(sketch.astype(F16), sent))
+    sk_own = after(sk_own, pieces)
     sk_far = swap(sk_own, "mp", 2)
-    sk_near = swap(jnp.stack([sk_own, sk_far]), "mp", 1)
-    sk_rel = jnp.stack([sk_own, sk_near[0], sk_far, sk_near[1]])
-    sk_abs = jnp.take(sk_rel, jnp.bitwise_xor(jnp.arange(n_mp, dtype=jnp.int32), mp), axis=0)
-    width = sketch.shape[1]
+    sk_parts = [sk_own, swap(sk_own, "mp", 1), sk_far, swap(sk_far, "mp", 1)]
     if width < blk:
-        sketch_all = sk_abs.reshape(n_mp, col_blocks, blk // width // n_mp, rank, width)
-        sketch_all = sketch_all.transpose(1, 3, 2, 0, 4).reshape(col_blocks, rank, blk)
-    else:
-        sketch_all = sk_abs.swapaxes(0, 1).reshape(n_dp * n_mp, rank, width)
-    sk_high, sk_low = split2_xla(sketch_all.astype(F32))
+        sk_abs = jnp.take(
+            jnp.stack(sk_parts), jnp.bitwise_xor(jnp.arange(n_mp, dtype=jnp.int32), mp), axis=0
+        )
+        sk_abs = sk_abs.reshape(n_mp, col_blocks, blk // width // n_mp, rank, width)
+        sk_abs = sk_abs.transpose(1, 3, 2, 0, 4).reshape(n_mp, per_shard, rank, blk)
+        sk_parts = [
+            lax.dynamic_index_in_dim(sk_abs, jnp.bitwise_xor(mp, i), 0, keepdims=False)
+            for i in range(n_mp)
+        ]
+    oh, ol = split2_xla(sk_parts[0].astype(F32))
+    sk_high, sk_low = split2_xla(jnp.concatenate(sk_parts, axis=0).astype(F32))
 
     sk_per = sk_high.shape[2] // blk
-    sk_quarter = col_blocks // sk_per // n_mp
     qh, ql = split2_xla(quarter16.astype(F32))
     cross = pl.pallas_call(
         cross_gram_kernel,
@@ -368,12 +390,7 @@
         compiler_params=params(),
         cost_estimate=SMALL,
         name="cross_gram",
-    )(
-        qh,
-        ql,
-        lax.dynamic_slice_in_dim(sk_high, mp * sk_quarter, sk_quarter, 0),
-        lax.dynamic_slice_in_dim(sk_low, mp * sk_quarter, sk_quarter, 0),
-    )
+    )(qh, ql, oh, ol)
     sketch_gram = pl.pallas_call(
         sketch_gram_kernel,
         in_specs=[VMEM] * 2,
@@ -395,11 +412,11 @@
         name="mixing",
     )(sketch_gram, cross)
 
-    far = swap(after(quarter16, cross), "mp", 2)
-    near = swap(jnp.stack([quarter16, far]), "mp", 1)
-    fh, fl = split2_xla(far.astype(F32))
-    nh, nl = split2_xla(near.astype(F32))
-    comp_parts = [qh, nh[0], fh, nh[1], ql, nl[0], fl, nl[1]]
+    quarter16 = after(quarter16, cross)
+    far = swap(quarter16, "mp", 2)
+    comp_parts = [quarter16, swap(quarter16, "mp", 1), far, swap(far, "mp", 1)]
+    comp_parts = [split2_xla(part.astype(F32)) for part in comp_parts]
+    comp_parts = [part[0] for part in comp_parts] + [part[1] for part in comp_parts]
 
     y_group = [y_own, swap(y_own, "mp", 1), y_x, swap(y_x, "mp", 1)]
     half_rows = outer * dev_rows
@@ -411,47 +428,50 @@
     n_windows = window_starts.shape[1]
     pat_half = jnp.take(pattern_rel, window_blocks.reshape(-1), axis=0).reshape(-1)
     hid_type = BF if window % 32 == 0 else F32
-    grad_half, top = pl.pallas_call(
+    grad_half = pl.pallas_call(
         functools.partial(grad_kernel, n_mp, per_shard, blk, window, n_windows),
         grid_spec=pltpu.PrefetchScalarGridSpec(
-            num_scalar_prefetch=2,
+            num_scalar_prefetch=3,
             grid=(outer,),
             in_specs=[ANY] * (2 * n_mp)
-            + [pl.BlockSpec((dev_rows, tok_rows), lambda i, a, b: (i, 0))] * 2,
-            out_specs=[
-                pl.BlockSpec((dev_rows, slots * blk), lambda i, a, b: (i, 0)),
-                pl.BlockSpec((8, 2 * blk), lambda i, a, b: (0, 0)),
-            ],
+            + [pl.BlockSpec((dev_rows, tok_rows), lambda i, a, b, c: (i, 0))] * 2,
+            out_specs=pl.BlockSpec((dev_rows, slots * blk), lambda i, a, b, c: (i, 0)),
             scratch_shapes=[
                 pltpu.VMEM((n_mp, 2 * tok_rows, shard_cols), BF),
                 pltpu.SemaphoreType.DMA((2 * n_mp,)),
             ],
         ),
-        out_shape=[
-            jax.ShapeDtypeStruct((half_rows, slots * blk), F32),
-            jax.ShapeDtypeStruct((8, 2 * blk), F32),
-        ],
+        out_shape=jax.ShapeDtypeStruct((half_rows, slots * blk), F32),
         compiler_params=params(),
         cost_estimate=SMALL,
         name="pair_grad",
     )(
         window_starts.reshape(-1),
         pat_half,
+        grad_scale[None],
         *own,
         *y_group,
         hid_own.reshape(half_rows, tok_rows).astype(hid_type),
         hid_got.reshape(half_rows, tok_rows).astype(hid_type),
     )
-    biggest = jnp.maximum(jnp.max(top), 1e-30)
-    scale = 16384.0 / biggest
-    packed = (grad_half * scale).astype(F16).reshape(outer, dev_rows, slots * blk)
-    lanes = [[2 * i + s for i in range(outer)] for s in range(2)]
-    unscale = lax.all_to_all(
-        jnp.broadcast_to(biggest / (16384.0 * all_tokens), (outer, 8, 128)),
-        "dp", 0, 0, axis_index_groups=lanes,
-    )
-    packed = lax.all_to_all(packed, "dp", 0, 0, axis_index_groups=lanes)
-    grad = jnp.sum(packed.astype(F32) * unscale[:, :1, :1], axis=0)
+    grad_half = grad_half.reshape(outer, dev_rows, slots * blk)
+    level = dp // 2
+
+    def block_of(index):
+        index = jnp.clip(index, 0, outer - 1)
+        return lax.dynamic_index_in_dim(grad_half, index, 0, keepdims=False)
+
+    grad = block_of(level)
+    if outer <= 4:
+        for d in sorted((d for d in range(1 - outer, outer) if d), key=lambda d: -abs(d)):
+            perm = [(i, i + 2 * d) for i in range(n_dp) if 0 <= i + 2 * d < n_dp]
+            got = lax.ppermute(block_of(level + d).astype(F16), "dp", perm)
+            grad = grad + got.astype(F32)
+    else:
+        lanes = [[2 * i + s for i in range(outer)] for s in range(2)]
+        got = lax.all_to_all(grad_half.astype(F16), "dp", 0, 0, axis_index_groups=lanes)
+        grad = jnp.sum(got.astype(F32), axis=0)
+    grad = grad * (1.0 / (grad_scale * all_tokens))
 
     input_grad = pl.pallas_call(
         functools.partial(input_grad_kernel, n_mp, per_shard, blk, per_step),
@@ -470,15 +490,14 @@
         compiler_params=params(),
         cost_estimate=SMALL,
         name="input_grad",
-    )(pat_all, *own, weights.reshape(mp_rows, slots * blk))
+    )(pat_all, *own, after(weights_2d, pieces))
 
     _, my_starts, my_blocks = windows_of(dp * dev_rows, dev_rows, blk)
-    pat_abs = jnp.take(pattern, my_blocks, axis=0).reshape(-1)
-    pat_rel = jnp.bitwise_xor(pat_abs, mp * per_shard)
+    my_pat = jnp.take(place(pattern), my_blocks, axis=0).reshape(-1)
     smem = pl.BlockSpec(memory_space=pltpu.SMEM)
     direction = pl.pallas_call(
         functools.partial(direction_kernel, sk_per, window, n_windows),
-        in_specs=[smem] * 3 + [VMEM] * 4 + [ANY] * len(comp_parts),
+        in_specs=[smem] * 2 + [VMEM] * 4 + [ANY] * len(comp_parts),
         out_specs=VMEM,
         out_shape=jax.ShapeDtypeStruct((dev_rows, slots, blk), F32),
         scratch_shapes=[
@@ -489,7 +508,7 @@
         compiler_params=params(),
         cost_estimate=SMALL,
         name="direction",
-    )(my_starts, pat_abs, pat_rel, grad, mixing, sk_high, sk_low, *comp_parts)
+    )(my_starts, my_pat, grad, mixing, sk_high, sk_low, *comp_parts)
     return (input_grad, direction.reshape(1, dev_rows, slots, blk))
 
 

time: 278 us -> 344 us (1.24)
  the two profiles are of different devices: /device:TPU:0 before, /device:TPU:9 now
where the time goes in v3:
time: 344 us; the launch traced here: 343 us
  waiting for transfers between devices  108 us (31%)
  Pallas kernels  66.3 us (19%)
  blocking collectives  54.7 us (16%)
  starting transfers between devices  51.3 us (15%)
  other arithmetic  34.3 us (10%)
  local copies, waits for them, and re-layouts  25.7 us (7%)
    ppermute x6, waiting for transfers between devices, per_device(): got = lax.ppermute(block_of(level + d).astype(F16), 'dp', perm)  56.8 us
    pmax x1, blocking collectives, per_device(): lax.pmax(jnp.broadcast_to(largest[:, None], (2, 128)), ('dp', 'mp'))  54.7 us
    ppermute x19, waiting for transfers between devices, swap(): return lax.ppermute(x, axis, [(i, i ^ bit) for i in range(size)])  35.1 us
    ppermute x19, starting transfers between devices, swap(): return lax.ppermute(x, axis, [(i, i ^ bit) for i in range(size)])  20.8 us
    pallas_call x1, Pallas kernels, per_device(): pl.pallas_call(functools.partial(compress_kernel, n_mp, per_shard, 1.0 /...  16 us
    pallas_call x1, Pallas kernels, per_device(): pl.pallas_call(mixing_kernel, in_specs=[VMEM] * 2, out_specs=VMEM, out_sh...  16 us
    all_to_all x2, waiting for transfers between devices, over_dp(): lax.all_to_all(jnp.broadcast_to(x[None], (n_dp, *x.shape)), 'dp', 0, 0)  15.6 us
    ppermute x6, starting transfers between devices, per_device(): got = lax.ppermute(block_of(level + d).astype(F16), 'dp', perm)  14.8 us
  transfers between devices with their start and end apart: 28, of which 8 were waited for; matrix products, arithmetic and copies ran while one was open for 15% of the time, Pallas kernels for 12%

profile of v3, /device:TPU:9, one launch (start us, length us, event | category | flops | bytes accessed | tf_op | source)
XLA Modules:
  0.0 342.6 jit_solution(17192535124208342322)
XLA Ops:
  4.0 5.9 %all-to-all-start = ((f16[8,128,704]{1,2,0:T(8,128)(2,1)}), f16[8,128,704]{1,2,0:T(8,128)(2,1)}, u32[]{:S(2)}, u32[]{:S(2)}) async-start(f16[8,128,704]{1,2,0:T(8,128)(2,1)} %broadcast_in_dim.56), calls=%async_computation | async-start | bytes 2883584 | tf_op jit(solution)/shard_map/all_to_all | solution.py:288
  14.0 2.9 copy.33
  16.9 7.9 %copy.44 = bf16[448,8,8,128]{3,1,2,0:T(8,128)(2,1)} copy(bf16[448,8,8,128]{3,2,1,0:T(8,128)(2,1)} %bitcast.68) | data formatting | bytes 14680064
  26.2 15.6 %all-to-all-done = f16[8,128,704]{1,2,0:T(8,128)(2,1)} async-done(((f16[8,128,704]{1,2,0:T(8,128)(2,1)}), f16[8,128,704]{1,2,0:T(8,128)(2,1)}, u32[]{:S(2)}, u32[]{:S(2)}) %all-to-all-start) | async-done | bytes 1441824 | tf_op jit(solution)/shard_map/all_to_all | solution.py:288
  51.2 2.7 copy.38.refs_5_
  53.9 16.0 %compress.1 = f32[64,128,128]{2,1,0:T(8,128)} custom-call(s32[224]{0:T(256)S(1)} %reshape.441.pat, s32[224]{0:T(256)S(1)} %reshape.444.pat_out, bf16[256,2048]{1,0:T(8,128)(2,1)S(1)} %copy-done.2, bf16[256,2048]{1,0:T(8,128)(2,1)} %collective-permute-done.2.refs_1_, bf16[256,2048]{1,0:T(8,128)(2,1)} %collective-permute-done.refs_2_, ...), custom_call_target="tpu_custom_call" | custom-call | flops 1 | bytes 1 | tf_op jit(solution)/shard_map/compress/pallas_call | solution.py:333
  69.9 2.7 convert.6
  80.9 29.0 %collective-permute-done.6 = f16[16,128,128]{2,1,0:T(8,128)(2,1)} collective-permute-done((f16[16,128,128]{2,1,0:T(8,128)(2,1)}, f16[16,128,128]{2,1,0:T(8,128)(2,1)}, u32[]{:S(2)}, u32[]{:S(2)}) %collective-permute-start.6) | collective-permute-done | bytes 524320 | tf_op jit(solution)/shard_map/ppermute | solution.py:282
  112.4 4.5 %all-to-all-start.1 = ((f16[8,256,128]{2,1,0:T(8,128)(2,1)}), f16[8,256,128]{2,1,0:T(8,128)(2,1)}, u32[]{:S(2)}, u32[]{:S(2)}) async-start(f16[8,256,128]{2,1,0:T(8,128)(2,1)} %bitcast.8), calls=%async_computation.1 | async-start | bytes 1048576 | tf_op jit(solution)/shard_map/all_to_all | solution.py:363
  122.9 54.7 %pmax.7 = f32[2,128]{1,0:T(2,128)S(1)} all-reduce(f32[2,128]{1,0:T(2,128)S(1)} %broadcast_in_dim.63), channel_id=1, replica_groups=mesh['dp'=8,'mp'=4] {'dp','mp'}, use_global_device_ids=true, to_apply=%region_2.3 | all-reduce | flops 256 | bytes 2048 | tf_op jit(solution)/shard_map/pmax | solution.py:291
  180.4 5.3 %all-to-all-start.2 = ((f16[8,256,128]{2,1,0:T(8,128)(2,1)}), f16[8,256,128]{2,1,0:T(8,128)(2,1)}, u32[]{:S(2)}, u32[]{:S(2)}) async-start(f16[8,256,128]{2,1,0:T(8,128)(2,1)} %broadcast_in_dim.65), calls=%async_computation.2 | async-start | bytes 1048576 | tf_op jit(solution)/shard_map/all_to_all | solution.py:288
  187.4 10.4 %pair_grad.1 = f32[1792,1024]{1,0:T(8,128)} custom-call(s32[16]{0:T(128)S(1)} %reshape.446.starts, s32[128]{0:T(128)S(1)} %select_n.237.pat, f32[1]{0:T(128)} %bitcast.17.scale, bf16[256,2048]{1,0:T(8,128)(2,1)S(1)} %copy-done.2, bf16[256,2048]{1,0:T(8,128)(2,1)} %collective-permute-done.2.refs_1_, bf16[256,2048]{1,0:T(8,128)(2,1)} %collective-permute-done.refs_2_, ...), custom_call_target="tpu_custom_call" | custom-call | flops 1 | bytes 1 | tf_op jit(solution)/shard_map/pair_grad/pallas_call | solution.py:431
  197.8 7.1 %fusion.16 = (f16[448,1024]{1,0:T(8,128)(2,1)}, f16[448,1024]{1,0:T(8,128)(2,1)}, f16[448,1024]{1,0:T(8,128)(2,1)}, f16[448,1024]{1,0:T(8,128)(2,1)}, f16[448,1024]{1,0:T(8,128)(2,1)}, /*index=5*/f16[448,1024]{1,0:T(8,128)(2,1)}) fusion(f32[4,448,1024]{2,1,0:T(8,128)} %bitcast.65, s32[]{:T(128)S(6)} %min.23, s32[]{:T(128)S(6)} %min.28, s32[]{:T(128)S(6)} %min.27, ...), kind=kLoop, calls=%fused_computation.46 | loop fusion | flops 2752512 | bytes 16515096 | tf_op jit(solution)/shard_map/convert_element_type | solution.py:468
  204.9 3.0 collective-permute-start.16
  207.9 3.2 collective-permute-start.15
  211.1 5.0 %collective-permute-start.14 = (f16[448,1024]{1,0:T(8,128)(2,1)}, f16[448,1024]{1,0:T(8,128)(2,1)}, u32[]{:S(2)}, u32[]{:S(2)}) collective-permute-start(f16[448,1024]{1,0:T(8,128)(2,1)} %get-tuple-element.29), channel_id=1, source_target_pairs={{0,16},{4,20},{8,24},{12,28},{1,17},{5,21},{9,25},{13,29},{2,18},{... | collective-permute-start | bytes 2752520 | tf_op jit(solution)/shard_map/ppermute | solution.py:468
  221.6 5.1 %collective-permute-done.16 = f16[448,1024]{1,0:T(8,128)(2,1)} collective-permute-done((f16[448,1024]{1,0:T(8,128)(2,1)}, f16[448,1024]{1,0:T(8,128)(2,1)}, u32[]{:S(2)}, u32[]{:S(2)}) %collective-permute-start.16) | collective-permute-done | bytes 917536 | tf_op jit(solution)/shard_map/ppermute | solution.py:468
  230.1 3.6 %collective-permute-done.20 = f32[128,256]{1,0:T(8,128)S(1)} collective-permute-done((f32[128,256]{1,0:T(8,128)S(1)}, f32[128,256]{1,0:T(8,128)S(1)}, u32[]{:S(2)}, u32[]{:S(2)}) %collective-permute-start.20) | collective-permute-done | bytes 131104 | tf_op jit(solution)/shard_map/ppermute | solution.py:282
  235.0 49.7 %collective-permute-done.14 = f16[448,1024]{1,0:T(8,128)(2,1)} collective-permute-done((f16[448,1024]{1,0:T(8,128)(2,1)}, f16[448,1024]{1,0:T(8,128)(2,1)}, u32[]{:S(2)}, u32[]{:S(2)}) %collective-permute-start.14) | collective-permute-done | bytes 917536 | tf_op jit(solution)/shard_map/ppermute | solution.py:468
  284.6 3.1 collective-permute-start.21
  289.6 11.6 %input_grad.1 = bf16[256,3584]{1,0:T(8,128)(2,1)} custom-call(s32[224]{0:T(256)S(1)} %reshape.441.pat, bf16[256,2048]{1,0:T(8,128)(2,1)S(1)} %copy-done.2, bf16[256,2048]{1,0:T(8,128)(2,1)} %collective-permute-done.2.refs_1_, bf16[256,2048]{1,0:T(8,128)(2,1)} %collective-permute-done.refs_2_, bf16[256,2048]{1,0:T(8,128)(2,1)} %collective-permute-done.3.refs_3_, ...), custom_call_target="tpu_custom_call" | custom-call | flops 1 | bytes 1 | tf_op jit(solution)/shard_map/input_grad/pallas_call | solution.py:476
  302.9 5.6 %fusion.6.refs_0_ = f32[448,1024]{1,0:T(8,128)} fusion(f16[448,1024]{1,0:T(8,128)(2,1)} %collective-permute-done.16, f16[448,1024]{1,0:T(8,128)(2,1)} %collective-permute-done.15, f16[448,1024]{1,0:T(8,128)(2,1)} %collective-permute-done.14, f16[448,1024]{1,0:T(8,128)(2,1)} %collective-permute-done.13, f16[448,1024]{1,0:T(8,128)(2,1)} %collective-permute-done.12, ...), kind=kLoop, calls=%fused_computation.13 | loop fusion | flops 5963776 | bytes 9175048 | tf_op jit(solution)/shard_map/mul | solution.py:474
  313.4 16.0 %mixing.1.refs_1_ = f32[256,256]{1,0:T(8,128)S(1)} custom-call(f32[128,128]{1,0:T(8,128)S(1)} %sketch_gram.1.ss_ref, f32[128,256]{1,0:T(8,128)S(1)} %add.337.cross_ref), custom_call_target="tpu_custom_call" | custom-call | flops 1 | bytes 1 | tf_op jit(solution)/shard_map/mixing/pallas_call | solution.py:405
  332.9 9.6 %direction.1 = f32[448,8,128]{2,1,0:T(8,128)} custom-call(s32[4]{0:T(128)S(1)} %pad_add_fusion.2.starts, s32[32]{0:T(128)S(1)} %select_n.225.pat, f32[448,1024]{1,0:T(8,128)} %fusion.6.refs_0_, f32[256,256]{1,0:T(8,128)S(1)} %mixing.1.refs_1_, bf16[32,128,256]{2,1,0:T(8,128)(2,1)} %copy-done.1, bf16[32,128,256]{2,1,0:T(8,128)(2,1)} %copy-done, ...), custom_call_target="tpu_custom_call" | custom-call | flops 1 | bytes 1 | tf_op jit(solution)/shard_map/direction/pallas_call | solution.py:498
  (118 shorter events, 59.9 us)
Async XLA Ops:
  4.0 37.8 %all-to-all-start = ((f16[8,128,704]{1,2,0:T(8,128)(2,1)}), f16[8,128,704]{1,2,0:T(8,128)(2,1)}, u32[]{:S(2)}, u32[]{:S(2)}) async-start(f16[8,128,704]{1,2,0:T(8,128)(2,1)} %broadcast_in_dim.56), calls=%async_computation | async-start | bytes 2883584 | tf_op jit(solution)/shard_map/all_to_all | solution.py:288
  9.8 38.0 %collective-permute-start = (bf16[256,2048]{1,0:T(8,128)(2,1)S(1)}, bf16[256,2048]{1,0:T(8,128)(2,1)}, u32[]{:S(2)}, u32[]{:S(2)}) collective-permute-start(bf16[256,2048]{1,0:T(8,128)(2,1)S(1)} %copy-done.2), channel_id=1, source_target_pairs={{0,2},{1,3},{2,0},{3,1},{4,6},{5,7},{6,4},{7,5},{8,10},{9,11},{10,... | collective-permute-start | bytes 3145736 | tf_op jit(solution)/shard_map/ppermute | solution.py:282
  11.0 38.0 %collective-permute-start.1 = (bf16[256,2048]{1,0:T(8,128)(2,1)S(1)}, bf16[256,2048]{1,0:T(8,128)(2,1)}, u32[]{:S(2)}, u32[]{:S(2)}) collective-permute-start(bf16[256,2048]{1,0:T(8,128)(2,1)S(1)} %copy-done.2), channel_id=1, source_target_pairs={{0,4},{4,0},{8,12},{12,8},{16,20},{20,16},{24,28},{28,24},{1,5},{5... | collective-permute-start | bytes 3145736 | tf_op jit(solution)/shard_map/ppermute | solution.py:282
  12.2 36.8 %collective-permute-start.2 = (bf16[256,2048]{1,0:T(8,128)(2,1)S(1)}, bf16[256,2048]{1,0:T(8,128)(2,1)}, u32[]{:S(2)}, u32[]{:S(2)}) collective-permute-start(bf16[256,2048]{1,0:T(8,128)(2,1)S(1)} %copy-done.2), channel_id=1, source_target_pairs={{0,1},{1,0},{2,3},{3,2},{4,5},{5,4},{6,7},{7,6},{8,9},{9,8},{10,11... | collective-permute-start | bytes 3145736 | tf_op jit(solution)/shard_map/ppermute | solution.py:282
  49.0 4.9 %collective-permute-start.3 = (bf16[256,2048]{1,0:T(8,128)(2,1)}, bf16[256,2048]{1,0:T(8,128)(2,1)}, u32[]{:S(2)}, u32[]{:S(2)}) collective-permute-start(bf16[256,2048]{1,0:T(8,128)(2,1)} %collective-permute-done.refs_2_), channel_id=1, source_target_pairs={{0,1},{1,0},{2,3},{3,2},{4,5},{5,4},{6,7},{7,6},{8,9},{9,8},{10,11... | collective-permute-start | bytes 3145736 | tf_op jit(solution)/shard_map/ppermute | solution.py:282
  74.1 45.4 %collective-permute-start.8 = (bf16[256,2048]{1,0:T(8,128)(2,1)}, bf16[256,2048]{1,0:T(8,128)(2,1)}, u32[]{:S(2)}, u32[]{:S(2)}) collective-permute-start(bf16[256,2048]{1,0:T(8,128)(2,1)} %collective-permute-done.1.refs_4_), channel_id=1, source_target_pairs={{0,2},{1,3},{2,0},{3,1},{4,6},{5,7},{6,4},{7,5},{8,10},{9,11},{10,... | collective-permute-start | bytes 3145736 | tf_op jit(solution)/shard_map/ppermute | solution.py:282
  75.3 5.6 %collective-permute-start.4 = (f16[16,128,128]{2,1,0:T(8,128)(2,1)}, f16[16,128,128]{2,1,0:T(8,128)(2,1)}, u32[]{:S(2)}, u32[]{:S(2)}) collective-permute-start(f16[16,128,128]{2,1,0:T(8,128)(2,1)} %get-tuple-element.34), channel_id=1, source_target_pairs={{0,1},{1,0},{2,3},{3,2},{4,5},{5,4},{6,7},{7,6},{8,9},{9,8},{10,11... | collective-permute-start | bytes 1572872 | tf_op jit(solution)/shard_map/ppermute | solution.py:282
  78.4 31.5 %collective-permute-start.6 = (f16[16,128,128]{2,1,0:T(8,128)(2,1)}, f16[16,128,128]{2,1,0:T(8,128)(2,1)}, u32[]{:S(2)}, u32[]{:S(2)}) collective-permute-start(f16[16,128,128]{2,1,0:T(8,128)(2,1)} %fusion.13), channel_id=1, source_target_pairs={{0,2},{1,3},{2,0},{3,1},{4,6},{5,7},{6,4},{7,5},{8,10},{9,11},{10,... | collective-permute-start | bytes 1572872 | tf_op jit(solution)/shard_map/ppermute | solution.py:282
  112.4 65.9 %all-to-all-start.1 = ((f16[8,256,128]{2,1,0:T(8,128)(2,1)}), f16[8,256,128]{2,1,0:T(8,128)(2,1)}, u32[]{:S(2)}, u32[]{:S(2)}) async-start(f16[8,256,128]{2,1,0:T(8,128)(2,1)} %bitcast.8), calls=%async_computation.1 | async-start | bytes 1048576 | tf_op jit(solution)/shard_map/all_to_all | solution.py:363
  117.6 69.8 %collective-permute-start.7 = (bf16[256,2048]{1,0:T(8,128)(2,1)}, bf16[256,2048]{1,0:T(8,128)(2,1)}, u32[]{:S(2)}, u32[]{:S(2)}) collective-permute-start(bf16[256,2048]{1,0:T(8,128)(2,1)} %collective-permute-done.1.refs_4_), channel_id=1, source_target_pairs={{0,1},{1,0},{2,3},{3,2},{4,5},{5,4},{6,7},{7,6},{8,9},{9,8},{10,11... | collective-permute-start | bytes 3145736 | tf_op jit(solution)/shard_map/ppermute | solution.py:282
  119.5 67.9 %collective-permute-start.9 = (bf16[256,2048]{1,0:T(8,128)(2,1)}, bf16[256,2048]{1,0:T(8,128)(2,1)}, u32[]{:S(2)}, u32[]{:S(2)}) collective-permute-start(bf16[256,2048]{1,0:T(8,128)(2,1)} %collective-permute-done.8.refs_6_), channel_id=1, source_target_pairs={{0,1},{1,0},{2,3},{3,2},{4,5},{5,4},{6,7},{7,6},{8,9},{9,8},{10,11... | collective-permute-start | bytes 3145736 | tf_op jit(solution)/shard_map/ppermute | solution.py:282
  120.3 67.0 %collective-permute-start.10 = (bf16[4,448,256]{2,1,0:T(8,128)(2,1)}, bf16[4,448,256]{2,1,0:T(8,128)(2,1)S(1)}, u32[]{:S(2)}, u32[]{:S(2)}) collective-permute-start(bf16[4,448,256]{2,1,0:T(8,128)(2,1)} %get-tuple-element.22), channel_id=1, source_target_pairs={{0,4},{4,0},{8,12},{12,8},{16,20},{20,16},{24,28},{28,24},{1,5},{5... | collective-permute-start | bytes 2752520 | tf_op jit(solution)/shard_map/ppermute | solution.py:282
  180.4 38.9 %all-to-all-start.2 = ((f16[8,256,128]{2,1,0:T(8,128)(2,1)}), f16[8,256,128]{2,1,0:T(8,128)(2,1)}, u32[]{:S(2)}, u32[]{:S(2)}) async-start(f16[8,256,128]{2,1,0:T(8,128)(2,1)} %broadcast_in_dim.65), calls=%async_computation.2 | async-start | bytes 1048576 | tf_op jit(solution)/shard_map/all_to_all | solution.py:288
  204.9 21.8 %collective-permute-start.16 = (f16[448,1024]{1,0:T(8,128)(2,1)}, f16[448,1024]{1,0:T(8,128)(2,1)}, u32[]{:S(2)}, u32[]{:S(2)}) collective-permute-start(f16[448,1024]{1,0:T(8,128)(2,1)} %get-tuple-element.27), channel_id=1, source_target_pairs={{0,8},{4,12},{8,16},{12,20},{16,24},{20,28},{1,9},{5,13},{9,17},{1... | collective-permute-start | bytes 2752520 | tf_op jit(solution)/shard_map/ppermute | solution.py:468
  207.9 21.6 %collective-permute-start.15 = (f16[448,1024]{1,0:T(8,128)(2,1)}, f16[448,1024]{1,0:T(8,128)(2,1)}, u32[]{:S(2)}, u32[]{:S(2)}) collective-permute-start(f16[448,1024]{1,0:T(8,128)(2,1)} %get-tuple-element.28), channel_id=1, source_target_pairs={{8,0},{12,4},{16,8},{20,12},{24,16},{28,20},{9,1},{13,5},{17,9},{2... | collective-permute-start | bytes 2752520 | tf_op jit(solution)/shard_map/ppermute | solution.py:468
  211.1 73.5 %collective-permute-start.14 = (f16[448,1024]{1,0:T(8,128)(2,1)}, f16[448,1024]{1,0:T(8,128)(2,1)}, u32[]{:S(2)}, u32[]{:S(2)}) collective-permute-start(f16[448,1024]{1,0:T(8,128)(2,1)} %get-tuple-element.29), channel_id=1, source_target_pairs={{0,16},{4,20},{8,24},{12,28},{1,17},{5,21},{9,25},{13,29},{2,18},{... | collective-permute-start | bytes 2752520 | tf_op jit(solution)/shard_map/ppermute | solution.py:468
  216.2 85.1 %collective-permute-start.13 = (f16[448,1024]{1,0:T(8,128)(2,1)}, f16[448,1024]{1,0:T(8,128)(2,1)}, u32[]{:S(2)}, u32[]{:S(2)}) collective-permute-start(f16[448,1024]{1,0:T(8,128)(2,1)} %get-tuple-element.30), channel_id=1, source_target_pairs={{16,0},{20,4},{24,8},{28,12},{17,1},{21,5},{25,9},{29,13},{18,2},{... | collective-permute-start | bytes 2752520 | tf_op jit(solution)/shard_map/ppermute | solution.py:468
  217.5 85.4 %collective-permute-start.12 = (f16[448,1024]{1,0:T(8,128)(2,1)}, f16[448,1024]{1,0:T(8,128)(2,1)}, u32[]{:S(2)}, u32[]{:S(2)}) collective-permute-start(f16[448,1024]{1,0:T(8,128)(2,1)} %get-tuple-element.31), channel_id=1, source_target_pairs={{0,24},{4,28},{1,25},{5,29},{2,26},{6,30},{3,27},{7,31}} | collective-permute-start | bytes 2752520 | tf_op jit(solution)/shard_map/ppermute | solution.py:468
  226.7 76.2 %collective-permute-start.11 = (f16[448,1024]{1,0:T(8,128)(2,1)}, f16[448,1024]{1,0:T(8,128)(2,1)S(1)}, u32[]{:S(2)}, u32[]{:S(2)}) collective-permute-start(f16[448,1024]{1,0:T(8,128)(2,1)} %get-tuple-element.26), channel_id=1, source_target_pairs={{24,0},{28,4},{25,1},{29,5},{26,2},{30,6},{27,3},{31,7}} | collective-permute-start | bytes 2752520 | tf_op jit(solution)/shard_map/ppermute | solution.py:468
  233.7 54.1 %collective-permute-start.18 = (f16[8,128,256]{2,1,0:T(8,128)(2,1)S(1)}, f16[8,128,256]{2,1,0:T(8,128)(2,1)S(1)}, u32[]{:S(2)}, u32[]{:S(2)}) collective-permute-start(f16[8,128,256]{2,1,0:T(8,128)(2,1)S(1)} %copy.41), channel_id=1, source_target_pairs={{0,2},{1,3},{2,0},{3,1},{4,6},{5,7},{6,4},{7,5},{8,10},{9,11},{10,... | collective-permute-start | bytes 1572872 | tf_op jit(solution)/shard_map/ppermute | solution.py:282
  287.8 20.6 %collective-permute-start.17 = (f16[8,128,256]{2,1,0:T(8,128)(2,1)S(1)}, f16[8,128,256]{2,1,0:T(8,128)(2,1)}, u32[]{:S(2)}, u32[]{:S(2)}) collective-permute-start(f16[8,128,256]{2,1,0:T(8,128)(2,1)S(1)} %copy.41), channel_id=1, source_target_pairs={{0,1},{1,0},{2,3},{3,2},{4,5},{5,4},{6,7},{7,6},{8,9},{9,8},{10,11... | collective-permute-start | bytes 1572872 | tf_op jit(solution)/shard_map/ppermute | solution.py:282
  289.4 19.0 %collective-permute-start.19 = (f16[8,128,256]{2,1,0:T(8,128)(2,1)S(1)}, f16[8,128,256]{2,1,0:T(8,128)(2,1)}, u32[]{:S(2)}, u32[]{:S(2)}) collective-permute-start(f16[8,128,256]{2,1,0:T(8,128)(2,1)S(1)} %collective-permute-done.18), channel_id=1, source_target_pairs={{0,1},{1,0},{2,3},{3,2},{4,5},{5,4},{6,7},{7,6},{8,9},{9,8},{10,11... | collective-permute-start | bytes 1572872 | tf_op jit(solution)/shard_map/ppermute | solution.py:282
  301.3 29.3 %collective-permute-start.23 = (f16[16,128,128]{2,1,0:T(8,128)(2,1)}, f16[16,128,128]{2,1,0:T(8,128)(2,1)S(1)}, u32[]{:S(2)}, u32[]{:S(2)}) collective-permute-start(f16[16,128,128]{2,1,0:T(8,128)(2,1)} %bitcast.29), channel_id=1, source_target_pairs={{0,2},{1,3},{2,0},{3,1},{4,6},{5,7},{6,4},{7,5},{8,10},{9,11},{10,... | collective-permute-start | bytes 1572872 | tf_op jit(solution)/shard_map/ppermute | solution.py:282
  312.6 18.4 %collective-permute-start.22 = (f16[16,128,128]{2,1,0:T(8,128)(2,1)}, f16[16,128,128]{2,1,0:T(8,128)(2,1)S(1)}, u32[]{:S(2)}, u32[]{:S(2)}) collective-permute-start(f16[16,128,128]{2,1,0:T(8,128)(2,1)} %bitcast.29), channel_id=1, source_target_pairs={{0,1},{1,0},{2,3},{3,2},{4,5},{5,4},{6,7},{7,6},{8,9},{9,8},{10,11... | collective-permute-start | bytes 1572872 | tf_op jit(solution)/shard_map/ppermute | solution.py:282
  (10 other events, 107.3 us)

commit v4 on v3

--- a/solution.py
+++ b/solution.py
@@ -74,7 +74,7 @@
         row = pl.program_id(0) * per_step + u
         span = slice(u * blk, (u + 1) * blk)
         hid = hid_ref[span, :]
-        ph, pl_ = split2(proj_ref[:, span])
+        ph, pl_ = split2(proj_ref[span, :].T)
         left = jnp.concatenate(split2((dot(ph, hid) + dot(pl_, hid)) * scale), axis=0)
         cols = [pat[row * SLOTS + j] for j in range(SLOTS)]
         parts = []
@@ -93,7 +93,7 @@
             out_ref[c] = total
 
 
-def grad_kernel(n_shards, per_shard, blk, window, n_windows, starts, pat, scale, *refs):
+def grad_kernel(n_shards, per_shard, blk, window, n_windows, order, starts, pat, scale, *refs):
     shards = refs[: 2 * n_shards]
     own_ref, got_ref, out_ref, held, sems = refs[2 * n_shards :]
     toks = own_ref.shape[1]
@@ -109,7 +109,7 @@
         )
 
     for w in range(n_windows):
-        index = pl.program_id(0) * n_windows + w
+        index = order[pl.program_id(0)] * n_windows + w
         rows = pl.ds(pl.multiple_of(starts[index], window // 2 if window >= 32 else 8), window)
         hid = jnp.concatenate([own_ref[rows, :], got_ref[rows, :]], axis=1).astype(BF)
         for j in range(0, SLOTS, 2):
@@ -287,38 +287,45 @@
     def over_dp(x):
         return lax.all_to_all(jnp.broadcast_to(x[None], (n_dp, *x.shape)), "dp", 0, 0)
 
-    largest = jnp.stack([jnp.max(jnp.abs(hidden)), jnp.max(jnp.abs(cotangent))]).astype(F32)
-    largest = lax.pmax(jnp.broadcast_to(largest[:, None], (2, 128)), ("dp", "mp"))
-    bound = jnp.maximum(largest[0, 0] * largest[1, 0] * all_tokens, 1e-30)
-    grad_scale = 32768.0 / bound
+    def exponent(x):
+        top = jnp.max(jnp.abs(x)).astype(F32)
+        return jnp.floor(jnp.log2(jnp.maximum(top, 1e-15))) + 1.0
 
     width = sketch.shape[1]
-    proj16 = (projection.reshape(rank, dev_rows) * PROJ_SCALE).astype(F16)
-    early = over_dp(jnp.concatenate([sketch.astype(F16), proj16], axis=1))
-    proj_all = early[:, :, width:].transpose(1, 0, 2).reshape(rank, mp_rows).astype(F32)
-    sk_own = early[:, :, :width]
+    core_half = swap(cotangent, "mp", 1)
+    exponents = jnp.stack([exponent(hidden), exponent(cotangent)])
+    exponents = jnp.broadcast_to(jnp.repeat(exponents, 8)[:, None], (16, rank))
+    proj_t = projection.reshape(rank, dev_rows).T * PROJ_SCALE
+    early = jnp.concatenate([proj_t, exponents], axis=0).astype(F16)
+    early = over_dp(after(early, core_half))
+    proj_all = early[:, :dev_rows].reshape(mp_rows, rank).astype(F32)
+    peaks = jnp.max(early[:, dev_rows:].astype(F32), axis=0)
     hid_t = hidden.T
     hid_parts = hid_t.reshape(outer, 2, dev_rows, tok_rows)
     hid_own = lax.dynamic_index_in_dim(hid_parts, side, 1, keepdims=False)
     hid_send = lax.dynamic_index_in_dim(hid_parts, 1 - side, 1, keepdims=False)
-    x_half, y_own, core_half, proj_all, sk_own, hid_t, hid_own, hid_send, weights_2d = (
+    x_half, y_own, core_half, hid_t, hid_own, hid_send, weights_2d, proj_all, peaks = (
         lax.optimization_barrier(
             (
                 swap(cotangent, "mp", 2),
                 swap(cotangent, "dp", 1),
-                swap(cotangent, "mp", 1),
-                proj_all,
-                sk_own,
+                core_half,
                 hid_t,
                 hid_own,
                 hid_send,
                 weights.reshape(mp_rows, slots * blk),
+                proj_all,
+                peaks,
             )
         )
     )
     own = [cotangent, core_half, x_half, swap(x_half, "mp", 1)]
     y_x = swap(y_own, "mp", 2)
+    y_core = swap(y_own, "mp", 1)
     hid_got = swap(hid_send, "dp", 1)
+    for bit in (1, 2):
+        peaks = jnp.maximum(peaks, swap(peaks, "mp", bit))
+    sk_own = over_dp(after(sketch.astype(F16), x_half))
     pattern_rel = jnp.bitwise_xor(pattern, mp * per_shard)
 
     def place(block):
@@ -340,7 +347,7 @@
             in_specs=[ANY] * n_mp
             + [
                 pl.BlockSpec((per_step * blk, tok_rows), lambda i, a, b: (i, 0)),
-                pl.BlockSpec((rank, per_step * blk), lambda i, a, b: (0, i)),
+                pl.BlockSpec((per_step * blk, rank), lambda i, a, b: (i, 0)),
             ],
             out_specs=pl.BlockSpec((col_blocks, rank, blk), lambda i, a, b: (0, 0, 0)),
             scratch_shapes=[
@@ -354,71 +361,20 @@
         name="compress",
     )(pat_all, place(pattern).reshape(-1), *own, hid_t, proj_all)
 
+    partial_c, y_x, y_core, hid_got, peaks, sk_own = lax.optimization_barrier(
+        (partial_c, y_x, y_core, hid_got, peaks, sk_own)
+    )
+    y_group = [y_own, y_core, y_x, swap(y_x, "mp", 1)]
     quarters = partial_c.reshape(n_mp, per_shard, rank, blk)
     got_far = swap(quarters[3].astype(F16), "mp", 1)
     got_near = swap(quarters[1].astype(F16), "mp", 1)
     far_half = (quarters[2] + got_far.astype(F32)).astype(F16)
-    quarter = (quarters[0] + got_near.astype(F32)) + swap(far_half, "mp", 2).astype(F32)
-    pieces = quarter.astype(F16).reshape(n_dp, per_shard * rank // n_dp, blk)
-    pieces = lax.all_to_all(pieces, "dp", 0, 0)
-    piece = jnp.sum(pieces.astype(F32), axis=0).astype(F16)
-    quarter16 = over_dp(piece).reshape(per_shard, rank, blk)
-
-    sk_own = after(sk_own, pieces)
-    sk_far = swap(sk_own, "mp", 2)
-    sk_parts = [sk_own, swap(sk_own, "mp", 1), sk_far, swap(sk_far, "mp", 1)]
-    if width < blk:
-        sk_abs = jnp.take(
-            jnp.stack(sk_parts), jnp.bitwise_xor(jnp.arange(n_mp, dtype=jnp.int32), mp), axis=0
-        )
-        sk_abs = sk_abs.reshape(n_mp, col_blocks, blk // width // n_mp, rank, width)
-        sk_abs = sk_abs.transpose(1, 3, 2, 0, 4).reshape(n_mp, per_shard, rank, blk)
-        sk_parts = [
-            lax.dynamic_index_in_dim(sk_abs, jnp.bitwise_xor(mp, i), 0, keepdims=False)
-            for i in range(n_mp)
-        ]
-    oh, ol = split2_xla(sk_parts[0].astype(F32))
-    sk_high, sk_low = split2_xla(jnp.concatenate(sk_parts, axis=0).astype(F32))
-
-    sk_per = sk_high.shape[2] // blk
-    qh, ql = split2_xla(quarter16.astype(F32))
-    cross = pl.pallas_call(
-        cross_gram_kernel,
-        in_specs=[VMEM] * 4,
-        out_specs=VMEM,
-        out_shape=jax.ShapeDtypeStruct((rank, 2 * rank), F32),
-        compiler_params=params(),
-        cost_estimate=SMALL,
-        name="cross_gram",
-    )(qh, ql, oh, ol)
-    sketch_gram = pl.pallas_call(
-        sketch_gram_kernel,
-        in_specs=[VMEM] * 2,
-        out_specs=VMEM,
-        out_shape=jax.ShapeDtypeStruct((rank, rank), F32),
-        compiler_params=params(),
-        cost_estimate=SMALL,
-        name="sketch_gram",
-    )(sk_high, sk_low)
-    cross = cross + swap(cross, "mp", 2)
-    cross = cross + swap(cross, "mp", 1)
-    mixing = pl.pallas_call(
-        mixing_kernel,
-        in_specs=[VMEM] * 2,
-        out_specs=VMEM,
-        out_shape=jax.ShapeDtypeStruct((2 * rank, 2 * rank), F32),
-        compiler_params=params(),
-        cost_estimate=SMALL,
-        name="mixing",
-    )(sketch_gram, cross)
-
-    quarter16 = after(quarter16, cross)
-    far = swap(quarter16, "mp", 2)
-    comp_parts = [quarter16, swap(quarter16, "mp", 1), far, swap(far, "mp", 1)]
-    comp_parts = [split2_xla(part.astype(F32)) for part in comp_parts]
-    comp_parts = [part[0] for part in comp_parts] + [part[1] for part in comp_parts]
-
-    y_group = [y_own, swap(y_own, "mp", 1), y_x, swap(y_x, "mp", 1)]
+    near_half = quarters[0] + got_near.astype(F32)
+    far_half, near_half, y_last = lax.optimization_barrier((far_half, near_half, y_group[3]))
+    y_group[3] = y_last
+    far_sum = swap(far_half, "mp", 2)
+
+    grad_scale = jnp.exp2(14.0 - peaks[0, 0] - peaks[8, 0] - math.log2(all_tokens))
     half_rows = outer * dev_rows
     devices = 2 * jnp.arange(outer, dtype=jnp.int32) + side
     window, _, _ = windows_of(dp * dev_rows, dev_rows, blk)
@@ -428,50 +384,65 @@
     n_windows = window_starts.shape[1]
     pat_half = jnp.take(pattern_rel, window_blocks.reshape(-1), axis=0).reshape(-1)
     hid_type = BF if window % 32 == 0 else F32
-    grad_half = pl.pallas_call(
-        functools.partial(grad_kernel, n_mp, per_shard, blk, window, n_windows),
-        grid_spec=pltpu.PrefetchScalarGridSpec(
-            num_scalar_prefetch=3,
-            grid=(outer,),
-            in_specs=[ANY] * (2 * n_mp)
-            + [pl.BlockSpec((dev_rows, tok_rows), lambda i, a, b, c: (i, 0))] * 2,
-            out_specs=pl.BlockSpec((dev_rows, slots * blk), lambda i, a, b, c: (i, 0)),
-            scratch_shapes=[
-                pltpu.VMEM((n_mp, 2 * tok_rows, shard_cols), BF),
-                pltpu.SemaphoreType.DMA((2 * n_mp,)),
-            ],
-        ),
-        out_shape=jax.ShapeDtypeStruct((half_rows, slots * blk), F32),
-        compiler_params=params(),
-        cost_estimate=SMALL,
-        name="pair_grad",
-    )(
-        window_starts.reshape(-1),
-        pat_half,
-        grad_scale[None],
-        *own,
-        *y_group,
-        hid_own.reshape(half_rows, tok_rows).astype(hid_type),
-        hid_got.reshape(half_rows, tok_rows).astype(hid_type),
-    )
-    grad_half = grad_half.reshape(outer, dev_rows, slots * blk)
-    level = dp // 2
-
-    def block_of(index):
-        index = jnp.clip(index, 0, outer - 1)
-        return lax.dynamic_index_in_dim(grad_half, index, 0, keepdims=False)
-
-    grad = block_of(level)
-    if outer <= 4:
-        for d in sorted((d for d in range(1 - outer, outer) if d), key=lambda d: -abs(d)):
-            perm = [(i, i + 2 * d) for i in range(n_dp) if 0 <= i + 2 * d < n_dp]
-            got = lax.ppermute(block_of(level + d).astype(F16), "dp", perm)
-            grad = grad + got.astype(F32)
-    else:
-        lanes = [[2 * i + s for i in range(outer)] for s in range(2)]
-        got = lax.all_to_all(grad_half.astype(F16), "dp", 0, 0, axis_index_groups=lanes)
-        grad = jnp.sum(got.astype(F32), axis=0)
-    grad = grad * (1.0 / (grad_scale * all_tokens))
+
+    def pair_grad(blocks, shards):
+        order = jnp.bitwise_xor(jnp.asarray(blocks, jnp.int32), dp // 2)
+        out = pl.pallas_call(
+            functools.partial(grad_kernel, n_mp, per_shard, blk, window, n_windows),
+            grid_spec=pltpu.PrefetchScalarGridSpec(
+                num_scalar_prefetch=4,
+                grid=(len(blocks),),
+                in_specs=[ANY] * (2 * n_mp)
+                + [pl.BlockSpec((dev_rows, tok_rows), lambda i, o, a, b, c: (o[i], 0))] * 2,
+                out_specs=pl.BlockSpec((dev_rows, slots * blk), lambda i, o, a, b, c: (i, 0)),
+                scratch_shapes=[
+                    pltpu.VMEM((n_mp, 2 * tok_rows, shard_cols), BF),
+                    pltpu.SemaphoreType.DMA((2 * n_mp,)),
+                ],
+            ),
+            out_shape=jax.ShapeDtypeStruct((len(blocks) * dev_rows, slots * blk), F32),
+            compiler_params=params(),
+            cost_estimate=SMALL,
+            name="pair_grad",
+        )(
+            order,
+            window_starts.reshape(-1),
+            pat_half,
+            grad_scale[None],
+            *shards,
+            hid_own.reshape(half_rows, tok_rows).astype(hid_type),
+            hid_got.reshape(half_rows, tok_rows).astype(hid_type),
+        )
+        out = out.reshape(len(blocks), dev_rows, slots * blk)
+        return {block: out[i] for i, block in enumerate(blocks)}
+
+    crossing = [i for i in range(outer) if i & 2][::-1]
+    staying = [i for i in range(outer) if not i & 2][::-1]
+    sums = pair_grad(crossing, own + y_group)
+    sent = {i: sums[i].astype(F16) for i in crossing if i & 1}
+    got = {i: swap(sent[i], "dp", 2) for i in crossing if i & 1}
+    sums.update(pair_grad(staying, own[:3] + [after(own[3], *sent.values())] + y_group))
+    sent = {i: sums[i].astype(F16) for i in staying if i & 1}
+    got.update({i: swap(sent[i], "dp", 2) for i in staying if i & 1})
+    far_sum, near_half, _ = lax.optimization_barrier((far_sum, near_half, list(sent.values())))
+
+    quarter = near_half + far_sum.astype(F32)
+    pieces = quarter.astype(F16).reshape(n_dp, per_shard * rank // n_dp, blk)
+    pieces = lax.all_to_all(pieces, "dp", 0, 0)
+
+    level = 1
+    while level < outer:
+        if level > 1:
+            got = {}
+            for i in [i for i in sums if i & level]:
+                got[i] = swap(sums[i].astype(F16), "dp", 2 * level)
+        for i in got:
+            sums[i ^ level] = sums[i ^ level] + got[i].astype(F32)
+        sums = {i: part for i, part in sums.items() if not i & level}
+        if level == 1 and outer > 2:
+            sums[2], pieces = lax.optimization_barrier((sums[2].astype(F16), pieces))
+        level *= 2
+    grad = sums[0] * (1.0 / (grad_scale * all_tokens))
 
     input_grad = pl.pallas_call(
         functools.partial(input_grad_kernel, n_mp, per_shard, blk, per_step),
@@ -490,7 +461,68 @@
         compiler_params=params(),
         cost_estimate=SMALL,
         name="input_grad",
-    )(pat_all, *own, after(weights_2d, pieces))
+    )(pat_all, *own, after(weights_2d, quarter))
+    pieces, input_grad = lax.optimization_barrier((pieces, input_grad))
+
+    piece = jnp.sum(pieces.astype(F32), axis=0).astype(F16)
+    quarter16 = over_dp(piece).reshape(per_shard, rank, blk)
+
+    sk_own = after(sk_own, quarter)
+    sk_far = swap(sk_own, "mp", 2)
+    sk_parts = [sk_own, swap(sk_own, "mp", 1), sk_far, swap(sk_far, "mp", 1)]
+    if width < blk:
+        sk_abs = jnp.take(
+            jnp.stack(sk_parts), jnp.bitwise_xor(jnp.arange(n_mp, dtype=jnp.int32), mp), axis=0
+        )
+        sk_abs = sk_abs.reshape(n_mp, col_blocks, blk // width // n_mp, rank, width)
+        sk_abs = sk_abs.transpose(1, 3, 2, 0, 4).reshape(n_mp, per_shard, rank, blk)
+        sk_parts = [
+            lax.dynamic_index_in_dim(sk_abs, jnp.bitwise_xor(mp, i), 0, keepdims=False)
+            for i in range(n_mp)
+        ]
+    oh, ol = split2_xla(sk_parts[0].astype(F32))
+    sk_high, sk_low = split2_xla(jnp.concatenate(sk_parts, axis=0).astype(F32))
+
+    sk_per = sk_high.shape[2] // blk
+    sketch_gram = pl.pallas_call(
+        sketch_gram_kernel,
+        in_specs=[VMEM] * 2,
+        out_specs=VMEM,
+        out_shape=jax.ShapeDtypeStruct((rank, rank), F32),
+        compiler_params=params(),
+        cost_estimate=SMALL,
+        name="sketch_gram",
+    )(sk_high, sk_low)
+    quarter16, sketch_gram, sk_high, sk_low, oh, ol = lax.optimization_barrier(
+        (quarter16, sketch_gram, sk_high, sk_low, oh, ol)
+    )
+    qh, ql = split2_xla(quarter16.astype(F32))
+    cross = pl.pallas_call(
+        cross_gram_kernel,
+        in_specs=[VMEM] * 4,
+        out_specs=VMEM,
+        out_shape=jax.ShapeDtypeStruct((rank, 2 * rank), F32),
+        compiler_params=params(),
+        cost_estimate=SMALL,
+        name="cross_gram",
+    )(qh, ql, oh, ol)
+    cross = cross + swap(cross, "mp", 2)
+    cross = cross + swap(cross, "mp", 1)
+    mixing = pl.pallas_call(
+        mixing_kernel,
+        in_specs=[VMEM] * 2,
+        out_specs=VMEM,
+        out_shape=jax.ShapeDtypeStruct((2 * rank, 2 * rank), F32),
+        compiler_params=params(),
+        cost_estimate=SMALL,
+        name="mixing",
+    )(sketch_gram, cross)
+
+    quarter16 = after(quarter16, cross)
+    far = swap(quarter16, "mp", 2)
+    comp_parts = [quarter16, swap(quarter16, "mp", 1), far, swap(far, "mp", 1)]
+    comp_parts = [split2_xla(part.astype(F32)) for part in comp_parts]
+    comp_parts = [part[0] for part in comp_parts] + [part[1] for part in comp_parts]
 
     _, my_starts, my_blocks = windows_of(dp * dev_rows, dev_rows, blk)
     my_pat = jnp.take(place(pattern), my_blocks, axis=0).reshape(-1)

time: 344 us -> 242 us (0.70)
  the two profiles are of different devices: /device:TPU:9 before, /device:TPU:0 now
where the time goes in v4:
time: 242 us; the launch traced here: 240 us
  Pallas kernels  71.6 us (30%)
  waiting for transfers between devices  63.8 us (26%)
  starting transfers between devices  41.9 us (17%)
  other arithmetic  31.7 us (13%)
  local copies, waits for them, and re-layouts  26.5 us (11%)
  between operations  4.24 us (2%)
    ppermute x24, waiting for transfers between devices, swap(): return lax.ppermute(x, axis, [(i, i ^ bit) for i in range(size)])  56 us
    ppermute x24, starting transfers between devices, swap(): return lax.ppermute(x, axis, [(i, i ^ bit) for i in range(size)])  19.1 us
    all_to_all x3, starting transfers between devices, over_dp(): lax.all_to_all(jnp.broadcast_to(x[None], (n_dp, *x.shape)), 'dp', 0, 0)  18.5 us
    unnamed x33, local copies, waits for them, and re-layouts  16.5 us
    pallas_call x2, Pallas kernels, pair_grad(): pl.pallas_call(functools.partial(grad_kernel, n_mp, per_shard, blk, windo...  16.3 us
    pallas_call x1, Pallas kernels, per_device(): pl.pallas_call(mixing_kernel, in_specs=[VMEM] * 2, out_specs=VMEM, out_sh...  16 us
    pallas_call x1, Pallas kernels, per_device(): pl.pallas_call(functools.partial(compress_kernel, n_mp, per_shard, 1.0 /...  16 us
    pallas_call x1, Pallas kernels, per_device(): pl.pallas_call(functools.partial(input_grad_kernel, n_mp, per_shard, blk,...  11 us
  transfers between devices with their start and end apart: 28, of which 12 were waited for; matrix products, arithmetic and copies ran while one was open for 21% of the time, Pallas kernels for 26%

profile of v4, /device:TPU:0, one launch (start us, length us, event | category | flops | bytes accessed | tf_op | source)
XLA Modules:
  0.0 239.7 jit_solution(9414097551107480681)
XLA Ops:
  8.5 6.9 %all-to-all-start = ((f16[8,464,128]{2,1,0:T(8,128)(2,1)}), f16[8,464,128]{2,1,0:T(8,128)(2,1)}, u32[]{:S(2)}, u32[]{:S(2)}) async-start(f16[8,464,128]{2,1,0:T(8,128)(2,1)} %broadcast_in_dim.73), calls=%async_computation | async-start | bytes 1900544 | tf_op jit(solution)/shard_map/all_to_all | solution.py:288
  18.9 3.8 %copy.25 = bf16[256,3584]{0,1:T(8,128)(2,1)} copy(bf16[256,3584]{1,0:T(8,128)(2,1)} %param.9) | data formatting | bytes 3670016 | tf_op args[1]
  23.1 7.9 %copy.28 = bf16[448,8,8,128]{3,1,2,0:T(8,128)(2,1)} copy(bf16[448,8,8,128]{3,2,1,0:T(8,128)(2,1)} %bitcast.41) | data formatting | bytes 14680064
  31.0 2.9 %dynamic-slice_bitcast_fusion = (bf16[4,448,256]{2,1,0:T(8,128)(2,1)}, bf16[4,448,256]{2,1,0:T(8,128)(2,1)}) fusion(bf16[4,2,448,256]{3,2,1,0:T(8,128)(2,1)} %bitcast.36, s32[]{:T(128)S(6)} %select_n.221, s32[]{:T(128)S(6)} %select_n.220), kind=kLoop, calls=%fused_computation.39 | loop fusion | bytes 3670024 | tf_op jit(solution)/shard_map/jit(dynamic_index_in_dim)/squeeze | solution.py:306
  33.9 5.9 %all-to-all-done = f16[8,464,128]{2,1,0:T(8,128)(2,1)} async-done(((f16[8,464,128]{2,1,0:T(8,128)(2,1)}), f16[8,464,128]{2,1,0:T(8,128)(2,1)}, u32[]{:S(2)}, u32[]{:S(2)}) %all-to-all-start) | async-done | bytes 950304 | tf_op jit(solution)/shard_map/all_to_all | solution.py:288
  43.4 7.8 %collective-permute-done.1.refs_4_ = bf16[256,2048]{1,0:T(8,128)(2,1)} collective-permute-done((bf16[256,2048]{1,0:T(8,128)(2,1)S(1)}, bf16[256,2048]{1,0:T(8,128)(2,1)}, u32[]{:S(2)}, u32[]{:S(2)}) %collective-permute-start.1) | collective-permute-done | bytes 1048608 | tf_op jit(solution)/shard_map/ppermute | solution.py:282
  54.3 5.7 %all-to-all-start.1 = ((f16[8,128,256]{2,1,0:T(8,128)(2,1)}), f16[8,128,256]{2,1,0:T(8,128)(2,1)}, u32[]{:S(2)}, u32[]{:S(2)}) async-start(f16[8,128,256]{2,1,0:T(8,128)(2,1)} %broadcast_in_dim.74), calls=%async_computation.1 | async-start | bytes 1048576 | tf_op jit(solution)/shard_map/all_to_all | solution.py:288
  63.0 13.0 %collective-permute-done.8 = f32[16,128]{1,0:T(8,128)S(1)} collective-permute-done((f32[16,128]{1,0:T(8,128)S(1)}, f32[16,128]{1,0:T(8,128)S(1)}, u32[]{:S(2)}, u32[]{:S(2)}) %collective-permute-start.8) | collective-permute-done | bytes 8224 | tf_op jit(solution)/shard_map/ppermute | solution.py:282
  77.5 16.0 %compress.1 = f32[64,128,128]{2,1,0:T(8,128)} custom-call(s32[224]{0:T(256)S(1)} %reshape.430.pat, s32[224]{0:T(256)S(1)} %reshape.431.pat_out, bf16[256,2048]{1,0:T(8,128)(2,1)S(1)} %copy-done, bf16[256,2048]{1,0:T(8,128)(2,1)S(1)} %collective-permute-done.2.refs_1_, bf16[256,2048]{1,0:T(8,128)(2,1)S(1)} %collective-permute-done.refs_2_, ...), custom_call_target="tpu_custom_call" | custom-call | flops 1 | bytes 1 | tf_op jit(solution)/shard_map/compress/pallas_call | solution.py:340
  93.5 2.8 %convert.22 = f16[64,128,128]{2,1,0:T(8,128)(2,1)S(1)} convert(f32[64,128,128]{2,1,0:T(8,128)} %compress.1) | non-fusion elementwise | flops 1048576 | bytes 6291456 | tf_op jit(solution)/shard_map/convert.4
  102.5 8.2 %pair_grad.2 = f32[896,1024]{1,0:T(8,128)} custom-call(s32[2]{0:T(128)S(1)} %broadcast_xor_fusion.2.order, s32[16]{0:T(128)S(1)} %reshape.429.starts, s32[128]{0:T(128)S(1)} %select_n.215.pat, f32[1]{0:T(128)} %bitcast.11.scale, bf16[256,2048]{1,0:T(8,128)(2,1)S(1)} %copy-done, bf16[256,2048]{1,0:T(8,128)(2,1)S(1)} %collective-permute-done.2.refs_1_, ...), custom_call_target="tpu_custom_call" | custom-call | flops 1 | bytes 1 | tf_op jit(solution)/shard_map/pair_grad/pallas_call | solution.py:390
  110.7 2.6 %slice_convert_fusion.1 = f16[448,1024]{1,0:T(8,128)(2,1)} fusion(f32[896,1024]{1,0:T(8,128)} %pair_grad.2), kind=kLoop, calls=%fused_computation.11 | loop fusion | flops 458752 | bytes 2752512 | tf_op jit(solution)/shard_map/convert.2
  114.8 8.2 %pair_grad.3 = f32[896,1024]{1,0:T(8,128)} custom-call(s32[2]{0:T(128)S(1)} %broadcast_xor_fusion.1.order, s32[16]{0:T(128)S(1)} %reshape.429.starts, s32[128]{0:T(128)S(1)} %select_n.215.pat, f32[1]{0:T(128)} %bitcast.11.scale, bf16[256,2048]{1,0:T(8,128)(2,1)S(1)} %copy-done, bf16[256,2048]{1,0:T(8,128)(2,1)S(1)} %collective-permute-done.2.refs_1_, ...), custom_call_target="tpu_custom_call" | custom-call | flops 1 | bytes 1 | tf_op jit(solution)/shard_map/pair_grad/pallas_call | solution.py:390
  122.9 2.6 %slice_convert_fusion = f16[448,1024]{1,0:T(8,128)(2,1)} fusion(f32[896,1024]{1,0:T(8,128)} %pair_grad.3), kind=kLoop, calls=%fused_computation.10 | loop fusion | flops 458752 | bytes 2752512 | tf_op jit(solution)/shard_map/convert.1
  126.5 4.3 %all-to-all-start.2 = ((f16[8,256,128]{2,1,0:T(8,128)(2,1)}), f16[8,256,128]{2,1,0:T(8,128)(2,1)}, u32[]{:S(2)}, u32[]{:S(2)}) async-start(f16[8,256,128]{2,1,0:T(8,128)(2,1)} %bitcast.42), calls=%async_computation.2 | async-start | bytes 1048576 | tf_op jit(solution)/shard_map/all_to_all | solution.py:431
  131.9 11.0 %input_grad.1 = bf16[256,3584]{1,0:T(8,128)(2,1)} custom-call(s32[224]{0:T(256)S(1)} %reshape.430.pat, bf16[256,2048]{1,0:T(8,128)(2,1)S(1)} %copy-done, bf16[256,2048]{1,0:T(8,128)(2,1)S(1)} %collective-permute-done.2.refs_1_, bf16[256,2048]{1,0:T(8,128)(2,1)S(1)} %collective-permute-done.refs_2_, bf16[256,2048]{1,0:T(8,128)(2,1)} %collective-permute-done.3.refs_3_, ...), custom_call_target="tpu_custom_call" | custom-call | flops 1 | bytes 1 | tf_op jit(solution)/shard_map/input_grad/pallas_call | solution.py:447
  142.9 2.4 %fusion.3 = f16[448,1024]{1,0:T(8,128)(2,1)} fusion(f32[896,1024]{1,0:T(8,128)S(1)} %copy-done.7, f16[448,1024]{1,0:T(8,128)(2,1)} %collective-permute-done.12), kind=kLoop, calls=%fused_computation.13 | loop fusion | flops 1376256 | bytes 3670016 | tf_op jit(solution)/shard_map/convert_element_type | solution.py:443
  147.4 5.9 %all-to-all-start.3 = ((f16[8,256,128]{2,1,0:T(8,128)(2,1)}), f16[8,256,128]{2,1,0:T(8,128)(2,1)}, u32[]{:S(2)}, u32[]{:S(2)}) async-start(f16[8,256,128]{2,1,0:T(8,128)(2,1)} %broadcast_in_dim.79), calls=%async_computation.3 | async-start | bytes 1048576 | tf_op jit(solution)/shard_map/all_to_all | solution.py:288
  173.3 4.0 %collective-permute-done.19 = f32[128,256]{1,0:T(8,128)S(1)} collective-permute-done((f32[128,256]{1,0:T(8,128)S(1)}, f32[128,256]{1,0:T(8,128)S(1)}, u32[]{:S(2)}, u32[]{:S(2)}) %collective-permute-start.19) | collective-permute-done | bytes 131104 | tf_op jit(solution)/shard_map/ppermute | solution.py:282
  179.7 21.9 %collective-permute-done.14 = f16[448,1024]{1,0:T(8,128)(2,1)} collective-permute-done((f16[448,1024]{1,0:T(8,128)(2,1)}, f16[448,1024]{1,0:T(8,128)(2,1)}, u32[]{:S(2)}, u32[]{:S(2)}) %collective-permute-start.14) | collective-permute-done | bytes 917536 | tf_op jit(solution)/shard_map/ppermute | solution.py:282
  201.6 4.8 %collective-permute-done.15 = f16[448,1024]{1,0:T(8,128)(2,1)} collective-permute-done((f16[448,1024]{1,0:T(8,128)(2,1)}, f16[448,1024]{1,0:T(8,128)(2,1)}, u32[]{:S(2)}, u32[]{:S(2)}) %collective-permute-start.15) | collective-permute-done | bytes 917536 | tf_op jit(solution)/shard_map/ppermute | solution.py:282
  206.5 3.8 %fusion.2.refs_0_ = f32[448,1024]{1,0:T(8,128)} fusion(f32[896,1024]{1,0:T(8,128)} %pair_grad.3, f16[448,1024]{1,0:T(8,128)(2,1)} %collective-permute-done.15, f16[448,1024]{1,0:T(8,128)(2,1)} %collective-permute-done.14, f32[]{:T(128)} %bitcast.20), kind=kLoop, calls=%fused_computation.9 | loop fusion | flops 2293760 | bytes 5505028 | tf_op jit(solution)/shard_map/mul | solution.py:445
  210.3 16.0 %mixing.1.refs_1_ = f32[256,256]{1,0:T(8,128)S(1)} custom-call(f32[128,128]{1,0:T(8,128)S(1)} %sketch_gram.1.ss_ref, f32[128,256]{1,0:T(8,128)S(1)} %add.303.cross_ref), custom_call_target="tpu_custom_call" | custom-call | flops 1 | bytes 1 | tf_op jit(solution)/shard_map/mixing/pallas_call | solution.py:511
  230.0 9.5 %direction.1 = f32[448,8,128]{2,1,0:T(8,128)} custom-call(s32[4]{0:T(128)S(1)} %pad_add_fusion.2.starts, s32[32]{0:T(128)S(1)} %select_n.231.pat, f32[448,1024]{1,0:T(8,128)} %fusion.2.refs_0_, f32[256,256]{1,0:T(8,128)S(1)} %mixing.1.refs_1_, bf16[32,128,256]{2,1,0:T(8,128)(2,1)} %copy-done.2, bf16[32,128,256]{2,1,0:T(8,128)(2,1)} %copy-done.1, ...), custom_call_target="tpu_custom_call" | custom-call | flops 1 | bytes 1 | tf_op jit(solution)/shard_map/direction/pallas_call | solution.py:530
  (143 shorter events, 57.6 us)
Async XLA Ops:
  0.6 6.8 %collective-permute-start.2 = (bf16[256,2048]{1,0:T(8,128)(2,1)}, bf16[256,2048]{1,0:T(8,128)(2,1)S(1)}, u32[]{:S(2)}, u32[]{:S(2)}) collective-permute-start(bf16[256,2048]{1,0:T(8,128)(2,1)} %refs_0_.7), channel_id=1, source_target_pairs={{0,1},{1,0},{2,3},{3,2},{4,5},{5,4},{6,7},{7,6},{8,9},{9,8},{10,11... | collective-permute-start | bytes 3145736 | tf_op jit(solution)/shard_map/ppermute | solution.py:282
  8.5 31.3 %all-to-all-start = ((f16[8,464,128]{2,1,0:T(8,128)(2,1)}), f16[8,464,128]{2,1,0:T(8,128)(2,1)}, u32[]{:S(2)}, u32[]{:S(2)}) async-start(f16[8,464,128]{2,1,0:T(8,128)(2,1)} %broadcast_in_dim.73), calls=%async_computation | async-start | bytes 1900544 | tf_op jit(solution)/shard_map/all_to_all | solution.py:288
  15.4 27.9 %collective-permute-start = (bf16[256,2048]{1,0:T(8,128)(2,1)S(1)}, bf16[256,2048]{1,0:T(8,128)(2,1)S(1)}, u32[]{:S(2)}, u32[]{:S(2)}) collective-permute-start(bf16[256,2048]{1,0:T(8,128)(2,1)S(1)} %copy-done), channel_id=1, source_target_pairs={{0,2},{1,3},{2,0},{3,1},{4,6},{5,7},{6,4},{7,5},{8,10},{9,11},{10,... | collective-permute-start | bytes 3145736 | tf_op jit(solution)/shard_map/ppermute | solution.py:282
  17.0 34.2 %collective-permute-start.1 = (bf16[256,2048]{1,0:T(8,128)(2,1)S(1)}, bf16[256,2048]{1,0:T(8,128)(2,1)}, u32[]{:S(2)}, u32[]{:S(2)}) collective-permute-start(bf16[256,2048]{1,0:T(8,128)(2,1)S(1)} %copy-done), channel_id=1, source_target_pairs={{0,4},{4,0},{8,12},{12,8},{16,20},{20,16},{24,28},{28,24},{1,5},{5... | collective-permute-start | bytes 3145736 | tf_op jit(solution)/shard_map/ppermute | solution.py:282
  51.1 42.3 %collective-permute-start.4 = (bf16[256,2048]{1,0:T(8,128)(2,1)}, bf16[256,2048]{1,0:T(8,128)(2,1)}, u32[]{:S(2)}, u32[]{:S(2)}) collective-permute-start(bf16[256,2048]{1,0:T(8,128)(2,1)} %collective-permute-done.1.refs_4_), channel_id=1, source_target_pairs={{0,2},{1,3},{2,0},{3,1},{4,6},{5,7},{6,4},{7,5},{8,10},{9,11},{10,... | collective-permute-start | bytes 3145736 | tf_op jit(solution)/shard_map/ppermute | solution.py:282
  52.6 40.9 %collective-permute-start.5 = (bf16[256,2048]{1,0:T(8,128)(2,1)}, bf16[256,2048]{1,0:T(8,128)(2,1)}, u32[]{:S(2)}, u32[]{:S(2)}) collective-permute-start(bf16[256,2048]{1,0:T(8,128)(2,1)} %collective-permute-done.1.refs_4_), channel_id=1, source_target_pairs={{0,1},{1,0},{2,3},{3,2},{4,5},{5,4},{6,7},{7,6},{8,9},{9,8},{10,11... | collective-permute-start | bytes 3145736 | tf_op jit(solution)/shard_map/ppermute | solution.py:282
  52.6 23.3 %collective-permute-start.3 = (bf16[256,2048]{1,0:T(8,128)(2,1)S(1)}, bf16[256,2048]{1,0:T(8,128)(2,1)}, u32[]{:S(2)}, u32[]{:S(2)}) collective-permute-start(bf16[256,2048]{1,0:T(8,128)(2,1)S(1)} %collective-permute-done.refs_2_), channel_id=1, source_target_pairs={{0,1},{1,0},{2,3},{3,2},{4,5},{5,4},{6,7},{7,6},{8,9},{9,8},{10,11... | collective-permute-start | bytes 3145736 | tf_op jit(solution)/shard_map/ppermute | solution.py:282
  53.1 40.3 %collective-permute-start.6 = (bf16[4,448,256]{2,1,0:T(8,128)(2,1)}, bf16[4,448,256]{2,1,0:T(8,128)(2,1)}, u32[]{:S(2)}, u32[]{:S(2)}) collective-permute-start(bf16[4,448,256]{2,1,0:T(8,128)(2,1)} %get-tuple-element.44), channel_id=1, source_target_pairs={{0,4},{4,0},{8,12},{12,8},{16,20},{20,16},{24,28},{28,24},{1,5},{5... | collective-permute-start | bytes 2752520 | tf_op jit(solution)/shard_map/ppermute | solution.py:282
  54.3 39.2 %all-to-all-start.1 = ((f16[8,128,256]{2,1,0:T(8,128)(2,1)}), f16[8,128,256]{2,1,0:T(8,128)(2,1)}, u32[]{:S(2)}, u32[]{:S(2)}) async-start(f16[8,128,256]{2,1,0:T(8,128)(2,1)} %broadcast_in_dim.74), calls=%async_computation.1 | async-start | bytes 1048576 | tf_op jit(solution)/shard_map/all_to_all | solution.py:288
  62.0 13.9 %collective-permute-start.8 = (f32[16,128]{1,0:T(8,128)S(1)}, f32[16,128]{1,0:T(8,128)S(1)}, u32[]{:S(2)}, u32[]{:S(2)}) collective-permute-start(f32[16,128]{1,0:T(8,128)S(1)} %max.14), channel_id=1, source_target_pairs={{0,2},{1,3},{2,0},{3,1},{4,6},{5,7},{6,4},{7,5},{8,10},{9,11},{10,... | collective-permute-start | bytes 24584 | tf_op jit(solution)/shard_map/ppermute | solution.py:282
  96.4 4.6 %collective-permute-start.11 = (bf16[256,2048]{1,0:T(8,128)(2,1)}, bf16[256,2048]{1,0:T(8,128)(2,1)S(1)}, u32[]{:S(2)}, u32[]{:S(2)}) collective-permute-start(bf16[256,2048]{1,0:T(8,128)(2,1)} %collective-permute-done.4.refs_6_), channel_id=1, source_target_pairs={{0,1},{1,0},{2,3},{3,2},{4,5},{5,4},{6,7},{7,6},{8,9},{9,8},{10,11... | collective-permute-start | bytes 3145736 | tf_op jit(solution)/shard_map/ppermute | solution.py:282
  97.4 3.2 %collective-permute-start.9 = (f16[16,128,128]{2,1,0:T(8,128)(2,1)S(1)}, f16[16,128,128]{2,1,0:T(8,128)(2,1)S(1)}, u32[]{:S(2)}, u32[]{:S(2)}) collective-permute-start(f16[16,128,128]{2,1,0:T(8,128)(2,1)S(1)} %get-tuple-element.81), channel_id=1, source_target_pairs={{0,1},{1,0},{2,3},{3,2},{4,5},{5,4},{6,7},{7,6},{8,9},{9,8},{10,11... | collective-permute-start | bytes 1572872 | tf_op jit(solution)/shard_map/ppermute | solution.py:282
  100.9 24.6 %collective-permute-start.13 = (f16[16,128,128]{2,1,0:T(8,128)(2,1)S(1)}, f16[16,128,128]{2,1,0:T(8,128)(2,1)S(1)}, u32[]{:S(2)}, u32[]{:S(2)}) collective-permute-start(f16[16,128,128]{2,1,0:T(8,128)(2,1)S(1)} %get-tuple-element.54), channel_id=1, source_target_pairs={{0,2},{1,3},{2,0},{3,1},{4,6},{5,7},{6,4},{7,5},{8,10},{9,11},{10,... | collective-permute-start | bytes 1572872 | tf_op jit(solution)/shard_map/ppermute | solution.py:282
  113.3 29.6 %collective-permute-start.12 = (f16[448,1024]{1,0:T(8,128)(2,1)}, f16[448,1024]{1,0:T(8,128)(2,1)}, u32[]{:S(2)}, u32[]{:S(2)}) collective-permute-start(f16[448,1024]{1,0:T(8,128)(2,1)} %slice_convert_fusion.1), channel_id=1, source_target_pairs={{0,8},{4,12},{8,0},{12,4},{16,24},{20,28},{24,16},{28,20},{1,9},{5... | collective-permute-start | bytes 2752520 | tf_op jit(solution)/shard_map/ppermute | solution.py:282
  126.5 18.9 %all-to-all-start.2 = ((f16[8,256,128]{2,1,0:T(8,128)(2,1)}), f16[8,256,128]{2,1,0:T(8,128)(2,1)}, u32[]{:S(2)}, u32[]{:S(2)}) async-start(f16[8,256,128]{2,1,0:T(8,128)(2,1)} %bitcast.42), calls=%async_computation.2 | async-start | bytes 1048576 | tf_op jit(solution)/shard_map/all_to_all | solution.py:431
  130.9 22.5 %collective-permute-start.17 = (f16[8,128,256]{2,1,0:T(8,128)(2,1)}, f16[8,128,256]{2,1,0:T(8,128)(2,1)}, u32[]{:S(2)}, u32[]{:S(2)}) collective-permute-start(f16[8,128,256]{2,1,0:T(8,128)(2,1)} %all-to-all-done.1), channel_id=1, source_target_pairs={{0,2},{1,3},{2,0},{3,1},{4,6},{5,7},{6,4},{7,5},{8,10},{9,11},{10,... | collective-permute-start | bytes 1572872 | tf_op jit(solution)/shard_map/ppermute | solution.py:282
  147.4 21.6 %all-to-all-start.3 = ((f16[8,256,128]{2,1,0:T(8,128)(2,1)}), f16[8,256,128]{2,1,0:T(8,128)(2,1)}, u32[]{:S(2)}, u32[]{:S(2)}) async-start(f16[8,256,128]{2,1,0:T(8,128)(2,1)} %broadcast_in_dim.79), calls=%async_computation.3 | async-start | bytes 1048576 | tf_op jit(solution)/shard_map/all_to_all | solution.py:288
  153.4 7.7 %collective-permute-start.16 = (f16[8,128,256]{2,1,0:T(8,128)(2,1)}, f16[8,128,256]{2,1,0:T(8,128)(2,1)S(1)}, u32[]{:S(2)}, u32[]{:S(2)}) collective-permute-start(f16[8,128,256]{2,1,0:T(8,128)(2,1)} %all-to-all-done.1), channel_id=1, source_target_pairs={{0,1},{1,0},{2,3},{3,2},{4,5},{5,4},{6,7},{7,6},{8,9},{9,8},{10,11... | collective-permute-start | bytes 1572872 | tf_op jit(solution)/shard_map/ppermute | solution.py:282
  153.4 8.5 %collective-permute-start.18 = (f16[8,128,256]{2,1,0:T(8,128)(2,1)}, f16[8,128,256]{2,1,0:T(8,128)(2,1)}, u32[]{:S(2)}, u32[]{:S(2)}) collective-permute-start(f16[8,128,256]{2,1,0:T(8,128)(2,1)} %collective-permute-done.17), channel_id=1, source_target_pairs={{0,1},{1,0},{2,3},{3,2},{4,5},{5,4},{6,7},{7,6},{8,9},{9,8},{10,11... | collective-permute-start | bytes 1572872 | tf_op jit(solution)/shard_map/ppermute | solution.py:282
  154.6 47.1 %collective-permute-start.14 = (f16[448,1024]{1,0:T(8,128)(2,1)}, f16[448,1024]{1,0:T(8,128)(2,1)}, u32[]{:S(2)}, u32[]{:S(2)}) collective-permute-start(f16[448,1024]{1,0:T(8,128)(2,1)} %slice_convert_fusion), channel_id=1, source_target_pairs={{0,8},{4,12},{8,0},{12,4},{16,24},{20,28},{24,16},{28,20},{1,9},{5... | collective-permute-start | bytes 2752520 | tf_op jit(solution)/shard_map/ppermute | solution.py:282
  158.7 47.8 %collective-permute-start.15 = (f16[448,1024]{1,0:T(8,128)(2,1)}, f16[448,1024]{1,0:T(8,128)(2,1)}, u32[]{:S(2)}, u32[]{:S(2)}) collective-permute-start(f16[448,1024]{1,0:T(8,128)(2,1)} %fusion.3), channel_id=1, source_target_pairs={{0,16},{4,20},{8,24},{12,28},{16,0},{20,4},{24,8},{28,12},{1,17},{... | collective-permute-start | bytes 2752520 | tf_op jit(solution)/shard_map/ppermute | solution.py:282
  172.3 5.0 %collective-permute-start.19 = (f32[128,256]{1,0:T(8,128)S(1)}, f32[128,256]{1,0:T(8,128)S(1)}, u32[]{:S(2)}, u32[]{:S(2)}) collective-permute-start(f32[128,256]{1,0:T(8,128)S(1)} %cross_gram.1), channel_id=1, source_target_pairs={{0,2},{1,3},{2,0},{3,1},{4,6},{5,7},{6,4},{7,5},{8,10},{9,11},{10,... | collective-permute-start | bytes 393224 | tf_op jit(solution)/shard_map/ppermute | solution.py:282
  178.8 48.8 %collective-permute-start.22 = (f16[16,128,128]{2,1,0:T(8,128)(2,1)}, f16[16,128,128]{2,1,0:T(8,128)(2,1)S(1)}, u32[]{:S(2)}, u32[]{:S(2)}) collective-permute-start(f16[16,128,128]{2,1,0:T(8,128)(2,1)} %bitcast.21), channel_id=1, source_target_pairs={{0,2},{1,3},{2,0},{3,1},{4,6},{5,7},{6,4},{7,5},{8,10},{9,11},{10,... | collective-permute-start | bytes 1572872 | tf_op jit(solution)/shard_map/ppermute | solution.py:282
  210.3 18.2 %collective-permute-start.21 = (f16[16,128,128]{2,1,0:T(8,128)(2,1)}, f16[16,128,128]{2,1,0:T(8,128)(2,1)S(1)}, u32[]{:S(2)}, u32[]{:S(2)}) collective-permute-start(f16[16,128,128]{2,1,0:T(8,128)(2,1)} %bitcast.21), channel_id=1, source_target_pairs={{0,1},{1,0},{2,3},{3,2},{4,5},{5,4},{6,7},{7,6},{8,9},{9,8},{10,11... | collective-permute-start | bytes 1572872 | tf_op jit(solution)/shard_map/ppermute | solution.py:282
  (19 other events, 82.3 us)

commit v5 on v4

--- a/solution.py
+++ b/solution.py
@@ -60,21 +60,26 @@
     return held[shard, :, pl.ds(offset, size)]
 
 
-def compress_kernel(n_shards, per_shard, scale, per_step, pat, pat_out, *refs):
+def compress_kernel(n_shards, per_shard, scale, per_step, pat, pat_out, places, *refs):
     shards = refs[:n_shards]
-    hid_ref, proj_ref, out_ref, held, sems = refs[n_shards:]
+    hid_ref, parts_ref, out_ref, held, proj, sems = refs[n_shards:]
     blk = out_ref.shape[1]
+    n_parts, part_rows = parts_ref.shape[:2]
 
     @pl.when(pl.program_id(0) == 0)
     def _():
-        load_all([(ref, held.at[i]) for i, ref in enumerate(shards)], sems)
+        loads = [(ref, held.at[i]) for i, ref in enumerate(shards)]
+        for i in range(n_parts):
+            rows = pl.ds(pl.multiple_of(places[i] * part_rows, 8), part_rows)
+            loads.append((parts_ref.at[i], proj.at[rows]))
+        load_all(loads, sems)
         out_ref[...] = jnp.zeros_like(out_ref)
 
     for u in range(per_step):
         row = pl.program_id(0) * per_step + u
         span = slice(u * blk, (u + 1) * blk)
         hid = hid_ref[span, :]
-        ph, pl_ = split2(proj_ref[span, :].T)
+        ph, pl_ = split2(proj[pl.ds(pl.multiple_of(row * blk, blk), blk), :].T)
         left = jnp.concatenate(split2((dot(ph, hid) + dot(pl_, hid)) * scale), axis=0)
         cols = [pat[row * SLOTS + j] for j in range(SLOTS)]
         parts = []
@@ -93,9 +98,9 @@
             out_ref[c] = total
 
 
-def grad_kernel(n_shards, per_shard, blk, window, n_windows, order, starts, pat, scale, *refs):
+def grad_kernel(n_shards, per_shard, blk, window, n_windows, order, starts, pat, *refs):
     shards = refs[: 2 * n_shards]
-    own_ref, got_ref, out_ref, held, sems = refs[2 * n_shards :]
+    own_ref, got_ref, out_ref, top_ref, held, sems = refs[2 * n_shards :]
     toks = own_ref.shape[1]
 
     @pl.when(pl.program_id(0) == 0)
@@ -107,7 +112,9 @@
             ],
             sems,
         )
-
+        top_ref[...] = jnp.zeros_like(top_ref)
+
+    top = top_ref[...]
     for w in range(n_windows):
         index = order[pl.program_id(0)] * n_windows + w
         rows = pl.ds(pl.multiple_of(starts[index], window // 2 if window >= 32 else 8), window)
@@ -117,7 +124,12 @@
                 [column_block(held, pat[index * SLOTS + j + i], per_shard, blk) for i in (0, 1)],
                 axis=1,
             )
-            out_ref[rows, j * blk : (j + 2) * blk] = dot(hid, chosen) * scale[0]
+            part = dot(hid, chosen)
+            out_ref[rows, j * blk : (j + 2) * blk] = part
+            size = jnp.abs(part)
+            for i in range(0, window, 8):
+                top = jnp.maximum(top, size[i : i + 8])
+    top_ref[...] = top
 
 
 def input_grad_kernel(n_shards, per_shard, blk, per_step, pat, *refs):
@@ -284,27 +296,27 @@
     def after(x, *others):
         return lax.optimization_barrier((x, *others))[0]
 
+    few = n_dp <= 8
+
     def over_dp(x):
+        if few:
+            return jnp.stack([x] + [swap(x, "dp", bits) for bits in range(1, n_dp)])
         return lax.all_to_all(jnp.broadcast_to(x[None], (n_dp, *x.shape)), "dp", 0, 0)
-
-    def exponent(x):
-        top = jnp.max(jnp.abs(x)).astype(F32)
-        return jnp.floor(jnp.log2(jnp.maximum(top, 1e-15))) + 1.0
 
     width = sketch.shape[1]
     core_half = swap(cotangent, "mp", 1)
-    exponents = jnp.stack([exponent(hidden), exponent(cotangent)])
-    exponents = jnp.broadcast_to(jnp.repeat(exponents, 8)[:, None], (16, rank))
-    proj_t = projection.reshape(rank, dev_rows).T * PROJ_SCALE
-    early = jnp.concatenate([proj_t, exponents], axis=0).astype(F16)
-    early = over_dp(after(early, core_half))
-    proj_all = early[:, :dev_rows].reshape(mp_rows, rank).astype(F32)
-    peaks = jnp.max(early[:, dev_rows:].astype(F32), axis=0)
+    proj_t = (projection.reshape(rank, dev_rows).T * PROJ_SCALE).astype(F16)
+    proj_all = over_dp(after(proj_t, core_half)).astype(F32)
+    if few:
+        places = jnp.bitwise_xor(jnp.arange(n_dp, dtype=jnp.int32), dp)
+    else:
+        proj_all = proj_all.reshape(1, mp_rows, rank)
+        places = jnp.zeros((1,), jnp.int32)
     hid_t = hidden.T
     hid_parts = hid_t.reshape(outer, 2, dev_rows, tok_rows)
     hid_own = lax.dynamic_index_in_dim(hid_parts, side, 1, keepdims=False)
     hid_send = lax.dynamic_index_in_dim(hid_parts, 1 - side, 1, keepdims=False)
-    x_half, y_own, core_half, hid_t, hid_own, hid_send, weights_2d, proj_all, peaks = (
+    x_half, y_own, core_half, hid_t, hid_own, hid_send, weights_2d, proj_all = (
         lax.optimization_barrier(
             (
                 swap(cotangent, "mp", 2),
@@ -315,7 +327,6 @@
                 hid_send,
                 weights.reshape(mp_rows, slots * blk),
                 proj_all,
-                peaks,
             )
         )
     )
@@ -323,8 +334,6 @@
     y_x = swap(y_own, "mp", 2)
     y_core = swap(y_own, "mp", 1)
     hid_got = swap(hid_send, "dp", 1)
-    for bit in (1, 2):
-        peaks = jnp.maximum(peaks, swap(peaks, "mp", bit))
     sk_own = over_dp(after(sketch.astype(F16), x_half))
     pattern_rel = jnp.bitwise_xor(pattern, mp * per_shard)
 
@@ -334,7 +343,10 @@
         per = width // blk
         shard, rest = block // per, block % per
         near_mp = jnp.bitwise_xor(shard % n_mp, mp)
-        return (near_mp * n_dp + shard // n_mp) * per + rest
+        far_dp = shard // n_mp
+        if few:
+            far_dp = jnp.bitwise_xor(far_dp, dp)
+        return (near_mp * n_dp + far_dp) * per + rest
 
     pat_all = pattern_rel.reshape(-1)
     partial_c = pl.pallas_call(
@@ -342,27 +354,25 @@
             compress_kernel, n_mp, per_shard, 1.0 / (PROJ_SCALE * all_tokens), per_step
         ),
         grid_spec=pltpu.PrefetchScalarGridSpec(
-            num_scalar_prefetch=2,
+            num_scalar_prefetch=3,
             grid=(block_rows // per_step,),
             in_specs=[ANY] * n_mp
-            + [
-                pl.BlockSpec((per_step * blk, tok_rows), lambda i, a, b: (i, 0)),
-                pl.BlockSpec((per_step * blk, rank), lambda i, a, b: (i, 0)),
-            ],
-            out_specs=pl.BlockSpec((col_blocks, rank, blk), lambda i, a, b: (0, 0, 0)),
+            + [pl.BlockSpec((per_step * blk, tok_rows), lambda i, a, b, c: (i, 0)), ANY],
+            out_specs=pl.BlockSpec((col_blocks, rank, blk), lambda i, a, b, c: (0, 0, 0)),
             scratch_shapes=[
                 pltpu.VMEM((n_mp, tok_rows, shard_cols), BF),
-                pltpu.SemaphoreType.DMA((n_mp,)),
+                pltpu.VMEM((mp_rows, rank), F32),
+                pltpu.SemaphoreType.DMA((n_mp + len(places),)),
             ],
         ),
         out_shape=jax.ShapeDtypeStruct((col_blocks, rank, blk), F32),
         compiler_params=params(),
         cost_estimate=SMALL,
         name="compress",
-    )(pat_all, place(pattern).reshape(-1), *own, hid_t, proj_all)
-
-    partial_c, y_x, y_core, hid_got, peaks, sk_own = lax.optimization_barrier(
-        (partial_c, y_x, y_core, hid_got, peaks, sk_own)
+    )(pat_all, place(pattern).reshape(-1), places, *own, hid_t, proj_all)
+
+    partial_c, y_x, y_core, hid_got, sk_own = lax.optimization_barrier(
+        (partial_c, y_x, y_core, hid_got, sk_own)
     )
     y_group = [y_own, y_core, y_x, swap(y_x, "mp", 1)]
     quarters = partial_c.reshape(n_mp, per_shard, rank, blk)
@@ -374,7 +384,6 @@
     y_group[3] = y_last
     far_sum = swap(far_half, "mp", 2)
 
-    grad_scale = jnp.exp2(14.0 - peaks[0, 0] - peaks[8, 0] - math.log2(all_tokens))
     half_rows = outer * dev_rows
     devices = 2 * jnp.arange(outer, dtype=jnp.int32) + side
     window, _, _ = windows_of(dp * dev_rows, dev_rows, blk)
@@ -387,20 +396,26 @@
 
     def pair_grad(blocks, shards):
         order = jnp.bitwise_xor(jnp.asarray(blocks, jnp.int32), dp // 2)
-        out = pl.pallas_call(
+        out, top = pl.pallas_call(
             functools.partial(grad_kernel, n_mp, per_shard, blk, window, n_windows),
             grid_spec=pltpu.PrefetchScalarGridSpec(
-                num_scalar_prefetch=4,
+                num_scalar_prefetch=3,
                 grid=(len(blocks),),
                 in_specs=[ANY] * (2 * n_mp)
-                + [pl.BlockSpec((dev_rows, tok_rows), lambda i, o, a, b, c: (o[i], 0))] * 2,
-                out_specs=pl.BlockSpec((dev_rows, slots * blk), lambda i, o, a, b, c: (i, 0)),
+                + [pl.BlockSpec((dev_rows, tok_rows), lambda i, o, a, b: (o[i], 0))] * 2,
+                out_specs=[
+                    pl.BlockSpec((dev_rows, slots * blk), lambda i, o, a, b: (i, 0)),
+                    pl.BlockSpec((8, 2 * blk), lambda i, o, a, b: (0, 0)),
+                ],
                 scratch_shapes=[
                     pltpu.VMEM((n_mp, 2 * tok_rows, shard_cols), BF),
                     pltpu.SemaphoreType.DMA((2 * n_mp,)),
                 ],
             ),
-            out_shape=jax.ShapeDtypeStruct((len(blocks) * dev_rows, slots * blk), F32),
+            out_shape=[
+                jax.ShapeDtypeStruct((len(blocks) * dev_rows, slots * blk), F32),
+                jax.ShapeDtypeStruct((8, 2 * blk), F32),
+            ],
             compiler_params=params(),
             cost_estimate=SMALL,
             name="pair_grad",
@@ -408,41 +423,63 @@
             order,
             window_starts.reshape(-1),
             pat_half,
-            grad_scale[None],
             *shards,
             hid_own.reshape(half_rows, tok_rows).astype(hid_type),
             hid_got.reshape(half_rows, tok_rows).astype(hid_type),
         )
         out = out.reshape(len(blocks), dev_rows, slots * blk)
-        return {block: out[i] for i, block in enumerate(blocks)}
+        top = jnp.maximum(jnp.max(top), 1e-30)
+        return {block: (out[i], top) for i, block in enumerate(blocks)}
+
+    def pack(part):
+        value, top = part
+        return (value * (16384.0 / top)).astype(F16), jnp.broadcast_to(top, (8, 128))
+
+    def send(packed, bit):
+        top = swap(packed[1], "dp", bit)
+        return swap(packed[0], "dp", bit), top
+
+    def add(part, got):
+        value, top = part
+        far = got[1][0, 0]
+        return value + got[0].astype(F32) * (far * (1.0 / 16384.0)), top + far
 
     crossing = [i for i in range(outer) if i & 2][::-1]
     staying = [i for i in range(outer) if not i & 2][::-1]
     sums = pair_grad(crossing, own + y_group)
-    sent = {i: sums[i].astype(F16) for i in crossing if i & 1}
-    got = {i: swap(sent[i], "dp", 2) for i in crossing if i & 1}
-    sums.update(pair_grad(staying, own[:3] + [after(own[3], *sent.values())] + y_group))
-    sent = {i: sums[i].astype(F16) for i in staying if i & 1}
-    got.update({i: swap(sent[i], "dp", 2) for i in staying if i & 1})
-    far_sum, near_half, _ = lax.optimization_barrier((far_sum, near_half, list(sent.values())))
+    sent = {i: pack(sums[i]) for i in crossing if i & 1}
+    got = {i: send(part, 2) for i, part in sent.items()}
+    before = [part[0] for part in sent.values()]
+    sums.update(pair_grad(staying, own[:3] + [after(own[3], *before)] + y_group))
+    sent = {i: pack(sums[i]) for i in staying if i & 1}
+    got.update({i: send(part, 2) for i, part in sent.items()})
+    before = [part[0] for part in sent.values()]
+    far_sum, near_half, _ = lax.optimization_barrier((far_sum, near_half, before))
 
     quarter = near_half + far_sum.astype(F32)
     pieces = quarter.astype(F16).reshape(n_dp, per_shard * rank // n_dp, blk)
-    pieces = lax.all_to_all(pieces, "dp", 0, 0)
+    if few:
+        pieces = [pieces[0]] + [swap(pieces[bits], "dp", bits) for bits in range(1, n_dp)]
+    else:
+        pieces = list(lax.all_to_all(pieces, "dp", 0, 0))
 
     level = 1
     while level < outer:
         if level > 1:
-            got = {}
-            for i in [i for i in sums if i & level]:
-                got[i] = swap(sums[i].astype(F16), "dp", 2 * level)
+            got = {i: send(pack(sums[i]), 2 * level) for i in sums if i & level}
         for i in got:
-            sums[i ^ level] = sums[i ^ level] + got[i].astype(F32)
+            sums[i ^ level] = add(sums[i ^ level], got[i])
         sums = {i: part for i, part in sums.items() if not i & level}
         if level == 1 and outer > 2:
-            sums[2], pieces = lax.optimization_barrier((sums[2].astype(F16), pieces))
+            crossed, pieces = lax.optimization_barrier((pack(sums[2]), pieces))
+            got = {2: send(crossed, 4)}
+            if outer > 4:
+                got.update({i: send(pack(sums[i]), 4) for i in sums if i & 2 and i > 2})
+            for i in got:
+                sums[i ^ 2] = add(sums[i ^ 2], got[i]) if outer > 4 else sums[i ^ 2]
+            sums = {i: part for i, part in sums.items() if not i & 2}
+            level = 2
         level *= 2
-    grad = sums[0] * (1.0 / (grad_scale * all_tokens))
 
     input_grad = pl.pallas_call(
         functools.partial(input_grad_kernel, n_mp, per_shard, blk, per_step),
@@ -464,7 +501,7 @@
     )(pat_all, *own, after(weights_2d, quarter))
     pieces, input_grad = lax.optimization_barrier((pieces, input_grad))
 
-    piece = jnp.sum(pieces.astype(F32), axis=0).astype(F16)
+    piece = sum(part.astype(F32) for part in pieces).astype(F16)
     quarter16 = over_dp(piece).reshape(per_shard, rank, blk)
 
     sk_own = after(sk_own, quarter)
@@ -524,6 +561,12 @@
     comp_parts = [split2_xla(part.astype(F32)) for part in comp_parts]
     comp_parts = [part[0] for part in comp_parts] + [part[1] for part in comp_parts]
 
+    kept, mixing, comp_parts, sk_high, sk_low = lax.optimization_barrier(
+        (sums[0], mixing, comp_parts, sk_high, sk_low)
+    )
+    if outer == 4:
+        kept = add(kept, got[2])
+    grad = kept[0] * (1.0 / all_tokens)
     _, my_starts, my_blocks = windows_of(dp * dev_rows, dev_rows, blk)
     my_pat = jnp.take(place(pattern), my_blocks, axis=0).reshape(-1)
     smem = pl.BlockSpec(memory_space=pltpu.SMEM)

time: 242 us -> 306 us (1.26)
  waiting for transfers between devices: 63.8 us -> 104 us
  starting transfers between devices: 41.9 us -> 80.7 us
  other arithmetic: 31.7 us -> 24.2 us
  local copies, waits for them, and re-layouts: 26.5 us -> 22.1 us
  Pallas kernels: 71.6 us -> 68.2 us
    ppermute x24 -> x53, starting transfers between devices: 19.1 us -> 80.7 us  [swap(): return lax.ppermute(x, axis, [(i, i ^ bit) for i in range(size)])]
    ppermute x24 -> x53, waiting for transfers between devices: 56 us -> 104 us  [swap(): return lax.ppermute(x, axis, [(i, i ^ bit) for i in range(size)])]
    all_to_all x4 -> x0, starting transfers between devices: 22.8 us -> none  [the longest x3 18.5 us: over_dp(): lax.all_to_all(jnp.broadcast_to(x[None], (n_dp, *x.shape)), 'dp', 0, 0)]
    all_to_all x4 -> x0, waiting for transfers between devices: 7.77 us -> none  [the longest x3 7.72 us: over_dp(): lax.all_to_all(jnp.broadcast_to(x[None], (n_dp, *x.shape)), 'dp', 0, 0)]
    convert_element_type x3 -> x5, other arithmetic: 3.83 us -> 9.42 us  [the longest x3 8.05 us: pack(): (value * (16384.0 / top)).astype(F16)]
    convert_element_type x7, other arithmetic: 7.5 us -> 2.64 us  [split2_xla(): return (high.astype(BF), (value - high).astype(BF))]
    another operation x4 -> x1, other arithmetic: 8.12 us -> 3.75 us
    reduce_max x3 -> x2, other arithmetic: 5.09 us -> 1.22 us  [pair_grad(): top = jnp.maximum(jnp.max(top), 1e-30)]
  transfers between devices with their start and end apart: 28 -> 53, of which waited for: 12 -> 21; matrix products, arithmetic and copies ran while one was open for 21% -> 13% of each run, Pallas kernels for 26% -> 19%
where the time goes in v5:
time: 306 us; the launch traced here: 305 us
  waiting for transfers between devices  104 us (34%)
  starting transfers between devices  80.7 us (26%)
  Pallas kernels  68.2 us (22%)
  other arithmetic  24.2 us (8%)
  local copies, waits for them, and re-layouts  22.1 us (7%)
  between operations  5.58 us (2%)
    ppermute x53, waiting for transfers between devices, swap(): return lax.ppermute(x, axis, [(i, i ^ bit) for i in range(size)])  104 us
    ppermute x53, starting transfers between devices, swap(): return lax.ppermute(x, axis, [(i, i ^ bit) for i in range(size)])  80.7 us
    pallas_call x1, Pallas kernels, per_device(): pl.pallas_call(mixing_kernel, in_specs=[VMEM] * 2, out_specs=VMEM, out_sh...  16 us
    unnamed x71, local copies, waits for them, and re-layouts  15.9 us
    pallas_call x1, Pallas kernels, per_device(): pl.pallas_call(functools.partial(compress_kernel, n_mp, per_shard, 1.0 /...  15.4 us
    pallas_call x2, Pallas kernels, pair_grad(): pl.pallas_call(functools.partial(grad_kernel, n_mp, per_shard, blk, windo...  14.1 us
    pallas_call x1, Pallas kernels, per_device(): pl.pallas_call(functools.partial(input_grad_kernel, n_mp, per_shard, blk,...  10.4 us
    pallas_call x1, Pallas kernels, per_device(): pl.pallas_call(functools.partial(direction_kernel, sk_per, window, n_wind...  9.53 us
  transfers between devices with their start and end apart: 53, of which 21 were waited for; matrix products, arithmetic and copies ran while one was open for 13% of the time, Pallas kernels for 19%

profile of v5, /device:TPU:0, one launch (start us, length us, event | category | flops | bytes accessed | tf_op | source)
XLA Modules:
  0.0 304.8 jit_solution(9610682985423425162)
XLA Ops:
  7.6 3.8 %copy.21 = bf16[256,3584]{0,1:T(8,128)(2,1)} copy(bf16[256,3584]{1,0:T(8,128)(2,1)} %param.9) | data formatting | bytes 3670016 | tf_op args[1]
  11.4 8.0 %copy.28 = bf16[448,8,8,128]{3,1,2,0:T(8,128)(2,1)} copy(bf16[448,8,8,128]{3,2,1,0:T(8,128)(2,1)} %bitcast.94) | data formatting | bytes 14680064
  25.0 8.4 %collective-permute-done.3 = f16[448,128]{1,0:T(8,128)(2,1)S(1)} collective-permute-done((f16[448,128]{1,0:T(8,128)(2,1)S(1)}, f16[448,128]{1,0:T(8,128)(2,1)S(1)}, u32[]{:S(2)}, u32[]{:S(2)}) %collective-permute-start.3) | collective-permute-done | bytes 114720 | tf_op jit(solution)/shard_map/ppermute | solution.py:294
  37.4 3.7 %collective-permute-start.8 = (f16[448,128]{1,0:T(8,128)(2,1)S(1)}, f16[448,128]{1,0:T(8,128)(2,1)S(1)}, u32[]{:S(2)}, u32[]{:S(2)}) collective-permute-start(f16[448,128]{1,0:T(8,128)(2,1)S(1)} %fusion.7), channel_id=1, source_target_pairs={{0,24},{4,28},{8,16},{12,20},{16,8},{20,12},{24,0},{28,4},{1,25},{... | collective-permute-start | bytes 344072 | tf_op jit(solution)/shard_map/ppermute | solution.py:294
  41.1 4.6 %collective-permute-done.6 = f16[448,128]{1,0:T(8,128)(2,1)S(1)} collective-permute-done((f16[448,128]{1,0:T(8,128)(2,1)S(1)}, f16[448,128]{1,0:T(8,128)(2,1)S(1)}, u32[]{:S(2)}, u32[]{:S(2)}) %collective-permute-start.6) | collective-permute-done | bytes 114720 | tf_op jit(solution)/shard_map/ppermute | solution.py:294
  45.8 4.2 %collective-permute-start.9 = (f16[448,128]{1,0:T(8,128)(2,1)S(1)}, f16[448,128]{1,0:T(8,128)(2,1)S(1)}, u32[]{:S(2)}, u32[]{:S(2)}) collective-permute-start(f16[448,128]{1,0:T(8,128)(2,1)S(1)} %fusion.7), channel_id=1, source_target_pairs={{0,28},{4,24},{8,20},{12,16},{16,12},{20,8},{24,4},{28,0},{1,29},{... | collective-permute-start | bytes 344072 | tf_op jit(solution)/shard_map/ppermute | solution.py:294
  68.9 3.4 %collective-permute-start.18 = (f16[128,256]{1,0:T(8,128)(2,1)S(1)}, f16[128,256]{1,0:T(8,128)(2,1)S(1)}, u32[]{:S(2)}, u32[]{:S(2)}) collective-permute-start(f16[128,256]{1,0:T(8,128)(2,1)S(1)} %convert_element_type.144), channel_id=1, source_target_pairs={{0,20},{4,16},{8,28},{12,24},{16,4},{20,0},{24,12},{28,8},{1,21},{... | collective-permute-start | bytes 196616 | tf_op jit(solution)/shard_map/ppermute | solution.py:294
  75.1 4.1 %collective-permute-start.19 = (f16[128,256]{1,0:T(8,128)(2,1)S(1)}, f16[128,256]{1,0:T(8,128)(2,1)S(1)}, u32[]{:S(2)}, u32[]{:S(2)}) collective-permute-start(f16[128,256]{1,0:T(8,128)(2,1)S(1)} %convert_element_type.144), channel_id=1, source_target_pairs={{0,24},{4,28},{8,16},{12,20},{16,8},{20,12},{24,0},{28,4},{1,25},{... | collective-permute-start | bytes 196616 | tf_op jit(solution)/shard_map/ppermute | solution.py:294
  81.6 6.0 %collective-permute-start.20 = (f16[128,256]{1,0:T(8,128)(2,1)S(1)}, f16[128,256]{1,0:T(8,128)(2,1)S(1)}, u32[]{:S(2)}, u32[]{:S(2)}) collective-permute-start(f16[128,256]{1,0:T(8,128)(2,1)S(1)} %convert_element_type.144), channel_id=1, source_target_pairs={{0,28},{4,24},{8,20},{12,16},{16,12},{20,8},{24,4},{28,0},{1,29},{... | collective-permute-start | bytes 196616 | tf_op jit(solution)/shard_map/ppermute | solution.py:294
  90.0 15.4 %compress.1 = f32[64,128,128]{2,1,0:T(8,128)} custom-call(s32[224]{0:T(256)S(1)} %reshape.434.pat, s32[224]{0:T(256)S(1)} %reshape.435.pat_out, s32[8]{0:T(128)S(1)} %iota_xor_fusion.places, bf16[256,2048]{1,0:T(8,128)(2,1)S(1)} %copy-done.2, bf16[256,2048]{1,0:T(8,128)(2,1)S(1)} %collective-permute-done.2.refs_1_, ...), custom_call_target="tpu_custom_call" | custom-call | flops 1 | bytes 1 | tf_op jit(solution)/shard_map/compress/pallas_call | solution.py:352
  105.5 3.8 %convert.4 = f16[64,128,128]{2,1,0:T(8,128)(2,1)S(1)} convert(f32[64,128,128]{2,1,0:T(8,128)} %compress.1) | non-fusion elementwise | flops 1048576 | bytes 6291456 | tf_op jit(solution)/shard_map/convert.1
  116.5 7.0 %pair_grad.2 = (f32[896,1024]{1,0:T(8,128)}, f32[8,256]{1,0:T(8,128)S(1)}) custom-call(s32[2]{0:T(128)S(1)} %broadcast_xor_fusion.2.order, s32[16]{0:T(128)S(1)} %reshape.431.starts, s32[128]{0:T(128)S(1)} %select_n.215.pat, bf16[256,2048]{1,0:T(8,128)(2,1)S(1)} %copy-done.2, bf16[256,2048]{1,0:T(8,128)(2,1)S(1)} %collective-permute-done.2.refs_1_, ...), custom_call_target="tpu_custom_call" | custom-call | flops 1 | bytes 1 | tf_op jit(solution)/shard_map/pair_grad/pallas_call | solution.py:399
  130.8 7.1 %pair_grad.3 = (f32[896,1024]{1,0:T(8,128)}, f32[8,256]{1,0:T(8,128)S(1)}) custom-call(s32[2]{0:T(128)S(1)} %broadcast_xor_fusion.1.order, s32[16]{0:T(128)S(1)} %reshape.431.starts, s32[128]{0:T(128)S(1)} %select_n.215.pat, bf16[256,2048]{1,0:T(8,128)(2,1)S(1)} %copy-done.2, bf16[256,2048]{1,0:T(8,128)(2,1)S(1)} %collective-permute-done.2.refs_1_, ...), custom_call_target="tpu_custom_call" | custom-call | flops 1 | bytes 1 | tf_op jit(solution)/shard_map/pair_grad/pallas_call | solution.py:399
  145.9 5.0 %collective-permute-done.25 = f32[8,128]{1,0:T(8,128)S(1)} collective-permute-done((f32[8,128]{1,0:T(8,128)S(1)}, f32[8,128]{1,0:T(8,128)S(1)}, u32[]{:S(2)}, u32[]{:S(2)}) %collective-permute-start.25) | collective-permute-done | bytes 4128 | tf_op jit(solution)/shard_map/ppermute | solution.py:294
  153.5 4.4 %collective-permute-start.30 = (f16[256,128]{1,0:T(8,128)(2,1)}, f16[256,128]{1,0:T(8,128)(2,1)S(1)}, u32[]{:S(2)}, u32[]{:S(2)}) collective-permute-start(f16[256,128]{1,0:T(8,128)(2,1)} %bitcast.104), channel_id=1, source_target_pairs={{0,16},{4,20},{8,24},{12,28},{16,0},{20,4},{24,8},{28,12},{1,17},{... | collective-permute-start | bytes 196616 | tf_op jit(solution)/shard_map/ppermute | solution.py:294
  159.1 10.4 %input_grad.1 = bf16[256,3584]{1,0:T(8,128)(2,1)} custom-call(s32[224]{0:T(256)S(1)} %reshape.434.pat, bf16[256,2048]{1,0:T(8,128)(2,1)S(1)} %copy-done.2, bf16[256,2048]{1,0:T(8,128)(2,1)S(1)} %collective-permute-done.2.refs_1_, bf16[256,2048]{1,0:T(8,128)(2,1)S(1)} %collective-permute-done.refs_2_, bf16[256,2048]{1,0:T(8,128)(2,1)S(1)} %copy-done.5, ...), custom_call_target="tpu_custom_call" | custom-call | flops 1 | bytes 1 | tf_op jit(solution)/shard_map/input_grad/pallas_call | solution.py:484
  184.9 14.8 %collective-permute-done.37 = f16[256,128]{1,0:T(8,128)(2,1)S(1)} collective-permute-done((f16[256,128]{1,0:T(8,128)(2,1)S(1)}, f16[256,128]{1,0:T(8,128)(2,1)S(1)}, u32[]{:S(2)}, u32[]{:S(2)}) %collective-permute-start.37) | collective-permute-done | bytes 65568 | tf_op jit(solution)/shard_map/ppermute | solution.py:294
  206.3 3.4 %collective-permute-start.41 = (f16[256,128]{1,0:T(8,128)(2,1)S(1)}, f16[256,128]{1,0:T(8,128)(2,1)S(1)}, u32[]{:S(2)}, u32[]{:S(2)}) collective-permute-start(f16[256,128]{1,0:T(8,128)(2,1)S(1)} %get-tuple-element.133), channel_id=1, source_target_pairs={{0,24},{4,28},{8,16},{12,20},{16,8},{20,12},{24,0},{28,4},{1,25},{... | collective-permute-start | bytes 196616 | tf_op jit(solution)/shard_map/ppermute | solution.py:294
  212.6 4.3 %collective-permute-done.42 = f16[256,128]{1,0:T(8,128)(2,1)S(1)} collective-permute-done((f16[256,128]{1,0:T(8,128)(2,1)S(1)}, f16[256,128]{1,0:T(8,128)(2,1)S(1)}, u32[]{:S(2)}, u32[]{:S(2)}) %collective-permute-start.42) | collective-permute-done | bytes 65568 | tf_op jit(solution)/shard_map/ppermute | solution.py:294
  222.4 3.9 %collective-permute-done.46 = f32[128,256]{1,0:T(8,128)S(1)} collective-permute-done((f32[128,256]{1,0:T(8,128)S(1)}, f32[128,256]{1,0:T(8,128)S(1)}, u32[]{:S(2)}, u32[]{:S(2)}) %collective-permute-start.46) | collective-permute-done | bytes 131104 | tf_op jit(solution)/shard_map/ppermute | solution.py:294
  226.7 3.4 %collective-permute-done.35 = f32[8,128]{1,0:T(8,128)S(1)} collective-permute-done((f32[8,128]{1,0:T(8,128)S(1)}, f32[8,128]{1,0:T(8,128)S(1)}, u32[]{:S(2)}, u32[]{:S(2)}) %collective-permute-start.35) | collective-permute-done | bytes 4128 | tf_op jit(solution)/shard_map/ppermute | solution.py:294
  237.2 36.2 %collective-permute-done.52 = f32[8,128]{1,0:T(8,128)S(1)} collective-permute-done((f32[8,128]{1,0:T(8,128)S(1)}, f32[8,128]{1,0:T(8,128)S(1)}, u32[]{:S(2)}, u32[]{:S(2)}) %collective-permute-start.52) | collective-permute-done | bytes 4128 | tf_op jit(solution)/shard_map/ppermute | solution.py:294
  275.0 16.0 %mixing.1.refs_1_ = f32[256,256]{1,0:T(8,128)S(1)} custom-call(f32[128,128]{1,0:T(8,128)S(1)} %sketch_gram.1.ss_ref, f32[128,256]{1,0:T(8,128)S(1)} %add.325.cross_ref), custom_call_target="tpu_custom_call" | custom-call | flops 1 | bytes 1 | tf_op jit(solution)/shard_map/mixing/pallas_call | solution.py:548
  295.1 9.5 %direction.1 = f32[448,8,128]{2,1,0:T(8,128)} custom-call(s32[4]{0:T(128)S(1)} %pad_add_fusion.2.starts, s32[32]{0:T(128)S(1)} %select_n.231.pat, f32[448,1024]{1,0:T(8,128)} %add_multiply_fusion.refs_0_, f32[256,256]{1,0:T(8,128)S(1)} %mixing.1.refs_1_, bf16[32,128,256]{2,1,0:T(8,128)(2,1)} %copy-done.1, bf16[32,128,256]{2,1,0:T(8,128)(2,1)} %copy-done, ...), custom_call_target="tpu_custom_call" | custom-call | flops 1 | bytes 1 | tf_op jit(solution)/shard_map/direction/pallas_call | solution.py:573
  (229 shorter events, 108.5 us)
Async XLA Ops:
  0.6 54.1 %collective-permute-start = (bf16[256,2048]{1,0:T(8,128)(2,1)}, bf16[256,2048]{1,0:T(8,128)(2,1)S(1)}, u32[]{:S(2)}, u32[]{:S(2)}) collective-permute-start(bf16[256,2048]{1,0:T(8,128)(2,1)} %refs_0_.7), channel_id=1, source_target_pairs={{0,2},{1,3},{2,0},{3,1},{4,6},{5,7},{6,4},{7,5},{8,10},{9,11},{10,... | collective-permute-start | bytes 3145736 | tf_op jit(solution)/shard_map/ppermute | solution.py:294
  3.6 51.1 %collective-permute-start.1 = (bf16[256,2048]{1,0:T(8,128)(2,1)}, bf16[256,2048]{1,0:T(8,128)(2,1)}, u32[]{:S(2)}, u32[]{:S(2)}) collective-permute-start(bf16[256,2048]{1,0:T(8,128)(2,1)} %refs_0_.7), channel_id=1, source_target_pairs={{0,4},{4,0},{8,12},{12,8},{16,20},{20,16},{24,28},{28,24},{1,5},{5... | collective-permute-start | bytes 3145736 | tf_op jit(solution)/shard_map/ppermute | solution.py:294
  5.2 16.2 %collective-permute-start.2 = (bf16[256,2048]{1,0:T(8,128)(2,1)}, bf16[256,2048]{1,0:T(8,128)(2,1)S(1)}, u32[]{:S(2)}, u32[]{:S(2)}) collective-permute-start(bf16[256,2048]{1,0:T(8,128)(2,1)} %refs_0_.7), channel_id=1, source_target_pairs={{0,1},{1,0},{2,3},{3,2},{4,5},{5,4},{6,7},{7,6},{8,9},{9,8},{10,11... | collective-permute-start | bytes 3145736 | tf_op jit(solution)/shard_map/ppermute | solution.py:294
  22.0 14.1 %collective-permute-start.4 = (f16[448,128]{1,0:T(8,128)(2,1)S(1)}, f16[448,128]{1,0:T(8,128)(2,1)S(1)}, u32[]{:S(2)}, u32[]{:S(2)}) collective-permute-start(f16[448,128]{1,0:T(8,128)(2,1)S(1)} %fusion.7), channel_id=1, source_target_pairs={{0,8},{4,12},{8,0},{12,4},{16,24},{20,28},{24,16},{28,20},{1,9},{5... | collective-permute-start | bytes 344072 | tf_op jit(solution)/shard_map/ppermute | solution.py:294
  54.7 50.7 %collective-permute-start.11 = (bf16[256,2048]{1,0:T(8,128)(2,1)}, bf16[256,2048]{1,0:T(8,128)(2,1)S(1)}, u32[]{:S(2)}, u32[]{:S(2)}) collective-permute-start(bf16[256,2048]{1,0:T(8,128)(2,1)} %collective-permute-done.1.refs_4_), channel_id=1, source_target_pairs={{0,2},{1,3},{2,0},{3,1},{4,6},{5,7},{6,4},{7,5},{8,10},{9,11},{10,... | collective-permute-start | bytes 3145736 | tf_op jit(solution)/shard_map/ppermute | solution.py:294
  55.3 50.1 %collective-permute-start.12 = (bf16[256,2048]{1,0:T(8,128)(2,1)}, bf16[256,2048]{1,0:T(8,128)(2,1)S(1)}, u32[]{:S(2)}, u32[]{:S(2)}) collective-permute-start(bf16[256,2048]{1,0:T(8,128)(2,1)} %collective-permute-done.1.refs_4_), channel_id=1, source_target_pairs={{0,1},{1,0},{2,3},{3,2},{4,5},{5,4},{6,7},{7,6},{8,9},{9,8},{10,11... | collective-permute-start | bytes 3145736 | tf_op jit(solution)/shard_map/ppermute | solution.py:294
  55.3 34.6 %collective-permute-start.10 = (bf16[256,2048]{1,0:T(8,128)(2,1)S(1)}, bf16[256,2048]{1,0:T(8,128)(2,1)S(1)}, u32[]{:S(2)}, u32[]{:S(2)}) collective-permute-start(bf16[256,2048]{1,0:T(8,128)(2,1)S(1)} %collective-permute-done.refs_2_), channel_id=1, source_target_pairs={{0,1},{1,0},{2,3},{3,2},{4,5},{5,4},{6,7},{7,6},{8,9},{9,8},{10,11... | collective-permute-start | bytes 3145736 | tf_op jit(solution)/shard_map/ppermute | solution.py:294
  66.2 39.2 %collective-permute-start.13 = (bf16[4,448,256]{2,1,0:T(8,128)(2,1)S(1)}, bf16[4,448,256]{2,1,0:T(8,128)(2,1)S(1)}, u32[]{:S(2)}, u32[]{:S(2)}) collective-permute-start(bf16[4,448,256]{2,1,0:T(8,128)(2,1)S(1)} %get-tuple-element.73), channel_id=1, source_target_pairs={{0,4},{4,0},{8,12},{12,8},{16,20},{20,16},{24,28},{28,24},{1,5},{5... | collective-permute-start | bytes 2752520 | tf_op jit(solution)/shard_map/ppermute | solution.py:294
  115.0 27.1 %collective-permute-start.26 = (f16[16,128,128]{2,1,0:T(8,128)(2,1)}, f16[16,128,128]{2,1,0:T(8,128)(2,1)}, u32[]{:S(2)}, u32[]{:S(2)}) collective-permute-start(f16[16,128,128]{2,1,0:T(8,128)(2,1)} %get-tuple-element.83), channel_id=1, source_target_pairs={{0,2},{1,3},{2,0},{3,1},{4,6},{5,7},{6,4},{7,5},{8,10},{9,11},{10,... | collective-permute-start | bytes 1572872 | tf_op jit(solution)/shard_map/ppermute | solution.py:294
  127.6 44.4 %collective-permute-start.24 = (f16[448,1024]{1,0:T(8,128)(2,1)}, f16[448,1024]{1,0:T(8,128)(2,1)}, u32[]{:S(2)}, u32[]{:S(2)}) collective-permute-start(f16[448,1024]{1,0:T(8,128)(2,1)} %multiply_convert_fusion.2), channel_id=1, source_target_pairs={{0,8},{4,12},{8,0},{12,4},{16,24},{20,28},{24,16},{28,20},{1,9},{5... | collective-permute-start | bytes 2752520 | tf_op jit(solution)/shard_map/ppermute | solution.py:294
  127.6 23.2 %collective-permute-start.25 = (f32[8,128]{1,0:T(8,128)S(1)}, f32[8,128]{1,0:T(8,128)S(1)}, u32[]{:S(2)}, u32[]{:S(2)}) collective-permute-start(f32[8,128]{1,0:T(8,128)S(1)} %broadcast_in_dim.47), channel_id=1, source_target_pairs={{0,8},{4,12},{8,0},{12,4},{16,24},{20,28},{24,16},{28,20},{1,9},{5... | collective-permute-start | bytes 12296 | tf_op jit(solution)/shard_map/ppermute | solution.py:294
  144.1 25.4 %collective-permute-start.27 = (f16[256,128]{1,0:T(8,128)(2,1)}, f16[256,128]{1,0:T(8,128)(2,1)S(1)}, u32[]{:S(2)}, u32[]{:S(2)}) collective-permute-start(f16[256,128]{1,0:T(8,128)(2,1)} %bitcast.28), channel_id=1, source_target_pairs={{0,4},{4,0},{8,12},{12,8},{16,20},{20,16},{24,28},{28,24},{1,5},{5... | collective-permute-start | bytes 196616 | tf_op jit(solution)/shard_map/ppermute | solution.py:294
  145.2 24.4 %collective-permute-start.28 = (f16[256,128]{1,0:T(8,128)(2,1)}, f16[256,128]{1,0:T(8,128)(2,1)S(1)}, u32[]{:S(2)}, u32[]{:S(2)}) collective-permute-start(f16[256,128]{1,0:T(8,128)(2,1)} %bitcast.29), channel_id=1, source_target_pairs={{0,8},{4,12},{8,0},{12,4},{16,24},{20,28},{24,16},{28,20},{1,9},{5... | collective-permute-start | bytes 196616 | tf_op jit(solution)/shard_map/ppermute | solution.py:294
  152.7 24.1 %collective-permute-start.29 = (f16[256,128]{1,0:T(8,128)(2,1)}, f16[256,128]{1,0:T(8,128)(2,1)S(1)}, u32[]{:S(2)}, u32[]{:S(2)}) collective-permute-start(f16[256,128]{1,0:T(8,128)(2,1)} %bitcast.105), channel_id=1, source_target_pairs={{0,12},{4,8},{8,4},{12,0},{16,28},{20,24},{24,20},{28,16},{1,13},{... | collective-permute-start | bytes 196616 | tf_op jit(solution)/shard_map/ppermute | solution.py:294
  153.5 23.3 %collective-permute-start.30 = (f16[256,128]{1,0:T(8,128)(2,1)}, f16[256,128]{1,0:T(8,128)(2,1)S(1)}, u32[]{:S(2)}, u32[]{:S(2)}) collective-permute-start(f16[256,128]{1,0:T(8,128)(2,1)} %bitcast.104), channel_id=1, source_target_pairs={{0,16},{4,20},{8,24},{12,28},{16,0},{20,4},{24,8},{28,12},{1,17},{... | collective-permute-start | bytes 196616 | tf_op jit(solution)/shard_map/ppermute | solution.py:294
  176.8 58.5 %collective-permute-start.34 = (f16[448,1024]{1,0:T(8,128)(2,1)}, f16[448,1024]{1,0:T(8,128)(2,1)S(1)}, u32[]{:S(2)}, u32[]{:S(2)}) collective-permute-start(f16[448,1024]{1,0:T(8,128)(2,1)} %multiply_convert_fusion), channel_id=1, source_target_pairs={{0,8},{4,12},{8,0},{12,4},{16,24},{20,28},{24,16},{28,20},{1,9},{5... | collective-permute-start | bytes 2752520 | tf_op jit(solution)/shard_map/ppermute | solution.py:294
  176.8 35.7 %collective-permute-start.44 = (f16[8,128,256]{2,1,0:T(8,128)(2,1)S(1)}, f16[8,128,256]{2,1,0:T(8,128)(2,1)S(1)}, u32[]{:S(2)}, u32[]{:S(2)}) collective-permute-start(f16[8,128,256]{2,1,0:T(8,128)(2,1)S(1)} %copy-done.18), channel_id=1, source_target_pairs={{0,2},{1,3},{2,0},{3,1},{4,6},{5,7},{6,4},{7,5},{8,10},{9,11},{10,... | collective-permute-start | bytes 1572872 | tf_op jit(solution)/shard_map/ppermute | solution.py:294
  178.2 38.6 %collective-permute-start.43 = (f16[8,128,256]{2,1,0:T(8,128)(2,1)S(1)}, f16[8,128,256]{2,1,0:T(8,128)(2,1)S(1)}, u32[]{:S(2)}, u32[]{:S(2)}) collective-permute-start(f16[8,128,256]{2,1,0:T(8,128)(2,1)S(1)} %copy-done.18), channel_id=1, source_target_pairs={{0,1},{1,0},{2,3},{3,2},{4,5},{5,4},{6,7},{7,6},{8,9},{9,8},{10,11... | collective-permute-start | bytes 1572872 | tf_op jit(solution)/shard_map/ppermute | solution.py:294
  181.7 18.0 %collective-permute-start.37 = (f16[256,128]{1,0:T(8,128)(2,1)S(1)}, f16[256,128]{1,0:T(8,128)(2,1)S(1)}, u32[]{:S(2)}, u32[]{:S(2)}) collective-permute-start(f16[256,128]{1,0:T(8,128)(2,1)S(1)} %get-tuple-element.133), channel_id=1, source_target_pairs={{0,8},{4,12},{8,0},{12,4},{16,24},{20,28},{24,16},{28,20},{1,9},{5... | collective-permute-start | bytes 196616 | tf_op jit(solution)/shard_map/ppermute | solution.py:294
  184.1 17.4 %collective-permute-start.38 = (f16[256,128]{1,0:T(8,128)(2,1)S(1)}, f16[256,128]{1,0:T(8,128)(2,1)S(1)}, u32[]{:S(2)}, u32[]{:S(2)}) collective-permute-start(f16[256,128]{1,0:T(8,128)(2,1)S(1)} %get-tuple-element.133), channel_id=1, source_target_pairs={{0,12},{4,8},{8,4},{12,0},{16,28},{20,24},{24,20},{28,16},{1,13},{... | collective-permute-start | bytes 196616 | tf_op jit(solution)/shard_map/ppermute | solution.py:294
  231.2 62.3 %collective-permute-start.51 = (f16[448,1024]{1,0:T(8,128)(2,1)}, f16[448,1024]{1,0:T(8,128)(2,1)S(1)}, u32[]{:S(2)}, u32[]{:S(2)}) collective-permute-start(f16[448,1024]{1,0:T(8,128)(2,1)} %multiply_convert_fusion.1), channel_id=1, source_target_pairs={{0,16},{4,20},{8,24},{12,28},{16,0},{20,4},{24,8},{28,12},{1,17},{... | collective-permute-start | bytes 2752520 | tf_op jit(solution)/shard_map/ppermute | solution.py:294
  231.3 42.2 %collective-permute-start.52 = (f32[8,128]{1,0:T(8,128)S(1)}, f32[8,128]{1,0:T(8,128)S(1)}, u32[]{:S(2)}, u32[]{:S(2)}) collective-permute-start(f32[8,128]{1,0:T(8,128)S(1)} %broadcast_in_dim.48), channel_id=1, source_target_pairs={{0,16},{4,20},{8,24},{12,28},{16,0},{20,4},{24,8},{28,12},{1,17},{... | collective-permute-start | bytes 12296 | tf_op jit(solution)/shard_map/ppermute | solution.py:294
  234.2 56.9 %collective-permute-start.49 = (f16[16,128,128]{2,1,0:T(8,128)(2,1)S(1)}, f16[16,128,128]{2,1,0:T(8,128)(2,1)S(1)}, u32[]{:S(2)}, u32[]{:S(2)}) collective-permute-start(f16[16,128,128]{2,1,0:T(8,128)(2,1)S(1)} %bitcast.96), channel_id=1, source_target_pairs={{0,2},{1,3},{2,0},{3,1},{4,6},{5,7},{6,4},{7,5},{8,10},{9,11},{10,... | collective-permute-start | bytes 1572872 | tf_op jit(solution)/shard_map/ppermute | solution.py:294
  274.7 17.2 %collective-permute-start.48 = (f16[16,128,128]{2,1,0:T(8,128)(2,1)S(1)}, f16[16,128,128]{2,1,0:T(8,128)(2,1)S(1)}, u32[]{:S(2)}, u32[]{:S(2)}) collective-permute-start(f16[16,128,128]{2,1,0:T(8,128)(2,1)S(1)} %bitcast.97), channel_id=1, source_target_pairs={{0,1},{1,0},{2,3},{3,2},{4,5},{5,4},{6,7},{7,6},{8,9},{9,8},{10,11... | collective-permute-start | bytes 1572872 | tf_op jit(solution)/shard_map/ppermute | solution.py:294
  (53 other events, 506.4 us)

commit v6 on v4

--- a/solution.py
+++ b/solution.py
@@ -60,15 +60,27 @@
     return held[shard, :, pl.ds(offset, size)]
 
 
-def compress_kernel(n_shards, per_shard, scale, per_step, pat, pat_out, *refs):
+def compress_kernel(n_shards, per_shard, scale, per_step, peak_rows, pat, pat_out, *refs):
     shards = refs[:n_shards]
-    hid_ref, proj_ref, out_ref, held, sems = refs[n_shards:]
+    hid_ref, proj_ref, out_ref, top_ref, held, sems = refs[n_shards:]
     blk = out_ref.shape[1]
 
     @pl.when(pl.program_id(0) == 0)
     def _():
         load_all([(ref, held.at[i]) for i, ref in enumerate(shards)], sems)
         out_ref[...] = jnp.zeros_like(out_ref)
+        top_ref[...] = jnp.zeros_like(top_ref)
+
+    toks = held.shape[1]
+    start = jnp.minimum(pl.program_id(0) * peak_rows, toks - peak_rows)
+    top = top_ref[...]
+    for i in range(n_shards):
+        part = jnp.abs(held[i, pl.ds(pl.multiple_of(start, 16), peak_rows), :])
+        part = jnp.max(part.reshape(peak_rows // 16, 16, -1), axis=0).astype(F32)
+        part = jnp.maximum(part[:8], part[8:])
+        for j in range(0, part.shape[1], 128):
+            top = jnp.maximum(top, part[:, j : j + 128])
+    top_ref[...] = top
 
     for u in range(per_step):
         row = pl.program_id(0) * per_step + u
@@ -93,7 +105,7 @@
             out_ref[c] = total
 
 
-def grad_kernel(n_shards, per_shard, blk, window, n_windows, order, starts, pat, scale, *refs):
+def grad_kernel(n_shards, per_shard, blk, window, n_windows, order, starts, pat, *refs):
     shards = refs[: 2 * n_shards]
     own_ref, got_ref, out_ref, held, sems = refs[2 * n_shards :]
     toks = own_ref.shape[1]
@@ -117,7 +129,7 @@
                 [column_block(held, pat[index * SLOTS + j + i], per_shard, blk) for i in (0, 1)],
                 axis=1,
             )
-            out_ref[rows, j * blk : (j + 2) * blk] = dot(hid, chosen) * scale[0]
+            out_ref[rows, j * blk : (j + 2) * blk] = dot(hid, chosen)
 
 
 def input_grad_kernel(n_shards, per_shard, blk, per_step, pat, *refs):
@@ -287,24 +299,16 @@
     def over_dp(x):
         return lax.all_to_all(jnp.broadcast_to(x[None], (n_dp, *x.shape)), "dp", 0, 0)
 
-    def exponent(x):
-        top = jnp.max(jnp.abs(x)).astype(F32)
-        return jnp.floor(jnp.log2(jnp.maximum(top, 1e-15))) + 1.0
-
     width = sketch.shape[1]
     core_half = swap(cotangent, "mp", 1)
-    exponents = jnp.stack([exponent(hidden), exponent(cotangent)])
-    exponents = jnp.broadcast_to(jnp.repeat(exponents, 8)[:, None], (16, rank))
-    proj_t = projection.reshape(rank, dev_rows).T * PROJ_SCALE
-    early = jnp.concatenate([proj_t, exponents], axis=0).astype(F16)
-    early = over_dp(after(early, core_half))
-    proj_all = early[:, :dev_rows].reshape(mp_rows, rank).astype(F32)
-    peaks = jnp.max(early[:, dev_rows:].astype(F32), axis=0)
     hid_t = hidden.T
     hid_parts = hid_t.reshape(outer, 2, dev_rows, tok_rows)
     hid_own = lax.dynamic_index_in_dim(hid_parts, side, 1, keepdims=False)
     hid_send = lax.dynamic_index_in_dim(hid_parts, 1 - side, 1, keepdims=False)
-    x_half, y_own, core_half, hid_t, hid_own, hid_send, weights_2d, proj_all, peaks = (
+    proj_t = (projection.reshape(rank, dev_rows).T * PROJ_SCALE).astype(F16)
+    proj_all = over_dp(after(proj_t, core_half, hid_send)).reshape(mp_rows, rank).astype(F32)
+    top_hidden = jnp.max(jnp.abs(hidden)).astype(F32)
+    x_half, y_own, core_half, hid_t, hid_own, hid_send, weights_2d, proj_all, top_hidden = (
         lax.optimization_barrier(
             (
                 swap(cotangent, "mp", 2),
@@ -315,7 +319,7 @@
                 hid_send,
                 weights.reshape(mp_rows, slots * blk),
                 proj_all,
-                peaks,
+                top_hidden,
             )
         )
     )
@@ -323,8 +327,6 @@
     y_x = swap(y_own, "mp", 2)
     y_core = swap(y_own, "mp", 1)
     hid_got = swap(hid_send, "dp", 1)
-    for bit in (1, 2):
-        peaks = jnp.maximum(peaks, swap(peaks, "mp", bit))
     sk_own = over_dp(after(sketch.astype(F16), x_half))
     pattern_rel = jnp.bitwise_xor(pattern, mp * per_shard)
 
@@ -337,9 +339,14 @@
         return (near_mp * n_dp + shard // n_mp) * per + rest
 
     pat_all = pattern_rel.reshape(-1)
-    partial_c = pl.pallas_call(
+    partial_c, top = pl.pallas_call(
         functools.partial(
-            compress_kernel, n_mp, per_shard, 1.0 / (PROJ_SCALE * all_tokens), per_step
+            compress_kernel,
+            n_mp,
+            per_shard,
+            1.0 / (PROJ_SCALE * all_tokens),
+            per_step,
+            -(-tok_rows * per_step // block_rows // 16) * 16,
         ),
         grid_spec=pltpu.PrefetchScalarGridSpec(
             num_scalar_prefetch=2,
@@ -349,21 +356,36 @@
                 pl.BlockSpec((per_step * blk, tok_rows), lambda i, a, b: (i, 0)),
                 pl.BlockSpec((per_step * blk, rank), lambda i, a, b: (i, 0)),
             ],
-            out_specs=pl.BlockSpec((col_blocks, rank, blk), lambda i, a, b: (0, 0, 0)),
+            out_specs=[
+                pl.BlockSpec((col_blocks, rank, blk), lambda i, a, b: (0, 0, 0)),
+                pl.BlockSpec((8, 128), lambda i, a, b: (0, 0)),
+            ],
             scratch_shapes=[
                 pltpu.VMEM((n_mp, tok_rows, shard_cols), BF),
                 pltpu.SemaphoreType.DMA((n_mp,)),
             ],
         ),
-        out_shape=jax.ShapeDtypeStruct((col_blocks, rank, blk), F32),
+        out_shape=[
+            jax.ShapeDtypeStruct((col_blocks, rank, blk), F32),
+            jax.ShapeDtypeStruct((8, 128), F32),
+        ],
         compiler_params=params(),
         cost_estimate=SMALL,
         name="compress",
     )(pat_all, place(pattern).reshape(-1), *own, hid_t, proj_all)
 
-    partial_c, y_x, y_core, hid_got, peaks, sk_own = lax.optimization_barrier(
-        (partial_c, y_x, y_core, hid_got, peaks, sk_own)
-    )
+    partial_c, y_x, y_core, hid_got, sk_own, top = lax.optimization_barrier(
+        (partial_c, y_x, y_core, hid_got, sk_own, top)
+    )
+    tops = jnp.concatenate([top, jnp.broadcast_to(top_hidden, top.shape)], axis=0)
+    tops = jnp.maximum(tops, swap(tops, "dp", 1))
+    if n_dp <= 8:
+        others = [swap(tops, "dp", bits) for bits in range(2, n_dp, 2)]
+        tops = functools.reduce(jnp.maximum, others, tops)
+    else:
+        for bit in range(1, n_dp.bit_length() - 1):
+            tops = jnp.maximum(tops, swap(tops, "dp", 1 << bit))
+    bound = jnp.maximum(jnp.max(tops[:8]) * jnp.max(tops[8:]), 1e-30)
     y_group = [y_own, y_core, y_x, swap(y_x, "mp", 1)]
     quarters = partial_c.reshape(n_mp, per_shard, rank, blk)
     got_far = swap(quarters[3].astype(F16), "mp", 1)
@@ -374,7 +396,7 @@
     y_group[3] = y_last
     far_sum = swap(far_half, "mp", 2)
 
-    grad_scale = jnp.exp2(14.0 - peaks[0, 0] - peaks[8, 0] - math.log2(all_tokens))
+    grad_scale = (16384.0 / all_tokens) / bound
     half_rows = outer * dev_rows
     devices = 2 * jnp.arange(outer, dtype=jnp.int32) + side
     window, _, _ = windows_of(dp * dev_rows, dev_rows, blk)
@@ -390,11 +412,11 @@
         out = pl.pallas_call(
             functools.partial(grad_kernel, n_mp, per_shard, blk, window, n_windows),
             grid_spec=pltpu.PrefetchScalarGridSpec(
-                num_scalar_prefetch=4,
+                num_scalar_prefetch=3,
                 grid=(len(blocks),),
                 in_specs=[ANY] * (2 * n_mp)
-                + [pl.BlockSpec((dev_rows, tok_rows), lambda i, o, a, b, c: (o[i], 0))] * 2,
-                out_specs=pl.BlockSpec((dev_rows, slots * blk), lambda i, o, a, b, c: (i, 0)),
+                + [pl.BlockSpec((dev_rows, tok_rows), lambda i, o, a, b: (o[i], 0))] * 2,
+                out_specs=pl.BlockSpec((dev_rows, slots * blk), lambda i, o, a, b: (i, 0)),
                 scratch_shapes=[
                     pltpu.VMEM((n_mp, 2 * tok_rows, shard_cols), BF),
                     pltpu.SemaphoreType.DMA((2 * n_mp,)),
@@ -408,7 +430,6 @@
             order,
             window_starts.reshape(-1),
             pat_half,
-            grad_scale[None],
             *shards,
             hid_own.reshape(half_rows, tok_rows).astype(hid_type),
             hid_got.reshape(half_rows, tok_rows).astype(hid_type),
@@ -419,10 +440,10 @@
     crossing = [i for i in range(outer) if i & 2][::-1]
     staying = [i for i in range(outer) if not i & 2][::-1]
     sums = pair_grad(crossing, own + y_group)
-    sent = {i: sums[i].astype(F16) for i in crossing if i & 1}
+    sent = {i: (sums[i] * grad_scale).astype(F16) for i in crossing if i & 1}
     got = {i: swap(sent[i], "dp", 2) for i in crossing if i & 1}
     sums.update(pair_grad(staying, own[:3] + [after(own[3], *sent.values())] + y_group))
-    sent = {i: sums[i].astype(F16) for i in staying if i & 1}
+    sent = {i: (sums[i] * grad_scale).astype(F16) for i in staying if i & 1}
     got.update({i: swap(sent[i], "dp", 2) for i in staying if i & 1})
     far_sum, near_half, _ = lax.optimization_barrier((far_sum, near_half, list(sent.values())))
 
@@ -430,19 +451,18 @@
     pieces = quarter.astype(F16).reshape(n_dp, per_shard * rank // n_dp, blk)
     pieces = lax.all_to_all(pieces, "dp", 0, 0)
 
+    sums = {i: part * grad_scale for i, part in sums.items() if not i & 1}
     level = 1
     while level < outer:
         if level > 1:
-            got = {}
-            for i in [i for i in sums if i & level]:
-                got[i] = swap(sums[i].astype(F16), "dp", 2 * level)
-        for i in got:
-            sums[i ^ level] = sums[i ^ level] + got[i].astype(F32)
-        sums = {i: part for i, part in sums.items() if not i & level}
+            got = {i: swap(sums[i].astype(F16), "dp", 2 * level) for i in sums if i & level}
+        if 2 * level < outer:
+            for i in got:
+                sums[i ^ level] = sums[i ^ level] + got[i].astype(F32)
+            sums = {i: part for i, part in sums.items() if not i & level}
         if level == 1 and outer > 2:
             sums[2], pieces = lax.optimization_barrier((sums[2].astype(F16), pieces))
         level *= 2
-    grad = sums[0] * (1.0 / (grad_scale * all_tokens))
 
     input_grad = pl.pallas_call(
         functools.partial(input_grad_kernel, n_mp, per_shard, blk, per_step),
@@ -524,6 +544,12 @@
     comp_parts = [split2_xla(part.astype(F32)) for part in comp_parts]
     comp_parts = [part[0] for part in comp_parts] + [part[1] for part in comp_parts]
 
+    kept, mixing, comp_parts, sk_high, sk_low = lax.optimization_barrier(
+        (sums[0], mixing, comp_parts, sk_high, sk_low)
+    )
+    for part in got.values():
+        kept = kept + part.astype(F32)
+    grad = kept * (bound / 16384.0)
     _, my_starts, my_blocks = windows_of(dp * dev_rows, dev_rows, blk)
     my_pat = jnp.take(place(pattern), my_blocks, axis=0).reshape(-1)
     smem = pl.BlockSpec(memory_space=pltpu.SMEM)

time: 242 us -> 237 us (0.979)
  local copies, waits for them, and re-layouts: 26.5 us -> 23 us
    convert_element_type x1 -> x4, other arithmetic: 1.41 us -> 7.87 us  [the longest x1 2.67 us: per_device(): sent = {i: (sums[i] * grad_scale).astype(F16) for i in crossing if i & 1}]
    another operation x4 -> x1, other arithmetic: 8.12 us -> 2.68 us
    ppermute x24 -> x26, waiting for transfers between devices: 56 us -> 51.5 us  [swap(): return lax.ppermute(x, axis, [(i, i ^ bit) for i in range(size)])]
    all_to_all x3, waiting for transfers between devices: 7.72 us -> 11.5 us  [over_dp(): lax.all_to_all(jnp.broadcast_to(x[None], (n_dp, *x.shape)), 'dp', 0, 0)]
    reduce_max x3 -> x2, other arithmetic: 5.09 us -> 3.03 us  [the longest x1 2.35 us: per_device(): top_hidden = jnp.max(jnp.abs(hidden)).astype(F32)]
    unnamed x33 -> x31, local copies, waits for them, and re-layouts: 16.5 us -> 15.8 us
    ppermute x24 -> x26, starting transfers between devices: 19.1 us -> 19.2 us  [swap(): return lax.ppermute(x, axis, [(i, i ^ bit) for i in range(size)])]
  transfers between devices with their start and end apart: 28 -> 30, of which waited for: 12 -> 14; matrix products, arithmetic and copies ran while one was open for 21% -> 19% of each run, Pallas kernels for 26% -> 26%
where the time goes in v6:
time: 237 us; the launch traced here: 236 us
  Pallas kernels  71.5 us (30%)
  waiting for transfers between devices  63 us (27%)
  starting transfers between devices  42.8 us (18%)
  other arithmetic  31.8 us (13%)
  local copies, waits for them, and re-layouts  23 us (10%)
  between operations  3.32 us (1%)
    ppermute x26, waiting for transfers between devices, swap(): return lax.ppermute(x, axis, [(i, i ^ bit) for i in range(size)])  51.5 us
    ppermute x26, starting transfers between devices, swap(): return lax.ppermute(x, axis, [(i, i ^ bit) for i in range(size)])  19.2 us
    all_to_all x3, starting transfers between devices, over_dp(): lax.all_to_all(jnp.broadcast_to(x[None], (n_dp, *x.shape)), 'dp', 0, 0)  18.6 us
    pallas_call x2, Pallas kernels, pair_grad(): pl.pallas_call(functools.partial(grad_kernel, n_mp, per_shard, blk, windo...  16.3 us
    pallas_call x1, Pallas kernels, per_device(): pl.pallas_call(mixing_kernel, in_specs=[VMEM] * 2, out_specs=VMEM, out_sh...  16 us
    pallas_call x1, Pallas kernels, per_device(): pl.pallas_call(functools.partial(compress_kernel, n_mp, per_shard, 1.0 /...  15.9 us
    unnamed x31, local copies, waits for them, and re-layouts  15.8 us
    all_to_all x3, waiting for transfers between devices, over_dp(): lax.all_to_all(jnp.broadcast_to(x[None], (n_dp, *x.shape)), 'dp', 0, 0)  11.5 us
  transfers between devices with their start and end apart: 30, of which 14 were waited for; matrix products, arithmetic and copies ran while one was open for 19% of the time, Pallas kernels for 26%

profile of v6, /device:TPU:0, one launch (start us, length us, event | category | flops | bytes accessed | tf_op | source)
XLA Modules:
  0.0 235.5 jit_solution(5667423889129286887)
XLA Ops:
  1.1 2.9 %copy.21 = bf16[256,3584]{0,1:T(8,128)(2,1)S(1)} copy(bf16[256,3584]{1,0:T(8,128)(2,1)} %param.9) | data formatting | bytes 3670016 | tf_op args[1]
  7.8 6.9 %all-to-all-start = ((f16[8,448,128]{2,1,0:T(8,128)(2,1)}), f16[8,448,128]{2,1,0:T(8,128)(2,1)}, u32[]{:S(2)}, u32[]{:S(2)}) async-start(f16[8,448,128]{2,1,0:T(8,128)(2,1)} %broadcast_in_dim.57), calls=%async_computation | async-start | bytes 1835008 | tf_op jit(solution)/shard_map/all_to_all | solution.py:300
  20.8 7.9 %copy.28 = bf16[448,8,8,128]{3,1,2,0:T(8,128)(2,1)} copy(bf16[448,8,8,128]{3,2,1,0:T(8,128)(2,1)} %bitcast.37) | data formatting | bytes 14680064
  29.4 8.9 %all-to-all-done = f16[8,448,128]{2,1,0:T(8,128)(2,1)} async-done(((f16[8,448,128]{2,1,0:T(8,128)(2,1)}), f16[8,448,128]{2,1,0:T(8,128)(2,1)}, u32[]{:S(2)}, u32[]{:S(2)}) %all-to-all-start) | async-done | bytes 917536 | tf_op jit(solution)/shard_map/all_to_all | solution.py:300
  38.3 2.5 %bitcast_convert_fusion.refs_5_ = f32[3584,128]{1,0:T(8,128)} fusion(f16[8,448,128]{2,1,0:T(8,128)(2,1)} %all-to-all-done), kind=kLoop, calls=%fused_computation.40 | loop fusion | flops 458752 | bytes 2752512 | tf_op jit(solution)/shard_map/convert_element_type | solution.py:309
  40.9 9.2 %collective-permute-done.1.refs_4_ = bf16[256,2048]{1,0:T(8,128)(2,1)} collective-permute-done((bf16[256,2048]{1,0:T(8,128)(2,1)S(1)}, bf16[256,2048]{1,0:T(8,128)(2,1)}, u32[]{:S(2)}, u32[]{:S(2)}) %collective-permute-start.1) | collective-permute-done | bytes 1048608 | tf_op jit(solution)/shard_map/ppermute | solution.py:294
  53.6 5.7 %all-to-all-start.1 = ((f16[8,128,256]{2,1,0:T(8,128)(2,1)}), f16[8,128,256]{2,1,0:T(8,128)(2,1)}, u32[]{:S(2)}, u32[]{:S(2)}) async-start(f16[8,128,256]{2,1,0:T(8,128)(2,1)} %broadcast_in_dim.58), calls=%async_computation.1 | async-start | bytes 1048576 | tf_op jit(solution)/shard_map/all_to_all | solution.py:300
  61.6 15.9 %compress.1 = (f32[64,128,128]{2,1,0:T(8,128)}, f32[8,128]{1,0:T(8,128)S(1)}) custom-call(s32[224]{0:T(256)S(1)} %reshape.424.pat, s32[224]{0:T(256)S(1)} %reshape.425.pat_out, bf16[256,2048]{1,0:T(8,128)(2,1)S(1)} %copy-done.2, bf16[256,2048]{1,0:T(8,128)(2,1)S(1)} %collective-permute-done.2.refs_1_, bf16[256,2048]{1,0:T(8,128)(2,1)S(1)} %collective-permute-done.refs_2_, ...), custom_call_target="tpu_custom_call" | custom-call | flops 1 | bytes 1 | tf_op jit(solution)/shard_map/compress/pallas_call | solution.py:342
  77.6 2.4 %collective-permute-done.6 = bf16[4,448,256]{2,1,0:T(8,128)(2,1)} collective-permute-done((bf16[4,448,256]{2,1,0:T(8,128)(2,1)}, bf16[4,448,256]{2,1,0:T(8,128)(2,1)}, u32[]{:S(2)}, u32[]{:S(2)}) %collective-permute-start.6) | collective-permute-done | bytes 917536 | tf_op jit(solution)/shard_map/ppermute | solution.py:294
  80.7 2.7 %convert.5 = f16[64,128,128]{2,1,0:T(8,128)(2,1)S(1)} convert(f32[64,128,128]{2,1,0:T(8,128)} %get-tuple-element.64) | non-fusion elementwise | flops 1048576 | bytes 6291456 | tf_op jit(solution)/shard_map/convert.2
  87.1 3.3 %collective-permute-start.13 = (f32[16,128]{1,0:T(8,128)S(1)}, f32[16,128]{1,0:T(8,128)S(1)}, u32[]{:S(2)}, u32[]{:S(2)}) collective-permute-start(f32[16,128]{1,0:T(8,128)S(1)} %pad_maximum_fusion.1), channel_id=1, source_target_pairs={{0,24},{4,28},{8,16},{12,20},{16,8},{20,12},{24,0},{28,4},{1,25},{... | collective-permute-start | bytes 24584 | tf_op jit(solution)/shard_map/ppermute | solution.py:294
  101.1 8.2 %pair_grad.2 = f32[896,1024]{1,0:T(8,128)} custom-call(s32[2]{0:T(128)S(1)} %broadcast_xor_fusion.2.order, s32[16]{0:T(128)S(1)} %reshape.421.starts, s32[128]{0:T(128)S(1)} %select_n.215.pat, bf16[256,2048]{1,0:T(8,128)(2,1)S(1)} %copy-done.2, bf16[256,2048]{1,0:T(8,128)(2,1)S(1)} %collective-permute-done.2.refs_1_, ...), custom_call_target="tpu_custom_call" | custom-call | flops 1 | bytes 1 | tf_op jit(solution)/shard_map/pair_grad/pallas_call | solution.py:412
  109.3 2.7 %fusion.3 = f16[448,1024]{1,0:T(8,128)(2,1)} fusion(f32[896,1024]{1,0:T(8,128)} %pair_grad.2, f32[]{:T(128)S(6)} %div.132), kind=kLoop, calls=%fused_computation.12 | loop fusion | flops 917504 | bytes 2752516 | tf_op jit(solution)/shard_map/convert_element_type | solution.py:443
  111.9 8.2 %pair_grad.3 = f32[896,1024]{1,0:T(8,128)} custom-call(s32[2]{0:T(128)S(1)} %broadcast_xor_fusion.1.order, s32[16]{0:T(128)S(1)} %reshape.421.starts, s32[128]{0:T(128)S(1)} %select_n.215.pat, bf16[256,2048]{1,0:T(8,128)(2,1)S(1)} %copy-done.2, bf16[256,2048]{1,0:T(8,128)(2,1)S(1)} %collective-permute-done.2.refs_1_, ...), custom_call_target="tpu_custom_call" | custom-call | flops 1 | bytes 1 | tf_op jit(solution)/shard_map/pair_grad/pallas_call | solution.py:412
  120.1 2.7 %fusion.2 = f16[448,1024]{1,0:T(8,128)(2,1)} fusion(f32[896,1024]{1,0:T(8,128)} %pair_grad.3, f32[]{:T(128)S(6)} %div.132), kind=kLoop, calls=%fused_computation.10 | loop fusion | flops 917504 | bytes 2752516 | tf_op jit(solution)/shard_map/convert_element_type | solution.py:446
  123.7 5.1 %all-to-all-start.2 = ((f16[8,256,128]{2,1,0:T(8,128)(2,1)}), f16[8,256,128]{2,1,0:T(8,128)(2,1)}, u32[]{:S(2)}, u32[]{:S(2)}) async-start(f16[8,256,128]{2,1,0:T(8,128)(2,1)} %bitcast.38), calls=%async_computation.2 | async-start | bytes 1048576 | tf_op jit(solution)/shard_map/all_to_all | solution.py:452
  130.4 11.0 %input_grad.1 = bf16[256,3584]{1,0:T(8,128)(2,1)} custom-call(s32[224]{0:T(256)S(1)} %reshape.424.pat, bf16[256,2048]{1,0:T(8,128)(2,1)S(1)} %copy-done.2, bf16[256,2048]{1,0:T(8,128)(2,1)S(1)} %collective-permute-done.2.refs_1_, bf16[256,2048]{1,0:T(8,128)(2,1)S(1)} %collective-permute-done.refs_2_, bf16[256,2048]{1,0:T(8,128)(2,1)} %collective-permute-done.3.refs_3_, ...), custom_call_target="tpu_custom_call" | custom-call | flops 1 | bytes 1 | tf_op jit(solution)/shard_map/input_grad/pallas_call | solution.py:467
  141.4 2.5 %fusion.5 = f16[448,1024]{1,0:T(8,128)(2,1)} fusion(f32[896,1024]{1,0:T(8,128)S(1)} %copy-done.6, f16[448,1024]{1,0:T(8,128)(2,1)} %collective-permute-done.14, f32[]{:T(128)S(6)} %div.132), kind=kLoop, calls=%fused_computation.15 | loop fusion | flops 1835008 | bytes 3670020 | tf_op jit(solution)/shard_map/convert_element_type | solution.py:464
  145.9 6.0 %all-to-all-start.3 = ((f16[8,256,128]{2,1,0:T(8,128)(2,1)}), f16[8,256,128]{2,1,0:T(8,128)(2,1)}, u32[]{:S(2)}, u32[]{:S(2)}) async-start(f16[8,256,128]{2,1,0:T(8,128)(2,1)} %broadcast_in_dim.62), calls=%async_computation.3 | async-start | bytes 1048576 | tf_op jit(solution)/shard_map/all_to_all | solution.py:300
  167.4 4.3 %collective-permute-done.20 = f32[128,256]{1,0:T(8,128)S(1)} collective-permute-done((f32[128,256]{1,0:T(8,128)S(1)}, f32[128,256]{1,0:T(8,128)S(1)}, u32[]{:S(2)}, u32[]{:S(2)}) %collective-permute-start.20) | collective-permute-done | bytes 131104 | tf_op jit(solution)/shard_map/ppermute | solution.py:294
  173.9 6.2 %collective-permute-done.16 = f16[448,1024]{1,0:T(8,128)(2,1)} collective-permute-done((f16[448,1024]{1,0:T(8,128)(2,1)}, f16[448,1024]{1,0:T(8,128)(2,1)}, u32[]{:S(2)}, u32[]{:S(2)}) %collective-permute-start.16) | collective-permute-done | bytes 917536 | tf_op jit(solution)/shard_map/ppermute | solution.py:294
  185.5 16.0 %mixing.1.refs_1_ = f32[256,256]{1,0:T(8,128)S(1)} custom-call(f32[128,128]{1,0:T(8,128)S(1)} %sketch_gram.1.ss_ref, f32[128,256]{1,0:T(8,128)S(1)} %add.294.cross_ref), custom_call_target="tpu_custom_call" | custom-call | flops 1 | bytes 1 | tf_op jit(solution)/shard_map/mixing/pallas_call | solution.py:531
  203.9 20.2 %collective-permute-done.25 = f16[448,1024]{1,0:T(8,128)(2,1)S(1)} collective-permute-done((f16[448,1024]{1,0:T(8,128)(2,1)S(1)}, f16[448,1024]{1,0:T(8,128)(2,1)S(1)}, u32[]{:S(2)}, u32[]{:S(2)}) %collective-permute-start.25) | collective-permute-done | bytes 917536 | tf_op jit(solution)/shard_map/ppermute | solution.py:294
  225.8 9.5 %direction.1 = f32[448,8,128]{2,1,0:T(8,128)} custom-call(s32[4]{0:T(128)S(1)} %pad_add_fusion.2.starts, s32[32]{0:T(128)S(1)} %select_n.231.pat, f32[448,1024]{1,0:T(8,128)} %add_multiply_fusion.refs_0_, f32[256,256]{1,0:T(8,128)S(1)} %mixing.1.refs_1_, bf16[32,128,256]{2,1,0:T(8,128)(2,1)} %copy-done.1, bf16[32,128,256]{2,1,0:T(8,128)(2,1)} %copy-done, ...), custom_call_target="tpu_custom_call" | custom-call | flops 1 | bytes 1 | tf_op jit(solution)/shard_map/direction/pallas_call | solution.py:556
  (139 shorter events, 61.6 us)
Async XLA Ops:
  0.6 6.1 %collective-permute-start.2 = (bf16[256,2048]{1,0:T(8,128)(2,1)}, bf16[256,2048]{1,0:T(8,128)(2,1)S(1)}, u32[]{:S(2)}, u32[]{:S(2)}) collective-permute-start(bf16[256,2048]{1,0:T(8,128)(2,1)} %refs_0_.7), channel_id=1, source_target_pairs={{0,1},{1,0},{2,3},{3,2},{4,5},{5,4},{6,7},{7,6},{8,9},{9,8},{10,11... | collective-permute-start | bytes 3145736 | tf_op jit(solution)/shard_map/ppermute | solution.py:294
  7.8 30.6 %all-to-all-start = ((f16[8,448,128]{2,1,0:T(8,128)(2,1)}), f16[8,448,128]{2,1,0:T(8,128)(2,1)}, u32[]{:S(2)}, u32[]{:S(2)}) async-start(f16[8,448,128]{2,1,0:T(8,128)(2,1)} %broadcast_in_dim.57), calls=%async_computation | async-start | bytes 1835008 | tf_op jit(solution)/shard_map/all_to_all | solution.py:300
  14.6 26.2 %collective-permute-start = (bf16[256,2048]{1,0:T(8,128)(2,1)S(1)}, bf16[256,2048]{1,0:T(8,128)(2,1)S(1)}, u32[]{:S(2)}, u32[]{:S(2)}) collective-permute-start(bf16[256,2048]{1,0:T(8,128)(2,1)S(1)} %copy-done.2), channel_id=1, source_target_pairs={{0,2},{1,3},{2,0},{3,1},{4,6},{5,7},{6,4},{7,5},{8,10},{9,11},{10,... | collective-permute-start | bytes 3145736 | tf_op jit(solution)/shard_map/ppermute | solution.py:294
  16.2 33.8 %collective-permute-start.1 = (bf16[256,2048]{1,0:T(8,128)(2,1)S(1)}, bf16[256,2048]{1,0:T(8,128)(2,1)}, u32[]{:S(2)}, u32[]{:S(2)}) collective-permute-start(bf16[256,2048]{1,0:T(8,128)(2,1)S(1)} %copy-done.2), channel_id=1, source_target_pairs={{0,4},{4,0},{8,12},{12,8},{16,20},{20,16},{24,28},{28,24},{1,5},{5... | collective-permute-start | bytes 3145736 | tf_op jit(solution)/shard_map/ppermute | solution.py:294
  50.0 30.6 %collective-permute-start.4 = (bf16[256,2048]{1,0:T(8,128)(2,1)}, bf16[256,2048]{1,0:T(8,128)(2,1)}, u32[]{:S(2)}, u32[]{:S(2)}) collective-permute-start(bf16[256,2048]{1,0:T(8,128)(2,1)} %collective-permute-done.1.refs_4_), channel_id=1, source_target_pairs={{0,2},{1,3},{2,0},{3,1},{4,6},{5,7},{6,4},{7,5},{8,10},{9,11},{10,... | collective-permute-start | bytes 3145736 | tf_op jit(solution)/shard_map/ppermute | solution.py:294
  51.5 29.1 %collective-permute-start.5 = (bf16[256,2048]{1,0:T(8,128)(2,1)}, bf16[256,2048]{1,0:T(8,128)(2,1)}, u32[]{:S(2)}, u32[]{:S(2)}) collective-permute-start(bf16[256,2048]{1,0:T(8,128)(2,1)} %collective-permute-done.1.refs_4_), channel_id=1, source_target_pairs={{0,1},{1,0},{2,3},{3,2},{4,5},{5,4},{6,7},{7,6},{8,9},{9,8},{10,11... | collective-permute-start | bytes 3145736 | tf_op jit(solution)/shard_map/ppermute | solution.py:294
  51.5 8.6 %collective-permute-start.3 = (bf16[256,2048]{1,0:T(8,128)(2,1)S(1)}, bf16[256,2048]{1,0:T(8,128)(2,1)}, u32[]{:S(2)}, u32[]{:S(2)}) collective-permute-start(bf16[256,2048]{1,0:T(8,128)(2,1)S(1)} %collective-permute-done.refs_2_), channel_id=1, source_target_pairs={{0,1},{1,0},{2,3},{3,2},{4,5},{5,4},{6,7},{7,6},{8,9},{9,8},{10,11... | collective-permute-start | bytes 3145736 | tf_op jit(solution)/shard_map/ppermute | solution.py:294
  52.4 27.6 %collective-permute-start.6 = (bf16[4,448,256]{2,1,0:T(8,128)(2,1)}, bf16[4,448,256]{2,1,0:T(8,128)(2,1)}, u32[]{:S(2)}, u32[]{:S(2)}) collective-permute-start(bf16[4,448,256]{2,1,0:T(8,128)(2,1)} %get-tuple-element.59), channel_id=1, source_target_pairs={{0,4},{4,0},{8,12},{12,8},{16,20},{20,16},{24,28},{28,24},{1,5},{5... | collective-permute-start | bytes 2752520 | tf_op jit(solution)/shard_map/ppermute | solution.py:294
  53.6 27.1 %all-to-all-start.1 = ((f16[8,128,256]{2,1,0:T(8,128)(2,1)}), f16[8,128,256]{2,1,0:T(8,128)(2,1)}, u32[]{:S(2)}, u32[]{:S(2)}) async-start(f16[8,128,256]{2,1,0:T(8,128)(2,1)} %broadcast_in_dim.58), calls=%async_computation.1 | async-start | bytes 1048576 | tf_op jit(solution)/shard_map/all_to_all | solution.py:300
  84.9 13.3 %collective-permute-start.8 = (f16[16,128,128]{2,1,0:T(8,128)(2,1)}, f16[16,128,128]{2,1,0:T(8,128)(2,1)}, u32[]{:S(2)}, u32[]{:S(2)}) collective-permute-start(f16[16,128,128]{2,1,0:T(8,128)(2,1)} %get-tuple-element.110), channel_id=1, source_target_pairs={{0,1},{1,0},{2,3},{3,2},{4,5},{5,4},{6,7},{7,6},{8,9},{9,8},{10,11... | collective-permute-start | bytes 1572872 | tf_op jit(solution)/shard_map/ppermute | solution.py:294
  84.9 13.3 %collective-permute-start.7 = (f16[16,128,128]{2,1,0:T(8,128)(2,1)}, f16[16,128,128]{2,1,0:T(8,128)(2,1)}, u32[]{:S(2)}, u32[]{:S(2)}) collective-permute-start(f16[16,128,128]{2,1,0:T(8,128)(2,1)} %get-tuple-element.111), channel_id=1, source_target_pairs={{0,1},{1,0},{2,3},{3,2},{4,5},{5,4},{6,7},{7,6},{8,9},{9,8},{10,11... | collective-permute-start | bytes 1572872 | tf_op jit(solution)/shard_map/ppermute | solution.py:294
  85.5 15.0 %collective-permute-start.9 = (bf16[256,2048]{1,0:T(8,128)(2,1)}, bf16[256,2048]{1,0:T(8,128)(2,1)}, u32[]{:S(2)}, u32[]{:S(2)}) collective-permute-start(bf16[256,2048]{1,0:T(8,128)(2,1)} %collective-permute-done.4.refs_6_), channel_id=1, source_target_pairs={{0,1},{1,0},{2,3},{3,2},{4,5},{5,4},{6,7},{7,6},{8,9},{9,8},{10,11... | collective-permute-start | bytes 3145736 | tf_op jit(solution)/shard_map/ppermute | solution.py:294
  87.1 5.4 %collective-permute-start.13 = (f32[16,128]{1,0:T(8,128)S(1)}, f32[16,128]{1,0:T(8,128)S(1)}, u32[]{:S(2)}, u32[]{:S(2)}) collective-permute-start(f32[16,128]{1,0:T(8,128)S(1)} %pad_maximum_fusion.1), channel_id=1, source_target_pairs={{0,24},{4,28},{8,16},{12,20},{16,8},{20,12},{24,0},{28,4},{1,25},{... | collective-permute-start | bytes 24584 | tf_op jit(solution)/shard_map/ppermute | solution.py:294
  100.5 22.3 %collective-permute-start.15 = (f16[16,128,128]{2,1,0:T(8,128)(2,1)S(1)}, f16[16,128,128]{2,1,0:T(8,128)(2,1)S(1)}, u32[]{:S(2)}, u32[]{:S(2)}) collective-permute-start(f16[16,128,128]{2,1,0:T(8,128)(2,1)S(1)} %get-tuple-element.70), channel_id=1, source_target_pairs={{0,2},{1,3},{2,0},{3,1},{4,6},{5,7},{6,4},{7,5},{8,10},{9,11},{10,... | collective-permute-start | bytes 1572872 | tf_op jit(solution)/shard_map/ppermute | solution.py:294
  111.9 29.5 %collective-permute-start.14 = (f16[448,1024]{1,0:T(8,128)(2,1)}, f16[448,1024]{1,0:T(8,128)(2,1)}, u32[]{:S(2)}, u32[]{:S(2)}) collective-permute-start(f16[448,1024]{1,0:T(8,128)(2,1)} %fusion.3), channel_id=1, source_target_pairs={{0,8},{4,12},{8,0},{12,4},{16,24},{20,28},{24,16},{28,20},{1,9},{5... | collective-permute-start | bytes 2752520 | tf_op jit(solution)/shard_map/ppermute | solution.py:294
  123.7 20.2 %all-to-all-start.2 = ((f16[8,256,128]{2,1,0:T(8,128)(2,1)}), f16[8,256,128]{2,1,0:T(8,128)(2,1)}, u32[]{:S(2)}, u32[]{:S(2)}) async-start(f16[8,256,128]{2,1,0:T(8,128)(2,1)} %bitcast.38), calls=%async_computation.2 | async-start | bytes 1048576 | tf_op jit(solution)/shard_map/all_to_all | solution.py:452
  128.8 23.2 %collective-permute-start.18 = (f16[8,128,256]{2,1,0:T(8,128)(2,1)}, f16[8,128,256]{2,1,0:T(8,128)(2,1)}, u32[]{:S(2)}, u32[]{:S(2)}) collective-permute-start(f16[8,128,256]{2,1,0:T(8,128)(2,1)} %all-to-all-done.1), channel_id=1, source_target_pairs={{0,2},{1,3},{2,0},{3,1},{4,6},{5,7},{6,4},{7,5},{8,10},{9,11},{10,... | collective-permute-start | bytes 1572872 | tf_op jit(solution)/shard_map/ppermute | solution.py:294
  145.9 18.6 %all-to-all-start.3 = ((f16[8,256,128]{2,1,0:T(8,128)(2,1)}), f16[8,256,128]{2,1,0:T(8,128)(2,1)}, u32[]{:S(2)}, u32[]{:S(2)}) async-start(f16[8,256,128]{2,1,0:T(8,128)(2,1)} %broadcast_in_dim.62), calls=%async_computation.3 | async-start | bytes 1048576 | tf_op jit(solution)/shard_map/all_to_all | solution.py:300
  152.0 5.3 %collective-permute-start.19 = (f16[8,128,256]{2,1,0:T(8,128)(2,1)}, f16[8,128,256]{2,1,0:T(8,128)(2,1)}, u32[]{:S(2)}, u32[]{:S(2)}) collective-permute-start(f16[8,128,256]{2,1,0:T(8,128)(2,1)} %collective-permute-done.18), channel_id=1, source_target_pairs={{0,1},{1,0},{2,3},{3,2},{4,5},{5,4},{6,7},{7,6},{8,9},{9,8},{10,11... | collective-permute-start | bytes 1572872 | tf_op jit(solution)/shard_map/ppermute | solution.py:294
  153.2 26.9 %collective-permute-start.16 = (f16[448,1024]{1,0:T(8,128)(2,1)}, f16[448,1024]{1,0:T(8,128)(2,1)}, u32[]{:S(2)}, u32[]{:S(2)}) collective-permute-start(f16[448,1024]{1,0:T(8,128)(2,1)} %fusion.2), channel_id=1, source_target_pairs={{0,8},{4,12},{8,0},{12,4},{16,24},{20,28},{24,16},{28,20},{1,9},{5... | collective-permute-start | bytes 2752520 | tf_op jit(solution)/shard_map/ppermute | solution.py:294
  166.8 5.0 %collective-permute-start.20 = (f32[128,256]{1,0:T(8,128)S(1)}, f32[128,256]{1,0:T(8,128)S(1)}, u32[]{:S(2)}, u32[]{:S(2)}) collective-permute-start(f32[128,256]{1,0:T(8,128)S(1)} %cross_gram.1), channel_id=1, source_target_pairs={{0,2},{1,3},{2,0},{3,1},{4,6},{5,7},{6,4},{7,5},{8,10},{9,11},{10,... | collective-permute-start | bytes 393224 | tf_op jit(solution)/shard_map/ppermute | solution.py:294
  173.3 28.3 %collective-permute-start.23 = (f16[16,128,128]{2,1,0:T(8,128)(2,1)}, f16[16,128,128]{2,1,0:T(8,128)(2,1)S(1)}, u32[]{:S(2)}, u32[]{:S(2)}) collective-permute-start(f16[16,128,128]{2,1,0:T(8,128)(2,1)} %bitcast.17), channel_id=1, source_target_pairs={{0,2},{1,3},{2,0},{3,1},{4,6},{5,7},{6,4},{7,5},{8,10},{9,11},{10,... | collective-permute-start | bytes 1572872 | tf_op jit(solution)/shard_map/ppermute | solution.py:294
  182.2 41.9 %collective-permute-start.25 = (f16[448,1024]{1,0:T(8,128)(2,1)S(1)}, f16[448,1024]{1,0:T(8,128)(2,1)S(1)}, u32[]{:S(2)}, u32[]{:S(2)}) collective-permute-start(f16[448,1024]{1,0:T(8,128)(2,1)S(1)} %copy-done.7), channel_id=1, source_target_pairs={{0,16},{4,20},{8,24},{12,28},{16,0},{20,4},{24,8},{28,12},{1,17},{... | collective-permute-start | bytes 2752520 | tf_op jit(solution)/shard_map/ppermute | solution.py:294
  184.2 18.2 %collective-permute-start.22 = (f16[16,128,128]{2,1,0:T(8,128)(2,1)}, f16[16,128,128]{2,1,0:T(8,128)(2,1)S(1)}, u32[]{:S(2)}, u32[]{:S(2)}) collective-permute-start(f16[16,128,128]{2,1,0:T(8,128)(2,1)} %bitcast.17), channel_id=1, source_target_pairs={{0,1},{1,0},{2,3},{3,2},{4,5},{5,4},{6,7},{7,6},{8,9},{9,8},{10,11... | collective-permute-start | bytes 1572872 | tf_op jit(solution)/shard_map/ppermute | solution.py:294
  (20 other events, 134.3 us)

commit v7 on v4

--- a/solution.py
+++ b/solution.py
@@ -70,32 +70,34 @@
         load_all([(ref, held.at[i]) for i, ref in enumerate(shards)], sems)
         out_ref[...] = jnp.zeros_like(out_ref)
 
+    first = pl.program_id(0) * per_step
+    lefts = []
     for u in range(per_step):
-        row = pl.program_id(0) * per_step + u
         span = slice(u * blk, (u + 1) * blk)
         hid = hid_ref[span, :]
         ph, pl_ = split2(proj_ref[span, :].T)
-        left = jnp.concatenate(split2((dot(ph, hid) + dot(pl_, hid)) * scale), axis=0)
-        cols = [pat[row * SLOTS + j] for j in range(SLOTS)]
-        parts = []
+        lefts.append(((dot(ph, hid) + dot(pl_, hid)) * scale).astype(BF))
+    parts = []
+    for u in range(per_step):
+        cols = [pat[(first + u) * SLOTS + j] for j in range(SLOTS)]
         for j in range(0, SLOTS, 2):
             chosen = jnp.concatenate(
                 [column_block(held, c, per_shard, blk) for c in cols[j : j + 2]], axis=1
             )
-            part = dot(left, chosen)
-            parts.append(part[:blk] + part[blk:])
-        outs = [pat_out[row * SLOTS + j] for j in range(SLOTS)]
+            parts.append(dot(lefts[u], chosen))
+    for u in range(per_step):
+        outs = [pat_out[(first + u) * SLOTS + j] for j in range(SLOTS)]
         sums = [
-            out_ref[c] + parts[j // 2][:, (j % 2) * blk : (j % 2 + 1) * blk]
+            out_ref[c] + parts[(u * SLOTS + j) // 2][:, (j % 2) * blk : (j % 2 + 1) * blk]
             for j, c in enumerate(outs)
         ]
         for c, total in zip(outs, sums):
             out_ref[c] = total
 
 
-def grad_kernel(n_shards, per_shard, blk, window, n_windows, order, starts, pat, scale, *refs):
+def grad_kernel(n_shards, per_shard, blk, window, n_windows, order, starts, pat, *refs):
     shards = refs[: 2 * n_shards]
-    own_ref, got_ref, out_ref, held, sems = refs[2 * n_shards :]
+    own_ref, got_ref, out_ref, top_ref, held, sems = refs[2 * n_shards :]
     toks = own_ref.shape[1]
 
     @pl.when(pl.program_id(0) == 0)
@@ -107,7 +109,9 @@
             ],
             sems,
         )
-
+        top_ref[...] = jnp.zeros_like(top_ref)
+
+    top = top_ref[...]
     for w in range(n_windows):
         index = order[pl.program_id(0)] * n_windows + w
         rows = pl.ds(pl.multiple_of(starts[index], window // 2 if window >= 32 else 8), window)
@@ -117,7 +121,12 @@
                 [column_block(held, pat[index * SLOTS + j + i], per_shard, blk) for i in (0, 1)],
                 axis=1,
             )
-            out_ref[rows, j * blk : (j + 2) * blk] = dot(hid, chosen) * scale[0]
+            part = dot(hid, chosen)
+            out_ref[rows, j * blk : (j + 2) * blk] = part
+            size = jnp.abs(part)
+            for i in range(0, window, 8):
+                top = jnp.maximum(top, size[i : i + 8])
+    top_ref[...] = top
 
 
 def input_grad_kernel(n_shards, per_shard, blk, per_step, pat, *refs):
@@ -287,35 +296,27 @@
     def over_dp(x):
         return lax.all_to_all(jnp.broadcast_to(x[None], (n_dp, *x.shape)), "dp", 0, 0)
 
-    def exponent(x):
-        top = jnp.max(jnp.abs(x)).astype(F32)
-        return jnp.floor(jnp.log2(jnp.maximum(top, 1e-15))) + 1.0
-
     width = sketch.shape[1]
     core_half = swap(cotangent, "mp", 1)
-    exponents = jnp.stack([exponent(hidden), exponent(cotangent)])
-    exponents = jnp.broadcast_to(jnp.repeat(exponents, 8)[:, None], (16, rank))
-    proj_t = projection.reshape(rank, dev_rows).T * PROJ_SCALE
-    early = jnp.concatenate([proj_t, exponents], axis=0).astype(F16)
-    early = over_dp(after(early, core_half))
-    proj_all = early[:, :dev_rows].reshape(mp_rows, rank).astype(F32)
-    peaks = jnp.max(early[:, dev_rows:].astype(F32), axis=0)
     hid_t = hidden.T
     hid_parts = hid_t.reshape(outer, 2, dev_rows, tok_rows)
     hid_own = lax.dynamic_index_in_dim(hid_parts, side, 1, keepdims=False)
     hid_send = lax.dynamic_index_in_dim(hid_parts, 1 - side, 1, keepdims=False)
-    x_half, y_own, core_half, hid_t, hid_own, hid_send, weights_2d, proj_all, peaks = (
+    proj_t = (projection.reshape(rank, dev_rows).T * PROJ_SCALE).astype(F16)
+    x_part, y_part = swap(cotangent, "mp", 2), swap(cotangent, "dp", 1)
+    weights_2d = weights.reshape(mp_rows, slots * blk)
+    proj_all = over_dp(proj_t).reshape(mp_rows, rank).astype(F32)
+    x_half, y_own, core_half, hid_t, hid_own, hid_send, weights_2d, proj_all = (
         lax.optimization_barrier(
             (
-                swap(cotangent, "mp", 2),
-                swap(cotangent, "dp", 1),
+                x_part,
+                y_part,
                 core_half,
                 hid_t,
                 hid_own,
                 hid_send,
-                weights.reshape(mp_rows, slots * blk),
+                weights_2d,
                 proj_all,
-                peaks,
             )
         )
     )
@@ -323,9 +324,6 @@
     y_x = swap(y_own, "mp", 2)
     y_core = swap(y_own, "mp", 1)
     hid_got = swap(hid_send, "dp", 1)
-    for bit in (1, 2):
-        peaks = jnp.maximum(peaks, swap(peaks, "mp", bit))
-    sk_own = over_dp(after(sketch.astype(F16), x_half))
     pattern_rel = jnp.bitwise_xor(pattern, mp * per_shard)
 
     def place(block):
@@ -339,7 +337,11 @@
     pat_all = pattern_rel.reshape(-1)
     partial_c = pl.pallas_call(
         functools.partial(
-            compress_kernel, n_mp, per_shard, 1.0 / (PROJ_SCALE * all_tokens), per_step
+            compress_kernel,
+            n_mp,
+            per_shard,
+            1.0 / (PROJ_SCALE * all_tokens),
+            per_step,
         ),
         grid_spec=pltpu.PrefetchScalarGridSpec(
             num_scalar_prefetch=2,
@@ -361,20 +363,13 @@
         name="compress",
     )(pat_all, place(pattern).reshape(-1), *own, hid_t, proj_all)
 
-    partial_c, y_x, y_core, hid_got, peaks, sk_own = lax.optimization_barrier(
-        (partial_c, y_x, y_core, hid_got, peaks, sk_own)
-    )
+    partial_c, y_x, y_core, hid_got = lax.optimization_barrier((partial_c, y_x, y_core, hid_got))
     y_group = [y_own, y_core, y_x, swap(y_x, "mp", 1)]
     quarters = partial_c.reshape(n_mp, per_shard, rank, blk)
-    got_far = swap(quarters[3].astype(F16), "mp", 1)
-    got_near = swap(quarters[1].astype(F16), "mp", 1)
-    far_half = (quarters[2] + got_far.astype(F32)).astype(F16)
-    near_half = quarters[0] + got_near.astype(F32)
-    far_half, near_half, y_last = lax.optimization_barrier((far_half, near_half, y_group[3]))
-    y_group[3] = y_last
-    far_sum = swap(far_half, "mp", 2)
-
-    grad_scale = jnp.exp2(14.0 - peaks[0, 0] - peaks[8, 0] - math.log2(all_tokens))
+    to_far, to_near = quarters[3].astype(F16), quarters[1].astype(F16)
+    got_far, got_near = swap(to_far, "mp", 1), swap(to_near, "mp", 1)
+    y_group[3] = after(y_group[3], to_far, to_near)
+
     half_rows = outer * dev_rows
     devices = 2 * jnp.arange(outer, dtype=jnp.int32) + side
     window, _, _ = windows_of(dp * dev_rows, dev_rows, blk)
@@ -387,20 +382,26 @@
 
     def pair_grad(blocks, shards):
         order = jnp.bitwise_xor(jnp.asarray(blocks, jnp.int32), dp // 2)
-        out = pl.pallas_call(
+        out, top = pl.pallas_call(
             functools.partial(grad_kernel, n_mp, per_shard, blk, window, n_windows),
             grid_spec=pltpu.PrefetchScalarGridSpec(
-                num_scalar_prefetch=4,
+                num_scalar_prefetch=3,
                 grid=(len(blocks),),
                 in_specs=[ANY] * (2 * n_mp)
-                + [pl.BlockSpec((dev_rows, tok_rows), lambda i, o, a, b, c: (o[i], 0))] * 2,
-                out_specs=pl.BlockSpec((dev_rows, slots * blk), lambda i, o, a, b, c: (i, 0)),
+                + [pl.BlockSpec((dev_rows, tok_rows), lambda i, o, a, b: (o[i], 0))] * 2,
+                out_specs=[
+                    pl.BlockSpec((dev_rows, slots * blk), lambda i, o, a, b: (i, 0)),
+                    pl.BlockSpec((8, 2 * blk), lambda i, o, a, b: (0, 0)),
+                ],
                 scratch_shapes=[
                     pltpu.VMEM((n_mp, 2 * tok_rows, shard_cols), BF),
                     pltpu.SemaphoreType.DMA((2 * n_mp,)),
                 ],
             ),
-            out_shape=jax.ShapeDtypeStruct((len(blocks) * dev_rows, slots * blk), F32),
+            out_shape=[
+                jax.ShapeDtypeStruct((len(blocks) * dev_rows, slots * blk), F32),
+                jax.ShapeDtypeStruct((8, 2 * blk), F32),
+            ],
             compiler_params=params(),
             cost_estimate=SMALL,
             name="pair_grad",
@@ -408,21 +409,42 @@
             order,
             window_starts.reshape(-1),
             pat_half,
-            grad_scale[None],
             *shards,
             hid_own.reshape(half_rows, tok_rows).astype(hid_type),
             hid_got.reshape(half_rows, tok_rows).astype(hid_type),
         )
         out = out.reshape(len(blocks), dev_rows, slots * blk)
-        return {block: out[i] for i, block in enumerate(blocks)}
+        top = jnp.max(top)
+        return {block: (out[i], top) for i, block in enumerate(blocks)}
+
+    def pack(part):
+        value, top = part
+        exponent = 13.0 - jnp.floor(jnp.log2(jnp.maximum(top, 1e-30)))
+        below = jnp.broadcast_to(exponent, (16, value.shape[1]))
+        return jnp.concatenate([value * jnp.exp2(exponent), below], axis=0).astype(F16)
+
+    def unpack(message, first=0):
+        exponent = lax.dynamic_slice(message, (dev_rows + first, 0), (8, 128))[0, 0].astype(F32)
+        value = message[:dev_rows].astype(F32) * jnp.exp2(-exponent)
+        return value, jnp.exp2(14.0 - exponent)
+
+    def add(part, message, first=0):
+        value, top = unpack(message, first)
+        return part[0] + value, part[1] + top
 
     crossing = [i for i in range(outer) if i & 2][::-1]
     staying = [i for i in range(outer) if not i & 2][::-1]
     sums = pair_grad(crossing, own + y_group)
-    sent = {i: sums[i].astype(F16) for i in crossing if i & 1}
-    got = {i: swap(sent[i], "dp", 2) for i in crossing if i & 1}
-    sums.update(pair_grad(staying, own[:3] + [after(own[3], *sent.values())] + y_group))
-    sent = {i: sums[i].astype(F16) for i in staying if i & 1}
+    sent = {i: pack(sums[i]) for i in crossing if i & 1}
+    got_far, got_near, *before = lax.optimization_barrier((got_far, got_near, *sent.values()))
+    sent = dict(zip(sent, before))
+    got = {i: swap(sent[i], "dp", 2) for i in sent}
+    far_half = (quarters[2] + got_far.astype(F32)).astype(F16)
+    near_half = quarters[0] + got_near.astype(F32)
+    far_half, near_half, y_group[3] = lax.optimization_barrier((far_half, near_half, y_group[3]))
+    far_sum = swap(far_half, "mp", 2)
+    sums.update(pair_grad(staying, own + y_group))
+    sent = {i: pack(sums[i]) for i in staying if i & 1}
     got.update({i: swap(sent[i], "dp", 2) for i in staying if i & 1})
     far_sum, near_half, _ = lax.optimization_barrier((far_sum, near_half, list(sent.values())))
 
@@ -430,44 +452,25 @@
     pieces = quarter.astype(F16).reshape(n_dp, per_shard * rank // n_dp, blk)
     pieces = lax.all_to_all(pieces, "dp", 0, 0)
 
+    last = [got.pop(1)]
     level = 1
     while level < outer:
         if level > 1:
-            got = {}
-            for i in [i for i in sums if i & level]:
-                got[i] = swap(sums[i].astype(F16), "dp", 2 * level)
+            got = {i: swap(pack(sums[i]), "dp", 2 * level) for i in sums if i & level}
         for i in got:
-            sums[i ^ level] = sums[i ^ level] + got[i].astype(F32)
+            sums[i ^ level] = add(sums[i ^ level], got[i])
         sums = {i: part for i, part in sums.items() if not i & level}
-        if level == 1 and outer > 2:
-            sums[2], pieces = lax.optimization_barrier((sums[2].astype(F16), pieces))
+        if outer == 4:
+            crossed, pieces = lax.optimization_barrier((pack(sums[2]), pieces))
+            last.append(swap(crossed, "dp", 4))
+            break
         level *= 2
-    grad = sums[0] * (1.0 / (grad_scale * all_tokens))
-
-    input_grad = pl.pallas_call(
-        functools.partial(input_grad_kernel, n_mp, per_shard, blk, per_step),
-        grid_spec=pltpu.PrefetchScalarGridSpec(
-            num_scalar_prefetch=1,
-            grid=(block_rows // per_step,),
-            in_specs=[ANY] * n_mp
-            + [pl.BlockSpec((per_step * blk, slots * blk), lambda i, pat: (i, 0))],
-            out_specs=pl.BlockSpec((tok_rows, per_step * blk), lambda i, pat: (0, i)),
-            scratch_shapes=[
-                pltpu.VMEM((n_mp, tok_rows, shard_cols), BF),
-                pltpu.SemaphoreType.DMA((n_mp,)),
-            ],
-        ),
-        out_shape=jax.ShapeDtypeStruct((tok_rows, mp_rows), BF),
-        compiler_params=params(),
-        cost_estimate=SMALL,
-        name="input_grad",
-    )(pat_all, *own, after(weights_2d, quarter))
-    pieces, input_grad = lax.optimization_barrier((pieces, input_grad))
+
 
     piece = jnp.sum(pieces.astype(F32), axis=0).astype(F16)
     quarter16 = over_dp(piece).reshape(per_shard, rank, blk)
 
-    sk_own = after(sk_own, quarter)
+    sk_own = after(lax.all_gather(sketch, "dp"), quarter).astype(F16)
     sk_far = swap(sk_own, "mp", 2)
     sk_parts = [sk_own, swap(sk_own, "mp", 1), sk_far, swap(sk_far, "mp", 1)]
     if width < blk:
@@ -508,6 +511,25 @@
     )(qh, ql, oh, ol)
     cross = cross + swap(cross, "mp", 2)
     cross = cross + swap(cross, "mp", 1)
+    input_grad = pl.pallas_call(
+        functools.partial(input_grad_kernel, n_mp, per_shard, blk, per_step),
+        grid_spec=pltpu.PrefetchScalarGridSpec(
+            num_scalar_prefetch=1,
+            grid=(block_rows // per_step,),
+            in_specs=[ANY] * n_mp
+            + [pl.BlockSpec((per_step * blk, slots * blk), lambda i, pat: (i, 0))],
+            out_specs=pl.BlockSpec((tok_rows, per_step * blk), lambda i, pat: (0, i)),
+            scratch_shapes=[
+                pltpu.VMEM((n_mp, tok_rows, shard_cols), BF),
+                pltpu.SemaphoreType.DMA((n_mp,)),
+            ],
+        ),
+        out_shape=jax.ShapeDtypeStruct((tok_rows, mp_rows), BF),
+        compiler_params=params(),
+        cost_estimate=SMALL,
+        name="input_grad",
+    )(pat_all, *own, after(weights_2d, cross))
+    cross, input_grad = lax.optimization_barrier((cross, input_grad))
     mixing = pl.pallas_call(
         mixing_kernel,
         in_specs=[VMEM] * 2,
@@ -524,6 +546,10 @@
     comp_parts = [split2_xla(part.astype(F32)) for part in comp_parts]
     comp_parts = [part[0] for part in comp_parts] + [part[1] for part in comp_parts]
 
+    kept, mixing, first = lax.optimization_barrier((sums[0], mixing, jnp.int32(0)))
+    for message in last:
+        kept = add(kept, message, first)
+    grad = kept[0] * (1.0 / all_tokens)
     _, my_starts, my_blocks = windows_of(dp * dev_rows, dev_rows, blk)
     my_pat = jnp.take(place(pattern), my_blocks, axis=0).reshape(-1)
     smem = pl.BlockSpec(memory_space=pltpu.SMEM)

time: 242 us -> 227 us (0.938)
  waiting for transfers between devices: 63.8 us -> 39 us
  between operations: 4.24 us -> 18.8 us
  starting transfers between devices: 41.9 us -> 31.9 us
  local copies, waits for them, and re-layouts: 26.5 us -> 32.1 us
  other arithmetic: 31.7 us -> 35.6 us
  Pallas kernels: 71.6 us -> 68.6 us
    ppermute x24 -> x22, waiting for transfers between devices: 56 us -> 21.6 us  [swap(): return lax.ppermute(x, axis, [(i, i ^ bit) for i in range(size)])]
    all_to_all x3 -> x2, starting transfers between devices: 18.5 us -> 11.4 us  [over_dp(): lax.all_to_all(jnp.broadcast_to(x[None], (n_dp, *x.shape)), 'dp', 0, 0)]
    all_to_all x1, waiting for transfers between devices: 0.05 us -> 5.57 us  [per_device(): pieces = lax.all_to_all(pieces, 'dp', 0, 0)]
    all_to_all x3 -> x2, waiting for transfers between devices: 7.72 us -> 11.8 us  [over_dp(): lax.all_to_all(jnp.broadcast_to(x[None], (n_dp, *x.shape)), 'dp', 0, 0)]
    slice x0 -> x1, other arithmetic: none -> 3.84 us  [pair_grad(): return {block: (out[i], top) for i, block in enumerate(blocks)}]
    reduce_max x3 -> x2, other arithmetic: 5.09 us -> 1.27 us  [pair_grad(): top = jnp.max(top)]
    concatenate x1 -> x3, local copies, waits for them, and re-layouts: 0.08 us -> 3.42 us  [pack(): jnp.concatenate([value * jnp.exp2(exponent), below], axis=0).astype(F16)]
    pallas_call x1, Pallas kernels: 16 us -> 12.9 us  [per_device(): pl.pallas_call(functools.partial(compress_kernel, n_mp, per_shard, 1.0 /...]
  transfers between devices with their start and end apart: 28 -> 26, of which waited for: 12 -> 10; matrix products, arithmetic and copies ran while one was open for 21% -> 27% of each run, Pallas kernels for 26% -> 26%
where the time goes in v7:
time: 227 us; the launch traced here: 226 us
  Pallas kernels  68.6 us (30%)
  waiting for transfers between devices  39 us (17%)
  other arithmetic  35.6 us (16%)
  local copies, waits for them, and re-layouts  32.1 us (14%)
  starting transfers between devices  31.9 us (14%)
  between operations  18.8 us (8%)
    ppermute x22, waiting for transfers between devices, swap(): return lax.ppermute(x, axis, [(i, i ^ bit) for i in range(size)])  21.6 us
    unnamed x41, local copies, waits for them, and re-layouts  17.2 us
    pallas_call x2, Pallas kernels, pair_grad(): pl.pallas_call(functools.partial(grad_kernel, n_mp, per_shard, blk, windo...  16.5 us
    ppermute x22, starting transfers between devices, swap(): return lax.ppermute(x, axis, [(i, i ^ bit) for i in range(size)])  16.4 us
    pallas_call x1, Pallas kernels, per_device(): pl.pallas_call(mixing_kernel, in_specs=[VMEM] * 2, out_specs=VMEM, out_sh...  16 us
    pallas_call x1, Pallas kernels, per_device(): pl.pallas_call(functools.partial(compress_kernel, n_mp, per_shard, 1.0 /...  12.9 us
    all_to_all x2, waiting for transfers between devices, over_dp(): lax.all_to_all(jnp.broadcast_to(x[None], (n_dp, *x.shape)), 'dp', 0, 0)  11.8 us
    all_to_all x2, starting transfers between devices, over_dp(): lax.all_to_all(jnp.broadcast_to(x[None], (n_dp, *x.shape)), 'dp', 0, 0)  11.4 us
  transfers between devices with their start and end apart: 26, of which 10 were waited for; matrix products, arithmetic and copies ran while one was open for 27% of the time, Pallas kernels for 26%

profile of v7, /device:TPU:0, one launch (start us, length us, event | category | flops | bytes accessed | tf_op | source)
XLA Modules:
  0.0 226.0 jit_solution(17054719274049484360)
XLA Ops:
  9.3 7.3 %all-to-all-start = ((f16[8,448,128]{2,1,0:T(8,128)(2,1)}), f16[8,448,128]{2,1,0:T(8,128)(2,1)}, u32[]{:S(2)}, u32[]{:S(2)}) async-start(f16[8,448,128]{2,1,0:T(8,128)(2,1)} %broadcast_in_dim.53), calls=%async_computation | async-start | bytes 1835008 | tf_op jit(solution)/shard_map/all_to_all | solution.py:297
  20.2 3.8 %copy.21 = bf16[256,3584]{0,1:T(8,128)(2,1)} copy(bf16[256,3584]{1,0:T(8,128)(2,1)} %param.9) | data formatting | bytes 3670016 | tf_op args[1]
  24.0 7.9 %copy.28 = bf16[448,8,8,128]{3,1,2,0:T(8,128)(2,1)} copy(bf16[448,8,8,128]{3,2,1,0:T(8,128)(2,1)} %bitcast.42) | data formatting | bytes 14680064
  31.9 2.8 %dynamic-slice_bitcast_fusion = (bf16[4,448,256]{2,1,0:T(8,128)(2,1)}, bf16[4,448,256]{2,1,0:T(8,128)(2,1)}) fusion(bf16[4,2,448,256]{3,2,1,0:T(8,128)(2,1)} %bitcast.37, s32[]{:T(128)S(6)} %select_n.221, s32[]{:T(128)S(6)} %select_n.220), kind=kLoop, calls=%fused_computation.34 | loop fusion | bytes 3670024 | tf_op jit(solution)/shard_map/jit(dynamic_index_in_dim)/squeeze | solution.py:304
  34.7 8.6 %all-to-all-done = f16[8,448,128]{2,1,0:T(8,128)(2,1)} async-done(((f16[8,448,128]{2,1,0:T(8,128)(2,1)}), f16[8,448,128]{2,1,0:T(8,128)(2,1)}, u32[]{:S(2)}, u32[]{:S(2)}) %all-to-all-start) | async-done | bytes 917536 | tf_op jit(solution)/shard_map/all_to_all | solution.py:297
  43.4 2.5 %bitcast_convert_fusion.refs_5_ = f32[3584,128]{1,0:T(8,128)} fusion(f16[8,448,128]{2,1,0:T(8,128)(2,1)} %all-to-all-done), kind=kLoop, calls=%fused_computation.33 | loop fusion | flops 458752 | bytes 2752512 | tf_op jit(solution)/shard_map/convert_element_type | solution.py:308
  45.9 8.1 %collective-permute-done.1.refs_4_ = bf16[256,2048]{1,0:T(8,128)(2,1)} collective-permute-done((bf16[256,2048]{1,0:T(8,128)(2,1)S(1)}, bf16[256,2048]{1,0:T(8,128)(2,1)}, u32[]{:S(2)}, u32[]{:S(2)}) %collective-permute-start.1) | collective-permute-done | bytes 1048608 | tf_op jit(solution)/shard_map/ppermute | solution.py:291
  61.3 12.9 %compress.1 = f32[64,128,128]{2,1,0:T(8,128)} custom-call(s32[224]{0:T(256)S(1)} %reshape.443.pat, s32[224]{0:T(256)S(1)} %reshape.444.pat_out, bf16[256,2048]{1,0:T(8,128)(2,1)S(1)} %copy-done.2, bf16[256,2048]{1,0:T(8,128)(2,1)S(1)} %collective-permute-done.2.refs_1_, bf16[256,2048]{1,0:T(8,128)(2,1)S(1)} %collective-permute-done.refs_2_, ...), custom_call_target="tpu_custom_call" | custom-call | flops 1 | bytes 1 | tf_op jit(solution)/shard_map/compress/pallas_call | solution.py:338
  74.2 4.5 %collective-permute-done.6 = bf16[4,448,256]{2,1,0:T(8,128)(2,1)} collective-permute-done((bf16[4,448,256]{2,1,0:T(8,128)(2,1)}, bf16[4,448,256]{2,1,0:T(8,128)(2,1)}, u32[]{:S(2)}, u32[]{:S(2)}) %collective-permute-start.6) | collective-permute-done | bytes 917536 | tf_op jit(solution)/shard_map/ppermute | solution.py:291
  78.8 2.7 %convert.23 = f16[64,128,128]{2,1,0:T(8,128)(2,1)S(1)} convert(f32[64,128,128]{2,1,0:T(8,128)} %compress.1) | non-fusion elementwise | flops 1048576 | bytes 6291456 | tf_op jit(solution)/shard_map/convert.8
  84.7 8.2 %pair_grad.2 = (f32[896,1024]{1,0:T(8,128)}, f32[8,256]{1,0:T(8,128)S(1)}) custom-call(s32[2]{0:T(128)S(1)} %get-tuple-element.115.order, s32[16]{0:T(128)S(1)} %reshape.440.starts, s32[128]{0:T(128)S(1)} %select_n.219.pat, bf16[256,2048]{1,0:T(8,128)(2,1)S(1)} %copy-done.2, bf16[256,2048]{1,0:T(8,128)(2,1)S(1)} %collective-permute-done.2.refs_1_, ...), custom_call_target="tpu_custom_call" | custom-call | flops 1 | bytes 1 | tf_op jit(solution)/shard_map/pair_grad/pallas_call | solution.py:385
  97.5 2.7 %convert_add_fusion.1 = (f32[16,128,128]{2,1,0:T(8,128)}, f16[16,128,128]{2,1,0:T(8,128)(2,1)}) fusion(f16[16,128,128]{2,1,0:T(8,128)(2,1)} %collective-permute-done.9, f32[64,128,128]{2,1,0:T(8,128)S(1)} %copy-done.12, f16[16,128,128]{2,1,0:T(8,128)(2,1)} %collective-permute-done.8), kind=kLoop, calls=%fused_computation.31 | loop fusion | flops 1310720 | bytes 4718592 | tf_op jit(solution)/shard_map/add | solution.py:443
  102.5 8.2 %pair_grad.3 = (f32[896,1024]{1,0:T(8,128)}, f32[8,256]{1,0:T(8,128)S(1)}) custom-call(s32[2]{0:T(128)S(1)} %get-tuple-element.114.order, s32[16]{0:T(128)S(1)} %reshape.440.starts, s32[128]{0:T(128)S(1)} %select_n.219.pat, bf16[256,2048]{1,0:T(8,128)(2,1)S(1)} %copy-done.2, bf16[256,2048]{1,0:T(8,128)(2,1)S(1)} %collective-permute-done.2.refs_1_, ...), custom_call_target="tpu_custom_call" | custom-call | flops 1 | bytes 1 | tf_op jit(solution)/shard_map/pair_grad/pallas_call | solution.py:385
  112.1 3.8 %fusion.25 = (f32[448,1024]{1,0:T(8,128)}, f16[448,1024]{1,0:T(8,128)(2,1)S(1)}) fusion(f32[896,1024]{1,0:T(8,128)} %get-tuple-element.63, f32[]{:T(128)S(6)} %exp2.69), kind=kLoop, calls=%fused_computation.126 | loop fusion | flops 917504 | bytes 6422532 | tf_op jit(solution)/shard_map/slice | solution.py:418
  119.5 4.0 %all-to-all-start.1 = ((f16[8,256,128]{2,1,0:T(8,128)(2,1)}), f16[8,256,128]{2,1,0:T(8,128)(2,1)S(1)}, u32[]{:S(2)}, u32[]{:S(2)}) async-start(f16[8,256,128]{2,1,0:T(8,128)(2,1)} %bitcast.43), calls=%async_computation.1 | async-start | bytes 1048576 | tf_op jit(solution)/shard_map/all_to_all | solution.py:453
  132.5 5.6 %all-to-all-done.1 = f16[8,256,128]{2,1,0:T(8,128)(2,1)S(1)} async-done(((f16[8,256,128]{2,1,0:T(8,128)(2,1)}), f16[8,256,128]{2,1,0:T(8,128)(2,1)S(1)}, u32[]{:S(2)}, u32[]{:S(2)}) %all-to-all-start.1) | async-done | bytes 524320 | tf_op jit(solution)/shard_map/all_to_all | solution.py:453
  139.0 4.1 %all-to-all-start.2 = ((f16[8,256,128]{2,1,0:T(8,128)(2,1)}), f16[8,256,128]{2,1,0:T(8,128)(2,1)}, u32[]{:S(2)}, u32[]{:S(2)}) async-start(f16[8,256,128]{2,1,0:T(8,128)(2,1)} %broadcast_in_dim.54), calls=%async_computation.2 | async-start | bytes 1048576 | tf_op jit(solution)/shard_map/all_to_all | solution.py:297
  147.3 2.4 %collective-permute-start.18 = (f16[464,1024]{1,0:T(8,128)(2,1)}, f16[464,1024]{1,0:T(8,128)(2,1)}, u32[]{:S(2)}, u32[]{:S(2)}) collective-permute-start(f16[464,1024]{1,0:T(8,128)(2,1)} %concatenate.68), channel_id=1, source_target_pairs={{0,16},{4,20},{8,24},{12,28},{16,0},{20,4},{24,8},{28,12},{1,17},{... | collective-permute-start | bytes 2850824 | tf_op jit(solution)/shard_map/ppermute | solution.py:291
  156.1 3.1 %all-to-all-done.2 = f16[8,256,128]{2,1,0:T(8,128)(2,1)} async-done(((f16[8,256,128]{2,1,0:T(8,128)(2,1)}), f16[8,256,128]{2,1,0:T(8,128)(2,1)}, u32[]{:S(2)}, u32[]{:S(2)}) %all-to-all-start.2) | async-done | bytes 524320 | tf_op jit(solution)/shard_map/all_to_all | solution.py:297
  162.7 4.0 %collective-permute-done.15 = f32[128,256]{1,0:T(8,128)S(1)} collective-permute-done((f32[128,256]{1,0:T(8,128)S(1)}, f32[128,256]{1,0:T(8,128)S(1)}, u32[]{:S(2)}, u32[]{:S(2)}) %collective-permute-start.15) | collective-permute-done | bytes 131104 | tf_op jit(solution)/shard_map/ppermute | solution.py:291
  169.2 11.0 %input_grad.1 = bf16[256,3584]{1,0:T(8,128)(2,1)} custom-call(s32[224]{0:T(256)S(1)} %reshape.443.pat, bf16[256,2048]{1,0:T(8,128)(2,1)S(1)} %copy-done.2, bf16[256,2048]{1,0:T(8,128)(2,1)S(1)} %copy-done.6, bf16[256,2048]{1,0:T(8,128)(2,1)S(1)} %copy-done.4, bf16[256,2048]{1,0:T(8,128)(2,1)} %collective-permute-done.3.refs_3_, bf16[3584,1024]{1,0:T(8,128)(2,1)} %bitcast.41), custom_call_target="tpu_custom_call" | custom-call | flops 1 | bytes 1 | tf_op jit(solution)/shard_map/input_grad/pallas_call | solution.py:514
  181.3 16.0 %mixing.1.refs_1_ = f32[256,256]{1,0:T(8,128)S(1)} custom-call(f32[128,128]{1,0:T(8,128)S(1)} %sketch_gram.1.ss_ref, f32[128,256]{1,0:T(8,128)S(1)} %add.304.cross_ref), custom_call_target="tpu_custom_call" | custom-call | flops 1 | bytes 1 | tf_op jit(solution)/shard_map/mixing/pallas_call | solution.py:533
  202.0 3.8 %add_multiply_fusion.refs_0_ = f32[448,1024]{1,0:T(8,128)} fusion(f32[448,1024]{1,0:T(8,128)} %get-tuple-element.77, f16[464,1024]{1,0:T(8,128)(2,1)} %collective-permute-done.18, f16[464,1024]{1,0:T(8,128)(2,1)} %collective-permute-done.17, f32[]{:T(128)} %bitcast.22, f32[]{:T(128)} %bitcast.21), kind=kLoop, calls=%fused_computation.7 | loop fusion | flops 3211264 | bytes 5505032 | tf_op jit(solution)/shard_map/mul | solution.py:552
  209.6 9.5 %direction.1 = f32[448,8,128]{2,1,0:T(8,128)} custom-call(s32[4]{0:T(128)S(1)} %pad_add_fusion.2.starts, s32[32]{0:T(128)S(1)} %select_n.235.pat, f32[448,1024]{1,0:T(8,128)} %add_multiply_fusion.refs_0_, f32[256,256]{1,0:T(8,128)S(1)} %mixing.1.refs_1_, bf16[32,128,256]{2,1,0:T(8,128)(2,1)} %copy-done.1, bf16[32,128,256]{2,1,0:T(8,128)(2,1)} %copy-done, ...), custom_call_target="tpu_custom_call" | custom-call | flops 1 | bytes 1 | tf_op jit(solution)/shard_map/direction/pallas_call | solution.py:556
  (144 shorter events, 59.5 us)
Async XLA Ops:
  9.3 34.1 %all-to-all-start = ((f16[8,448,128]{2,1,0:T(8,128)(2,1)}), f16[8,448,128]{2,1,0:T(8,128)(2,1)}, u32[]{:S(2)}, u32[]{:S(2)}) async-start(f16[8,448,128]{2,1,0:T(8,128)(2,1)} %broadcast_in_dim.53), calls=%async_computation | async-start | bytes 1835008 | tf_op jit(solution)/shard_map/all_to_all | solution.py:297
  16.6 107.0 %all-gather.3.cloned.1.call-start = ((), (), s32[]{:S(2)}) async-start(), calls=%async_computation.3 | async-start | bytes 1179648 | tf_op jit(solution)/shard_map/all_gather | solution.py:473
  16.6 29.3 %collective-permute-start = (bf16[256,2048]{1,0:T(8,128)(2,1)S(1)}, bf16[256,2048]{1,0:T(8,128)(2,1)S(1)}, u32[]{:S(2)}, u32[]{:S(2)}) collective-permute-start(bf16[256,2048]{1,0:T(8,128)(2,1)S(1)} %copy-done.2), channel_id=1, source_target_pairs={{0,2},{1,3},{2,0},{3,1},{4,6},{5,7},{6,4},{7,5},{8,10},{9,11},{10,... | collective-permute-start | bytes 3145736 | tf_op jit(solution)/shard_map/ppermute | solution.py:291
  18.2 35.8 %collective-permute-start.1 = (bf16[256,2048]{1,0:T(8,128)(2,1)S(1)}, bf16[256,2048]{1,0:T(8,128)(2,1)}, u32[]{:S(2)}, u32[]{:S(2)}) collective-permute-start(bf16[256,2048]{1,0:T(8,128)(2,1)S(1)} %copy-done.2), channel_id=1, source_target_pairs={{0,4},{4,0},{8,12},{12,8},{16,20},{20,16},{24,28},{28,24},{1,5},{5... | collective-permute-start | bytes 3145736 | tf_op jit(solution)/shard_map/ppermute | solution.py:291
  20.1 33.9 %collective-permute-start.2 = (bf16[256,2048]{1,0:T(8,128)(2,1)S(1)}, bf16[256,2048]{1,0:T(8,128)(2,1)S(1)}, u32[]{:S(2)}, u32[]{:S(2)}) collective-permute-start(bf16[256,2048]{1,0:T(8,128)(2,1)S(1)} %copy-done.2), channel_id=1, source_target_pairs={{0,1},{1,0},{2,3},{3,2},{4,5},{5,4},{6,7},{7,6},{8,9},{9,8},{10,11... | collective-permute-start | bytes 3145736 | tf_op jit(solution)/shard_map/ppermute | solution.py:291
  54.0 24.7 %collective-permute-start.4 = (bf16[256,2048]{1,0:T(8,128)(2,1)}, bf16[256,2048]{1,0:T(8,128)(2,1)}, u32[]{:S(2)}, u32[]{:S(2)}) collective-permute-start(bf16[256,2048]{1,0:T(8,128)(2,1)} %collective-permute-done.1.refs_4_), channel_id=1, source_target_pairs={{0,2},{1,3},{2,0},{3,1},{4,6},{5,7},{6,4},{7,5},{8,10},{9,11},{10,... | collective-permute-start | bytes 3145736 | tf_op jit(solution)/shard_map/ppermute | solution.py:291
  55.5 23.2 %collective-permute-start.5 = (bf16[256,2048]{1,0:T(8,128)(2,1)}, bf16[256,2048]{1,0:T(8,128)(2,1)}, u32[]{:S(2)}, u32[]{:S(2)}) collective-permute-start(bf16[256,2048]{1,0:T(8,128)(2,1)} %collective-permute-done.1.refs_4_), channel_id=1, source_target_pairs={{0,1},{1,0},{2,3},{3,2},{4,5},{5,4},{6,7},{7,6},{8,9},{9,8},{10,11... | collective-permute-start | bytes 3145736 | tf_op jit(solution)/shard_map/ppermute | solution.py:291
  55.5 4.3 %collective-permute-start.3 = (bf16[256,2048]{1,0:T(8,128)(2,1)S(1)}, bf16[256,2048]{1,0:T(8,128)(2,1)}, u32[]{:S(2)}, u32[]{:S(2)}) collective-permute-start(bf16[256,2048]{1,0:T(8,128)(2,1)S(1)} %collective-permute-done.refs_2_), channel_id=1, source_target_pairs={{0,1},{1,0},{2,3},{3,2},{4,5},{5,4},{6,7},{7,6},{8,9},{9,8},{10,11... | collective-permute-start | bytes 3145736 | tf_op jit(solution)/shard_map/ppermute | solution.py:291
  56.1 22.6 %collective-permute-start.6 = (bf16[4,448,256]{2,1,0:T(8,128)(2,1)}, bf16[4,448,256]{2,1,0:T(8,128)(2,1)}, u32[]{:S(2)}, u32[]{:S(2)}) collective-permute-start(bf16[4,448,256]{2,1,0:T(8,128)(2,1)} %get-tuple-element.48), channel_id=1, source_target_pairs={{0,4},{4,0},{8,12},{12,8},{16,20},{20,16},{24,28},{28,24},{1,5},{5... | collective-permute-start | bytes 2752520 | tf_op jit(solution)/shard_map/ppermute | solution.py:291
  78.7 4.8 %collective-permute-start.7 = (bf16[256,2048]{1,0:T(8,128)(2,1)}, bf16[256,2048]{1,0:T(8,128)(2,1)}, u32[]{:S(2)}, u32[]{:S(2)}) collective-permute-start(bf16[256,2048]{1,0:T(8,128)(2,1)} %collective-permute-done.4.refs_6_), channel_id=1, source_target_pairs={{0,1},{1,0},{2,3},{3,2},{4,5},{5,4},{6,7},{7,6},{8,9},{9,8},{10,11... | collective-permute-start | bytes 3145736 | tf_op jit(solution)/shard_map/ppermute | solution.py:291
  82.8 14.7 %collective-permute-start.8 = (f16[16,128,128]{2,1,0:T(8,128)(2,1)}, f16[16,128,128]{2,1,0:T(8,128)(2,1)}, u32[]{:S(2)}, u32[]{:S(2)}) collective-permute-start(f16[16,128,128]{2,1,0:T(8,128)(2,1)} %get-tuple-element.95), channel_id=1, source_target_pairs={{0,1},{1,0},{2,3},{3,2},{4,5},{5,4},{6,7},{7,6},{8,9},{9,8},{10,11... | collective-permute-start | bytes 1572872 | tf_op jit(solution)/shard_map/ppermute | solution.py:291
  83.3 14.2 %collective-permute-start.9 = (f16[16,128,128]{2,1,0:T(8,128)(2,1)}, f16[16,128,128]{2,1,0:T(8,128)(2,1)}, u32[]{:S(2)}, u32[]{:S(2)}) collective-permute-start(f16[16,128,128]{2,1,0:T(8,128)(2,1)} %get-tuple-element.94), channel_id=1, source_target_pairs={{0,1},{1,0},{2,3},{3,2},{4,5},{5,4},{6,7},{7,6},{8,9},{9,8},{10,11... | collective-permute-start | bytes 1572872 | tf_op jit(solution)/shard_map/ppermute | solution.py:291
  100.2 16.8 %collective-permute-start.11 = (f16[16,128,128]{2,1,0:T(8,128)(2,1)}, f16[16,128,128]{2,1,0:T(8,128)(2,1)}, u32[]{:S(2)}, u32[]{:S(2)}) collective-permute-start(f16[16,128,128]{2,1,0:T(8,128)(2,1)} %get-tuple-element.60), channel_id=1, source_target_pairs={{0,2},{1,3},{2,0},{3,1},{4,6},{5,7},{6,4},{7,5},{8,10},{9,11},{10,... | collective-permute-start | bytes 1572872 | tf_op jit(solution)/shard_map/ppermute | solution.py:291
  101.0 25.7 %collective-permute-start.10 = (f16[464,1024]{1,0:T(8,128)(2,1)}, f16[464,1024]{1,0:T(8,128)(2,1)}, u32[]{:S(2)}, u32[]{:S(2)}) collective-permute-start(f16[464,1024]{1,0:T(8,128)(2,1)} %concatenate.67), channel_id=1, source_target_pairs={{0,8},{4,12},{8,0},{12,4},{16,24},{20,28},{24,16},{28,20},{1,9},{5... | collective-permute-start | bytes 2850824 | tf_op jit(solution)/shard_map/ppermute | solution.py:291
  119.5 18.5 %all-to-all-start.1 = ((f16[8,256,128]{2,1,0:T(8,128)(2,1)}), f16[8,256,128]{2,1,0:T(8,128)(2,1)S(1)}, u32[]{:S(2)}, u32[]{:S(2)}) async-start(f16[8,256,128]{2,1,0:T(8,128)(2,1)} %bitcast.43), calls=%async_computation.1 | async-start | bytes 1048576 | tf_op jit(solution)/shard_map/all_to_all | solution.py:453
  125.8 17.5 %collective-permute-start.13 = (f16[8,128,256]{2,1,0:T(8,128)(2,1)S(1)}, f16[8,128,256]{2,1,0:T(8,128)(2,1)}, u32[]{:S(2)}, u32[]{:S(2)}) collective-permute-start(f16[8,128,256]{2,1,0:T(8,128)(2,1)S(1)} %get-tuple-element.85), channel_id=1, source_target_pairs={{0,2},{1,3},{2,0},{3,1},{4,6},{5,7},{6,4},{7,5},{8,10},{9,11},{10,... | collective-permute-start | bytes 1572872 | tf_op jit(solution)/shard_map/ppermute | solution.py:291
  139.0 20.2 %all-to-all-start.2 = ((f16[8,256,128]{2,1,0:T(8,128)(2,1)}), f16[8,256,128]{2,1,0:T(8,128)(2,1)}, u32[]{:S(2)}, u32[]{:S(2)}) async-start(f16[8,256,128]{2,1,0:T(8,128)(2,1)} %broadcast_in_dim.54), calls=%async_computation.2 | async-start | bytes 1048576 | tf_op jit(solution)/shard_map/all_to_all | solution.py:297
  143.3 6.4 %collective-permute-start.12 = (f16[8,128,256]{2,1,0:T(8,128)(2,1)S(1)}, f16[8,128,256]{2,1,0:T(8,128)(2,1)S(1)}, u32[]{:S(2)}, u32[]{:S(2)}) collective-permute-start(f16[8,128,256]{2,1,0:T(8,128)(2,1)S(1)} %get-tuple-element.85), channel_id=1, source_target_pairs={{0,1},{1,0},{2,3},{3,2},{4,5},{5,4},{6,7},{7,6},{8,9},{9,8},{10,11... | collective-permute-start | bytes 1572872 | tf_op jit(solution)/shard_map/ppermute | solution.py:291
  143.3 7.3 %collective-permute-start.14 = (f16[8,128,256]{2,1,0:T(8,128)(2,1)}, f16[8,128,256]{2,1,0:T(8,128)(2,1)}, u32[]{:S(2)}, u32[]{:S(2)}) collective-permute-start(f16[8,128,256]{2,1,0:T(8,128)(2,1)} %collective-permute-done.13), channel_id=1, source_target_pairs={{0,1},{1,0},{2,3},{3,2},{4,5},{5,4},{6,7},{7,6},{8,9},{9,8},{10,11... | collective-permute-start | bytes 1572872 | tf_op jit(solution)/shard_map/ppermute | solution.py:291
  144.5 55.6 %collective-permute-start.17 = (f16[464,1024]{1,0:T(8,128)(2,1)}, f16[464,1024]{1,0:T(8,128)(2,1)}, u32[]{:S(2)}, u32[]{:S(2)}) collective-permute-start(f16[464,1024]{1,0:T(8,128)(2,1)} %concatenate.69), channel_id=1, source_target_pairs={{0,8},{4,12},{8,0},{12,4},{16,24},{20,28},{24,16},{28,20},{1,9},{5... | collective-permute-start | bytes 2850824 | tf_op jit(solution)/shard_map/ppermute | solution.py:291
  147.3 50.9 %collective-permute-start.18 = (f16[464,1024]{1,0:T(8,128)(2,1)}, f16[464,1024]{1,0:T(8,128)(2,1)}, u32[]{:S(2)}, u32[]{:S(2)}) collective-permute-start(f16[464,1024]{1,0:T(8,128)(2,1)} %concatenate.68), channel_id=1, source_target_pairs={{0,16},{4,20},{8,24},{12,28},{16,0},{20,4},{24,8},{28,12},{1,17},{... | collective-permute-start | bytes 2850824 | tf_op jit(solution)/shard_map/ppermute | solution.py:291
  161.6 5.0 %collective-permute-start.15 = (f32[128,256]{1,0:T(8,128)S(1)}, f32[128,256]{1,0:T(8,128)S(1)}, u32[]{:S(2)}, u32[]{:S(2)}) collective-permute-start(f32[128,256]{1,0:T(8,128)S(1)} %cross_gram.1), channel_id=1, source_target_pairs={{0,2},{1,3},{2,0},{3,1},{4,6},{5,7},{6,4},{7,5},{8,10},{9,11},{10,... | collective-permute-start | bytes 393224 | tf_op jit(solution)/shard_map/ppermute | solution.py:291
  180.2 28.3 %collective-permute-start.19 = (f16[16,128,128]{2,1,0:T(8,128)(2,1)}, f16[16,128,128]{2,1,0:T(8,128)(2,1)S(1)}, u32[]{:S(2)}, u32[]{:S(2)}) collective-permute-start(f16[16,128,128]{2,1,0:T(8,128)(2,1)} %bitcast.14), channel_id=1, source_target_pairs={{0,1},{1,0},{2,3},{3,2},{4,5},{5,4},{6,7},{7,6},{8,9},{9,8},{10,11... | collective-permute-start | bytes 1572872 | tf_op jit(solution)/shard_map/ppermute | solution.py:291
  180.4 26.7 %collective-permute-start.20 = (f16[16,128,128]{2,1,0:T(8,128)(2,1)}, f16[16,128,128]{2,1,0:T(8,128)(2,1)}, u32[]{:S(2)}, u32[]{:S(2)}) collective-permute-start(f16[16,128,128]{2,1,0:T(8,128)(2,1)} %bitcast.14), channel_id=1, source_target_pairs={{0,2},{1,3},{2,0},{3,1},{4,6},{5,7},{6,4},{7,5},{8,10},{9,11},{10,... | collective-permute-start | bytes 1572872 | tf_op jit(solution)/shard_map/ppermute | solution.py:291
  (21 other events, 204.3 us)
Sparse Core Ops, SparseCore 0:
  20.3 45.3 all-gather.2

commit v8 on v7

--- a/solution.py
+++ b/solution.py
@@ -60,14 +60,21 @@
     return held[shard, :, pl.ds(offset, size)]
 
 
-def compress_kernel(n_shards, per_shard, scale, per_step, pat, pat_out, *refs):
+def compress_kernel(n_shards, per_shard, scale, per_step, pat, pat_out, places, *refs):
     shards = refs[:n_shards]
-    hid_ref, proj_ref, out_ref, held, sems = refs[n_shards:]
+    hid_ref, *proj_refs, out_ref, held, proj, sems = refs[n_shards:]
     blk = out_ref.shape[1]
 
     @pl.when(pl.program_id(0) == 0)
     def _():
-        load_all([(ref, held.at[i]) for i, ref in enumerate(shards)], sems)
+        loads = [(ref, held.at[i]) for i, ref in enumerate(shards)]
+        for ref in proj_refs:
+            part_rows = ref.shape[1]
+            for i in range(ref.shape[0]):
+                place = places[len(loads) - n_shards]
+                rows = pl.ds(pl.multiple_of(place * part_rows, 8), part_rows)
+                loads.append((ref.at[i], proj.at[rows]))
+        load_all(loads, sems)
         out_ref[...] = jnp.zeros_like(out_ref)
 
     first = pl.program_id(0) * per_step
@@ -75,7 +82,8 @@
     for u in range(per_step):
         span = slice(u * blk, (u + 1) * blk)
         hid = hid_ref[span, :]
-        ph, pl_ = split2(proj_ref[span, :].T)
+        rows = pl.ds(pl.multiple_of((first + u) * blk, blk), blk)
+        ph, pl_ = split2(proj[rows, :].T)
         lefts.append(((dot(ph, hid) + dot(pl_, hid)) * scale).astype(BF))
     parts = []
     for u in range(per_step):
@@ -298,15 +306,50 @@
 
     width = sketch.shape[1]
     core_half = swap(cotangent, "mp", 1)
-    hid_t = hidden.T
+    proj_t = (projection.reshape(rank, dev_rows).T * PROJ_SCALE).astype(F16)
+    if width < blk:
+        sk_rows = sketch.reshape(width, rank)
+    else:
+        sk_rows = sketch.reshape(rank, width // blk, blk).swapaxes(0, 1).reshape(-1, blk)
+    early = jnp.concatenate([proj_t, sk_rows.astype(F16)], axis=0)
+    early, order = early[None], jnp.zeros((1,), jnp.int32)
+    bits = [1 << i for i in range(1, n_dp.bit_length() - 1)]
+    if n_dp > 8:
+        early, order, bits = over_dp(early[0]), jnp.arange(n_dp, dtype=jnp.int32), []
+    hidden_in, weights_in = hidden, weights
+    for bit in bits:
+        early = jnp.concatenate([early, swap(early, "dp", bit)], axis=0)
+        order = jnp.concatenate([order, jnp.bitwise_xor(order, bit)])
+        if bit == 2:
+            early, hidden_in, weights_in = lax.optimization_barrier((early, hidden, weights))
+    hid_t = hidden_in.T
     hid_parts = hid_t.reshape(outer, 2, dev_rows, tok_rows)
     hid_own = lax.dynamic_index_in_dim(hid_parts, side, 1, keepdims=False)
     hid_send = lax.dynamic_index_in_dim(hid_parts, 1 - side, 1, keepdims=False)
-    proj_t = (projection.reshape(rank, dev_rows).T * PROJ_SCALE).astype(F16)
+    weights_2d = weights_in.reshape(mp_rows, slots * blk)
+    if n_dp <= 8:
+        early, hid_own, hid_send, weights_2d = lax.optimization_barrier(
+            (early, hid_own, hid_send, weights_2d)
+        )
+        early = [early, swap(early, "dp", 1)]
+        order = jnp.concatenate([order, jnp.bitwise_xor(order, 1)])
+        places = jnp.bitwise_xor(order, dp)
+        sk_own = jnp.concatenate([part[:, dev_rows:] for part in early], axis=0)
+        far = jnp.bitwise_xor(jnp.arange(n_dp, dtype=jnp.int32), dp)
+        at = jnp.where(jnp.bitwise_and(far, 1) == 1, n_dp // 2, 0) + far // 2
+        sk_own = jnp.take(sk_own, at, axis=0, mode="clip")
+        proj_parts = [part[:, :dev_rows].astype(F32) for part in early]
+        hid_send = after(hid_send, early[1])
+    else:
+        sk_own = early[:, dev_rows:]
+        proj_parts = [early[:, :dev_rows].reshape(1, mp_rows, rank).astype(F32)]
+        places = jnp.zeros((1,), jnp.int32)
+    if width < blk:
+        sk_own = sk_own.reshape(n_dp, rank, width)
+    else:
+        sk_own = sk_own.reshape(per_shard, rank, blk)
     x_part, y_part = swap(cotangent, "mp", 2), swap(cotangent, "dp", 1)
-    weights_2d = weights.reshape(mp_rows, slots * blk)
-    proj_all = over_dp(proj_t).reshape(mp_rows, rank).astype(F32)
-    x_half, y_own, core_half, hid_t, hid_own, hid_send, weights_2d, proj_all = (
+    x_half, y_own, core_half, hid_t, hid_own, weights_2d = (
         lax.optimization_barrier(
             (
                 x_part,
@@ -314,9 +357,7 @@
                 core_half,
                 hid_t,
                 hid_own,
-                hid_send,
                 weights_2d,
-                proj_all,
             )
         )
     )
@@ -344,24 +385,23 @@
             per_step,
         ),
         grid_spec=pltpu.PrefetchScalarGridSpec(
-            num_scalar_prefetch=2,
+            num_scalar_prefetch=3,
             grid=(block_rows // per_step,),
             in_specs=[ANY] * n_mp
-            + [
-                pl.BlockSpec((per_step * blk, tok_rows), lambda i, a, b: (i, 0)),
-                pl.BlockSpec((per_step * blk, rank), lambda i, a, b: (i, 0)),
-            ],
-            out_specs=pl.BlockSpec((col_blocks, rank, blk), lambda i, a, b: (0, 0, 0)),
+            + [pl.BlockSpec((per_step * blk, tok_rows), lambda i, a, b, c: (i, 0))]
+            + [ANY] * len(proj_parts),
+            out_specs=pl.BlockSpec((col_blocks, rank, blk), lambda i, a, b, c: (0, 0, 0)),
             scratch_shapes=[
                 pltpu.VMEM((n_mp, tok_rows, shard_cols), BF),
-                pltpu.SemaphoreType.DMA((n_mp,)),
+                pltpu.VMEM((mp_rows, rank), F32),
+                pltpu.SemaphoreType.DMA((n_mp + len(places),)),
             ],
         ),
         out_shape=jax.ShapeDtypeStruct((col_blocks, rank, blk), F32),
         compiler_params=params(),
         cost_estimate=SMALL,
         name="compress",
-    )(pat_all, place(pattern).reshape(-1), *own, hid_t, proj_all)
+    )(pat_all, place(pattern).reshape(-1), places, *own, hid_t, *proj_parts)
 
     partial_c, y_x, y_core, hid_got = lax.optimization_barrier((partial_c, y_x, y_core, hid_got))
     y_group = [y_own, y_core, y_x, swap(y_x, "mp", 1)]
@@ -424,9 +464,10 @@
         return jnp.concatenate([value * jnp.exp2(exponent), below], axis=0).astype(F16)
 
     def unpack(message, first=0):
-        exponent = lax.dynamic_slice(message, (dev_rows + first, 0), (8, 128))[0, 0].astype(F32)
+        below = lax.dynamic_slice(message, (dev_rows + first, 0), (8, message.shape[1]))
+        exponent = below[:1].astype(F32)
         value = message[:dev_rows].astype(F32) * jnp.exp2(-exponent)
-        return value, jnp.exp2(14.0 - exponent)
+        return value, jnp.exp2(14.0 - jnp.max(exponent))
 
     def add(part, message, first=0):
         value, top = unpack(message, first)
@@ -450,6 +491,8 @@
 
     quarter = near_half + far_sum.astype(F32)
     pieces = quarter.astype(F16).reshape(n_dp, per_shard * rank // n_dp, blk)
+    if outer == 4:
+        pieces, got[3] = lax.optimization_barrier((pieces, got[3]))
     pieces = lax.all_to_all(pieces, "dp", 0, 0)
 
     last = [got.pop(1)]
@@ -470,7 +513,7 @@
     piece = jnp.sum(pieces.astype(F32), axis=0).astype(F16)
     quarter16 = over_dp(piece).reshape(per_shard, rank, blk)
 
-    sk_own = after(lax.all_gather(sketch, "dp"), quarter).astype(F16)
+    sk_own = after(sk_own, quarter)
     sk_far = swap(sk_own, "mp", 2)
     sk_parts = [sk_own, swap(sk_own, "mp", 1), sk_far, swap(sk_far, "mp", 1)]
     if width < blk:

time: 227 us -> 217 us (0.956)
  between operations: 18.8 us -> 4.25 us
  Pallas kernels: 68.6 us -> 74.2 us
  local copies, waits for them, and re-layouts: 32.1 us -> 27.3 us
  starting transfers between devices: 31.9 us -> 34.3 us
    ppermute x22 -> x25, waiting for transfers between devices: 21.6 us -> 35.7 us  [swap(): return lax.ppermute(x, axis, [(i, i ^ bit) for i in range(size)])]
    all_to_all x2 -> x1, waiting for transfers between devices: 11.8 us -> 0.39 us  [over_dp(): lax.all_to_all(jnp.broadcast_to(x[None], (n_dp, *x.shape)), 'dp', 0, 0)]
    ppermute x22 -> x25, starting transfers between devices: 16.4 us -> 26.4 us  [swap(): return lax.ppermute(x, axis, [(i, i ^ bit) for i in range(size)])]
    all_to_all x2 -> x1, starting transfers between devices: 11.4 us -> 4.14 us  [over_dp(): lax.all_to_all(jnp.broadcast_to(x[None], (n_dp, *x.shape)), 'dp', 0, 0)]
    unnamed x41 -> x44, local copies, waits for them, and re-layouts: 17.2 us -> 11.9 us
    optimization_barrier x0 -> x1, local copies, waits for them, and re-layouts: none -> 3.8 us  [per_device(): lax.optimization_barrier((early, hidden, weights))]
    convert_element_type x8 -> x7, other arithmetic: 9.98 us -> 7.02 us  [split2_xla(): return (high.astype(BF), (value - high).astype(BF))]
    exp2 x0 -> x3, other arithmetic: none -> 2.85 us  [unpack(): value = message[:dev_rows].astype(F32) * jnp.exp2(-exponent)]
  transfers between devices with their start and end apart: 26 -> 27, of which waited for: 10 -> 12; matrix products, arithmetic and copies ran while one was open for 27% -> 27% of each run, Pallas kernels for 26% -> 30%
where the time goes in v8:
time: 217 us; the launch traced here: 216 us
  Pallas kernels  74.2 us (34%)
  waiting for transfers between devices  39.9 us (18%)
  other arithmetic  36.3 us (17%)
  starting transfers between devices  34.3 us (16%)
  local copies, waits for them, and re-layouts  27.3 us (13%)
  between operations  4.25 us (2%)
    ppermute x25, waiting for transfers between devices, swap(): return lax.ppermute(x, axis, [(i, i ^ bit) for i in range(size)])  35.7 us
    ppermute x25, starting transfers between devices, swap(): return lax.ppermute(x, axis, [(i, i ^ bit) for i in range(size)])  26.4 us
    pallas_call x2, Pallas kernels, pair_grad(): pl.pallas_call(functools.partial(grad_kernel, n_mp, per_shard, blk, windo...  16.4 us
    pallas_call x1, Pallas kernels, per_device(): pl.pallas_call(mixing_kernel, in_specs=[VMEM] * 2, out_specs=VMEM, out_sh...  16 us
    pallas_call x1, Pallas kernels, per_device(): pl.pallas_call(functools.partial(compress_kernel, n_mp, per_shard, 1.0 /...  14.7 us
    unnamed x44, local copies, waits for them, and re-layouts  11.9 us
    pallas_call x1, Pallas kernels, per_device(): pl.pallas_call(functools.partial(input_grad_kernel, n_mp, per_shard, blk,...  11 us
    pallas_call x1, Pallas kernels, per_device(): pl.pallas_call(functools.partial(direction_kernel, sk_per, window, n_wind...  9.5 us
  transfers between devices with their start and end apart: 27, of which 12 were waited for; matrix products, arithmetic and copies ran while one was open for 27% of the time, Pallas kernels for 30%

profile of v8, /device:TPU:0, one launch (start us, length us, event | category | flops | bytes accessed | tf_op | source)
XLA Modules:
  0.0 216.2 jit_solution(2656101309575797855)
XLA Ops:
  2.6 3.1 %collective-permute-start.3 = (f16[1,704,128]{2,1,0:T(8,128)(2,1)S(1)}, f16[1,704,128]{2,1,0:T(8,128)(2,1)S(1)}, u32[]{:S(2)}, u32[]{:S(2)}) collective-permute-start(f16[1,704,128]{2,1,0:T(8,128)(2,1)S(1)} %maximum_bitcast_fusion), channel_id=1, source_target_pairs={{0,8},{4,12},{8,0},{12,4},{16,24},{20,28},{24,16},{28,20},{1,9},{5... | collective-permute-start | bytes 540680 | tf_op jit(solution)/shard_map/ppermute | solution.py:299
  5.7 4.5 %collective-permute-done.3 = f16[1,704,128]{2,1,0:T(8,128)(2,1)S(1)} collective-permute-done((f16[1,704,128]{2,1,0:T(8,128)(2,1)S(1)}, f16[1,704,128]{2,1,0:T(8,128)(2,1)S(1)}, u32[]{:S(2)}, u32[]{:S(2)}) %collective-permute-start.3) | collective-permute-done | bytes 180256 | tf_op jit(solution)/shard_map/ppermute | solution.py:299
  10.3 2.8 %collective-permute-start.4 = (f16[2,704,128]{2,1,0:T(8,128)(2,1)S(1)}, f16[2,704,128]{2,1,0:T(8,128)(2,1)S(1)}, u32[]{:S(2)}, u32[]{:S(2)}) collective-permute-start(f16[2,704,128]{2,1,0:T(8,128)(2,1)S(1)} %pad_maximum_fusion.3), channel_id=1, source_target_pairs={{0,16},{4,20},{8,24},{12,28},{16,0},{20,4},{24,8},{28,12},{1,17},{... | collective-permute-start | bytes 1081352 | tf_op jit(solution)/shard_map/ppermute | solution.py:299
  16.2 3.8 %copy.23 = bf16[256,3584]{0,1:T(8,128)(2,1)} copy(bf16[256,3584]{1,0:T(8,128)(2,1)} %param.9) | data formatting | bytes 3670016 | tf_op jit(solution)/shard_map/optimization_barrier | solution.py:324
  20.0 8.0 %copy.32 = bf16[448,8,8,128]{3,1,2,0:T(8,128)(2,1)} copy(bf16[448,8,8,128]{3,2,1,0:T(8,128)(2,1)} %bitcast.50) | data formatting | bytes 14680064
  31.5 7.9 %collective-permute-done.1.refs_4_ = bf16[256,2048]{1,0:T(8,128)(2,1)} collective-permute-done((bf16[256,2048]{1,0:T(8,128)(2,1)}, bf16[256,2048]{1,0:T(8,128)(2,1)}, u32[]{:S(2)}, u32[]{:S(2)}) %collective-permute-start.1) | collective-permute-done | bytes 1048608 | tf_op jit(solution)/shard_map/ppermute | solution.py:299
  41.9 12.6 %collective-permute-done.6 = f16[4,704,128]{2,1,0:T(8,128)(2,1)} collective-permute-done((f16[4,704,128]{2,1,0:T(8,128)(2,1)}, f16[4,704,128]{2,1,0:T(8,128)(2,1)}, u32[]{:S(2)}, u32[]{:S(2)}) %collective-permute-start.6) | collective-permute-done | bytes 720928 | tf_op jit(solution)/shard_map/ppermute | solution.py:299
  59.2 14.7 %compress.1 = f32[64,128,128]{2,1,0:T(8,128)} custom-call(s32[224]{0:T(256)S(1)} %reshape.490.pat, s32[224]{0:T(256)S(1)} %reshape.491.pat_out, s32[8]{0:T(128)S(1)} %broadcast_xor_fusion.1.places, bf16[256,2048]{1,0:T(8,128)(2,1)S(1)} %copy-done.2, bf16[256,2048]{1,0:T(8,128)(2,1)S(1)} %collective-permute-done.2.refs_1_, ...), custom_call_target="tpu_custom_call" | custom-call | flops 1 | bytes 1 | tf_op jit(solution)/shard_map/compress/pallas_call | solution.py:379
  73.9 2.9 %collective-permute-done.9 = bf16[4,448,256]{2,1,0:T(8,128)(2,1)} collective-permute-done((bf16[4,448,256]{2,1,0:T(8,128)(2,1)}, bf16[4,448,256]{2,1,0:T(8,128)(2,1)}, u32[]{:S(2)}, u32[]{:S(2)}) %collective-permute-start.9) | collective-permute-done | bytes 917536 | tf_op jit(solution)/shard_map/ppermute | solution.py:299
  76.9 2.7 %convert.22 = f16[64,128,128]{2,1,0:T(8,128)(2,1)S(1)} convert(f32[64,128,128]{2,1,0:T(8,128)} %compress.1) | non-fusion elementwise | flops 1048576 | bytes 6291456 | tf_op jit(solution)/shard_map/convert.7
  82.8 8.2 %pair_grad.2 = (f32[896,1024]{1,0:T(8,128)}, f32[8,256]{1,0:T(8,128)S(1)}) custom-call(s32[2]{0:T(128)S(1)} %get-tuple-element.133.order, s32[16]{0:T(128)S(1)} %reshape.487.starts, s32[128]{0:T(128)S(1)} %select_n.242.pat, bf16[256,2048]{1,0:T(8,128)(2,1)S(1)} %copy-done.2, bf16[256,2048]{1,0:T(8,128)(2,1)S(1)} %collective-permute-done.2.refs_1_, ...), custom_call_target="tpu_custom_call" | custom-call | flops 1 | bytes 1 | tf_op jit(solution)/shard_map/pair_grad/pallas_call | solution.py:425
  97.1 2.7 %convert_add_fusion.1 = (f32[16,128,128]{2,1,0:T(8,128)}, f16[16,128,128]{2,1,0:T(8,128)(2,1)}) fusion(f16[16,128,128]{2,1,0:T(8,128)(2,1)} %collective-permute-done.12, f32[64,128,128]{2,1,0:T(8,128)S(1)} %copy-done.11, f16[16,128,128]{2,1,0:T(8,128)(2,1)} %collective-permute-done.11), kind=kLoop, calls=%fused_computation.32 | loop fusion | flops 1310720 | bytes 4718592 | tf_op jit(solution)/shard_map/add | solution.py:484
  101.2 8.2 %pair_grad.3 = (f32[896,1024]{1,0:T(8,128)}, f32[8,256]{1,0:T(8,128)S(1)}) custom-call(s32[2]{0:T(128)S(1)} %get-tuple-element.132.order, s32[16]{0:T(128)S(1)} %reshape.487.starts, s32[128]{0:T(128)S(1)} %select_n.242.pat, bf16[256,2048]{1,0:T(8,128)(2,1)S(1)} %copy-done.2, bf16[256,2048]{1,0:T(8,128)(2,1)S(1)} %collective-permute-done.2.refs_1_, ...), custom_call_target="tpu_custom_call" | custom-call | flops 1 | bytes 1 | tf_op jit(solution)/shard_map/pair_grad/pallas_call | solution.py:425
  110.8 3.8 %fusion.33 = (f32[448,1024]{1,0:T(8,128)}, f16[448,1024]{1,0:T(8,128)(2,1)S(1)}) fusion(f32[896,1024]{1,0:T(8,128)} %get-tuple-element.76, f32[]{:T(128)S(6)} %exp2.45), kind=kLoop, calls=%fused_computation.151 | loop fusion | flops 917504 | bytes 6422532 | tf_op jit(solution)/shard_map/slice | solution.py:458
  119.3 3.8 %all-to-all-start = ((f16[8,256,128]{2,1,0:T(8,128)(2,1)}), f16[8,256,128]{2,1,0:T(8,128)(2,1)S(1)}, u32[]{:S(2)}, u32[]{:S(2)}) async-start(f16[8,256,128]{2,1,0:T(8,128)(2,1)} %bitcast.13), calls=%async_computation | async-start | bytes 1048576 | tf_op jit(solution)/shard_map/all_to_all | solution.py:496
  133.7 3.8 %all-to-all-done = f16[8,256,128]{2,1,0:T(8,128)(2,1)S(1)} async-done(((f16[8,256,128]{2,1,0:T(8,128)(2,1)}), f16[8,256,128]{2,1,0:T(8,128)(2,1)S(1)}, u32[]{:S(2)}, u32[]{:S(2)}) %all-to-all-start) | async-done | bytes 524320 | tf_op jit(solution)/shard_map/all_to_all | solution.py:496
  138.4 4.1 %all-to-all-start.1 = ((f16[8,256,128]{2,1,0:T(8,128)(2,1)}), f16[8,256,128]{2,1,0:T(8,128)(2,1)}, u32[]{:S(2)}, u32[]{:S(2)}) async-start(f16[8,256,128]{2,1,0:T(8,128)(2,1)} %broadcast_in_dim.61), calls=%async_computation.1 | async-start | bytes 1048576 | tf_op jit(solution)/shard_map/all_to_all | solution.py:305
  147.1 2.4 %collective-permute-start.21 = (f16[464,1024]{1,0:T(8,128)(2,1)}, f16[464,1024]{1,0:T(8,128)(2,1)}, u32[]{:S(2)}, u32[]{:S(2)}) collective-permute-start(f16[464,1024]{1,0:T(8,128)(2,1)} %concatenate.84), channel_id=1, source_target_pairs={{0,16},{4,20},{8,24},{12,28},{16,0},{20,4},{24,8},{28,12},{1,17},{... | collective-permute-start | bytes 2850824 | tf_op jit(solution)/shard_map/ppermute | solution.py:299
  152.6 4.3 %sketch_gram.1.ss_ref = f32[128,128]{1,0:T(8,128)S(1)} custom-call(bf16[64,128,128]{2,1,0:T(8,128)(2,1)S(1)} %get-tuple-element.97.sh_ref.refs_2_, bf16[64,128,128]{2,1,0:T(8,128)(2,1)S(1)} %get-tuple-element.98.sl_ref.refs_3_), custom_call_target="tpu_custom_call" | custom-call | flops 1 | bytes 1 | tf_op jit(solution)/shard_map/sketch_gram/pallas_call | solution.py:533
  163.9 3.4 %collective-permute-done.18 = f32[128,256]{1,0:T(8,128)S(1)} collective-permute-done((f32[128,256]{1,0:T(8,128)S(1)}, f32[128,256]{1,0:T(8,128)S(1)}, u32[]{:S(2)}, u32[]{:S(2)}) %collective-permute-start.18) | collective-permute-done | bytes 131104 | tf_op jit(solution)/shard_map/ppermute | solution.py:299
  168.8 11.0 %input_grad.1 = bf16[256,3584]{1,0:T(8,128)(2,1)} custom-call(s32[224]{0:T(256)S(1)} %reshape.490.pat, bf16[256,2048]{1,0:T(8,128)(2,1)S(1)} %copy-done.2, bf16[256,2048]{1,0:T(8,128)(2,1)S(1)} %copy-done.4, bf16[256,2048]{1,0:T(8,128)(2,1)S(1)} %copy-done.6, bf16[256,2048]{1,0:T(8,128)(2,1)} %collective-permute-done.5.refs_3_, bf16[3584,1024]{1,0:T(8,128)(2,1)} %bitcast.47), custom_call_target="tpu_custom_call" | custom-call | flops 1 | bytes 1 | tf_op jit(solution)/shard_map/input_grad/pallas_call | solution.py:557
  181.4 16.0 %mixing.1.refs_1_ = f32[256,256]{1,0:T(8,128)S(1)} custom-call(f32[128,128]{1,0:T(8,128)S(1)} %sketch_gram.1.ss_ref, f32[128,256]{1,0:T(8,128)S(1)} %add.323.cross_ref), custom_call_target="tpu_custom_call" | custom-call | flops 1 | bytes 1 | tf_op jit(solution)/shard_map/mixing/pallas_call | solution.py:576
  199.1 3.8 %add_multiply_fusion.refs_0_ = f32[448,1024]{1,0:T(8,128)} fusion(f32[448,1024]{1,0:T(8,128)} %get-tuple-element.93, f16[464,1024]{1,0:T(8,128)(2,1)} %collective-permute-done.21, f16[464,1024]{1,0:T(8,128)(2,1)} %collective-permute-done.20, f32[1024]{0:T(1024)S(1)} %bitcast.58, f32[1024]{0:T(1024)S(1)} %bitcast.59), kind=kLoop, calls=%fused_computation.8 | loop fusion | flops 3211264 | bytes 5513216 | tf_op jit(solution)/shard_map/mul | solution.py:595
  206.5 9.5 %direction.1 = f32[448,8,128]{2,1,0:T(8,128)} custom-call(s32[4]{0:T(128)S(1)} %pad_add_fusion.2.starts, s32[32]{0:T(128)S(1)} %select_n.260.pat, f32[448,1024]{1,0:T(8,128)} %add_multiply_fusion.refs_0_, f32[256,256]{1,0:T(8,128)S(1)} %mixing.1.refs_1_, bf16[64,128,128]{2,1,0:T(8,128)(2,1)} %copy-done.1, bf16[64,128,128]{2,1,0:T(8,128)(2,1)} %copy-done, ...), custom_call_target="tpu_custom_call" | custom-call | flops 1 | bytes 1 | tf_op jit(solution)/shard_map/direction/pallas_call | solution.py:599
  (157 shorter events, 63.8 us)
Async XLA Ops:
  2.6 7.6 %collective-permute-start.3 = (f16[1,704,128]{2,1,0:T(8,128)(2,1)S(1)}, f16[1,704,128]{2,1,0:T(8,128)(2,1)S(1)}, u32[]{:S(2)}, u32[]{:S(2)}) collective-permute-start(f16[1,704,128]{2,1,0:T(8,128)(2,1)S(1)} %maximum_bitcast_fusion), channel_id=1, source_target_pairs={{0,8},{4,12},{8,0},{12,4},{16,24},{20,28},{24,16},{28,20},{1,9},{5... | collective-permute-start | bytes 540680 | tf_op jit(solution)/shard_map/ppermute | solution.py:299
  10.3 19.0 %collective-permute-start.4 = (f16[2,704,128]{2,1,0:T(8,128)(2,1)S(1)}, f16[2,704,128]{2,1,0:T(8,128)(2,1)S(1)}, u32[]{:S(2)}, u32[]{:S(2)}) collective-permute-start(f16[2,704,128]{2,1,0:T(8,128)(2,1)S(1)} %pad_maximum_fusion.3), channel_id=1, source_target_pairs={{0,16},{4,20},{8,24},{12,28},{16,0},{20,4},{24,8},{28,12},{1,17},{... | collective-permute-start | bytes 1081352 | tf_op jit(solution)/shard_map/ppermute | solution.py:299
  13.1 18.4 %collective-permute-start.2 = (bf16[256,2048]{1,0:T(8,128)(2,1)}, bf16[256,2048]{1,0:T(8,128)(2,1)S(1)}, u32[]{:S(2)}, u32[]{:S(2)}) collective-permute-start(bf16[256,2048]{1,0:T(8,128)(2,1)} %refs_0_.7), channel_id=1, source_target_pairs={{0,1},{1,0},{2,3},{3,2},{4,5},{5,4},{6,7},{7,6},{8,9},{9,8},{10,11... | collective-permute-start | bytes 3145736 | tf_op jit(solution)/shard_map/ppermute | solution.py:299
  13.1 26.3 %collective-permute-start.1 = (bf16[256,2048]{1,0:T(8,128)(2,1)}, bf16[256,2048]{1,0:T(8,128)(2,1)}, u32[]{:S(2)}, u32[]{:S(2)}) collective-permute-start(bf16[256,2048]{1,0:T(8,128)(2,1)} %refs_0_.7), channel_id=1, source_target_pairs={{0,4},{4,0},{8,12},{12,8},{16,20},{20,16},{24,28},{28,24},{1,5},{5... | collective-permute-start | bytes 3145736 | tf_op jit(solution)/shard_map/ppermute | solution.py:299
  14.7 25.5 %collective-permute-start = (bf16[256,2048]{1,0:T(8,128)(2,1)}, bf16[256,2048]{1,0:T(8,128)(2,1)S(1)}, u32[]{:S(2)}, u32[]{:S(2)}) collective-permute-start(bf16[256,2048]{1,0:T(8,128)(2,1)} %refs_0_.7), channel_id=1, source_target_pairs={{0,2},{1,3},{2,0},{3,1},{4,6},{5,7},{6,4},{7,5},{8,10},{9,11},{10,... | collective-permute-start | bytes 3145736 | tf_op jit(solution)/shard_map/ppermute | solution.py:299
  30.4 24.1 %collective-permute-start.6 = (f16[4,704,128]{2,1,0:T(8,128)(2,1)}, f16[4,704,128]{2,1,0:T(8,128)(2,1)}, u32[]{:S(2)}, u32[]{:S(2)}) collective-permute-start(f16[4,704,128]{2,1,0:T(8,128)(2,1)} %pad_maximum_fusion.1), channel_id=1, source_target_pairs={{0,4},{4,0},{8,12},{12,8},{16,20},{20,16},{24,28},{28,24},{1,5},{5... | collective-permute-start | bytes 2162696 | tf_op jit(solution)/shard_map/ppermute | solution.py:299
  40.2 33.7 %collective-permute-start.8 = (bf16[256,2048]{1,0:T(8,128)(2,1)}, bf16[256,2048]{1,0:T(8,128)(2,1)}, u32[]{:S(2)}, u32[]{:S(2)}) collective-permute-start(bf16[256,2048]{1,0:T(8,128)(2,1)} %collective-permute-done.1.refs_4_), channel_id=1, source_target_pairs={{0,1},{1,0},{2,3},{3,2},{4,5},{5,4},{6,7},{7,6},{8,9},{9,8},{10,11... | collective-permute-start | bytes 3145736 | tf_op jit(solution)/shard_map/ppermute | solution.py:299
  40.2 33.7 %collective-permute-start.7 = (bf16[256,2048]{1,0:T(8,128)(2,1)}, bf16[256,2048]{1,0:T(8,128)(2,1)}, u32[]{:S(2)}, u32[]{:S(2)}) collective-permute-start(bf16[256,2048]{1,0:T(8,128)(2,1)} %collective-permute-done.1.refs_4_), channel_id=1, source_target_pairs={{0,2},{1,3},{2,0},{3,1},{4,6},{5,7},{6,4},{7,5},{8,10},{9,11},{10,... | collective-permute-start | bytes 3145736 | tf_op jit(solution)/shard_map/ppermute | solution.py:299
  41.7 17.5 %collective-permute-start.5 = (bf16[256,2048]{1,0:T(8,128)(2,1)S(1)}, bf16[256,2048]{1,0:T(8,128)(2,1)}, u32[]{:S(2)}, u32[]{:S(2)}) collective-permute-start(bf16[256,2048]{1,0:T(8,128)(2,1)S(1)} %collective-permute-done.refs_2_), channel_id=1, source_target_pairs={{0,1},{1,0},{2,3},{3,2},{4,5},{5,4},{6,7},{7,6},{8,9},{9,8},{10,11... | collective-permute-start | bytes 3145736 | tf_op jit(solution)/shard_map/ppermute | solution.py:299
  54.5 22.3 %collective-permute-start.9 = (bf16[4,448,256]{2,1,0:T(8,128)(2,1)}, bf16[4,448,256]{2,1,0:T(8,128)(2,1)}, u32[]{:S(2)}, u32[]{:S(2)}) collective-permute-start(bf16[4,448,256]{2,1,0:T(8,128)(2,1)} %get-tuple-element.62), channel_id=1, source_target_pairs={{0,4},{4,0},{8,12},{12,8},{16,20},{20,16},{24,28},{28,24},{1,5},{5... | collective-permute-start | bytes 2752520 | tf_op jit(solution)/shard_map/ppermute | solution.py:299
  80.8 14.6 %collective-permute-start.12 = (f16[16,128,128]{2,1,0:T(8,128)(2,1)}, f16[16,128,128]{2,1,0:T(8,128)(2,1)}, u32[]{:S(2)}, u32[]{:S(2)}) collective-permute-start(f16[16,128,128]{2,1,0:T(8,128)(2,1)} %get-tuple-element.108), channel_id=1, source_target_pairs={{0,1},{1,0},{2,3},{3,2},{4,5},{5,4},{6,7},{7,6},{8,9},{9,8},{10,11... | collective-permute-start | bytes 1572872 | tf_op jit(solution)/shard_map/ppermute | solution.py:299
  81.3 14.1 %collective-permute-start.11 = (f16[16,128,128]{2,1,0:T(8,128)(2,1)}, f16[16,128,128]{2,1,0:T(8,128)(2,1)}, u32[]{:S(2)}, u32[]{:S(2)}) collective-permute-start(f16[16,128,128]{2,1,0:T(8,128)(2,1)} %get-tuple-element.109), channel_id=1, source_target_pairs={{0,1},{1,0},{2,3},{3,2},{4,5},{5,4},{6,7},{7,6},{8,9},{9,8},{10,11... | collective-permute-start | bytes 1572872 | tf_op jit(solution)/shard_map/ppermute | solution.py:299
  95.4 23.8 %collective-permute-start.14 = (f16[464,1024]{1,0:T(8,128)(2,1)}, f16[464,1024]{1,0:T(8,128)(2,1)}, u32[]{:S(2)}, u32[]{:S(2)}) collective-permute-start(f16[464,1024]{1,0:T(8,128)(2,1)} %concatenate.82), channel_id=1, source_target_pairs={{0,8},{4,12},{8,0},{12,4},{16,24},{20,28},{24,16},{28,20},{1,9},{5... | collective-permute-start | bytes 2850824 | tf_op jit(solution)/shard_map/ppermute | solution.py:299
  99.7 16.0 %collective-permute-start.13 = (f16[16,128,128]{2,1,0:T(8,128)(2,1)}, f16[16,128,128]{2,1,0:T(8,128)(2,1)}, u32[]{:S(2)}, u32[]{:S(2)}) collective-permute-start(f16[16,128,128]{2,1,0:T(8,128)(2,1)} %get-tuple-element.73), channel_id=1, source_target_pairs={{0,2},{1,3},{2,0},{3,1},{4,6},{5,7},{6,4},{7,5},{8,10},{9,11},{10,... | collective-permute-start | bytes 1572872 | tf_op jit(solution)/shard_map/ppermute | solution.py:299
  119.3 18.2 %all-to-all-start = ((f16[8,256,128]{2,1,0:T(8,128)(2,1)}), f16[8,256,128]{2,1,0:T(8,128)(2,1)S(1)}, u32[]{:S(2)}, u32[]{:S(2)}) async-start(f16[8,256,128]{2,1,0:T(8,128)(2,1)} %bitcast.13), calls=%async_computation | async-start | bytes 1048576 | tf_op jit(solution)/shard_map/all_to_all | solution.py:496
  126.1 16.6 %collective-permute-start.16 = (f16[16,128,128]{2,1,0:T(8,128)(2,1)S(1)}, f16[16,128,128]{2,1,0:T(8,128)(2,1)S(1)}, u32[]{:S(2)}, u32[]{:S(2)}) collective-permute-start(f16[16,128,128]{2,1,0:T(8,128)(2,1)S(1)} %bitcast.51), channel_id=1, source_target_pairs={{0,2},{1,3},{2,0},{3,1},{4,6},{5,7},{6,4},{7,5},{8,10},{9,11},{10,... | collective-permute-start | bytes 1572872 | tf_op jit(solution)/shard_map/ppermute | solution.py:299
  138.4 20.2 %all-to-all-start.1 = ((f16[8,256,128]{2,1,0:T(8,128)(2,1)}), f16[8,256,128]{2,1,0:T(8,128)(2,1)}, u32[]{:S(2)}, u32[]{:S(2)}) async-start(f16[8,256,128]{2,1,0:T(8,128)(2,1)} %broadcast_in_dim.61), calls=%async_computation.1 | async-start | bytes 1048576 | tf_op jit(solution)/shard_map/all_to_all | solution.py:305
  142.7 6.8 %collective-permute-start.15 = (f16[16,128,128]{2,1,0:T(8,128)(2,1)S(1)}, f16[16,128,128]{2,1,0:T(8,128)(2,1)S(1)}, u32[]{:S(2)}, u32[]{:S(2)}) collective-permute-start(f16[16,128,128]{2,1,0:T(8,128)(2,1)S(1)} %bitcast.52), channel_id=1, source_target_pairs={{0,1},{1,0},{2,3},{3,2},{4,5},{5,4},{6,7},{7,6},{8,9},{9,8},{10,11... | collective-permute-start | bytes 1572872 | tf_op jit(solution)/shard_map/ppermute | solution.py:299
  142.7 7.6 %collective-permute-start.17 = (f16[16,128,128]{2,1,0:T(8,128)(2,1)S(1)}, f16[16,128,128]{2,1,0:T(8,128)(2,1)}, u32[]{:S(2)}, u32[]{:S(2)}) collective-permute-start(f16[16,128,128]{2,1,0:T(8,128)(2,1)S(1)} %collective-permute-done.16), channel_id=1, source_target_pairs={{0,1},{1,0},{2,3},{3,2},{4,5},{5,4},{6,7},{7,6},{8,9},{9,8},{10,11... | collective-permute-start | bytes 1572872 | tf_op jit(solution)/shard_map/ppermute | solution.py:299
  143.9 54.5 %collective-permute-start.20 = (f16[464,1024]{1,0:T(8,128)(2,1)}, f16[464,1024]{1,0:T(8,128)(2,1)}, u32[]{:S(2)}, u32[]{:S(2)}) collective-permute-start(f16[464,1024]{1,0:T(8,128)(2,1)} %concatenate.83), channel_id=1, source_target_pairs={{0,8},{4,12},{8,0},{12,4},{16,24},{20,28},{24,16},{28,20},{1,9},{5... | collective-permute-start | bytes 2850824 | tf_op jit(solution)/shard_map/ppermute | solution.py:299
  147.1 50.5 %collective-permute-start.21 = (f16[464,1024]{1,0:T(8,128)(2,1)}, f16[464,1024]{1,0:T(8,128)(2,1)}, u32[]{:S(2)}, u32[]{:S(2)}) collective-permute-start(f16[464,1024]{1,0:T(8,128)(2,1)} %concatenate.84), channel_id=1, source_target_pairs={{0,16},{4,20},{8,24},{12,28},{16,0},{20,4},{24,8},{28,12},{1,17},{... | collective-permute-start | bytes 2850824 | tf_op jit(solution)/shard_map/ppermute | solution.py:299
  162.3 5.0 %collective-permute-start.18 = (f32[128,256]{1,0:T(8,128)S(1)}, f32[128,256]{1,0:T(8,128)S(1)}, u32[]{:S(2)}, u32[]{:S(2)}) collective-permute-start(f32[128,256]{1,0:T(8,128)S(1)} %cross_gram.1), channel_id=1, source_target_pairs={{0,2},{1,3},{2,0},{3,1},{4,6},{5,7},{6,4},{7,5},{8,10},{9,11},{10,... | collective-permute-start | bytes 393224 | tf_op jit(solution)/shard_map/ppermute | solution.py:299
  179.8 24.4 %collective-permute-start.23 = (f16[16,128,128]{2,1,0:T(8,128)(2,1)}, f16[16,128,128]{2,1,0:T(8,128)(2,1)S(1)}, u32[]{:S(2)}, u32[]{:S(2)}) collective-permute-start(f16[16,128,128]{2,1,0:T(8,128)(2,1)} %bitcast.15), channel_id=1, source_target_pairs={{0,2},{1,3},{2,0},{3,1},{4,6},{5,7},{6,4},{7,5},{8,10},{9,11},{10,... | collective-permute-start | bytes 1572872 | tf_op jit(solution)/shard_map/ppermute | solution.py:299
  181.4 23.5 %collective-permute-start.22 = (f16[16,128,128]{2,1,0:T(8,128)(2,1)}, f16[16,128,128]{2,1,0:T(8,128)(2,1)S(1)}, u32[]{:S(2)}, u32[]{:S(2)}) collective-permute-start(f16[16,128,128]{2,1,0:T(8,128)(2,1)} %bitcast.15), channel_id=1, source_target_pairs={{0,1},{1,0},{2,3},{3,2},{4,5},{5,4},{6,7},{7,6},{8,9},{9,8},{10,11... | collective-permute-start | bytes 1572872 | tf_op jit(solution)/shard_map/ppermute | solution.py:299
  (24 other events, 278.8 us)

commit v9 on v8

--- a/solution.py
+++ b/solution.py
@@ -317,6 +317,7 @@
     if n_dp > 8:
         early, order, bits = over_dp(early[0]), jnp.arange(n_dp, dtype=jnp.int32), []
     hidden_in, weights_in = hidden, weights
+    x_part, y_part = swap(cotangent, "mp", 2), swap(cotangent, "dp", 1)
     for bit in bits:
         early = jnp.concatenate([early, swap(early, "dp", bit)], axis=0)
         order = jnp.concatenate([order, jnp.bitwise_xor(order, bit)])
@@ -328,8 +329,8 @@
     hid_send = lax.dynamic_index_in_dim(hid_parts, 1 - side, 1, keepdims=False)
     weights_2d = weights_in.reshape(mp_rows, slots * blk)
     if n_dp <= 8:
-        early, hid_own, hid_send, weights_2d = lax.optimization_barrier(
-            (early, hid_own, hid_send, weights_2d)
+        early, hid_own, hid_send, weights_2d, x_part, y_part = lax.optimization_barrier(
+            (early, hid_own, hid_send, weights_2d, x_part, y_part)
         )
         early = [early, swap(early, "dp", 1)]
         order = jnp.concatenate([order, jnp.bitwise_xor(order, 1)])
@@ -348,7 +349,6 @@
         sk_own = sk_own.reshape(n_dp, rank, width)
     else:
         sk_own = sk_own.reshape(per_shard, rank, blk)
-    x_part, y_part = swap(cotangent, "mp", 2), swap(cotangent, "dp", 1)
     x_half, y_own, core_half, hid_t, hid_own, weights_2d = (
         lax.optimization_barrier(
             (

time: 217 us -> 213 us (0.982)
  starting transfers between devices: 34.3 us -> 31.7 us
    ppermute x25, starting transfers between devices: 26.4 us -> 21.8 us  [swap(): return lax.ppermute(x, axis, [(i, i ^ bit) for i in range(size)])]
    ppermute x25, waiting for transfers between devices: 35.7 us -> 33.1 us  [swap(): return lax.ppermute(x, axis, [(i, i ^ bit) for i in range(size)])]
    unnamed x44 -> x42, local copies, waits for them, and re-layouts: 11.9 us -> 11.9 us
  transfers between devices with their start and end apart: 27 -> 27, of which waited for: 12 -> 11; matrix products, arithmetic and copies ran while one was open for 27% -> 28% of each run, Pallas kernels for 30% -> 30%
where the time goes in v9:
time: 213 us; the launch traced here: 212 us
  Pallas kernels  74.2 us (35%)
  waiting for transfers between devices  38 us (18%)
  other arithmetic  36.6 us (17%)
  starting transfers between devices  31.7 us (15%)
  local copies, waits for them, and re-layouts  27.2 us (13%)
  between operations  4.23 us (2%)
    ppermute x25, waiting for transfers between devices, swap(): return lax.ppermute(x, axis, [(i, i ^ bit) for i in range(size)])  33.1 us
    ppermute x25, starting transfers between devices, swap(): return lax.ppermute(x, axis, [(i, i ^ bit) for i in range(size)])  21.8 us
    pallas_call x2, Pallas kernels, pair_grad(): pl.pallas_call(functools.partial(grad_kernel, n_mp, per_shard, blk, windo...  16.4 us
    pallas_call x1, Pallas kernels, per_device(): pl.pallas_call(mixing_kernel, in_specs=[VMEM] * 2, out_specs=VMEM, out_sh...  16 us
    pallas_call x1, Pallas kernels, per_device(): pl.pallas_call(functools.partial(compress_kernel, n_mp, per_shard, 1.0 /...  14.7 us
    unnamed x42, local copies, waits for them, and re-layouts  11.9 us
    pallas_call x1, Pallas kernels, per_device(): pl.pallas_call(functools.partial(input_grad_kernel, n_mp, per_shard, blk,...  11 us
    pallas_call x1, Pallas kernels, per_device(): pl.pallas_call(functools.partial(direction_kernel, sk_per, window, n_wind...  9.5 us
  transfers between devices with their start and end apart: 27, of which 11 were waited for; matrix products, arithmetic and copies ran while one was open for 28% of the time, Pallas kernels for 30%

profile of v9, /device:TPU:0, one launch (start us, length us, event | category | flops | bytes accessed | tf_op | source)
XLA Modules:
  0.0 212.0 jit_solution(674498378823369012)
XLA Ops:
  0.6 3.0 %collective-permute-start.3 = (bf16[256,2048]{1,0:T(8,128)(2,1)}, bf16[256,2048]{1,0:T(8,128)(2,1)}, u32[]{:S(2)}, u32[]{:S(2)}) collective-permute-start(bf16[256,2048]{1,0:T(8,128)(2,1)} %refs_0_.7), channel_id=1, source_target_pairs={{0,4},{4,0},{8,12},{12,8},{16,20},{20,16},{24,28},{28,24},{1,5},{5... | collective-permute-start | bytes 3145736 | tf_op jit(solution)/shard_map/ppermute | solution.py:299
  8.7 4.2 %collective-permute-done = f16[1,704,128]{2,1,0:T(8,128)(2,1)S(1)} collective-permute-done((f16[1,704,128]{2,1,0:T(8,128)(2,1)S(1)}, f16[1,704,128]{2,1,0:T(8,128)(2,1)S(1)}, u32[]{:S(2)}, u32[]{:S(2)}) %collective-permute-start) | collective-permute-done | bytes 180256 | tf_op jit(solution)/shard_map/ppermute | solution.py:299
  13.0 2.7 %collective-permute-start.1 = (f16[2,704,128]{2,1,0:T(8,128)(2,1)S(1)}, f16[2,704,128]{2,1,0:T(8,128)(2,1)S(1)}, u32[]{:S(2)}, u32[]{:S(2)}) collective-permute-start(f16[2,704,128]{2,1,0:T(8,128)(2,1)S(1)} %pad_maximum_fusion.3), channel_id=1, source_target_pairs={{0,16},{4,20},{8,24},{12,28},{16,0},{20,4},{24,8},{28,12},{1,17},{... | collective-permute-start | bytes 1081352 | tf_op jit(solution)/shard_map/ppermute | solution.py:299
  15.7 3.8 %copy.23 = bf16[256,3584]{0,1:T(8,128)(2,1)} copy(bf16[256,3584]{1,0:T(8,128)(2,1)} %param.9) | data formatting | bytes 3670016 | tf_op jit(solution)/shard_map/optimization_barrier | solution.py:325
  19.5 8.0 %copy.32 = bf16[448,8,8,128]{3,1,2,0:T(8,128)(2,1)} copy(bf16[448,8,8,128]{3,2,1,0:T(8,128)(2,1)} %bitcast.50) | data formatting | bytes 14680064
  33.6 15.3 %collective-permute-done.6 = f16[4,704,128]{2,1,0:T(8,128)(2,1)} collective-permute-done((f16[4,704,128]{2,1,0:T(8,128)(2,1)}, f16[4,704,128]{2,1,0:T(8,128)(2,1)}, u32[]{:S(2)}, u32[]{:S(2)}) %collective-permute-start.6) | collective-permute-done | bytes 720928 | tf_op jit(solution)/shard_map/ppermute | solution.py:299
  52.6 14.7 %compress.1 = f32[64,128,128]{2,1,0:T(8,128)} custom-call(s32[224]{0:T(256)S(1)} %reshape.490.pat, s32[224]{0:T(256)S(1)} %reshape.491.pat_out, s32[8]{0:T(128)S(1)} %broadcast_xor_fusion.1.places, bf16[256,2048]{1,0:T(8,128)(2,1)S(1)} %copy-done.2, bf16[256,2048]{1,0:T(8,128)(2,1)S(1)} %collective-permute-done.4.refs_1_, ...), custom_call_target="tpu_custom_call" | custom-call | flops 1 | bytes 1 | tf_op jit(solution)/shard_map/compress/pallas_call | solution.py:379
  69.6 2.7 %convert.22 = f16[64,128,128]{2,1,0:T(8,128)(2,1)S(1)} convert(f32[64,128,128]{2,1,0:T(8,128)} %compress.1) | non-fusion elementwise | flops 1048576 | bytes 6291456 | tf_op jit(solution)/shard_map/convert.7
  75.5 8.2 %pair_grad.2 = (f32[896,1024]{1,0:T(8,128)}, f32[8,256]{1,0:T(8,128)S(1)}) custom-call(s32[2]{0:T(128)S(1)} %get-tuple-element.137.order, s32[16]{0:T(128)S(1)} %reshape.487.starts, s32[128]{0:T(128)S(1)} %select_n.242.pat, bf16[256,2048]{1,0:T(8,128)(2,1)S(1)} %copy-done.2, bf16[256,2048]{1,0:T(8,128)(2,1)S(1)} %collective-permute-done.4.refs_1_, ...), custom_call_target="tpu_custom_call" | custom-call | flops 1 | bytes 1 | tf_op jit(solution)/shard_map/pair_grad/pallas_call | solution.py:425
  88.1 3.0 %collective-permute-start.14 = (f16[464,1024]{1,0:T(8,128)(2,1)}, f16[464,1024]{1,0:T(8,128)(2,1)}, u32[]{:S(2)}, u32[]{:S(2)}) collective-permute-start(f16[464,1024]{1,0:T(8,128)(2,1)} %concatenate.82), channel_id=1, source_target_pairs={{0,8},{4,12},{8,0},{12,4},{16,24},{20,28},{24,16},{28,20},{1,9},{5... | collective-permute-start | bytes 2850824 | tf_op jit(solution)/shard_map/ppermute | solution.py:299
  91.1 2.7 %convert_add_fusion.1 = (f32[16,128,128]{2,1,0:T(8,128)}, f16[16,128,128]{2,1,0:T(8,128)(2,1)}) fusion(f16[16,128,128]{2,1,0:T(8,128)(2,1)} %collective-permute-done.12, f32[64,128,128]{2,1,0:T(8,128)S(1)} %copy-done.11, f16[16,128,128]{2,1,0:T(8,128)(2,1)} %collective-permute-done.11), kind=kLoop, calls=%fused_computation.32 | loop fusion | flops 1310720 | bytes 4718592 | tf_op jit(solution)/shard_map/add | solution.py:484
  94.3 8.2 %pair_grad.3 = (f32[896,1024]{1,0:T(8,128)}, f32[8,256]{1,0:T(8,128)S(1)}) custom-call(s32[2]{0:T(128)S(1)} %get-tuple-element.136.order, s32[16]{0:T(128)S(1)} %reshape.487.starts, s32[128]{0:T(128)S(1)} %select_n.242.pat, bf16[256,2048]{1,0:T(8,128)(2,1)S(1)} %copy-done.2, bf16[256,2048]{1,0:T(8,128)(2,1)S(1)} %collective-permute-done.4.refs_1_, ...), custom_call_target="tpu_custom_call" | custom-call | flops 1 | bytes 1 | tf_op jit(solution)/shard_map/pair_grad/pallas_call | solution.py:425
  103.8 3.8 %fusion.33 = (f32[448,1024]{1,0:T(8,128)}, f16[448,1024]{1,0:T(8,128)(2,1)S(1)}) fusion(f32[896,1024]{1,0:T(8,128)} %get-tuple-element.80, f32[]{:T(128)S(6)} %exp2.45), kind=kLoop, calls=%fused_computation.151 | loop fusion | flops 917504 | bytes 6422532 | tf_op jit(solution)/shard_map/slice | solution.py:458
  113.1 5.8 %all-to-all-start = ((f16[8,256,128]{2,1,0:T(8,128)(2,1)}), f16[8,256,128]{2,1,0:T(8,128)(2,1)S(1)}, u32[]{:S(2)}, u32[]{:S(2)}) async-start(f16[8,256,128]{2,1,0:T(8,128)(2,1)} %bitcast.13), calls=%async_computation | async-start | bytes 1048576 | tf_op jit(solution)/shard_map/all_to_all | solution.py:496
  128.5 4.8 %all-to-all-done = f16[8,256,128]{2,1,0:T(8,128)(2,1)S(1)} async-done(((f16[8,256,128]{2,1,0:T(8,128)(2,1)}), f16[8,256,128]{2,1,0:T(8,128)(2,1)S(1)}, u32[]{:S(2)}, u32[]{:S(2)}) %all-to-all-start) | async-done | bytes 524320 | tf_op jit(solution)/shard_map/all_to_all | solution.py:496
  134.3 4.1 %all-to-all-start.1 = ((f16[8,256,128]{2,1,0:T(8,128)(2,1)}), f16[8,256,128]{2,1,0:T(8,128)(2,1)}, u32[]{:S(2)}, u32[]{:S(2)}) async-start(f16[8,256,128]{2,1,0:T(8,128)(2,1)} %broadcast_in_dim.61), calls=%async_computation.1 | async-start | bytes 1048576 | tf_op jit(solution)/shard_map/all_to_all | solution.py:305
  142.9 2.4 %collective-permute-start.21 = (f16[464,1024]{1,0:T(8,128)(2,1)}, f16[464,1024]{1,0:T(8,128)(2,1)}, u32[]{:S(2)}, u32[]{:S(2)}) collective-permute-start(f16[464,1024]{1,0:T(8,128)(2,1)} %concatenate.84), channel_id=1, source_target_pairs={{0,16},{4,20},{8,24},{12,28},{16,0},{20,4},{24,8},{28,12},{1,17},{... | collective-permute-start | bytes 2850824 | tf_op jit(solution)/shard_map/ppermute | solution.py:299
  146.2 2.6 %fusion = (bf16[64,128,128]{2,1,0:T(8,128)(2,1)S(1)}, bf16[64,128,128]{2,1,0:T(8,128)(2,1)S(1)}) fusion(f16[16,128,128]{2,1,0:T(8,128)(2,1)} %collective-permute-done.17, f16[16,128,128]{2,1,0:T(8,128)(2,1)} %collective-permute-done.16, f16[16,128,128]{2,1,0:T(8,128)(2,1)} %copy-done.15, f16[16,128,128]{2,1,0:T(8,128)(2,1)} %bitcast.54), kind=kLoop, calls=%fused_computation.6 | loop fusion | flops 8388608 | bytes 6291456 | tf_op jit(solution)/shard_map/convert_element_type | solution.py:46
  148.7 4.3 %sketch_gram.1.ss_ref = f32[128,128]{1,0:T(8,128)S(1)} custom-call(bf16[64,128,128]{2,1,0:T(8,128)(2,1)S(1)} %get-tuple-element.101.sh_ref.refs_2_, bf16[64,128,128]{2,1,0:T(8,128)(2,1)S(1)} %get-tuple-element.102.sl_ref.refs_3_), custom_call_target="tpu_custom_call" | custom-call | flops 1 | bytes 1 | tf_op jit(solution)/shard_map/sketch_gram/pallas_call | solution.py:533
  158.9 4.3 %collective-permute-done.18 = f32[128,256]{1,0:T(8,128)S(1)} collective-permute-done((f32[128,256]{1,0:T(8,128)S(1)}, f32[128,256]{1,0:T(8,128)S(1)}, u32[]{:S(2)}, u32[]{:S(2)}) %collective-permute-start.18) | collective-permute-done | bytes 131104 | tf_op jit(solution)/shard_map/ppermute | solution.py:299
  164.7 11.0 %input_grad.1 = bf16[256,3584]{1,0:T(8,128)(2,1)} custom-call(s32[224]{0:T(256)S(1)} %reshape.490.pat, bf16[256,2048]{1,0:T(8,128)(2,1)S(1)} %copy-done.2, bf16[256,2048]{1,0:T(8,128)(2,1)S(1)} %copy-done.6, bf16[256,2048]{1,0:T(8,128)(2,1)S(1)} %copy-done.4, bf16[256,2048]{1,0:T(8,128)(2,1)} %collective-permute-done.5.refs_3_, bf16[3584,1024]{1,0:T(8,128)(2,1)} %bitcast.47), custom_call_target="tpu_custom_call" | custom-call | flops 1 | bytes 1 | tf_op jit(solution)/shard_map/input_grad/pallas_call | solution.py:557
  176.3 16.0 %mixing.1.refs_1_ = f32[256,256]{1,0:T(8,128)S(1)} custom-call(f32[128,128]{1,0:T(8,128)S(1)} %sketch_gram.1.ss_ref, f32[128,256]{1,0:T(8,128)S(1)} %add.323.cross_ref), custom_call_target="tpu_custom_call" | custom-call | flops 1 | bytes 1 | tf_op jit(solution)/shard_map/mixing/pallas_call | solution.py:576
  194.9 3.8 %add_multiply_fusion.refs_0_ = f32[448,1024]{1,0:T(8,128)} fusion(f32[448,1024]{1,0:T(8,128)} %get-tuple-element.97, f16[464,1024]{1,0:T(8,128)(2,1)} %collective-permute-done.21, f16[464,1024]{1,0:T(8,128)(2,1)} %collective-permute-done.20, f32[1024]{0:T(1024)S(1)} %bitcast.58, f32[1024]{0:T(1024)S(1)} %bitcast.59), kind=kLoop, calls=%fused_computation.8 | loop fusion | flops 3211264 | bytes 5513216 | tf_op jit(solution)/shard_map/mul | solution.py:595
  202.3 9.5 %direction.1 = f32[448,8,128]{2,1,0:T(8,128)} custom-call(s32[4]{0:T(128)S(1)} %pad_add_fusion.2.starts, s32[32]{0:T(128)S(1)} %select_n.260.pat, f32[448,1024]{1,0:T(8,128)} %add_multiply_fusion.refs_0_, f32[256,256]{1,0:T(8,128)S(1)} %mixing.1.refs_1_, bf16[64,128,128]{2,1,0:T(8,128)(2,1)} %copy-done.1, bf16[64,128,128]{2,1,0:T(8,128)(2,1)} %copy-done, ...), custom_call_target="tpu_custom_call" | custom-call | flops 1 | bytes 1 | tf_op jit(solution)/shard_map/direction/pallas_call | solution.py:599
  (155 shorter events, 58.8 us)
Async XLA Ops:
  0.6 30.9 %collective-permute-start.3 = (bf16[256,2048]{1,0:T(8,128)(2,1)}, bf16[256,2048]{1,0:T(8,128)(2,1)}, u32[]{:S(2)}, u32[]{:S(2)}) collective-permute-start(bf16[256,2048]{1,0:T(8,128)(2,1)} %refs_0_.7), channel_id=1, source_target_pairs={{0,4},{4,0},{8,12},{12,8},{16,20},{20,16},{24,28},{28,24},{1,5},{5... | collective-permute-start | bytes 3145736 | tf_op jit(solution)/shard_map/ppermute | solution.py:299
  3.7 27.9 %collective-permute-start.2 = (bf16[256,2048]{1,0:T(8,128)(2,1)}, bf16[256,2048]{1,0:T(8,128)(2,1)S(1)}, u32[]{:S(2)}, u32[]{:S(2)}) collective-permute-start(bf16[256,2048]{1,0:T(8,128)(2,1)} %refs_0_.7), channel_id=1, source_target_pairs={{0,2},{1,3},{2,0},{3,1},{4,6},{5,7},{6,4},{7,5},{8,10},{9,11},{10,... | collective-permute-start | bytes 3145736 | tf_op jit(solution)/shard_map/ppermute | solution.py:299
  7.1 5.8 %collective-permute-start = (f16[1,704,128]{2,1,0:T(8,128)(2,1)S(1)}, f16[1,704,128]{2,1,0:T(8,128)(2,1)S(1)}, u32[]{:S(2)}, u32[]{:S(2)}) collective-permute-start(f16[1,704,128]{2,1,0:T(8,128)(2,1)S(1)} %maximum_bitcast_fusion), channel_id=1, source_target_pairs={{0,8},{4,12},{8,0},{12,4},{16,24},{20,28},{24,16},{28,20},{1,9},{5... | collective-permute-start | bytes 540680 | tf_op jit(solution)/shard_map/ppermute | solution.py:299
  13.0 17.5 %collective-permute-start.1 = (f16[2,704,128]{2,1,0:T(8,128)(2,1)S(1)}, f16[2,704,128]{2,1,0:T(8,128)(2,1)S(1)}, u32[]{:S(2)}, u32[]{:S(2)}) collective-permute-start(f16[2,704,128]{2,1,0:T(8,128)(2,1)S(1)} %pad_maximum_fusion.3), channel_id=1, source_target_pairs={{0,16},{4,20},{8,24},{12,28},{16,0},{20,4},{24,8},{28,12},{1,17},{... | collective-permute-start | bytes 1081352 | tf_op jit(solution)/shard_map/ppermute | solution.py:299
  15.7 16.9 %collective-permute-start.4 = (bf16[256,2048]{1,0:T(8,128)(2,1)}, bf16[256,2048]{1,0:T(8,128)(2,1)S(1)}, u32[]{:S(2)}, u32[]{:S(2)}) collective-permute-start(bf16[256,2048]{1,0:T(8,128)(2,1)} %refs_0_.7), channel_id=1, source_target_pairs={{0,1},{1,0},{2,3},{3,2},{4,5},{5,4},{6,7},{7,6},{8,9},{9,8},{10,11... | collective-permute-start | bytes 3145736 | tf_op jit(solution)/shard_map/ppermute | solution.py:299
  31.5 17.4 %collective-permute-start.6 = (f16[4,704,128]{2,1,0:T(8,128)(2,1)}, f16[4,704,128]{2,1,0:T(8,128)(2,1)}, u32[]{:S(2)}, u32[]{:S(2)}) collective-permute-start(f16[4,704,128]{2,1,0:T(8,128)(2,1)} %pad_maximum_fusion.1), channel_id=1, source_target_pairs={{0,4},{4,0},{8,12},{12,8},{16,20},{20,16},{24,28},{28,24},{1,5},{5... | collective-permute-start | bytes 2162696 | tf_op jit(solution)/shard_map/ppermute | solution.py:299
  32.6 34.6 %collective-permute-start.8 = (bf16[256,2048]{1,0:T(8,128)(2,1)}, bf16[256,2048]{1,0:T(8,128)(2,1)}, u32[]{:S(2)}, u32[]{:S(2)}) collective-permute-start(bf16[256,2048]{1,0:T(8,128)(2,1)} %collective-permute-done.3.refs_4_), channel_id=1, source_target_pairs={{0,1},{1,0},{2,3},{3,2},{4,5},{5,4},{6,7},{7,6},{8,9},{9,8},{10,11... | collective-permute-start | bytes 3145736 | tf_op jit(solution)/shard_map/ppermute | solution.py:299
  32.7 34.6 %collective-permute-start.7 = (bf16[256,2048]{1,0:T(8,128)(2,1)}, bf16[256,2048]{1,0:T(8,128)(2,1)}, u32[]{:S(2)}, u32[]{:S(2)}) collective-permute-start(bf16[256,2048]{1,0:T(8,128)(2,1)} %collective-permute-done.3.refs_4_), channel_id=1, source_target_pairs={{0,2},{1,3},{2,0},{3,1},{4,6},{5,7},{6,4},{7,5},{8,10},{9,11},{10,... | collective-permute-start | bytes 3145736 | tf_op jit(solution)/shard_map/ppermute | solution.py:299
  33.4 19.1 %collective-permute-start.5 = (bf16[256,2048]{1,0:T(8,128)(2,1)S(1)}, bf16[256,2048]{1,0:T(8,128)(2,1)}, u32[]{:S(2)}, u32[]{:S(2)}) collective-permute-start(bf16[256,2048]{1,0:T(8,128)(2,1)S(1)} %collective-permute-done.2.refs_2_), channel_id=1, source_target_pairs={{0,1},{1,0},{2,3},{3,2},{4,5},{5,4},{6,7},{7,6},{8,9},{9,8},{10,11... | collective-permute-start | bytes 3145736 | tf_op jit(solution)/shard_map/ppermute | solution.py:299
  48.9 20.6 %collective-permute-start.9 = (bf16[4,448,256]{2,1,0:T(8,128)(2,1)}, bf16[4,448,256]{2,1,0:T(8,128)(2,1)}, u32[]{:S(2)}, u32[]{:S(2)}) collective-permute-start(bf16[4,448,256]{2,1,0:T(8,128)(2,1)} %get-tuple-element.66), channel_id=1, source_target_pairs={{0,4},{4,0},{8,12},{12,8},{16,20},{20,16},{24,28},{28,24},{1,5},{5... | collective-permute-start | bytes 2752520 | tf_op jit(solution)/shard_map/ppermute | solution.py:299
  73.5 14.6 %collective-permute-start.12 = (f16[16,128,128]{2,1,0:T(8,128)(2,1)}, f16[16,128,128]{2,1,0:T(8,128)(2,1)}, u32[]{:S(2)}, u32[]{:S(2)}) collective-permute-start(f16[16,128,128]{2,1,0:T(8,128)(2,1)} %get-tuple-element.112), channel_id=1, source_target_pairs={{0,1},{1,0},{2,3},{3,2},{4,5},{5,4},{6,7},{7,6},{8,9},{9,8},{10,11... | collective-permute-start | bytes 1572872 | tf_op jit(solution)/shard_map/ppermute | solution.py:299
  74.0 14.1 %collective-permute-start.11 = (f16[16,128,128]{2,1,0:T(8,128)(2,1)}, f16[16,128,128]{2,1,0:T(8,128)(2,1)}, u32[]{:S(2)}, u32[]{:S(2)}) collective-permute-start(f16[16,128,128]{2,1,0:T(8,128)(2,1)} %get-tuple-element.113), channel_id=1, source_target_pairs={{0,1},{1,0},{2,3},{3,2},{4,5},{5,4},{6,7},{7,6},{8,9},{9,8},{10,11... | collective-permute-start | bytes 1572872 | tf_op jit(solution)/shard_map/ppermute | solution.py:299
  88.1 25.0 %collective-permute-start.14 = (f16[464,1024]{1,0:T(8,128)(2,1)}, f16[464,1024]{1,0:T(8,128)(2,1)}, u32[]{:S(2)}, u32[]{:S(2)}) collective-permute-start(f16[464,1024]{1,0:T(8,128)(2,1)} %concatenate.82), channel_id=1, source_target_pairs={{0,8},{4,12},{8,0},{12,4},{16,24},{20,28},{24,16},{28,20},{1,9},{5... | collective-permute-start | bytes 2850824 | tf_op jit(solution)/shard_map/ppermute | solution.py:299
  93.8 15.0 %collective-permute-start.13 = (f16[16,128,128]{2,1,0:T(8,128)(2,1)}, f16[16,128,128]{2,1,0:T(8,128)(2,1)}, u32[]{:S(2)}, u32[]{:S(2)}) collective-permute-start(f16[16,128,128]{2,1,0:T(8,128)(2,1)} %get-tuple-element.77), channel_id=1, source_target_pairs={{0,2},{1,3},{2,0},{3,1},{4,6},{5,7},{6,4},{7,5},{8,10},{9,11},{10,... | collective-permute-start | bytes 1572872 | tf_op jit(solution)/shard_map/ppermute | solution.py:299
  113.1 20.2 %all-to-all-start = ((f16[8,256,128]{2,1,0:T(8,128)(2,1)}), f16[8,256,128]{2,1,0:T(8,128)(2,1)S(1)}, u32[]{:S(2)}, u32[]{:S(2)}) async-start(f16[8,256,128]{2,1,0:T(8,128)(2,1)} %bitcast.13), calls=%async_computation | async-start | bytes 1048576 | tf_op jit(solution)/shard_map/all_to_all | solution.py:496
  122.0 16.6 %collective-permute-start.16 = (f16[16,128,128]{2,1,0:T(8,128)(2,1)S(1)}, f16[16,128,128]{2,1,0:T(8,128)(2,1)}, u32[]{:S(2)}, u32[]{:S(2)}) collective-permute-start(f16[16,128,128]{2,1,0:T(8,128)(2,1)S(1)} %bitcast.51), channel_id=1, source_target_pairs={{0,2},{1,3},{2,0},{3,1},{4,6},{5,7},{6,4},{7,5},{8,10},{9,11},{10,... | collective-permute-start | bytes 1572872 | tf_op jit(solution)/shard_map/ppermute | solution.py:299
  134.3 20.2 %all-to-all-start.1 = ((f16[8,256,128]{2,1,0:T(8,128)(2,1)}), f16[8,256,128]{2,1,0:T(8,128)(2,1)}, u32[]{:S(2)}, u32[]{:S(2)}) async-start(f16[8,256,128]{2,1,0:T(8,128)(2,1)} %broadcast_in_dim.61), calls=%async_computation.1 | async-start | bytes 1048576 | tf_op jit(solution)/shard_map/all_to_all | solution.py:305
  138.5 6.8 %collective-permute-start.15 = (f16[16,128,128]{2,1,0:T(8,128)(2,1)S(1)}, f16[16,128,128]{2,1,0:T(8,128)(2,1)S(1)}, u32[]{:S(2)}, u32[]{:S(2)}) collective-permute-start(f16[16,128,128]{2,1,0:T(8,128)(2,1)S(1)} %bitcast.52), channel_id=1, source_target_pairs={{0,1},{1,0},{2,3},{3,2},{4,5},{5,4},{6,7},{7,6},{8,9},{9,8},{10,11... | collective-permute-start | bytes 1572872 | tf_op jit(solution)/shard_map/ppermute | solution.py:299
  138.6 7.6 %collective-permute-start.17 = (f16[16,128,128]{2,1,0:T(8,128)(2,1)}, f16[16,128,128]{2,1,0:T(8,128)(2,1)}, u32[]{:S(2)}, u32[]{:S(2)}) collective-permute-start(f16[16,128,128]{2,1,0:T(8,128)(2,1)} %collective-permute-done.16), channel_id=1, source_target_pairs={{0,1},{1,0},{2,3},{3,2},{4,5},{5,4},{6,7},{7,6},{8,9},{9,8},{10,11... | collective-permute-start | bytes 1572872 | tf_op jit(solution)/shard_map/ppermute | solution.py:299
  139.7 54.5 %collective-permute-start.20 = (f16[464,1024]{1,0:T(8,128)(2,1)}, f16[464,1024]{1,0:T(8,128)(2,1)}, u32[]{:S(2)}, u32[]{:S(2)}) collective-permute-start(f16[464,1024]{1,0:T(8,128)(2,1)} %concatenate.83), channel_id=1, source_target_pairs={{0,8},{4,12},{8,0},{12,4},{16,24},{20,28},{24,16},{28,20},{1,9},{5... | collective-permute-start | bytes 2850824 | tf_op jit(solution)/shard_map/ppermute | solution.py:299
  142.9 50.5 %collective-permute-start.21 = (f16[464,1024]{1,0:T(8,128)(2,1)}, f16[464,1024]{1,0:T(8,128)(2,1)}, u32[]{:S(2)}, u32[]{:S(2)}) collective-permute-start(f16[464,1024]{1,0:T(8,128)(2,1)} %concatenate.84), channel_id=1, source_target_pairs={{0,16},{4,20},{8,24},{12,28},{16,0},{20,4},{24,8},{28,12},{1,17},{... | collective-permute-start | bytes 2850824 | tf_op jit(solution)/shard_map/ppermute | solution.py:299
  158.2 5.0 %collective-permute-start.18 = (f32[128,256]{1,0:T(8,128)S(1)}, f32[128,256]{1,0:T(8,128)S(1)}, u32[]{:S(2)}, u32[]{:S(2)}) collective-permute-start(f32[128,256]{1,0:T(8,128)S(1)} %cross_gram.1), channel_id=1, source_target_pairs={{0,2},{1,3},{2,0},{3,1},{4,6},{5,7},{6,4},{7,5},{8,10},{9,11},{10,... | collective-permute-start | bytes 393224 | tf_op jit(solution)/shard_map/ppermute | solution.py:299
  175.7 24.3 %collective-permute-start.23 = (f16[16,128,128]{2,1,0:T(8,128)(2,1)}, f16[16,128,128]{2,1,0:T(8,128)(2,1)S(1)}, u32[]{:S(2)}, u32[]{:S(2)}) collective-permute-start(f16[16,128,128]{2,1,0:T(8,128)(2,1)} %bitcast.15), channel_id=1, source_target_pairs={{0,2},{1,3},{2,0},{3,1},{4,6},{5,7},{6,4},{7,5},{8,10},{9,11},{10,... | collective-permute-start | bytes 1572872 | tf_op jit(solution)/shard_map/ppermute | solution.py:299
  176.3 24.1 %collective-permute-start.22 = (f16[16,128,128]{2,1,0:T(8,128)(2,1)}, f16[16,128,128]{2,1,0:T(8,128)(2,1)S(1)}, u32[]{:S(2)}, u32[]{:S(2)}) collective-permute-start(f16[16,128,128]{2,1,0:T(8,128)(2,1)} %bitcast.15), channel_id=1, source_target_pairs={{0,1},{1,0},{2,3},{3,2},{4,5},{5,4},{6,7},{7,6},{8,9},{9,8},{10,11... | collective-permute-start | bytes 1572872 | tf_op jit(solution)/shard_map/ppermute | solution.py:299
  (23 other events, 258.8 us)

commit v10 on v9

--- a/solution.py
+++ b/solution.py
@@ -332,23 +332,16 @@
         early, hid_own, hid_send, weights_2d, x_part, y_part = lax.optimization_barrier(
             (early, hid_own, hid_send, weights_2d, x_part, y_part)
         )
-        early = [early, swap(early, "dp", 1)]
+        proj_near, sk_near = early[:, :dev_rows], early[:, dev_rows:]
+        proj_far = swap(proj_near, "dp", 1)
         order = jnp.concatenate([order, jnp.bitwise_xor(order, 1)])
         places = jnp.bitwise_xor(order, dp)
-        sk_own = jnp.concatenate([part[:, dev_rows:] for part in early], axis=0)
-        far = jnp.bitwise_xor(jnp.arange(n_dp, dtype=jnp.int32), dp)
-        at = jnp.where(jnp.bitwise_and(far, 1) == 1, n_dp // 2, 0) + far // 2
-        sk_own = jnp.take(sk_own, at, axis=0, mode="clip")
-        proj_parts = [part[:, :dev_rows].astype(F32) for part in early]
-        hid_send = after(hid_send, early[1])
+        proj_parts = [proj_near.astype(F32), proj_far.astype(F32)]
+        hid_send = after(hid_send, proj_far)
     else:
         sk_own = early[:, dev_rows:]
         proj_parts = [early[:, :dev_rows].reshape(1, mp_rows, rank).astype(F32)]
         places = jnp.zeros((1,), jnp.int32)
-    if width < blk:
-        sk_own = sk_own.reshape(n_dp, rank, width)
-    else:
-        sk_own = sk_own.reshape(per_shard, rank, blk)
     x_half, y_own, core_half, hid_t, hid_own, weights_2d = (
         lax.optimization_barrier(
             (
@@ -405,6 +398,15 @@
 
     partial_c, y_x, y_core, hid_got = lax.optimization_barrier((partial_c, y_x, y_core, hid_got))
     y_group = [y_own, y_core, y_x, swap(y_x, "mp", 1)]
+    if n_dp <= 8:
+        sk_own = jnp.concatenate([sk_near, swap(after(sk_near, hid_got), "dp", 1)], axis=0)
+        far = jnp.bitwise_xor(jnp.arange(n_dp, dtype=jnp.int32), dp)
+        at = jnp.where(jnp.bitwise_and(far, 1) == 1, n_dp // 2, 0) + far // 2
+        sk_own = jnp.take(sk_own, at, axis=0, mode="clip")
+    if width < blk:
+        sk_own = sk_own.reshape(n_dp, rank, width)
+    else:
+        sk_own = sk_own.reshape(per_shard, rank, blk)
     quarters = partial_c.reshape(n_mp, per_shard, rank, blk)
     to_far, to_near = quarters[3].astype(F16), quarters[1].astype(F16)
     got_far, got_near = swap(to_far, "mp", 1), swap(to_near, "mp", 1)

time: 213 us -> 208 us (0.977)
  waiting for transfers between devices: 38 us -> 30.8 us
    ppermute x25 -> x26, waiting for transfers between devices: 33.1 us -> 25.6 us  [swap(): return lax.ppermute(x, axis, [(i, i ^ bit) for i in range(size)])]
    ppermute x25 -> x26, starting transfers between devices: 21.8 us -> 23.7 us  [swap(): return lax.ppermute(x, axis, [(i, i ^ bit) for i in range(size)])]
    unnamed x42 -> x48, local copies, waits for them, and re-layouts: 11.9 us -> 12.8 us
  transfers between devices with their start and end apart: 27 -> 28, of which waited for: 11 -> 10; matrix products, arithmetic and copies ran while one was open for 28% -> 29% of each run, Pallas kernels for 30% -> 31%
where the time goes in v10:
time: 208 us; the launch traced here: 207 us
  Pallas kernels  74.1 us (36%)
  other arithmetic  37 us (18%)
  starting transfers between devices  33.7 us (16%)
  waiting for transfers between devices  30.8 us (15%)
  local copies, waits for them, and re-layouts  27.2 us (13%)
  between operations  4.51 us (2%)
    ppermute x26, waiting for transfers between devices, swap(): return lax.ppermute(x, axis, [(i, i ^ bit) for i in range(size)])  25.6 us
    ppermute x26, starting transfers between devices, swap(): return lax.ppermute(x, axis, [(i, i ^ bit) for i in range(size)])  23.7 us
    pallas_call x2, Pallas kernels, pair_grad(): pl.pallas_call(functools.partial(grad_kernel, n_mp, per_shard, blk, windo...  16.4 us
    pallas_call x1, Pallas kernels, per_device(): pl.pallas_call(mixing_kernel, in_specs=[VMEM] * 2, out_specs=VMEM, out_sh...  16 us
    pallas_call x1, Pallas kernels, per_device(): pl.pallas_call(functools.partial(compress_kernel, n_mp, per_shard, 1.0 /...  14.6 us
    unnamed x48, local copies, waits for them, and re-layouts  12.8 us
    pallas_call x1, Pallas kernels, per_device(): pl.pallas_call(functools.partial(input_grad_kernel, n_mp, per_shard, blk,...  11 us
    pallas_call x1, Pallas kernels, per_device(): pl.pallas_call(functools.partial(direction_kernel, sk_per, window, n_wind...  9.5 us
  transfers between devices with their start and end apart: 28, of which 10 were waited for; matrix products, arithmetic and copies ran while one was open for 29% of the time, Pallas kernels for 31%

profile of v10, /device:TPU:0, one launch (start us, length us, event | category | flops | bytes accessed | tf_op | source)
XLA Modules:
  0.0 207.2 jit_solution(10985664692200438933)
XLA Ops:
  0.6 3.0 %collective-permute-start.3 = (bf16[256,2048]{1,0:T(8,128)(2,1)}, bf16[256,2048]{1,0:T(8,128)(2,1)}, u32[]{:S(2)}, u32[]{:S(2)}) collective-permute-start(bf16[256,2048]{1,0:T(8,128)(2,1)} %refs_0_.7), channel_id=1, source_target_pairs={{0,4},{4,0},{8,12},{12,8},{16,20},{20,16},{24,28},{28,24},{1,5},{5... | collective-permute-start | bytes 3145736 | tf_op jit(solution)/shard_map/ppermute | solution.py:299
  8.7 4.2 %collective-permute-done = f16[1,704,128]{2,1,0:T(8,128)(2,1)S(1)} collective-permute-done((f16[1,704,128]{2,1,0:T(8,128)(2,1)S(1)}, f16[1,704,128]{2,1,0:T(8,128)(2,1)S(1)}, u32[]{:S(2)}, u32[]{:S(2)}) %collective-permute-start) | collective-permute-done | bytes 180256 | tf_op jit(solution)/shard_map/ppermute | solution.py:299
  13.0 2.7 %collective-permute-start.1 = (f16[2,704,128]{2,1,0:T(8,128)(2,1)S(1)}, f16[2,704,128]{2,1,0:T(8,128)(2,1)S(1)}, u32[]{:S(2)}, u32[]{:S(2)}) collective-permute-start(f16[2,704,128]{2,1,0:T(8,128)(2,1)S(1)} %pad_maximum_fusion.3), channel_id=1, source_target_pairs={{0,16},{4,20},{8,24},{12,28},{16,0},{20,4},{24,8},{28,12},{1,17},{... | collective-permute-start | bytes 1081352 | tf_op jit(solution)/shard_map/ppermute | solution.py:299
  15.7 3.8 %copy.23 = bf16[256,3584]{0,1:T(8,128)(2,1)} copy(bf16[256,3584]{1,0:T(8,128)(2,1)} %param.9) | data formatting | bytes 3670016 | tf_op jit(solution)/shard_map/optimization_barrier | solution.py:325
  19.4 8.0 %copy.32 = bf16[448,8,8,128]{3,1,2,0:T(8,128)(2,1)} copy(bf16[448,8,8,128]{3,2,1,0:T(8,128)(2,1)} %bitcast.50) | data formatting | bytes 14680064
  33.4 9.7 %collective-permute-done.6 = f16[4,448,128]{2,1,0:T(8,128)(2,1)S(1)} collective-permute-done((f16[4,448,128]{2,1,0:T(8,128)(2,1)S(1)}, f16[4,448,128]{2,1,0:T(8,128)(2,1)S(1)}, u32[]{:S(2)}, u32[]{:S(2)}) %collective-permute-start.6) | collective-permute-done | bytes 458784 | tf_op jit(solution)/shard_map/ppermute | solution.py:299
  47.1 14.6 %compress.1 = f32[64,128,128]{2,1,0:T(8,128)} custom-call(s32[224]{0:T(256)S(1)} %reshape.490.pat, s32[224]{0:T(256)S(1)} %reshape.491.pat_out, s32[8]{0:T(128)S(1)} %broadcast_xor_fusion.1.places, bf16[256,2048]{1,0:T(8,128)(2,1)S(1)} %copy-done.2, bf16[256,2048]{1,0:T(8,128)(2,1)S(1)} %collective-permute-done.4.refs_1_, ...), custom_call_target="tpu_custom_call" | custom-call | flops 1 | bytes 1 | tf_op jit(solution)/shard_map/compress/pallas_call | solution.py:372
  61.8 2.8 %collective-permute-done.9 = bf16[4,448,256]{2,1,0:T(8,128)(2,1)} collective-permute-done((bf16[4,448,256]{2,1,0:T(8,128)(2,1)}, bf16[4,448,256]{2,1,0:T(8,128)(2,1)}, u32[]{:S(2)}, u32[]{:S(2)}) %collective-permute-start.9) | collective-permute-done | bytes 917536 | tf_op jit(solution)/shard_map/ppermute | solution.py:299
  64.7 2.7 %convert.22 = f16[64,128,128]{2,1,0:T(8,128)(2,1)S(1)} convert(f32[64,128,128]{2,1,0:T(8,128)} %compress.1) | non-fusion elementwise | flops 1048576 | bytes 6291456 | tf_op jit(solution)/shard_map/convert.7
  70.7 8.2 %pair_grad.2 = (f32[896,1024]{1,0:T(8,128)}, f32[8,256]{1,0:T(8,128)S(1)}) custom-call(s32[2]{0:T(128)S(1)} %get-tuple-element.141.order, s32[16]{0:T(128)S(1)} %reshape.487.starts, s32[128]{0:T(128)S(1)} %select_n.242.pat, bf16[256,2048]{1,0:T(8,128)(2,1)S(1)} %copy-done.2, bf16[256,2048]{1,0:T(8,128)(2,1)S(1)} %collective-permute-done.4.refs_1_, ...), custom_call_target="tpu_custom_call" | custom-call | flops 1 | bytes 1 | tf_op jit(solution)/shard_map/pair_grad/pallas_call | solution.py:427
  83.4 3.0 %collective-permute-start.14 = (f16[464,1024]{1,0:T(8,128)(2,1)}, f16[464,1024]{1,0:T(8,128)(2,1)}, u32[]{:S(2)}, u32[]{:S(2)}) collective-permute-start(f16[464,1024]{1,0:T(8,128)(2,1)} %concatenate.82), channel_id=1, source_target_pairs={{0,8},{4,12},{8,0},{12,4},{16,24},{20,28},{24,16},{28,20},{1,9},{5... | collective-permute-start | bytes 2850824 | tf_op jit(solution)/shard_map/ppermute | solution.py:299
  86.4 2.7 %convert_add_fusion.1 = (f32[16,128,128]{2,1,0:T(8,128)}, f16[16,128,128]{2,1,0:T(8,128)(2,1)}) fusion(f16[16,128,128]{2,1,0:T(8,128)(2,1)} %collective-permute-done.12, f32[64,128,128]{2,1,0:T(8,128)S(1)} %copy-done.12, f16[16,128,128]{2,1,0:T(8,128)(2,1)} %collective-permute-done.11), kind=kLoop, calls=%fused_computation.32 | loop fusion | flops 1310720 | bytes 4718592 | tf_op jit(solution)/shard_map/add | solution.py:486
  91.2 8.2 %pair_grad.3 = (f32[896,1024]{1,0:T(8,128)}, f32[8,256]{1,0:T(8,128)S(1)}) custom-call(s32[2]{0:T(128)S(1)} %get-tuple-element.140.order, s32[16]{0:T(128)S(1)} %reshape.487.starts, s32[128]{0:T(128)S(1)} %select_n.242.pat, bf16[256,2048]{1,0:T(8,128)(2,1)S(1)} %copy-done.2, bf16[256,2048]{1,0:T(8,128)(2,1)S(1)} %collective-permute-done.4.refs_1_, ...), custom_call_target="tpu_custom_call" | custom-call | flops 1 | bytes 1 | tf_op jit(solution)/shard_map/pair_grad/pallas_call | solution.py:427
  100.8 3.8 %fusion.33 = (f32[448,1024]{1,0:T(8,128)}, f16[448,1024]{1,0:T(8,128)(2,1)S(1)}) fusion(f32[896,1024]{1,0:T(8,128)} %get-tuple-element.81, f32[]{:T(128)S(6)} %exp2.45), kind=kLoop, calls=%fused_computation.150 | loop fusion | flops 917504 | bytes 6422532 | tf_op jit(solution)/shard_map/slice | solution.py:460
  108.4 5.8 %all-to-all-start = ((f16[8,256,128]{2,1,0:T(8,128)(2,1)}), f16[8,256,128]{2,1,0:T(8,128)(2,1)S(1)}, u32[]{:S(2)}, u32[]{:S(2)}) async-start(f16[8,256,128]{2,1,0:T(8,128)(2,1)} %bitcast.13), calls=%async_computation | async-start | bytes 1048576 | tf_op jit(solution)/shard_map/all_to_all | solution.py:498
  123.5 5.1 %all-to-all-done = f16[8,256,128]{2,1,0:T(8,128)(2,1)S(1)} async-done(((f16[8,256,128]{2,1,0:T(8,128)(2,1)}), f16[8,256,128]{2,1,0:T(8,128)(2,1)S(1)}, u32[]{:S(2)}, u32[]{:S(2)}) %all-to-all-start) | async-done | bytes 524320 | tf_op jit(solution)/shard_map/all_to_all | solution.py:498
  129.5 4.1 %all-to-all-start.1 = ((f16[8,256,128]{2,1,0:T(8,128)(2,1)}), f16[8,256,128]{2,1,0:T(8,128)(2,1)}, u32[]{:S(2)}, u32[]{:S(2)}) async-start(f16[8,256,128]{2,1,0:T(8,128)(2,1)} %broadcast_in_dim.61), calls=%async_computation.1 | async-start | bytes 1048576 | tf_op jit(solution)/shard_map/all_to_all | solution.py:305
  141.4 2.6 %fusion = (bf16[64,128,128]{2,1,0:T(8,128)(2,1)S(1)}, bf16[64,128,128]{2,1,0:T(8,128)(2,1)S(1)}) fusion(f16[16,128,128]{2,1,0:T(8,128)(2,1)} %collective-permute-done.18, f16[16,128,128]{2,1,0:T(8,128)(2,1)} %collective-permute-done.17, f16[16,128,128]{2,1,0:T(8,128)(2,1)} %copy-done.17, f16[16,128,128]{2,1,0:T(8,128)(2,1)} %bitcast.54), kind=kLoop, calls=%fused_computation.6 | loop fusion | flops 8388608 | bytes 6291456 | tf_op jit(solution)/shard_map/convert_element_type | solution.py:46
  144.0 4.3 %sketch_gram.1.ss_ref = f32[128,128]{1,0:T(8,128)S(1)} custom-call(bf16[64,128,128]{2,1,0:T(8,128)(2,1)S(1)} %get-tuple-element.103.sh_ref.refs_2_, bf16[64,128,128]{2,1,0:T(8,128)(2,1)S(1)} %get-tuple-element.104.sl_ref.refs_3_), custom_call_target="tpu_custom_call" | custom-call | flops 1 | bytes 1 | tf_op jit(solution)/shard_map/sketch_gram/pallas_call | solution.py:535
  154.5 3.9 %collective-permute-done.19 = f32[128,256]{1,0:T(8,128)S(1)} collective-permute-done((f32[128,256]{1,0:T(8,128)S(1)}, f32[128,256]{1,0:T(8,128)S(1)}, u32[]{:S(2)}, u32[]{:S(2)}) %collective-permute-start.19) | collective-permute-done | bytes 131104 | tf_op jit(solution)/shard_map/ppermute | solution.py:299
  159.9 11.0 %input_grad.1 = bf16[256,3584]{1,0:T(8,128)(2,1)} custom-call(s32[224]{0:T(256)S(1)} %reshape.490.pat, bf16[256,2048]{1,0:T(8,128)(2,1)S(1)} %copy-done.2, bf16[256,2048]{1,0:T(8,128)(2,1)S(1)} %copy-done.6, bf16[256,2048]{1,0:T(8,128)(2,1)S(1)} %copy-done.4, bf16[256,2048]{1,0:T(8,128)(2,1)} %collective-permute-done.5.refs_3_, bf16[3584,1024]{1,0:T(8,128)(2,1)} %bitcast.47), custom_call_target="tpu_custom_call" | custom-call | flops 1 | bytes 1 | tf_op jit(solution)/shard_map/input_grad/pallas_call | solution.py:559
  172.0 16.0 %mixing.1.refs_1_ = f32[256,256]{1,0:T(8,128)S(1)} custom-call(f32[128,128]{1,0:T(8,128)S(1)} %sketch_gram.1.ss_ref, f32[128,256]{1,0:T(8,128)S(1)} %add.323.cross_ref), custom_call_target="tpu_custom_call" | custom-call | flops 1 | bytes 1 | tf_op jit(solution)/shard_map/mixing/pallas_call | solution.py:578
  190.1 3.8 %add_multiply_fusion.refs_0_ = f32[448,1024]{1,0:T(8,128)} fusion(f32[448,1024]{1,0:T(8,128)} %get-tuple-element.99, f16[464,1024]{1,0:T(8,128)(2,1)} %collective-permute-done.22, f16[464,1024]{1,0:T(8,128)(2,1)} %collective-permute-done.21, f32[1024]{0:T(1024)S(1)} %bitcast.58, f32[1024]{0:T(1024)S(1)} %bitcast.59), kind=kLoop, calls=%fused_computation.8 | loop fusion | flops 3211264 | bytes 5513216 | tf_op jit(solution)/shard_map/mul | solution.py:597
  197.5 9.5 %direction.1 = f32[448,8,128]{2,1,0:T(8,128)} custom-call(s32[4]{0:T(128)S(1)} %pad_add_fusion.2.starts, s32[32]{0:T(128)S(1)} %select_n.260.pat, f32[448,1024]{1,0:T(8,128)} %add_multiply_fusion.refs_0_, f32[256,256]{1,0:T(8,128)S(1)} %mixing.1.refs_1_, bf16[64,128,128]{2,1,0:T(8,128)(2,1)} %copy-done.1, bf16[64,128,128]{2,1,0:T(8,128)(2,1)} %copy-done, ...), custom_call_target="tpu_custom_call" | custom-call | flops 1 | bytes 1 | tf_op jit(solution)/shard_map/direction/pallas_call | solution.py:601
  (162 shorter events, 59.1 us)
Async XLA Ops:
  0.6 30.0 %collective-permute-start.3 = (bf16[256,2048]{1,0:T(8,128)(2,1)}, bf16[256,2048]{1,0:T(8,128)(2,1)}, u32[]{:S(2)}, u32[]{:S(2)}) collective-permute-start(bf16[256,2048]{1,0:T(8,128)(2,1)} %refs_0_.7), channel_id=1, source_target_pairs={{0,4},{4,0},{8,12},{12,8},{16,20},{20,16},{24,28},{28,24},{1,5},{5... | collective-permute-start | bytes 3145736 | tf_op jit(solution)/shard_map/ppermute | solution.py:299
  3.7 27.0 %collective-permute-start.2 = (bf16[256,2048]{1,0:T(8,128)(2,1)}, bf16[256,2048]{1,0:T(8,128)(2,1)S(1)}, u32[]{:S(2)}, u32[]{:S(2)}) collective-permute-start(bf16[256,2048]{1,0:T(8,128)(2,1)} %refs_0_.7), channel_id=1, source_target_pairs={{0,2},{1,3},{2,0},{3,1},{4,6},{5,7},{6,4},{7,5},{8,10},{9,11},{10,... | collective-permute-start | bytes 3145736 | tf_op jit(solution)/shard_map/ppermute | solution.py:299
  7.1 5.8 %collective-permute-start = (f16[1,704,128]{2,1,0:T(8,128)(2,1)S(1)}, f16[1,704,128]{2,1,0:T(8,128)(2,1)S(1)}, u32[]{:S(2)}, u32[]{:S(2)}) collective-permute-start(f16[1,704,128]{2,1,0:T(8,128)(2,1)S(1)} %maximum_bitcast_fusion), channel_id=1, source_target_pairs={{0,8},{4,12},{8,0},{12,4},{16,24},{20,28},{24,16},{28,20},{1,9},{5... | collective-permute-start | bytes 540680 | tf_op jit(solution)/shard_map/ppermute | solution.py:299
  8.7 23.6 %collective-permute-start.4 = (bf16[256,2048]{1,0:T(8,128)(2,1)}, bf16[256,2048]{1,0:T(8,128)(2,1)S(1)}, u32[]{:S(2)}, u32[]{:S(2)}) collective-permute-start(bf16[256,2048]{1,0:T(8,128)(2,1)} %refs_0_.7), channel_id=1, source_target_pairs={{0,1},{1,0},{2,3},{3,2},{4,5},{5,4},{6,7},{7,6},{8,9},{9,8},{10,11... | collective-permute-start | bytes 3145736 | tf_op jit(solution)/shard_map/ppermute | solution.py:299
  13.0 17.5 %collective-permute-start.1 = (f16[2,704,128]{2,1,0:T(8,128)(2,1)S(1)}, f16[2,704,128]{2,1,0:T(8,128)(2,1)S(1)}, u32[]{:S(2)}, u32[]{:S(2)}) collective-permute-start(f16[2,704,128]{2,1,0:T(8,128)(2,1)S(1)} %pad_maximum_fusion.3), channel_id=1, source_target_pairs={{0,16},{4,20},{8,24},{12,28},{16,0},{20,4},{24,8},{28,12},{1,17},{... | collective-permute-start | bytes 1081352 | tf_op jit(solution)/shard_map/ppermute | solution.py:299
  31.8 11.4 %collective-permute-start.6 = (f16[4,448,128]{2,1,0:T(8,128)(2,1)S(1)}, f16[4,448,128]{2,1,0:T(8,128)(2,1)S(1)}, u32[]{:S(2)}, u32[]{:S(2)}) collective-permute-start(f16[4,448,128]{2,1,0:T(8,128)(2,1)S(1)} %get-tuple-element.120), channel_id=1, source_target_pairs={{0,4},{4,0},{8,12},{12,8},{16,20},{20,16},{24,28},{28,24},{1,5},{5... | collective-permute-start | bytes 1376264 | tf_op jit(solution)/shard_map/ppermute | solution.py:299
  32.3 29.4 %collective-permute-start.8 = (bf16[256,2048]{1,0:T(8,128)(2,1)}, bf16[256,2048]{1,0:T(8,128)(2,1)}, u32[]{:S(2)}, u32[]{:S(2)}) collective-permute-start(bf16[256,2048]{1,0:T(8,128)(2,1)} %collective-permute-done.3.refs_4_), channel_id=1, source_target_pairs={{0,1},{1,0},{2,3},{3,2},{4,5},{5,4},{6,7},{7,6},{8,9},{9,8},{10,11... | collective-permute-start | bytes 3145736 | tf_op jit(solution)/shard_map/ppermute | solution.py:299
  32.4 29.3 %collective-permute-start.7 = (bf16[256,2048]{1,0:T(8,128)(2,1)}, bf16[256,2048]{1,0:T(8,128)(2,1)}, u32[]{:S(2)}, u32[]{:S(2)}) collective-permute-start(bf16[256,2048]{1,0:T(8,128)(2,1)} %collective-permute-done.3.refs_4_), channel_id=1, source_target_pairs={{0,2},{1,3},{2,0},{3,1},{4,6},{5,7},{6,4},{7,5},{8,10},{9,11},{10,... | collective-permute-start | bytes 3145736 | tf_op jit(solution)/shard_map/ppermute | solution.py:299
  33.2 13.8 %collective-permute-start.5 = (bf16[256,2048]{1,0:T(8,128)(2,1)S(1)}, bf16[256,2048]{1,0:T(8,128)(2,1)}, u32[]{:S(2)}, u32[]{:S(2)}) collective-permute-start(bf16[256,2048]{1,0:T(8,128)(2,1)S(1)} %collective-permute-done.2.refs_2_), channel_id=1, source_target_pairs={{0,1},{1,0},{2,3},{3,2},{4,5},{5,4},{6,7},{7,6},{8,9},{9,8},{10,11... | collective-permute-start | bytes 3145736 | tf_op jit(solution)/shard_map/ppermute | solution.py:299
  43.9 20.7 %collective-permute-start.9 = (bf16[4,448,256]{2,1,0:T(8,128)(2,1)}, bf16[4,448,256]{2,1,0:T(8,128)(2,1)}, u32[]{:S(2)}, u32[]{:S(2)}) collective-permute-start(bf16[4,448,256]{2,1,0:T(8,128)(2,1)} %get-tuple-element.67), channel_id=1, source_target_pairs={{0,4},{4,0},{8,12},{12,8},{16,20},{20,16},{24,28},{28,24},{1,5},{5... | collective-permute-start | bytes 2752520 | tf_op jit(solution)/shard_map/ppermute | solution.py:299
  68.7 14.7 %collective-permute-start.12 = (f16[16,128,128]{2,1,0:T(8,128)(2,1)}, f16[16,128,128]{2,1,0:T(8,128)(2,1)}, u32[]{:S(2)}, u32[]{:S(2)}) collective-permute-start(f16[16,128,128]{2,1,0:T(8,128)(2,1)} %get-tuple-element.114), channel_id=1, source_target_pairs={{0,1},{1,0},{2,3},{3,2},{4,5},{5,4},{6,7},{7,6},{8,9},{9,8},{10,11... | collective-permute-start | bytes 1572872 | tf_op jit(solution)/shard_map/ppermute | solution.py:299
  69.2 14.2 %collective-permute-start.11 = (f16[16,128,128]{2,1,0:T(8,128)(2,1)}, f16[16,128,128]{2,1,0:T(8,128)(2,1)}, u32[]{:S(2)}, u32[]{:S(2)}) collective-permute-start(f16[16,128,128]{2,1,0:T(8,128)(2,1)} %get-tuple-element.115), channel_id=1, source_target_pairs={{0,1},{1,0},{2,3},{3,2},{4,5},{5,4},{6,7},{7,6},{8,9},{9,8},{10,11... | collective-permute-start | bytes 1572872 | tf_op jit(solution)/shard_map/ppermute | solution.py:299
  83.4 25.0 %collective-permute-start.14 = (f16[464,1024]{1,0:T(8,128)(2,1)}, f16[464,1024]{1,0:T(8,128)(2,1)}, u32[]{:S(2)}, u32[]{:S(2)}) collective-permute-start(f16[464,1024]{1,0:T(8,128)(2,1)} %concatenate.82), channel_id=1, source_target_pairs={{0,8},{4,12},{8,0},{12,4},{16,24},{20,28},{24,16},{28,20},{1,9},{5... | collective-permute-start | bytes 2850824 | tf_op jit(solution)/shard_map/ppermute | solution.py:299
  89.1 16.6 %collective-permute-start.13 = (f16[16,128,128]{2,1,0:T(8,128)(2,1)}, f16[16,128,128]{2,1,0:T(8,128)(2,1)}, u32[]{:S(2)}, u32[]{:S(2)}) collective-permute-start(f16[16,128,128]{2,1,0:T(8,128)(2,1)} %get-tuple-element.78), channel_id=1, source_target_pairs={{0,2},{1,3},{2,0},{3,1},{4,6},{5,7},{6,4},{7,5},{8,10},{9,11},{10,... | collective-permute-start | bytes 1572872 | tf_op jit(solution)/shard_map/ppermute | solution.py:299
  90.6 23.7 %collective-permute-start.15 = (f16[4,256,128]{2,1,0:T(8,128)(2,1)S(1)}, f16[4,256,128]{2,1,0:T(8,128)(2,1)}, u32[]{:S(2)}, u32[]{:S(2)}) collective-permute-start(f16[4,256,128]{2,1,0:T(8,128)(2,1)S(1)} %slice.69), channel_id=1, source_target_pairs={{0,4},{4,0},{8,12},{12,8},{16,20},{20,16},{24,28},{28,24},{1,5},{5... | collective-permute-start | bytes 786440 | tf_op jit(solution)/shard_map/ppermute | solution.py:299
  108.4 20.2 %all-to-all-start = ((f16[8,256,128]{2,1,0:T(8,128)(2,1)}), f16[8,256,128]{2,1,0:T(8,128)(2,1)S(1)}, u32[]{:S(2)}, u32[]{:S(2)}) async-start(f16[8,256,128]{2,1,0:T(8,128)(2,1)} %bitcast.13), calls=%async_computation | async-start | bytes 1048576 | tf_op jit(solution)/shard_map/all_to_all | solution.py:498
  116.2 17.6 %collective-permute-start.17 = (f16[16,128,128]{2,1,0:T(8,128)(2,1)S(1)}, f16[16,128,128]{2,1,0:T(8,128)(2,1)}, u32[]{:S(2)}, u32[]{:S(2)}) collective-permute-start(f16[16,128,128]{2,1,0:T(8,128)(2,1)S(1)} %bitcast.51), channel_id=1, source_target_pairs={{0,2},{1,3},{2,0},{3,1},{4,6},{5,7},{6,4},{7,5},{8,10},{9,11},{10,... | collective-permute-start | bytes 1572872 | tf_op jit(solution)/shard_map/ppermute | solution.py:299
  129.5 20.2 %all-to-all-start.1 = ((f16[8,256,128]{2,1,0:T(8,128)(2,1)}), f16[8,256,128]{2,1,0:T(8,128)(2,1)}, u32[]{:S(2)}, u32[]{:S(2)}) async-start(f16[8,256,128]{2,1,0:T(8,128)(2,1)} %broadcast_in_dim.61), calls=%async_computation.1 | async-start | bytes 1048576 | tf_op jit(solution)/shard_map/all_to_all | solution.py:305
  133.8 6.8 %collective-permute-start.16 = (f16[16,128,128]{2,1,0:T(8,128)(2,1)S(1)}, f16[16,128,128]{2,1,0:T(8,128)(2,1)S(1)}, u32[]{:S(2)}, u32[]{:S(2)}) collective-permute-start(f16[16,128,128]{2,1,0:T(8,128)(2,1)S(1)} %bitcast.52), channel_id=1, source_target_pairs={{0,1},{1,0},{2,3},{3,2},{4,5},{5,4},{6,7},{7,6},{8,9},{9,8},{10,11... | collective-permute-start | bytes 1572872 | tf_op jit(solution)/shard_map/ppermute | solution.py:299
  133.8 7.6 %collective-permute-start.18 = (f16[16,128,128]{2,1,0:T(8,128)(2,1)}, f16[16,128,128]{2,1,0:T(8,128)(2,1)}, u32[]{:S(2)}, u32[]{:S(2)}) collective-permute-start(f16[16,128,128]{2,1,0:T(8,128)(2,1)} %collective-permute-done.17), channel_id=1, source_target_pairs={{0,1},{1,0},{2,3},{3,2},{4,5},{5,4},{6,7},{7,6},{8,9},{9,8},{10,11... | collective-permute-start | bytes 1572872 | tf_op jit(solution)/shard_map/ppermute | solution.py:299
  135.0 54.4 %collective-permute-start.21 = (f16[464,1024]{1,0:T(8,128)(2,1)}, f16[464,1024]{1,0:T(8,128)(2,1)}, u32[]{:S(2)}, u32[]{:S(2)}) collective-permute-start(f16[464,1024]{1,0:T(8,128)(2,1)} %concatenate.83), channel_id=1, source_target_pairs={{0,8},{4,12},{8,0},{12,4},{16,24},{20,28},{24,16},{28,20},{1,9},{5... | collective-permute-start | bytes 2850824 | tf_op jit(solution)/shard_map/ppermute | solution.py:299
  138.2 50.5 %collective-permute-start.22 = (f16[464,1024]{1,0:T(8,128)(2,1)}, f16[464,1024]{1,0:T(8,128)(2,1)}, u32[]{:S(2)}, u32[]{:S(2)}) collective-permute-start(f16[464,1024]{1,0:T(8,128)(2,1)} %concatenate.84), channel_id=1, source_target_pairs={{0,16},{4,20},{8,24},{12,28},{16,0},{20,4},{24,8},{28,12},{1,17},{... | collective-permute-start | bytes 2850824 | tf_op jit(solution)/shard_map/ppermute | solution.py:299
  170.9 24.3 %collective-permute-start.24 = (f16[16,128,128]{2,1,0:T(8,128)(2,1)}, f16[16,128,128]{2,1,0:T(8,128)(2,1)S(1)}, u32[]{:S(2)}, u32[]{:S(2)}) collective-permute-start(f16[16,128,128]{2,1,0:T(8,128)(2,1)} %bitcast.15), channel_id=1, source_target_pairs={{0,2},{1,3},{2,0},{3,1},{4,6},{5,7},{6,4},{7,5},{8,10},{9,11},{10,... | collective-permute-start | bytes 1572872 | tf_op jit(solution)/shard_map/ppermute | solution.py:299
  172.0 23.6 %collective-permute-start.23 = (f16[16,128,128]{2,1,0:T(8,128)(2,1)}, f16[16,128,128]{2,1,0:T(8,128)(2,1)S(1)}, u32[]{:S(2)}, u32[]{:S(2)}) collective-permute-start(f16[16,128,128]{2,1,0:T(8,128)(2,1)} %bitcast.15), channel_id=1, source_target_pairs={{0,1},{1,0},{2,3},{3,2},{4,5},{5,4},{6,7},{7,6},{8,9},{9,8},{10,11... | collective-permute-start | bytes 1572872 | tf_op jit(solution)/shard_map/ppermute | solution.py:299
  (27 other events, 265.9 us)

commit v11 on v10

--- a/solution.py
+++ b/solution.py
@@ -290,7 +290,7 @@
     per_shard = shard_cols // blk
     col_blocks = per_shard * n_mp
     outer = n_dp // 2
-    per_step = 4 if block_rows % 4 == 0 else 1
+    per_step = 7 if block_rows % 7 == 0 else 1
     dp, mp = lax.axis_index("dp"), lax.axis_index("mp")
     side = dp % 2
 

time: 208 us -> 208 us (level)
  transfers between devices with their start and end apart: 28 -> 28, of which waited for: 10 -> 10; matrix products, arithmetic and copies ran while one was open for 29% -> 29% of each run, Pallas kernels for 31% -> 30%
where the time goes in v11:
time: 208 us; the launch traced here: 207 us
  Pallas kernels  72.4 us (35%)
  other arithmetic  37 us (18%)
  starting transfers between devices  33.6 us (16%)
  waiting for transfers between devices  32.5 us (16%)
  local copies, waits for them, and re-layouts  27.2 us (13%)
  between operations  4.52 us (2%)
    ppermute x26, waiting for transfers between devices, swap(): return lax.ppermute(x, axis, [(i, i ^ bit) for i in range(size)])  27.3 us
    ppermute x26, starting transfers between devices, swap(): return lax.ppermute(x, axis, [(i, i ^ bit) for i in range(size)])  23.7 us
    pallas_call x2, Pallas kernels, pair_grad(): pl.pallas_call(functools.partial(grad_kernel, n_mp, per_shard, blk, windo...  16.4 us
    pallas_call x1, Pallas kernels, per_device(): pl.pallas_call(mixing_kernel, in_specs=[VMEM] * 2, out_specs=VMEM, out_sh...  16 us
    pallas_call x1, Pallas kernels, per_device(): pl.pallas_call(functools.partial(compress_kernel, n_mp, per_shard, 1.0 /...  14.2 us
    unnamed x48, local copies, waits for them, and re-layouts  12.8 us
    pallas_call x1, Pallas kernels, per_device(): pl.pallas_call(functools.partial(input_grad_kernel, n_mp, per_shard, blk,...  9.79 us
    pallas_call x1, Pallas kernels, per_device(): pl.pallas_call(functools.partial(direction_kernel, sk_per, window, n_wind...  9.5 us
  transfers between devices with their start and end apart: 28, of which 10 were waited for; matrix products, arithmetic and copies ran while one was open for 29% of the time, Pallas kernels for 30%

profile of v11, /device:TPU:0, one launch (start us, length us, event | category | flops | bytes accessed | tf_op | source)
XLA Modules:
  0.0 207.2 jit_solution(15286605522851588784)
XLA Ops:
  0.6 3.0 %collective-permute-start.3 = (bf16[256,2048]{1,0:T(8,128)(2,1)}, bf16[256,2048]{1,0:T(8,128)(2,1)}, u32[]{:S(2)}, u32[]{:S(2)}) collective-permute-start(bf16[256,2048]{1,0:T(8,128)(2,1)} %refs_0_.7), channel_id=1, source_target_pairs={{0,4},{4,0},{8,12},{12,8},{16,20},{20,16},{24,28},{28,24},{1,5},{5... | collective-permute-start | bytes 3145736 | tf_op jit(solution)/shard_map/ppermute | solution.py:299
  8.7 4.2 %collective-permute-done = f16[1,704,128]{2,1,0:T(8,128)(2,1)S(1)} collective-permute-done((f16[1,704,128]{2,1,0:T(8,128)(2,1)S(1)}, f16[1,704,128]{2,1,0:T(8,128)(2,1)S(1)}, u32[]{:S(2)}, u32[]{:S(2)}) %collective-permute-start) | collective-permute-done | bytes 180256 | tf_op jit(solution)/shard_map/ppermute | solution.py:299
  13.0 2.7 %collective-permute-start.1 = (f16[2,704,128]{2,1,0:T(8,128)(2,1)S(1)}, f16[2,704,128]{2,1,0:T(8,128)(2,1)S(1)}, u32[]{:S(2)}, u32[]{:S(2)}) collective-permute-start(f16[2,704,128]{2,1,0:T(8,128)(2,1)S(1)} %pad_maximum_fusion.3), channel_id=1, source_target_pairs={{0,16},{4,20},{8,24},{12,28},{16,0},{20,4},{24,8},{28,12},{1,17},{... | collective-permute-start | bytes 1081352 | tf_op jit(solution)/shard_map/ppermute | solution.py:299
  15.7 3.8 %copy.23 = bf16[256,3584]{0,1:T(8,128)(2,1)} copy(bf16[256,3584]{1,0:T(8,128)(2,1)} %param.9) | data formatting | bytes 3670016 | tf_op jit(solution)/shard_map/optimization_barrier | solution.py:325
  19.4 8.0 %copy.32 = bf16[448,8,8,128]{3,1,2,0:T(8,128)(2,1)} copy(bf16[448,8,8,128]{3,2,1,0:T(8,128)(2,1)} %bitcast.50) | data formatting | bytes 14680064
  33.4 9.7 %collective-permute-done.6 = f16[4,448,128]{2,1,0:T(8,128)(2,1)S(1)} collective-permute-done((f16[4,448,128]{2,1,0:T(8,128)(2,1)S(1)}, f16[4,448,128]{2,1,0:T(8,128)(2,1)S(1)}, u32[]{:S(2)}, u32[]{:S(2)}) %collective-permute-start.6) | collective-permute-done | bytes 458784 | tf_op jit(solution)/shard_map/ppermute | solution.py:299
  47.1 14.2 %compress.1 = f32[64,128,128]{2,1,0:T(8,128)} custom-call(s32[224]{0:T(256)S(1)} %reshape.490.pat, s32[224]{0:T(256)S(1)} %reshape.491.pat_out, s32[8]{0:T(128)S(1)} %broadcast_xor_fusion.1.places, bf16[256,2048]{1,0:T(8,128)(2,1)S(1)} %copy-done.2, bf16[256,2048]{1,0:T(8,128)(2,1)S(1)} %collective-permute-done.4.refs_1_, ...), custom_call_target="tpu_custom_call" | custom-call | flops 1 | bytes 1 | tf_op jit(solution)/shard_map/compress/pallas_call | solution.py:372
  61.3 3.3 %collective-permute-done.9 = bf16[4,448,256]{2,1,0:T(8,128)(2,1)} collective-permute-done((bf16[4,448,256]{2,1,0:T(8,128)(2,1)}, bf16[4,448,256]{2,1,0:T(8,128)(2,1)}, u32[]{:S(2)}, u32[]{:S(2)}) %collective-permute-start.9) | collective-permute-done | bytes 917536 | tf_op jit(solution)/shard_map/ppermute | solution.py:299
  64.7 2.7 %convert.22 = f16[64,128,128]{2,1,0:T(8,128)(2,1)S(1)} convert(f32[64,128,128]{2,1,0:T(8,128)} %compress.1) | non-fusion elementwise | flops 1048576 | bytes 6291456 | tf_op jit(solution)/shard_map/convert.7
  70.7 8.2 %pair_grad.2 = (f32[896,1024]{1,0:T(8,128)}, f32[8,256]{1,0:T(8,128)S(1)}) custom-call(s32[2]{0:T(128)S(1)} %get-tuple-element.141.order, s32[16]{0:T(128)S(1)} %reshape.487.starts, s32[128]{0:T(128)S(1)} %select_n.242.pat, bf16[256,2048]{1,0:T(8,128)(2,1)S(1)} %copy-done.2, bf16[256,2048]{1,0:T(8,128)(2,1)S(1)} %collective-permute-done.4.refs_1_, ...), custom_call_target="tpu_custom_call" | custom-call | flops 1 | bytes 1 | tf_op jit(solution)/shard_map/pair_grad/pallas_call | solution.py:427
  83.4 3.0 %collective-permute-start.14 = (f16[464,1024]{1,0:T(8,128)(2,1)}, f16[464,1024]{1,0:T(8,128)(2,1)}, u32[]{:S(2)}, u32[]{:S(2)}) collective-permute-start(f16[464,1024]{1,0:T(8,128)(2,1)} %concatenate.82), channel_id=1, source_target_pairs={{0,8},{4,12},{8,0},{12,4},{16,24},{20,28},{24,16},{28,20},{1,9},{5... | collective-permute-start | bytes 2850824 | tf_op jit(solution)/shard_map/ppermute | solution.py:299
  86.4 2.7 %convert_add_fusion.1 = (f32[16,128,128]{2,1,0:T(8,128)}, f16[16,128,128]{2,1,0:T(8,128)(2,1)}) fusion(f16[16,128,128]{2,1,0:T(8,128)(2,1)} %collective-permute-done.12, f32[64,128,128]{2,1,0:T(8,128)S(1)} %copy-done.12, f16[16,128,128]{2,1,0:T(8,128)(2,1)} %collective-permute-done.11), kind=kLoop, calls=%fused_computation.32 | loop fusion | flops 1310720 | bytes 4718592 | tf_op jit(solution)/shard_map/add | solution.py:486
  91.2 8.2 %pair_grad.3 = (f32[896,1024]{1,0:T(8,128)}, f32[8,256]{1,0:T(8,128)S(1)}) custom-call(s32[2]{0:T(128)S(1)} %get-tuple-element.140.order, s32[16]{0:T(128)S(1)} %reshape.487.starts, s32[128]{0:T(128)S(1)} %select_n.242.pat, bf16[256,2048]{1,0:T(8,128)(2,1)S(1)} %copy-done.2, bf16[256,2048]{1,0:T(8,128)(2,1)S(1)} %collective-permute-done.4.refs_1_, ...), custom_call_target="tpu_custom_call" | custom-call | flops 1 | bytes 1 | tf_op jit(solution)/shard_map/pair_grad/pallas_call | solution.py:427
  100.8 3.8 %fusion.33 = (f32[448,1024]{1,0:T(8,128)}, f16[448,1024]{1,0:T(8,128)(2,1)S(1)}) fusion(f32[896,1024]{1,0:T(8,128)} %get-tuple-element.81, f32[]{:T(128)S(6)} %exp2.45), kind=kLoop, calls=%fused_computation.150 | loop fusion | flops 917504 | bytes 6422532 | tf_op jit(solution)/shard_map/slice | solution.py:460
  108.4 5.8 %all-to-all-start = ((f16[8,256,128]{2,1,0:T(8,128)(2,1)}), f16[8,256,128]{2,1,0:T(8,128)(2,1)S(1)}, u32[]{:S(2)}, u32[]{:S(2)}) async-start(f16[8,256,128]{2,1,0:T(8,128)(2,1)} %bitcast.13), calls=%async_computation | async-start | bytes 1048576 | tf_op jit(solution)/shard_map/all_to_all | solution.py:498
  123.5 5.1 %all-to-all-done = f16[8,256,128]{2,1,0:T(8,128)(2,1)S(1)} async-done(((f16[8,256,128]{2,1,0:T(8,128)(2,1)}), f16[8,256,128]{2,1,0:T(8,128)(2,1)S(1)}, u32[]{:S(2)}, u32[]{:S(2)}) %all-to-all-start) | async-done | bytes 524320 | tf_op jit(solution)/shard_map/all_to_all | solution.py:498
  129.6 4.1 %all-to-all-start.1 = ((f16[8,256,128]{2,1,0:T(8,128)(2,1)}), f16[8,256,128]{2,1,0:T(8,128)(2,1)}, u32[]{:S(2)}, u32[]{:S(2)}) async-start(f16[8,256,128]{2,1,0:T(8,128)(2,1)} %broadcast_in_dim.61), calls=%async_computation.1 | async-start | bytes 1048576 | tf_op jit(solution)/shard_map/all_to_all | solution.py:305
  141.4 2.6 %fusion = (bf16[64,128,128]{2,1,0:T(8,128)(2,1)S(1)}, bf16[64,128,128]{2,1,0:T(8,128)(2,1)S(1)}) fusion(f16[16,128,128]{2,1,0:T(8,128)(2,1)} %collective-permute-done.18, f16[16,128,128]{2,1,0:T(8,128)(2,1)} %collective-permute-done.17, f16[16,128,128]{2,1,0:T(8,128)(2,1)} %copy-done.17, f16[16,128,128]{2,1,0:T(8,128)(2,1)} %bitcast.54), kind=kLoop, calls=%fused_computation.6 | loop fusion | flops 8388608 | bytes 6291456 | tf_op jit(solution)/shard_map/convert_element_type | solution.py:46
  144.0 4.3 %sketch_gram.1.ss_ref = f32[128,128]{1,0:T(8,128)S(1)} custom-call(bf16[64,128,128]{2,1,0:T(8,128)(2,1)S(1)} %get-tuple-element.103.sh_ref.refs_2_, bf16[64,128,128]{2,1,0:T(8,128)(2,1)S(1)} %get-tuple-element.104.sl_ref.refs_3_), custom_call_target="tpu_custom_call" | custom-call | flops 1 | bytes 1 | tf_op jit(solution)/shard_map/sketch_gram/pallas_call | solution.py:535
  154.6 3.9 %collective-permute-done.19 = f32[128,256]{1,0:T(8,128)S(1)} collective-permute-done((f32[128,256]{1,0:T(8,128)S(1)}, f32[128,256]{1,0:T(8,128)S(1)}, u32[]{:S(2)}, u32[]{:S(2)}) %collective-permute-start.19) | collective-permute-done | bytes 131104 | tf_op jit(solution)/shard_map/ppermute | solution.py:299
  159.9 9.8 %input_grad.1 = bf16[256,3584]{1,0:T(8,128)(2,1)} custom-call(s32[224]{0:T(256)S(1)} %reshape.490.pat, bf16[256,2048]{1,0:T(8,128)(2,1)S(1)} %copy-done.2, bf16[256,2048]{1,0:T(8,128)(2,1)S(1)} %copy-done.6, bf16[256,2048]{1,0:T(8,128)(2,1)S(1)} %copy-done.4, bf16[256,2048]{1,0:T(8,128)(2,1)} %collective-permute-done.5.refs_3_, bf16[3584,1024]{1,0:T(8,128)(2,1)} %bitcast.47), custom_call_target="tpu_custom_call" | custom-call | flops 1 | bytes 1 | tf_op jit(solution)/shard_map/input_grad/pallas_call | solution.py:559
  170.8 16.0 %mixing.1.refs_1_ = f32[256,256]{1,0:T(8,128)S(1)} custom-call(f32[128,128]{1,0:T(8,128)S(1)} %sketch_gram.1.ss_ref, f32[128,256]{1,0:T(8,128)S(1)} %add.323.cross_ref), custom_call_target="tpu_custom_call" | custom-call | flops 1 | bytes 1 | tf_op jit(solution)/shard_map/mixing/pallas_call | solution.py:578
  190.2 3.8 %add_multiply_fusion.refs_0_ = f32[448,1024]{1,0:T(8,128)} fusion(f32[448,1024]{1,0:T(8,128)} %get-tuple-element.99, f16[464,1024]{1,0:T(8,128)(2,1)} %collective-permute-done.22, f16[464,1024]{1,0:T(8,128)(2,1)} %collective-permute-done.21, f32[1024]{0:T(1024)S(1)} %bitcast.58, f32[1024]{0:T(1024)S(1)} %bitcast.59), kind=kLoop, calls=%fused_computation.8 | loop fusion | flops 3211264 | bytes 5513216 | tf_op jit(solution)/shard_map/mul | solution.py:597
  197.6 9.5 %direction.1 = f32[448,8,128]{2,1,0:T(8,128)} custom-call(s32[4]{0:T(128)S(1)} %pad_add_fusion.2.starts, s32[32]{0:T(128)S(1)} %select_n.260.pat, f32[448,1024]{1,0:T(8,128)} %add_multiply_fusion.refs_0_, f32[256,256]{1,0:T(8,128)S(1)} %mixing.1.refs_1_, bf16[64,128,128]{2,1,0:T(8,128)(2,1)} %copy-done.1, bf16[64,128,128]{2,1,0:T(8,128)(2,1)} %copy-done, ...), custom_call_target="tpu_custom_call" | custom-call | flops 1 | bytes 1 | tf_op jit(solution)/shard_map/direction/pallas_call | solution.py:601
  (162 shorter events, 60.3 us)
Async XLA Ops:
  0.6 30.0 %collective-permute-start.3 = (bf16[256,2048]{1,0:T(8,128)(2,1)}, bf16[256,2048]{1,0:T(8,128)(2,1)}, u32[]{:S(2)}, u32[]{:S(2)}) collective-permute-start(bf16[256,2048]{1,0:T(8,128)(2,1)} %refs_0_.7), channel_id=1, source_target_pairs={{0,4},{4,0},{8,12},{12,8},{16,20},{20,16},{24,28},{28,24},{1,5},{5... | collective-permute-start | bytes 3145736 | tf_op jit(solution)/shard_map/ppermute | solution.py:299
  3.7 27.0 %collective-permute-start.2 = (bf16[256,2048]{1,0:T(8,128)(2,1)}, bf16[256,2048]{1,0:T(8,128)(2,1)S(1)}, u32[]{:S(2)}, u32[]{:S(2)}) collective-permute-start(bf16[256,2048]{1,0:T(8,128)(2,1)} %refs_0_.7), channel_id=1, source_target_pairs={{0,2},{1,3},{2,0},{3,1},{4,6},{5,7},{6,4},{7,5},{8,10},{9,11},{10,... | collective-permute-start | bytes 3145736 | tf_op jit(solution)/shard_map/ppermute | solution.py:299
  7.1 5.8 %collective-permute-start = (f16[1,704,128]{2,1,0:T(8,128)(2,1)S(1)}, f16[1,704,128]{2,1,0:T(8,128)(2,1)S(1)}, u32[]{:S(2)}, u32[]{:S(2)}) collective-permute-start(f16[1,704,128]{2,1,0:T(8,128)(2,1)S(1)} %maximum_bitcast_fusion), channel_id=1, source_target_pairs={{0,8},{4,12},{8,0},{12,4},{16,24},{20,28},{24,16},{28,20},{1,9},{5... | collective-permute-start | bytes 540680 | tf_op jit(solution)/shard_map/ppermute | solution.py:299
  8.7 23.6 %collective-permute-start.4 = (bf16[256,2048]{1,0:T(8,128)(2,1)}, bf16[256,2048]{1,0:T(8,128)(2,1)S(1)}, u32[]{:S(2)}, u32[]{:S(2)}) collective-permute-start(bf16[256,2048]{1,0:T(8,128)(2,1)} %refs_0_.7), channel_id=1, source_target_pairs={{0,1},{1,0},{2,3},{3,2},{4,5},{5,4},{6,7},{7,6},{8,9},{9,8},{10,11... | collective-permute-start | bytes 3145736 | tf_op jit(solution)/shard_map/ppermute | solution.py:299
  13.0 17.5 %collective-permute-start.1 = (f16[2,704,128]{2,1,0:T(8,128)(2,1)S(1)}, f16[2,704,128]{2,1,0:T(8,128)(2,1)S(1)}, u32[]{:S(2)}, u32[]{:S(2)}) collective-permute-start(f16[2,704,128]{2,1,0:T(8,128)(2,1)S(1)} %pad_maximum_fusion.3), channel_id=1, source_target_pairs={{0,16},{4,20},{8,24},{12,28},{16,0},{20,4},{24,8},{28,12},{1,17},{... | collective-permute-start | bytes 1081352 | tf_op jit(solution)/shard_map/ppermute | solution.py:299
  31.8 11.4 %collective-permute-start.6 = (f16[4,448,128]{2,1,0:T(8,128)(2,1)S(1)}, f16[4,448,128]{2,1,0:T(8,128)(2,1)S(1)}, u32[]{:S(2)}, u32[]{:S(2)}) collective-permute-start(f16[4,448,128]{2,1,0:T(8,128)(2,1)S(1)} %get-tuple-element.120), channel_id=1, source_target_pairs={{0,4},{4,0},{8,12},{12,8},{16,20},{20,16},{24,28},{28,24},{1,5},{5... | collective-permute-start | bytes 1376264 | tf_op jit(solution)/shard_map/ppermute | solution.py:299
  32.3 29.0 %collective-permute-start.8 = (bf16[256,2048]{1,0:T(8,128)(2,1)}, bf16[256,2048]{1,0:T(8,128)(2,1)}, u32[]{:S(2)}, u32[]{:S(2)}) collective-permute-start(bf16[256,2048]{1,0:T(8,128)(2,1)} %collective-permute-done.3.refs_4_), channel_id=1, source_target_pairs={{0,1},{1,0},{2,3},{3,2},{4,5},{5,4},{6,7},{7,6},{8,9},{9,8},{10,11... | collective-permute-start | bytes 3145736 | tf_op jit(solution)/shard_map/ppermute | solution.py:299
  32.4 28.9 %collective-permute-start.7 = (bf16[256,2048]{1,0:T(8,128)(2,1)}, bf16[256,2048]{1,0:T(8,128)(2,1)}, u32[]{:S(2)}, u32[]{:S(2)}) collective-permute-start(bf16[256,2048]{1,0:T(8,128)(2,1)} %collective-permute-done.3.refs_4_), channel_id=1, source_target_pairs={{0,2},{1,3},{2,0},{3,1},{4,6},{5,7},{6,4},{7,5},{8,10},{9,11},{10,... | collective-permute-start | bytes 3145736 | tf_op jit(solution)/shard_map/ppermute | solution.py:299
  33.2 13.8 %collective-permute-start.5 = (bf16[256,2048]{1,0:T(8,128)(2,1)S(1)}, bf16[256,2048]{1,0:T(8,128)(2,1)}, u32[]{:S(2)}, u32[]{:S(2)}) collective-permute-start(bf16[256,2048]{1,0:T(8,128)(2,1)S(1)} %collective-permute-done.2.refs_2_), channel_id=1, source_target_pairs={{0,1},{1,0},{2,3},{3,2},{4,5},{5,4},{6,7},{7,6},{8,9},{9,8},{10,11... | collective-permute-start | bytes 3145736 | tf_op jit(solution)/shard_map/ppermute | solution.py:299
  43.9 20.7 %collective-permute-start.9 = (bf16[4,448,256]{2,1,0:T(8,128)(2,1)}, bf16[4,448,256]{2,1,0:T(8,128)(2,1)}, u32[]{:S(2)}, u32[]{:S(2)}) collective-permute-start(bf16[4,448,256]{2,1,0:T(8,128)(2,1)} %get-tuple-element.67), channel_id=1, source_target_pairs={{0,4},{4,0},{8,12},{12,8},{16,20},{20,16},{24,28},{28,24},{1,5},{5... | collective-permute-start | bytes 2752520 | tf_op jit(solution)/shard_map/ppermute | solution.py:299
  68.7 14.7 %collective-permute-start.12 = (f16[16,128,128]{2,1,0:T(8,128)(2,1)}, f16[16,128,128]{2,1,0:T(8,128)(2,1)}, u32[]{:S(2)}, u32[]{:S(2)}) collective-permute-start(f16[16,128,128]{2,1,0:T(8,128)(2,1)} %get-tuple-element.114), channel_id=1, source_target_pairs={{0,1},{1,0},{2,3},{3,2},{4,5},{5,4},{6,7},{7,6},{8,9},{9,8},{10,11... | collective-permute-start | bytes 1572872 | tf_op jit(solution)/shard_map/ppermute | solution.py:299
  69.2 14.2 %collective-permute-start.11 = (f16[16,128,128]{2,1,0:T(8,128)(2,1)}, f16[16,128,128]{2,1,0:T(8,128)(2,1)}, u32[]{:S(2)}, u32[]{:S(2)}) collective-permute-start(f16[16,128,128]{2,1,0:T(8,128)(2,1)} %get-tuple-element.115), channel_id=1, source_target_pairs={{0,1},{1,0},{2,3},{3,2},{4,5},{5,4},{6,7},{7,6},{8,9},{9,8},{10,11... | collective-permute-start | bytes 1572872 | tf_op jit(solution)/shard_map/ppermute | solution.py:299
  83.4 25.0 %collective-permute-start.14 = (f16[464,1024]{1,0:T(8,128)(2,1)}, f16[464,1024]{1,0:T(8,128)(2,1)}, u32[]{:S(2)}, u32[]{:S(2)}) collective-permute-start(f16[464,1024]{1,0:T(8,128)(2,1)} %concatenate.82), channel_id=1, source_target_pairs={{0,8},{4,12},{8,0},{12,4},{16,24},{20,28},{24,16},{28,20},{1,9},{5... | collective-permute-start | bytes 2850824 | tf_op jit(solution)/shard_map/ppermute | solution.py:299
  89.1 16.6 %collective-permute-start.13 = (f16[16,128,128]{2,1,0:T(8,128)(2,1)}, f16[16,128,128]{2,1,0:T(8,128)(2,1)}, u32[]{:S(2)}, u32[]{:S(2)}) collective-permute-start(f16[16,128,128]{2,1,0:T(8,128)(2,1)} %get-tuple-element.78), channel_id=1, source_target_pairs={{0,2},{1,3},{2,0},{3,1},{4,6},{5,7},{6,4},{7,5},{8,10},{9,11},{10,... | collective-permute-start | bytes 1572872 | tf_op jit(solution)/shard_map/ppermute | solution.py:299
  90.6 23.7 %collective-permute-start.15 = (f16[4,256,128]{2,1,0:T(8,128)(2,1)S(1)}, f16[4,256,128]{2,1,0:T(8,128)(2,1)}, u32[]{:S(2)}, u32[]{:S(2)}) collective-permute-start(f16[4,256,128]{2,1,0:T(8,128)(2,1)S(1)} %slice.69), channel_id=1, source_target_pairs={{0,4},{4,0},{8,12},{12,8},{16,20},{20,16},{24,28},{28,24},{1,5},{5... | collective-permute-start | bytes 786440 | tf_op jit(solution)/shard_map/ppermute | solution.py:299
  108.4 20.2 %all-to-all-start = ((f16[8,256,128]{2,1,0:T(8,128)(2,1)}), f16[8,256,128]{2,1,0:T(8,128)(2,1)S(1)}, u32[]{:S(2)}, u32[]{:S(2)}) async-start(f16[8,256,128]{2,1,0:T(8,128)(2,1)} %bitcast.13), calls=%async_computation | async-start | bytes 1048576 | tf_op jit(solution)/shard_map/all_to_all | solution.py:498
  116.2 17.6 %collective-permute-start.17 = (f16[16,128,128]{2,1,0:T(8,128)(2,1)S(1)}, f16[16,128,128]{2,1,0:T(8,128)(2,1)}, u32[]{:S(2)}, u32[]{:S(2)}) collective-permute-start(f16[16,128,128]{2,1,0:T(8,128)(2,1)S(1)} %bitcast.51), channel_id=1, source_target_pairs={{0,2},{1,3},{2,0},{3,1},{4,6},{5,7},{6,4},{7,5},{8,10},{9,11},{10,... | collective-permute-start | bytes 1572872 | tf_op jit(solution)/shard_map/ppermute | solution.py:299
  129.6 20.2 %all-to-all-start.1 = ((f16[8,256,128]{2,1,0:T(8,128)(2,1)}), f16[8,256,128]{2,1,0:T(8,128)(2,1)}, u32[]{:S(2)}, u32[]{:S(2)}) async-start(f16[8,256,128]{2,1,0:T(8,128)(2,1)} %broadcast_in_dim.61), calls=%async_computation.1 | async-start | bytes 1048576 | tf_op jit(solution)/shard_map/all_to_all | solution.py:305
  133.8 6.8 %collective-permute-start.16 = (f16[16,128,128]{2,1,0:T(8,128)(2,1)S(1)}, f16[16,128,128]{2,1,0:T(8,128)(2,1)S(1)}, u32[]{:S(2)}, u32[]{:S(2)}) collective-permute-start(f16[16,128,128]{2,1,0:T(8,128)(2,1)S(1)} %bitcast.52), channel_id=1, source_target_pairs={{0,1},{1,0},{2,3},{3,2},{4,5},{5,4},{6,7},{7,6},{8,9},{9,8},{10,11... | collective-permute-start | bytes 1572872 | tf_op jit(solution)/shard_map/ppermute | solution.py:299
  133.8 7.6 %collective-permute-start.18 = (f16[16,128,128]{2,1,0:T(8,128)(2,1)}, f16[16,128,128]{2,1,0:T(8,128)(2,1)}, u32[]{:S(2)}, u32[]{:S(2)}) collective-permute-start(f16[16,128,128]{2,1,0:T(8,128)(2,1)} %collective-permute-done.17), channel_id=1, source_target_pairs={{0,1},{1,0},{2,3},{3,2},{4,5},{5,4},{6,7},{7,6},{8,9},{9,8},{10,11... | collective-permute-start | bytes 1572872 | tf_op jit(solution)/shard_map/ppermute | solution.py:299
  135.0 54.5 %collective-permute-start.21 = (f16[464,1024]{1,0:T(8,128)(2,1)}, f16[464,1024]{1,0:T(8,128)(2,1)}, u32[]{:S(2)}, u32[]{:S(2)}) collective-permute-start(f16[464,1024]{1,0:T(8,128)(2,1)} %concatenate.83), channel_id=1, source_target_pairs={{0,8},{4,12},{8,0},{12,4},{16,24},{20,28},{24,16},{28,20},{1,9},{5... | collective-permute-start | bytes 2850824 | tf_op jit(solution)/shard_map/ppermute | solution.py:299
  138.2 50.5 %collective-permute-start.22 = (f16[464,1024]{1,0:T(8,128)(2,1)}, f16[464,1024]{1,0:T(8,128)(2,1)}, u32[]{:S(2)}, u32[]{:S(2)}) collective-permute-start(f16[464,1024]{1,0:T(8,128)(2,1)} %concatenate.84), channel_id=1, source_target_pairs={{0,16},{4,20},{8,24},{12,28},{16,0},{20,4},{24,8},{28,12},{1,17},{... | collective-permute-start | bytes 2850824 | tf_op jit(solution)/shard_map/ppermute | solution.py:299
  169.8 25.6 %collective-permute-start.24 = (f16[16,128,128]{2,1,0:T(8,128)(2,1)}, f16[16,128,128]{2,1,0:T(8,128)(2,1)S(1)}, u32[]{:S(2)}, u32[]{:S(2)}) collective-permute-start(f16[16,128,128]{2,1,0:T(8,128)(2,1)} %bitcast.15), channel_id=1, source_target_pairs={{0,2},{1,3},{2,0},{3,1},{4,6},{5,7},{6,4},{7,5},{8,10},{9,11},{10,... | collective-permute-start | bytes 1572872 | tf_op jit(solution)/shard_map/ppermute | solution.py:299
  170.8 24.8 %collective-permute-start.23 = (f16[16,128,128]{2,1,0:T(8,128)(2,1)}, f16[16,128,128]{2,1,0:T(8,128)(2,1)S(1)}, u32[]{:S(2)}, u32[]{:S(2)}) collective-permute-start(f16[16,128,128]{2,1,0:T(8,128)(2,1)} %bitcast.15), channel_id=1, source_target_pairs={{0,1},{1,0},{2,3},{3,2},{4,5},{5,4},{6,7},{7,6},{8,9},{9,8},{10,11... | collective-permute-start | bytes 1572872 | tf_op jit(solution)/shard_map/ppermute | solution.py:299
  (27 other events, 265.9 us)
